TPU v7x, 32 devices: a whole 2x2x4 slice. The times are simulated.
32 devices in a mesh: ctx: 4 (over y, x), shard: 8 (over z, core).
Axes of the slice: x: 2, y: 2, z: 4, core: 2. Of those that a mesh axis runs over, the one named last changes fastest.
Arguments:
- tokens: bfloat16 [8, 1024, 1536], P('shard', 'ctx'), may hold values from -6 to 6
- cotangent: bfloat16 [8, 1024, 1536], P('shard', 'ctx'), may hold values from -6 to 6
- routes: int32 [2, 8, 1024, 4], P(None, 'shard', 'ctx'), may hold values from 0 to 7, all different within a row; in each aligned block of 256 rows (0 to 255, 256 to 511, ..., all dimensions but the last counted through in order) at most 160 rows name the same one
- gate_weights: float32 [2, 8, 1024, 4], P(None, 'shard', 'ctx'), may hold values from 0.1 to 0.4
- lengths: int32 [8, 3], P('shard'), may hold values from 1 to 768, 1024 in all within a row
- block_map: int32 [8], replicated, may hold values from 0 to 7, each once
- w_qkv: float32 [2, 1536, 2048], P(None, ('ctx', 'shard')), may hold values from -0.15625 to 0.15625
- w_out: float32 [2, 1536, 1536], P(None, ('ctx', 'shard')), may hold values from -3 to 3
- w_gateup: float32 [2, 8, 1536, 1536], P(None, None, ('ctx', 'shard')), may hold values from -0.15625 to 0.15625
- w_down: float32 [2, 8, 768, 1536], P(None, None, ('ctx', 'shard')), may hold values from -0.625 to 0.625
- gains: float32 [2, 2, 1536], P(None, None, ('ctx', 'shard')), may hold values from 0.5 to 1.5
- m_qkv: float32 [2, 1536, 2048], P(None, ('ctx', 'shard')), may hold values from -64 to 64
- v_qkv: float32 [2, 1536, 2048], P(None, ('ctx', 'shard')), may hold values from 409.6 to 1638.4
- m_out: float32 [2, 1536, 1536], P(None, ('ctx', 'shard')), may hold values from -6 to 6
- v_out: float32 [2, 1536, 1536], P(None, ('ctx', 'shard')), may hold values from 1.6 to 6.4
- m_gateup: float32 [2, 8, 1536, 1536], P(None, None, ('ctx', 'shard')), may hold values from -16 to 16
- v_gateup: float32 [2, 8, 1536, 1536], P(None, None, ('ctx', 'shard')), may hold values from 24.576 to 98.304
- m_down: float32 [2, 8, 768, 1536], P(None, None, ('ctx', 'shard')), may hold values from -6 to 6
- v_down: float32 [2, 8, 768, 1536], P(None, None, ('ctx', 'shard')), may hold values from 4.096 to 16.384
- m_gains: float32 [2, 2, 1536], P(None, None, ('ctx', 'shard')), may hold values from -64 to 64
- v_gains: float32 [2, 2, 1536], P(None, None, ('ctx', 'shard')), may hold values from 409.6 to 1638.4
Outputs:
- output: bfloat16 [8, 1024, 1536], P('shard', 'ctx')
- input_grad: float32 [8, 1024, 1536], P('shard', 'ctx')
- new_qkv: float32 [2, 1536, 2048], P(None, ('ctx', 'shard'))
- moment_qkv: float32 [2, 1536, 2048], P(None, ('ctx', 'shard'))
- second_qkv: float32 [2, 1536, 2048], P(None, ('ctx', 'shard'))
- new_out: float32 [2, 1536, 1536], P(None, ('ctx', 'shard'))
- moment_out: float32 [2, 1536, 1536], P(None, ('ctx', 'shard'))
- second_out: float32 [2, 1536, 1536], P(None, ('ctx', 'shard'))
- new_gateup: float32 [2, 8, 1536, 1536], P(None, None, ('ctx', 'shard'))
- moment_gateup: float32 [2, 8, 1536, 1536], P(None, None, ('ctx', 'shard'))
- second_gateup: float32 [2, 8, 1536, 1536], P(None, None, ('ctx', 'shard'))
- new_down: float32 [2, 8, 768, 1536], P(None, None, ('ctx', 'shard'))
- moment_down: float32 [2, 8, 768, 1536], P(None, None, ('ctx', 'shard'))
- second_down: float32 [2, 8, 768, 1536], P(None, None, ('ctx', 'shard'))
- new_gains: float32 [2, 2, 1536], P(None, None, ('ctx', 'shard'))
- moment_gains: float32 [2, 2, 1536], P(None, None, ('ctx', 'shard'))
- second_gains: float32 [2, 2, 1536], P(None, None, ('ctx', 'shard'))
Inputs may be any that keep to these rules, and one draw needn't show every extreme that they name: `routes`: each row names 4 different experts; among the 256 rows of one device (aligned blocks along the length) no expert is named by more than 160 rows. `block_map`: A permutation; the rows of ctx index i hold the stored blocks 2 i and 2 i + 1, each of 128 positions. `lengths`: the 3 documents of each sequence in position order; they sum to 1024.
All inputs are finite; a program needn't handle non-finite values.
Results may differ from a plain program's by a relative error of at most 0.02.
The roundings to bfloat16 on the way count: a program that leaves them out, or rounds other values in their place, can miss the bound.
Values may be sent and summed in bfloat16 or wider, within the bound.
A program may use at most 576 MiB of HBM per device.

v0:
```python
import jax
import jax.numpy as jnp
from jax import lax
from jax.sharding import PartitionSpec as P

D = 1536
H = 12
KVH = 2
HD = 128
F = 768
TOP = 4
EXPERTS = 8
LAYERS = 2
STEP = 10
CAP = 160


NORM_EPS = 1e-06
ROPE_BASE = 1000000.0
BETA_ONE = 0.9
BETA_TWO = 0.95
ADAM_EPS = 1e-08
DECAY = 0.1
MASKED = -1e30


def rope_tables(positions):
    half_width = HD // 2
    frequency = ROPE_BASE ** (-(jnp.arange(half_width, dtype=jnp.float32) * 2.0 / HD))
    angles = positions.astype(jnp.float32)[:, None] * frequency[None, :]
    return (jnp.cos(angles)[:, None, :], jnp.sin(angles)[:, None, :])


def rotate(vectors, cosine_table, sine_table):
    half_width = vectors.shape[-1] // 2
    first_half = vectors[..., :half_width]
    second_half = vectors[..., half_width:]
    return jnp.concatenate(
        [
            first_half * cosine_table - second_half * sine_table,
            second_half * cosine_table + first_half * sine_table,
        ],
        axis=-1,
    )


def rotate_back(gradient, cosine_table, sine_table):
    half_width = gradient.shape[-1] // 2
    first_half = gradient[..., :half_width]
    second_half = gradient[..., half_width:]
    return jnp.concatenate(
        [
            first_half * cosine_table + second_half * sine_table,
            second_half * cosine_table - first_half * sine_table,
        ],
        axis=-1,
    )


def dispatch(route_rows, gate_rows):
    row_count = route_rows.shape[0]
    flat_routes = route_rows.reshape(-1)
    onehot = (flat_routes[:, None] == jnp.arange(EXPERTS, dtype=jnp.int32)[None, :]).astype(
        jnp.int32
    )
    slot_rank = jnp.sum((jnp.cumsum(onehot, axis=0) - onehot) * onehot, axis=1)
    owners = jnp.arange(flat_routes.shape[0], dtype=jnp.int32) // TOP
    slot_rows = (
        jnp.full((EXPERTS, CAP), row_count, jnp.int32).at[flat_routes, slot_rank].set(owners)
    )
    slot_gates = (
        jnp.zeros((EXPERTS, CAP), jnp.float32).at[flat_routes, slot_rank].set(gate_rows.reshape(-1))
    )
    return (slot_rows, slot_gates)


def positions_docs(block_map, lengths_row, first_block, block_count, block_rows):
    blocks = lax.dynamic_slice_in_dim(block_map, first_block, block_count)
    offsets = jnp.arange(block_rows, dtype=jnp.int32)
    positions = (blocks[:, None] * block_rows + offsets[None, :]).reshape(-1)
    bounds = jnp.cumsum(lengths_row)
    documents = jnp.sum((positions[:, None] >= bounds[None, :]).astype(jnp.int32), axis=1)
    return (positions, documents)


def normalize(values, gain_row):
    row_scale = lax.rsqrt(jnp.mean(values * values, axis=-1, keepdims=True) + NORM_EPS)
    return (values * row_scale * gain_row, row_scale)


def normalize_back(gradient, values, row_scale, gain_row):
    unit_rows = values * row_scale
    inner_grad = gradient * gain_row
    input_grad = row_scale * (
        inner_grad - unit_rows * jnp.mean(inner_grad * unit_rows, axis=-1, keepdims=True)
    )
    return (input_grad, jnp.sum(gradient * unit_rows, axis=0))


def adamw(parameter, moment, second, gradient, step_rate, decay_rate):
    moment = BETA_ONE * moment + (1.0 - BETA_ONE) * gradient
    second = BETA_TWO * second + (1.0 - BETA_TWO) * gradient * gradient
    direction = (
        moment / (1.0 - BETA_ONE**STEP) / (jnp.sqrt(second / (1.0 - BETA_TWO**STEP)) + ADAM_EPS)
    )
    return (parameter - step_rate * (direction + decay_rate * parameter), moment, second)


def layer_shards(w_qkv, w_out, w_gateup, w_down, gains, layer_index):
    return (
        w_qkv[layer_index].astype(jnp.bfloat16),
        w_out[layer_index].astype(jnp.bfloat16),
        w_gateup[layer_index].astype(jnp.bfloat16),
        w_down[layer_index].astype(jnp.bfloat16),
        gains[layer_index].astype(jnp.bfloat16),
    )


def gather_forward(shards):
    return (
        lax.all_gather(shards[0], ("ctx", "shard"), axis=0, tiled=True),
        lax.all_gather(shards[1], ("ctx", "shard"), axis=0, tiled=True),
        lax.all_gather(shards[2], ("ctx", "shard"), axis=1, tiled=True),
        lax.all_gather(shards[3], ("ctx", "shard"), axis=1, tiled=True),
        lax.all_gather(shards[4], ("ctx", "shard"), axis=1, tiled=True),
    )


def gather_backward(shards):
    return (
        lax.all_gather(shards[0], ("ctx", "shard"), axis=0, tiled=True),
        lax.all_gather(shards[1], ("ctx", "shard"), axis=0, tiled=True),
        lax.all_gather(shards[2], ("ctx", "shard"), axis=1, tiled=True),
        lax.all_gather(shards[3], ("ctx", "shard"), axis=1, tiled=True),
        lax.all_gather(shards[4], ("ctx", "shard"), axis=1, tiled=True),
    )


def glu_value(gate_input, up_input):
    return jax.nn.gelu(gate_input, approximate=False) * up_input


def attention_forward(queries, keys_all, values_all, allowed):
    group_size = H // KVH
    score_scale = HD ** (-0.5)
    outputs = []
    totals = []
    for head_group in range(KVH):
        query_part = queries[:, head_group * group_size : (head_group + 1) * group_size, :]
        scores = (
            jnp.einsum(
                "tjd,kd->jtk",
                query_part,
                keys_all[:, head_group, :],
                preferred_element_type=jnp.float32,
            )
            * score_scale
        )
        scores = jnp.where(allowed[None], scores, MASKED)
        row_max = jnp.max(scores, axis=-1, keepdims=True)
        exponent = jnp.exp(scores - row_max)
        row_total = jnp.sum(exponent, axis=-1, keepdims=True)
        probabilities = (exponent / row_total).astype(jnp.bfloat16)
        outputs.append(
            jnp.einsum(
                "jtk,kd->tjd",
                probabilities,
                values_all[:, head_group, :],
                preferred_element_type=jnp.float32,
            )
        )
        totals.append(row_max + jnp.log(row_total))
    return (jnp.concatenate(outputs, axis=1), totals)


def attention_backward(queries, keys_all, values_all, allowed, totals, grad_attended):
    group_size = H // KVH
    score_scale = HD ** (-0.5)
    grad_queries = []
    grad_keys = []
    grad_values = []
    for head_group in range(KVH):
        query_part = queries[:, head_group * group_size : (head_group + 1) * group_size, :]
        grad_part = grad_attended[:, head_group * group_size : (head_group + 1) * group_size, :]
        keys_part = keys_all[:, head_group, :]
        scores = (
            jnp.einsum("tjd,kd->jtk", query_part, keys_part, preferred_element_type=jnp.float32)
            * score_scale
        )
        probabilities = jnp.where(allowed[None], jnp.exp(scores - totals[head_group]), 0.0)
        grad_probs = jnp.einsum(
            "tjd,kd->jtk",
            grad_part,
            values_all[:, head_group, :],
            preferred_element_type=jnp.float32,
        )
        grad_scores = probabilities * (
            grad_probs - jnp.sum(probabilities * grad_probs, axis=-1, keepdims=True)
        )
        grad_scores = grad_scores.astype(jnp.bfloat16)
        grad_queries.append(
            jnp.einsum("jtk,kd->tjd", grad_scores, keys_part, preferred_element_type=jnp.float32)
            * score_scale
        )
        grad_keys.append(
            jnp.einsum("jtk,tjd->kd", grad_scores, query_part, preferred_element_type=jnp.float32)
            * score_scale
        )
        grad_values.append(
            jnp.einsum(
                "jtk,tjd->kd",
                probabilities.astype(jnp.bfloat16),
                grad_part,
                preferred_element_type=jnp.float32,
            )
        )
    return (
        jnp.concatenate(grad_queries, axis=1),
        jnp.stack(grad_keys, axis=1),
        jnp.stack(grad_values, axis=1),
    )


def layer_forward(stream, weights, route_rows, gate_rows, allowed, cosine_table, sine_table):
    qkv_w, out_w, gateup_w, down_w, gain_w = weights
    row_count = stream.shape[0]
    gain_full = gain_w.astype(jnp.float32)
    normed, scale_one = normalize(stream, gain_full[0])
    attn_in = normed.astype(jnp.bfloat16)
    projected = jnp.dot(attn_in, qkv_w, preferred_element_type=jnp.float32)
    queries = rotate(
        projected[:, : H * HD].reshape(row_count, H, HD), cosine_table, sine_table
    ).astype(jnp.bfloat16)
    keys_local = rotate(
        projected[:, H * HD : (H + KVH) * HD].reshape(row_count, KVH, HD), cosine_table, sine_table
    ).astype(jnp.bfloat16)
    values_local = projected[:, (H + KVH) * HD :].reshape(row_count, KVH, HD).astype(jnp.bfloat16)
    keys_all, values_all = (
        lax.all_gather(keys_local, "ctx", axis=0, tiled=True),
        lax.all_gather(values_local, "ctx", axis=0, tiled=True),
    )
    attended, totals = attention_forward(queries, keys_all, values_all, allowed)
    attended_low = attended.reshape(row_count, H * HD).astype(jnp.bfloat16)
    middle_stream = stream + jnp.dot(attended_low, out_w, preferred_element_type=jnp.float32)
    normed_two, scale_two = normalize(middle_stream, gain_full[1])
    expert_in = normed_two.astype(jnp.bfloat16)
    slot_rows, slot_gates = dispatch(route_rows, gate_rows)
    padded = jnp.concatenate([expert_in, jnp.zeros((1, D), jnp.bfloat16)], axis=0)
    slot_in = padded[slot_rows]
    gate_up = jnp.einsum("ecd,edf->ecf", slot_in, gateup_w, preferred_element_type=jnp.float32)
    activated = glu_value(gate_up[..., :F], gate_up[..., F:]).astype(jnp.bfloat16)
    result = jnp.einsum(
        "ecf,efd->ecd", activated, down_w, preferred_element_type=jnp.float32
    ).astype(jnp.bfloat16)
    weighted = result.astype(jnp.float32) * slot_gates[..., None]
    merged = (
        jnp.zeros((row_count + 1, D), jnp.float32)
        .at[slot_rows.reshape(-1)]
        .add(weighted.reshape(-1, D))
    )
    record = {
        "stream": stream,
        "scale_one": scale_one,
        "attn_in": attn_in,
        "queries": queries,
        "keys_all": keys_all,
        "values_all": values_all,
        "totals": totals,
        "attended": attended_low,
        "middle": middle_stream,
        "scale_two": scale_two,
        "slot_rows": slot_rows,
        "slot_gates": slot_gates,
        "slot_in": slot_in,
        "gate_up": gate_up,
        "activated": activated,
        "weights": weights,
    }
    return (record, middle_stream + merged[:row_count])


def layer_backward(gradient, record, weights, allowed, cosine_table, sine_table):
    qkv_w, out_w, gateup_w, down_w, gain_w = weights
    gain_full = gain_w.astype(jnp.float32)
    row_count = gradient.shape[0]
    slot_rows = record["slot_rows"]
    padded_grad = jnp.concatenate([gradient, jnp.zeros((1, D), jnp.float32)], axis=0)
    slot_grad = (padded_grad[slot_rows] * record["slot_gates"][..., None]).astype(jnp.bfloat16)
    grad_down = jnp.einsum(
        "ecf,ecd->efd", record["activated"], slot_grad, preferred_element_type=jnp.float32
    )
    grad_act = jnp.einsum("ecd,efd->ecf", slot_grad, down_w, preferred_element_type=jnp.float32)
    gate_up = record["gate_up"]
    unused, pull = jax.vjp(glu_value, gate_up[..., :F], gate_up[..., F:])
    grad_gate, grad_up = pull(grad_act)
    grad_glu = jnp.concatenate([grad_gate, grad_up], axis=-1).astype(jnp.bfloat16)
    grad_gateup = jnp.einsum(
        "ecd,ecf->edf", record["slot_in"], grad_glu, preferred_element_type=jnp.float32
    )
    grad_slots = jnp.einsum("ecf,edf->ecd", grad_glu, gateup_w, preferred_element_type=jnp.float32)
    grad_normed = (
        jnp.zeros((row_count + 1, D), jnp.float32)
        .at[slot_rows.reshape(-1)]
        .add(grad_slots.reshape(-1, D))[:row_count]
    )
    grad_in_two, grad_gain_two = normalize_back(
        grad_normed, record["middle"], record["scale_two"], gain_full[1]
    )
    grad_middle = gradient + grad_in_two
    grad_middle_low = grad_middle.astype(jnp.bfloat16)
    grad_out = jnp.dot(record["attended"].T, grad_middle_low, preferred_element_type=jnp.float32)
    grad_attended = jnp.dot(grad_middle_low, out_w.T, preferred_element_type=jnp.float32)
    grad_attended = grad_attended.astype(jnp.bfloat16).reshape(row_count, H, HD)
    grad_queries, grad_keys_all, grad_values_all = attention_backward(
        record["queries"],
        record["keys_all"],
        record["values_all"],
        allowed,
        record["totals"],
        grad_attended,
    )
    grad_keys, grad_values = (
        lax.psum_scatter(
            grad_keys_all.astype(jnp.bfloat16), "ctx", scatter_dimension=0, tiled=True
        ).astype(jnp.float32),
        lax.psum_scatter(
            grad_values_all.astype(jnp.bfloat16), "ctx", scatter_dimension=0, tiled=True
        ).astype(jnp.float32),
    )
    grad_projected = jnp.concatenate(
        [
            rotate_back(grad_queries, cosine_table, sine_table).reshape(row_count, H * HD),
            rotate_back(grad_keys, cosine_table, sine_table).reshape(row_count, KVH * HD),
            grad_values.reshape(row_count, KVH * HD),
        ],
        axis=1,
    ).astype(jnp.bfloat16)
    grad_qkv = jnp.dot(record["attn_in"].T, grad_projected, preferred_element_type=jnp.float32)
    grad_normed_one = jnp.dot(grad_projected, qkv_w.T, preferred_element_type=jnp.float32)
    grad_in_one, grad_gain_one = normalize_back(
        grad_normed_one, record["stream"], record["scale_one"], gain_full[0]
    )
    grad_gains = jnp.stack([grad_gain_one, grad_gain_two])
    return (grad_middle + grad_in_one, (grad_qkv, grad_out, grad_gateup, grad_down, grad_gains))


def on_device(
    tokens,
    cotangent,
    routes,
    gate_weights,
    lengths,
    block_map,
    w_qkv,
    w_out,
    w_gateup,
    w_down,
    gains,
    m_qkv,
    v_qkv,
    m_out,
    v_out,
    m_gateup,
    v_gateup,
    m_down,
    v_down,
    m_gains,
    v_gains,
):
    row_count = tokens.shape[1]
    ctx_size = lax.axis_size("ctx")
    block_rows = row_count // 2
    own_pos, own_doc = positions_docs(
        block_map, lengths[0], 2 * lax.axis_index("ctx"), 2, block_rows
    )
    key_pos, key_doc = positions_docs(block_map, lengths[0], 0, 2 * ctx_size, block_rows)
    allowed = (own_doc[:, None] == key_doc[None, :]) & (key_pos[None, :] <= own_pos[:, None])
    cosine_table, sine_table = rope_tables(own_pos)
    stream = tokens[0].astype(jnp.float32)
    records = []
    for layer_index in range(LAYERS):
        weights = gather_forward(layer_shards(w_qkv, w_out, w_gateup, w_down, gains, layer_index))
        record, stream = layer_forward(
            stream,
            weights,
            routes[layer_index, 0],
            gate_weights[layer_index, 0],
            allowed,
            cosine_table,
            sine_table,
        )
        records.append(record)
    output = stream.astype(jnp.bfloat16)[None]
    gradient = cotangent[0].astype(jnp.float32)
    rates = (D ** (-0.5), 0.5, D ** (-0.5), (F // 8) ** (-0.5), 1.0)
    decays = (DECAY, DECAY, DECAY, DECAY, 0.0)
    params = (w_qkv, w_out, w_gateup, w_down, gains)
    firsts = (m_qkv, m_out, m_gateup, m_down, m_gains)
    seconds = (v_qkv, v_out, v_gateup, v_down, v_gains)
    updated = [[None] * LAYERS for which in range(15)]
    for layer_index in reversed(range(LAYERS)):
        weights = gather_backward(layer_shards(w_qkv, w_out, w_gateup, w_down, gains, layer_index))
        gradient, layer_grads = layer_backward(
            gradient, records[layer_index], weights, allowed, cosine_table, sine_table
        )
        reduced = (
            lax.psum_scatter(layer_grads[0], ("ctx", "shard"), scatter_dimension=0, tiled=True),
            lax.psum_scatter(layer_grads[1], ("ctx", "shard"), scatter_dimension=0, tiled=True),
            lax.psum_scatter(layer_grads[2], ("ctx", "shard"), scatter_dimension=1, tiled=True),
            lax.psum_scatter(layer_grads[3], ("ctx", "shard"), scatter_dimension=1, tiled=True),
            lax.psum_scatter(layer_grads[4], ("ctx", "shard"), scatter_dimension=1, tiled=True),
        )
        for which in range(5):
            fresh = adamw(
                params[which][layer_index],
                firsts[which][layer_index],
                seconds[which][layer_index],
                reduced[which],
                rates[which],
                decays[which],
            )
            updated[3 * which][layer_index] = fresh[0]
            updated[3 * which + 1][layer_index] = fresh[1]
            updated[3 * which + 2][layer_index] = fresh[2]
    stacked = [jnp.stack(pieces) for pieces in updated]
    return (
        output,
        gradient[None],
        stacked[0],
        stacked[1],
        stacked[2],
        stacked[3],
        stacked[4],
        stacked[5],
        stacked[6],
        stacked[7],
        stacked[8],
        stacked[9],
        stacked[10],
        stacked[11],
        stacked[12],
        stacked[13],
        stacked[14],
    )


def solution(mesh):
    placed = (
        P("shard", "ctx", None),
        P("shard", "ctx", None),
        P(None, "shard", "ctx", None),
        P(None, "shard", "ctx", None),
        P("shard", None),
        P(),
        P(None, ("ctx", "shard"), None),
        P(None, ("ctx", "shard"), None),
        P(None, None, ("ctx", "shard"), None),
        P(None, None, ("ctx", "shard"), None),
        P(None, None, ("ctx", "shard")),
        P(None, ("ctx", "shard"), None),
        P(None, ("ctx", "shard"), None),
        P(None, ("ctx", "shard"), None),
        P(None, ("ctx", "shard"), None),
        P(None, None, ("ctx", "shard"), None),
        P(None, None, ("ctx", "shard"), None),
        P(None, None, ("ctx", "shard"), None),
        P(None, None, ("ctx", "shard"), None),
        P(None, None, ("ctx", "shard")),
        P(None, None, ("ctx", "shard")),
    )
    return jax.shard_map(
        on_device,
        mesh=mesh,
        in_specs=placed,
        out_specs=(
            P("shard", "ctx", None),
            P("shard", "ctx", None),
            P(None, ("ctx", "shard"), None),
            P(None, ("ctx", "shard"), None),
            P(None, ("ctx", "shard"), None),
            P(None, ("ctx", "shard"), None),
            P(None, ("ctx", "shard"), None),
            P(None, ("ctx", "shard"), None),
            P(None, None, ("ctx", "shard"), None),
            P(None, None, ("ctx", "shard"), None),
            P(None, None, ("ctx", "shard"), None),
            P(None, None, ("ctx", "shard"), None),
            P(None, None, ("ctx", "shard"), None),
            P(None, None, ("ctx", "shard"), None),
            P(None, None, ("ctx", "shard")),
            P(None, None, ("ctx", "shard")),
            P(None, None, ("ctx", "shard")),
        ),
        check_vma=False,
    )
```

profile of v0, /device:TPU:0, one launch (start us, length us, event | category | flops | bytes accessed | tf_op | source)
XLA Modules:
  0.0 4190.6 jit_solution(4968963975998092522)
XLA Ops:
  20.6 43.2 %all-gather.1 = bf16[32,48,2]{1,2,0:T(2,128)(2,1)S(1)} all-gather(bf16[1,48,2]{1,2,0:T(2,128)(2,1)S(1)} %get-tuple-element.123), channel_id=1, replica_groups=mesh['ctx'=4,'shard'=8] {'ctx','shard'}, dimensions={0}, use_global_device_ids=true | all-gather | bytes 6336 | tf_op jit(solution)/shard_map/all_gather | solution.py:125
  63.9 36.6 all-gather
  106.8 4.3 scatter_custom_fusion.7
  116.2 4.3 scatter_custom_fusion.4
  121.1 4.6 scatter_custom_fusion.5
  126.1 6.0 gather_fusion.2
  134.5 4.7 fusion.221
  147.4 9.5 all_gather.55
  157.0 19.5 all_gather.54
  191.1 5.6 gather_fusion
  197.9 169.6 %all-gather.15.cloned.1.call-done = bf16[8,1536,1536]{2,1,0:T(8,128)(2,1)} async-done(((bf16[8,48,1536]{2,1,0:T(8,128)(2,1)}), bf16[8,1536,1536]{2,1,0:T(8,128)(2,1)}) %all-gather.15.cloned.1.call-update) | async-done | bytes 37748752 | tf_op jit(solution)/shard_map/all_gather | solution.py:123
  367.5 20.1 fusion.302
  387.6 11.1 multiply_convert_fusion.5
  398.7 95.3 %all-gather.17.cloned.1.call-done = bf16[8,768,1536]{2,1,0:T(8,128)(2,1)} async-done(((bf16[8,24,1536]{2,1,0:T(8,128)(2,1)}), bf16[8,768,1536]{2,1,0:T(8,128)(2,1)}) %all-gather.17.cloned.1.call-update) | async-done | bytes 18874384 | tf_op jit(solution)/shard_map/all_gather | solution.py:124
  494.0 13.2 convert_multiply_fusion.1
  507.2 18.0 scatter_custom_fusion
  528.1 37.0 all-gather.19.cloned.1.call-done
  565.0 5.1 fusion.293
  580.0 10.0 all_gather.62
  590.0 14.4 all_gather.61
  616.8 15.2 all-gather.21.cloned.1.call-done
  636.4 5.6 gather_fusion.1
  642.0 207.6 %all-gather.23.cloned.1.call-done = bf16[8,1536,1536]{2,1,0:T(8,128)(2,1)} async-done(((bf16[8,48,1536]{2,1,0:T(8,128)(2,1)}), bf16[8,1536,1536]{2,1,0:T(8,128)(2,1)}) %all-gather.23.cloned.1.call-update) | async-done | bytes 37748752 | tf_op jit(solution)/shard_map/all_gather | solution.py:123
  849.7 20.0 fusion.303
  869.7 106.6 %all-gather.25.cloned.1.call-done = bf16[8,768,1536]{2,1,0:T(8,128)(2,1)} async-done(((bf16[8,24,1536]{2,1,0:T(8,128)(2,1)}), bf16[8,768,1536]{2,1,0:T(8,128)(2,1)}) %all-gather.25.cloned.1.call-update) | async-done | bytes 18874384 | tf_op jit(solution)/shard_map/all_gather | solution.py:124
  976.3 22.0 add_convert_fusion.1
  998.3 8.0 multiply_convert_fusion.3
  1006.3 21.0 fusion.65
  1027.3 18.0 scatter_custom_fusion.2
  1045.4 12.7 convert_multiply_fusion
  1058.0 18.4 scatter_custom_fusion.1
  1088.1 9.0 fusion.9
  1097.8 7.3 fusion.11
  1128.7 4.9 reduce-scatter.19.cloned.1.call-done
  1135.5 26.3 reduce-scatter.21.cloned.1.call-done
  1163.5 6.3 multiply_reduce_fusion.1
  1176.0 6.2 gather_fusion.3
  1182.2 17.5 add_convert_fusion
  1199.7 20.4 fusion.63
  1220.1 18.2 scatter_custom_fusion.3
  1242.9 4.3 convolution_convert_fusion.2
  1250.7 8.8 fusion.3
  1259.6 7.2 fusion.5
  1287.7 9.3 reduce-scatter.23.cloned.1.call-done
  1298.3 27.0 reduce-scatter.25.cloned.1.call-done
  1326.4 6.8 fusion.84
  1334.5 5.0 fusion.189
  1341.2 5.0 fusion.186
  1347.8 7.1 fusion.174
  1356.1 6.4 fusion.172
  1364.1 18.2 fusion.87
  1383.9 18.2 fusion.89
  1403.6 28.7 fusion.64
  1433.9 29.1 fusion.62
  1467.6 57.8 %reduce-scatter.43.cloned.1.call-done = f32[48,2]{1,0:T(8,128)} async-done(((f32[1536,2]{1,0:T(8,128)}), f32[48,2]{1,0:T(8,128)}) %reduce-scatter.43.cloned.1.call-update) | async-done | bytes 400
  1528.0 137.8 %reduce-scatter.33.cloned.1.call-done = f32[48,1536]{1,0:T(8,128)} async-done(((f32[1536,1536]{1,0:T(8,128)}), f32[48,1536]{1,0:T(8,128)}) %reduce-scatter.33.cloned.1.call-update) | async-done | bytes 294928 | tf_op jit(solution)/shard_map/reduce_scatter | solution.py:408
  1665.8 141.4 %reduce-scatter.31.cloned.1.call-done = f32[48,1536]{1,0:T(8,128)} async-done(((f32[1536,1536]{1,0:T(8,128)}), f32[48,1536]{1,0:T(8,128)}) %reduce-scatter.31.cloned.1.call-update) | async-done | bytes 294928 | tf_op jit(solution)/shard_map/reduce_scatter | solution.py:408
  1811.8 155.8 %reduce-scatter.29.cloned.1.call-done = f32[48,2048]{1,0:T(8,128)} async-done(((f32[1536,2048]{1,0:T(8,128)}), f32[48,2048]{1,0:T(8,128)}) %reduce-scatter.29.cloned.1.call-update) | async-done | bytes 393232 | tf_op jit(solution)/shard_map/reduce_scatter | solution.py:407
  1967.6 161.4 %reduce-scatter.27.cloned.1.call-done = f32[48,2048]{1,0:T(8,128)} async-done(((f32[1536,2048]{1,0:T(8,128)}), f32[48,2048]{1,0:T(8,128)}) %reduce-scatter.27.cloned.1.call-update) | async-done | bytes 393232 | tf_op jit(solution)/shard_map/reduce_scatter | solution.py:407
  2134.1 347.7 %reduce-scatter.41.cloned.1.call-done = f32[8,24,1536]{2,1,0:T(8,128)} async-done(((f32[8,768,1536]{2,1,0:T(8,128)}), f32[8,24,1536]{2,1,0:T(8,128)}) %reduce-scatter.41.cloned.1.call-update) | async-done | bytes 1179664 | tf_op jit(solution)/shard_map/reduce_scatter | solution.py:410
  2481.8 353.4 %reduce-scatter.39.cloned.1.call-done = f32[8,24,1536]{2,1,0:T(8,128)} async-done(((f32[8,768,1536]{2,1,0:T(8,128)}), f32[8,24,1536]{2,1,0:T(8,128)}) %reduce-scatter.39.cloned.1.call-update) | async-done | bytes 1179664 | tf_op jit(solution)/shard_map/reduce_scatter | solution.py:410
  2843.8 656.9 %reduce-scatter.37.cloned.1.call-done = f32[8,48,1536]{2,1,0:T(8,128)} async-done(((f32[8,1536,1536]{2,1,0:T(8,128)}), f32[8,48,1536]{2,1,0:T(8,128)}) %reduce-scatter.37.cloned.1.call-update) | async-done | bytes 2359312 | tf_op jit(solution)/shard_map/reduce_scatter | solution.py:409
  3500.7 666.5 %reduce-scatter.35.cloned.1.call-done = f32[8,48,1536]{2,1,0:T(8,128)} async-done(((f32[8,1536,1536]{2,1,0:T(8,128)}), f32[8,48,1536]{2,1,0:T(8,128)}) %reduce-scatter.35.cloned.1.call-update) | async-done | bytes 2359312 | tf_op jit(solution)/shard_map/reduce_scatter | solution.py:409
  4167.3 8.2 fusion.77
  (486 shorter events, 202.2 us)
Async XLA Ops:
  7.2 127.3 %all-gather.11.cloned.1.call-start = ((), (), s32[]{:S(2)}) async-start(), calls=%async_computation.14 | async-start | bytes 6488064 | tf_op jit(solution)/shard_map/all_gather | solution.py:121
  9.3 177.1 %all-gather.13.cloned.1.call-start = ((), (), s32[]{:S(2)}) async-start(), calls=%async_computation.15 | async-start | bytes 4866048 | tf_op jit(solution)/shard_map/all_gather | solution.py:122
  11.2 356.3 %all-gather.15.cloned.1.call-start = ((), (), s32[]{:S(2)}) async-start(), calls=%async_computation.16 | async-start | bytes 38928384 | tf_op jit(solution)/shard_map/all_gather | solution.py:123
  15.4 88.0 %copy-start.96 = (f32[2,1,256,4]{2,3,1,0:T(4,128)S(1)}, f32[2,1,256,4]{2,3,1,0:T(4,128)}, u32[]{:S(2)}) copy-start(f32[2,1,256,4]{2,3,1,0:T(4,128)} %param.24) | copy-start | bytes 24580
  15.4 91.2 %copy-start.104 = (s32[2]{0:T(128)S(1)}, s32[2]{0:T(128)}, u32[]{:S(2)}) copy-start(s32[2]{0:T(128)} %constant.245) | copy-start | bytes 28
  15.4 91.3 %copy-start.103 = (s32[2]{0:T(128)S(1)}, s32[2]{0:T(128)}, u32[]{:S(2)}) copy-start(s32[2]{0:T(128)} %constant.248) | copy-start | bytes 28
  15.4 110.3 %copy-start.55 = (bf16[1,256,1536]{2,1,0:T(8,128)(2,1)S(1)}, bf16[1,256,1536]{2,1,0:T(8,128)(2,1)}, u32[]{:S(2)}) copy-start(bf16[1,256,1536]{2,1,0:T(8,128)(2,1)} %param.22) | copy-start | bytes 2359300
  15.4 478.6 %all-gather.17.cloned.1.call-start = ((), (), s32[]{:S(2)}) async-start(), calls=%async_computation.17 | async-start | bytes 19464192 | tf_op jit(solution)/shard_map/all_gather | solution.py:124
  16.7 548.4 %all-gather.19.cloned.1.call-start = ((), (), s32[]{:S(2)}) async-start(), calls=%async_computation.18 | async-start | bytes 6488064 | tf_op jit(solution)/shard_map/all_gather | solution.py:121
  17.2 614.8 %all-gather.21.cloned.1.call-start = ((), (), s32[]{:S(2)}) async-start(), calls=%async_computation.19 | async-start | bytes 4866048 | tf_op jit(solution)/shard_map/all_gather | solution.py:122
  17.8 831.9 %all-gather.23.cloned.1.call-start = ((), (), s32[]{:S(2)}) async-start(), calls=%async_computation.20 | async-start | bytes 38928384 | tf_op jit(solution)/shard_map/all_gather | solution.py:123
  18.6 957.8 %all-gather.25.cloned.1.call-start = ((), (), s32[]{:S(2)}) async-start(), calls=%async_computation.21 | async-start | bytes 19464192 | tf_op jit(solution)/shard_map/all_gather | solution.py:124
  19.3 1114.2 %reduce-scatter.19.cloned.1.call-start = ((), (), s32[]{:S(2)}) async-start(), calls=%async_computation.22 | async-start | bytes 655360 | tf_op jit(solution)/shard_map/reduce_scatter | solution.py:323
  125.8 368.2 %copy-start.69 = (f32[8,160]{1,0:T(8,128)}, f32[8,160]{1,0:T(8,128)S(1)}, u32[]{:S(2)}) copy-start(f32[8,160]{1,0:T(8,128)S(1)} %reshape.630) | copy-start | bytes 15364
  132.1 375.1 %copy-start.97 = (s32[1280]{0:T(1024)}, s32[1280]{0:T(1024)S(1)}, u32[]{:S(2)}) copy-start(s32[1280]{0:T(1024)S(1)} %fusion.239) | copy-start | bytes 15364
  132.9 58.2 %copy-start.86 = (s32[2048]{0:T(1024)}, s32[2048]{0:T(1024)S(1)}, u32[]{:S(2)}) copy-start(s32[2048]{0:T(1024)S(1)} %pad_clamp_fusion.1) | copy-start | bytes 24580
  133.2 431.8 %copy-start.80 = (f32[1536]{0:T(1024)}, f32[1536]{0:T(1024)S(1)}, u32[]{:S(2)}) copy-start(f32[1536]{0:T(1024)S(1)} %get-tuple-element.34) | copy-start | bytes 18436
  133.3 57.5 %copy-start.82 = (f32[1536]{0:T(1024)}, f32[1536]{0:T(1024)S(1)}, u32[]{:S(2)}) copy-start(f32[1536]{0:T(1024)S(1)} %get-tuple-element.35) | copy-start | bytes 18436
  134.1 470.3 %copy-start.39 = (f32[256,64]{1,0:T(8,128)}, f32[256,64]{1,0:T(8,128)S(1)}, u32[]{:S(2)}) copy-start(f32[256,64]{1,0:T(8,128)S(1)} %get-tuple-element.125) | copy-start | bytes 196612
  134.1 470.3 %copy-start.41 = (f32[256,64]{1,0:T(8,128)}, f32[256,64]{1,0:T(8,128)S(1)}, u32[]{:S(2)}) copy-start(f32[256,64]{1,0:T(8,128)S(1)} %get-tuple-element.126) | copy-start | bytes 196612
  146.9 29.6 copy-start.46
  157.0 21.6 copy-start.50
  190.8 334.5 %copy-start.4 = (f32[256,1536]{1,0:T(8,128)}, f32[256,1536]{1,0:T(8,128)S(1)}, u32[]{:S(2)}) copy-start(f32[256,1536]{1,0:T(8,128)S(1)} %get-tuple-element.133) | copy-start | bytes 4718596
  528.1 42.1 %copy-start.92 = (f32[256]{0:T(256)}, f32[256]{0:T(256)S(1)}, u32[]{:S(2)}) copy-start(f32[256]{0:T(256)S(1)} %add_rsqrt_fusion.1) | copy-start | bytes 3076
  590.0 18.1 copy-start.52
  604.4 9.5 copy-start.64
  613.9 18.1 copy-start.12
  849.7 126.7 %copy-start.67 = (f32[8,160]{1,0:T(8,128)S(1)}, f32[8,160]{1,0:T(8,128)}, u32[]{:S(2)}) copy-start(f32[8,160]{1,0:T(8,128)} %reshape.638) | copy-start | bytes 15364
  1006.3 39.0 copy-start.9
  1058.0 20.9 copy-start.22
  1058.0 20.9 copy-start.56
  1087.0 10.0 copy-start.58
  1087.0 10.0 slice-start.4
  1087.0 10.0 slice-start.6
  1088.0 9.0 slice-start.5
  1088.0 9.7 slice-start.7
  1110.4 51.4 %reduce-scatter.21.cloned.1.call-start = ((), (), s32[]{:S(2)}) async-start(), calls=%async_computation.23 | async-start | bytes 655360 | tf_op jit(solution)/shard_map/reduce_scatter | solution.py:326
  1122.7 174.3 %reduce-scatter.23.cloned.1.call-start = ((), (), s32[]{:S(2)}) async-start(), calls=%async_computation.24 | async-start | bytes 655360 | tf_op jit(solution)/shard_map/reduce_scatter | solution.py:323
  1127.0 36.5 copy-start.13
  1127.0 36.4 copy-start.81
  1163.5 9.4 copy-start.16
  1199.7 38.7 copy-start.5
  1199.7 38.7 copy-start.83
  1199.7 38.7 copy-start.94
  1248.4 11.1 slice-start
  1248.4 11.1 slice-start.2
  1272.1 53.2 %reduce-scatter.25.cloned.1.call-start = ((), (), s32[]{:S(2)}) async-start(), calls=%async_computation.25 | async-start | bytes 655360 | tf_op jit(solution)/shard_map/reduce_scatter | solution.py:326
  1281.3 181.8 %reduce-scatter.45.cloned.1.call-start = ((), (), s32[]{:S(2)}) async-start(), calls=%async_computation.35 | async-start | bytes 811008
  1286.0 40.3 copy-start.28
  1286.0 40.3 copy-start.78
  1287.7 237.7 %reduce-scatter.43.cloned.1.call-start = ((), (), s32[]{:S(2)}) async-start(), calls=%async_computation.34 | async-start | bytes 811008
  1334.5 331.4 %reduce-scatter.33.cloned.1.call-start = ((), (), s32[]{:S(2)}) async-start(), calls=%async_computation.29 | async-start | bytes 9732096 | tf_op jit(solution)/shard_map/reduce_scatter | solution.py:408
  1339.6 467.6 %reduce-scatter.31.cloned.1.call-start = ((), (), s32[]{:S(2)}) async-start(), calls=%async_computation.28 | async-start | bytes 9732096 | tf_op jit(solution)/shard_map/reduce_scatter | solution.py:408
  1346.2 621.4 %reduce-scatter.29.cloned.1.call-start = ((), (), s32[]{:S(2)}) async-start(), calls=%async_computation.27 | async-start | bytes 12976128 | tf_op jit(solution)/shard_map/reduce_scatter | solution.py:407
  1355.0 774.1 %reduce-scatter.27.cloned.1.call-start = ((), (), s32[]{:S(2)}) async-start(), calls=%async_computation.26 | async-start | bytes 12976128 | tf_op jit(solution)/shard_map/reduce_scatter | solution.py:407
  1362.6 1119.2 %reduce-scatter.41.cloned.1.call-start = ((), (), s32[]{:S(2)}) async-start(), calls=%async_computation.33 | async-start | bytes 38928384 | tf_op jit(solution)/shard_map/reduce_scatter | solution.py:410
  1382.4 1452.8 %reduce-scatter.39.cloned.1.call-start = ((), (), s32[]{:S(2)}) async-start(), calls=%async_computation.32 | async-start | bytes 38928384 | tf_op jit(solution)/shard_map/reduce_scatter | solution.py:410
  1402.1 2098.6 %reduce-scatter.37.cloned.1.call-start = ((), (), s32[]{:S(2)}) async-start(), calls=%async_computation.31 | async-start | bytes 77856768 | tf_op jit(solution)/shard_map/reduce_scatter | solution.py:409
  1432.4 2734.9 %reduce-scatter.35.cloned.1.call-start = ((), (), s32[]{:S(2)}) async-start(), calls=%async_computation.30 | async-start | bytes 77856768 | tf_op jit(solution)/shard_map/reduce_scatter | solution.py:409
  1463.0 63.2 %copy-start.99 = (f32[2,2,48]{2,1,0:T(2,128)S(1)}, f32[2,2,48]{2,1,0:T(2,128)}, u32[]{:S(2)}) copy-start(f32[2,2,48]{2,1,0:T(2,128)} %param.31) | copy-start | bytes 2308
  1463.1 63.2 %copy-start.100 = (f32[2,2,48]{2,1,0:T(2,128)S(1)}, f32[2,2,48]{2,1,0:T(2,128)}, u32[]{:S(2)}) copy-start(f32[2,2,48]{2,1,0:T(2,128)} %param.40) | copy-start | bytes 2308
  1463.1 63.2 %copy-start.101 = (f32[2,2,48]{2,1,0:T(2,128)S(1)}, f32[2,2,48]{2,1,0:T(2,128)}, u32[]{:S(2)}) copy-start(f32[2,2,48]{2,1,0:T(2,128)} %param.41) | copy-start | bytes 2308
  1467.6 661.4 %copy-start.66 = (f32[2,48,2048]{2,1,0:T(8,128)S(1)}, f32[2,48,2048]{2,1,0:T(8,128)}, u32[]{:S(2)}) copy-start(f32[2,48,2048]{2,1,0:T(8,128)} %param.27) | copy-start | bytes 2359300
  1811.8 1023.4 %copy-start.48 = (f32[2,8,24,1536]{3,2,1,0:T(8,128)S(1)}, f32[2,8,24,1536]{3,2,1,0:T(8,128)}, u32[]{:S(2)}) copy-start(f32[2,8,24,1536]{3,2,1,0:T(8,128)} %param.30) | copy-start | bytes 7077892
  (73 other events, 256.7 us)
Sparse Core Ops, SparseCore 0:
  11.6 72.3 all-gather.10
  87.6 62.1 all-gather.12
  153.6 213.8 all-gather.14
  371.1 122.8 all-gather.16
  497.4 67.5 all-gather.18
  568.5 63.5 all-gather.20
  635.8 213.8 all-gather.22
  853.4 122.8 all-gather.24
  1110.5 22.9 reduce-scatter.18
  1137.0 24.7 reduce-scatter.20
  1272.2 24.7 reduce-scatter.22
  1300.5 24.7 reduce-scatter.24
  1330.4 95.4 reduce-scatter.44
  1430.9 94.5 reduce-scatter.42
  1531.2 134.6 reduce-scatter.32
  1672.6 134.5 reduce-scatter.30
  1813.1 154.5 reduce-scatter.28
  1974.5 154.4 reduce-scatter.26
  2135.5 346.2 reduce-scatter.40
  2489.2 345.9 reduce-scatter.38
  2841.6 659.0 reduce-scatter.36
  3508.3 658.9 reduce-scatter.34
where the time goes:
time: 4200 us; the launch traced here: 4190 us
  waiting for transfers between devices  3380 us (80%)
  matrix products  376 us (9%)
  other arithmetic  186 us (4%)
  blocking collectives  133 us (3%)
  local copies, waits for them, and re-layouts  97.4 us (2%)
    reduce_scatter x2, waiting for transfers between devices, on_device(): lax.psum_scatter(layer_grads[2], ('ctx', 'shard'), scatter_dimension=1, t...  1320 us
    reduce_scatter x2, waiting for transfers between devices, on_device(): lax.psum_scatter(layer_grads[3], ('ctx', 'shard'), scatter_dimension=1, t...  701 us
    all_gather x2, waiting for transfers between devices, gather_forward(): lax.all_gather(shards[2], ('ctx', 'shard'), axis=1, tiled=True)  377 us
    reduce_scatter x2, waiting for transfers between devices, on_device(): lax.psum_scatter(layer_grads[0], ('ctx', 'shard'), scatter_dimension=0, t...  317 us
    reduce_scatter x2, waiting for transfers between devices, on_device(): lax.psum_scatter(layer_grads[1], ('ctx', 'shard'), scatter_dimension=0, t...  279 us
    all_gather x2, waiting for transfers between devices, gather_forward(): lax.all_gather(shards[3], ('ctx', 'shard'), axis=1, tiled=True)  202 us
  transfers between devices with their start and end apart: 22, of which 19 were waited for; matrix products, arithmetic and copies ran while one was open for 9% of the time, Pallas kernels for 0%

commit v1 on v0

v1 whole, which is shorter than its diff:
```python
import functools

import jax
import jax.numpy as jnp
from jax import lax
from jax.experimental import pallas as pl
from jax.experimental.pallas import tpu as pltpu
from jax.sharding import Mesh
from jax.sharding import PartitionSpec as P

D = 1536
H = 12
KVH = 2
HD = 128
F = 768
TOP = 4
EXPERTS = 8
LAYERS = 2
STEP = 10
CAP = 160


NORM_EPS = 1e-06
ROPE_BASE = 1000000.0
BETA_ONE = 0.9
BETA_TWO = 0.95
ADAM_EPS = 1e-08
DECAY = 0.1
MASKED = -1e30


def rope_tables(positions):
    half_width = HD // 2
    frequency = ROPE_BASE ** (-(jnp.arange(half_width, dtype=jnp.float32) * 2.0 / HD))
    angles = positions.astype(jnp.float32)[:, None] * frequency[None, :]
    return (jnp.cos(angles)[:, None, :], jnp.sin(angles)[:, None, :])


def rotate(vectors, cosine_table, sine_table):
    half_width = vectors.shape[-1] // 2
    first_half = vectors[..., :half_width]
    second_half = vectors[..., half_width:]
    return jnp.concatenate(
        [
            first_half * cosine_table - second_half * sine_table,
            second_half * cosine_table + first_half * sine_table,
        ],
        axis=-1,
    )


def rotate_back(gradient, cosine_table, sine_table):
    half_width = gradient.shape[-1] // 2
    first_half = gradient[..., :half_width]
    second_half = gradient[..., half_width:]
    return jnp.concatenate(
        [
            first_half * cosine_table + second_half * sine_table,
            second_half * cosine_table - first_half * sine_table,
        ],
        axis=-1,
    )


def normalize(values, gain_row):
    row_scale = lax.rsqrt(jnp.mean(values * values, axis=-1, keepdims=True) + NORM_EPS)
    return (values * row_scale * gain_row, row_scale)


def normalize_back(gradient, values, row_scale, gain_row):
    unit_rows = values * row_scale
    inner_grad = gradient * gain_row
    input_grad = row_scale * (
        inner_grad - unit_rows * jnp.mean(inner_grad * unit_rows, axis=-1, keepdims=True)
    )
    return (input_grad, jnp.sum(gradient * unit_rows, axis=0))


def adamw(parameter, moment, second, gradient, step_rate, decay_rate):
    moment = BETA_ONE * moment + (1.0 - BETA_ONE) * gradient
    second = BETA_TWO * second + (1.0 - BETA_TWO) * gradient * gradient
    direction = (
        moment / (1.0 - BETA_ONE**STEP) / (jnp.sqrt(second / (1.0 - BETA_TWO**STEP)) + ADAM_EPS)
    )
    return (parameter - step_rate * (direction + decay_rate * parameter), moment, second)


def glu_value(gate_input, up_input):
    return jax.nn.gelu(gate_input, approximate=False) * up_input


def attention_forward(queries, keys_all, values_all, allowed):
    group_size = H // KVH
    score_scale = HD ** (-0.5)
    outputs = []
    totals = []
    for head_group in range(KVH):
        query_part = queries[:, head_group * group_size : (head_group + 1) * group_size, :]
        scores = (
            jnp.einsum(
                "tjd,kd->jtk",
                query_part,
                keys_all[:, head_group, :],
                preferred_element_type=jnp.float32,
            )
            * score_scale
        )
        scores = jnp.where(allowed[None], scores, MASKED)
        row_max = jnp.max(scores, axis=-1, keepdims=True)
        exponent = jnp.exp(scores - row_max)
        row_total = jnp.sum(exponent, axis=-1, keepdims=True)
        probabilities = (exponent / row_total).astype(jnp.bfloat16)
        outputs.append(
            jnp.einsum(
                "jtk,kd->tjd",
                probabilities,
                values_all[:, head_group, :],
                preferred_element_type=jnp.float32,
            )
        )
        totals.append(row_max + jnp.log(row_total))
    return (jnp.concatenate(outputs, axis=1), totals)


def attention_backward(queries, keys_all, values_all, allowed, totals, grad_attended):
    group_size = H // KVH
    score_scale = HD ** (-0.5)
    grad_queries = []
    grad_keys = []
    grad_values = []
    for head_group in range(KVH):
        query_part = queries[:, head_group * group_size : (head_group + 1) * group_size, :]
        grad_part = grad_attended[:, head_group * group_size : (head_group + 1) * group_size, :]
        keys_part = keys_all[:, head_group, :]
        scores = (
            jnp.einsum("tjd,kd->jtk", query_part, keys_part, preferred_element_type=jnp.float32)
            * score_scale
        )
        probabilities = jnp.where(allowed[None], jnp.exp(scores - totals[head_group]), 0.0)
        grad_probs = jnp.einsum(
            "tjd,kd->jtk",
            grad_part,
            values_all[:, head_group, :],
            preferred_element_type=jnp.float32,
        )
        grad_scores = probabilities * (
            grad_probs - jnp.sum(probabilities * grad_probs, axis=-1, keepdims=True)
        )
        grad_scores = grad_scores.astype(jnp.bfloat16)
        grad_queries.append(
            jnp.einsum("jtk,kd->tjd", grad_scores, keys_part, preferred_element_type=jnp.float32)
            * score_scale
        )
        grad_keys.append(
            jnp.einsum("jtk,tjd->kd", grad_scores, query_part, preferred_element_type=jnp.float32)
            * score_scale
        )
        grad_values.append(
            jnp.einsum(
                "jtk,tjd->kd",
                probabilities.astype(jnp.bfloat16),
                grad_part,
                preferred_element_type=jnp.float32,
            )
        )
    return (
        jnp.concatenate(grad_queries, axis=1),
        jnp.stack(grad_keys, axis=1),
        jnp.stack(grad_values, axis=1),
    )


CTX = ("yo", "xi")
SHARD = ("zo", "zi", "core")
ALL = CTX + SHARD
GROUP = ("xi", "zi")
REPLICAS = ("yo", "zo", "core")


def flat_index(axes):
    index = 0
    for axis in axes:
        index = index * lax.axis_size(axis) + lax.axis_index(axis)
    return index


def shift_permutation(axes, offsets, back=False):
    sizes = [lax.axis_size(axis) for axis in axes]
    pairs = []
    for first in range(sizes[0]):
        for second in range(sizes[1]):
            target = ((first + offsets[0]) % sizes[0], (second + offsets[1]) % sizes[1])
            here = first * sizes[1] + second
            there = target[0] * sizes[1] + target[1]
            pairs.append((there, here) if back else (here, there))
    return pairs


def offsets_of(axes):
    sizes = [lax.axis_size(axis) for axis in axes]
    return [(a, b) for a in range(sizes[0]) for b in range(sizes[1])]


def send(value, axes, offsets, back=False):
    if offsets == (0, 0):
        return value
    return lax.ppermute(value, axes, shift_permutation(axes, offsets, back))


def source_index(axes, offsets):
    sizes = [lax.axis_size(axis) for axis in axes]
    return lax.rem(lax.axis_index(axes[0]) - offsets[0] + sizes[0], sizes[0]) * sizes[1] + lax.rem(
        lax.axis_index(axes[1]) - offsets[1] + sizes[1], sizes[1]
    )


def target_index(axes, offsets):
    sizes = [lax.axis_size(axis) for axis in axes]
    return lax.rem(lax.axis_index(axes[0]) + offsets[0], sizes[0]) * sizes[1] + lax.rem(
        lax.axis_index(axes[1]) + offsets[1], sizes[1]
    )


def positions_docs(block_map, lengths_row, ctx_index, block_rows):
    blocks = lax.dynamic_slice_in_dim(block_map, 2 * ctx_index, 2)
    offsets = jnp.arange(block_rows, dtype=jnp.int32)
    positions = (blocks[:, None] * block_rows + offsets[None, :]).reshape(-1)
    bounds = jnp.cumsum(lengths_row)
    documents = jnp.sum((positions[:, None] >= bounds[None, :]).astype(jnp.int32), axis=1)
    return (positions, documents)


def dispatch_tables(routes, gates):
    rows = routes.shape[0]
    hits = (routes[None] == jnp.arange(EXPERTS, dtype=jnp.int32)[:, None, None]).astype(jnp.float32)
    member = jnp.sum(hits, axis=-1)
    gate = jnp.sum(hits * gates[None], axis=-1)
    before = (jnp.arange(rows)[:, None] < jnp.arange(rows)[None, :]).astype(jnp.float32)
    rank = jnp.dot(member, before, preferred_element_type=jnp.float32)
    return jnp.stack([jnp.where(member > 0, rank, -1.0), gate], axis=1)


def selection(ranks):
    slots = jnp.arange(CAP, dtype=jnp.float32)
    return (ranks[:, None, :] == slots[None, :, None]).astype(jnp.bfloat16)


MESH = pl.DeviceIdType.MESH
QKV = (H + 2 * KVH) * HD


class Place:
    def __init__(self, sizes):
        self.yo_size, self.zo_size = sizes
        self.yo, self.xi, self.zo, self.zi, self.core = [lax.axis_index(axis) for axis in ALL]
        self.y_steps = range(1, self.yo_size)
        self.z_steps = range(1, self.zo_size)
        self.column = [(a, b) for a in range(self.zo_size) for b in range(2)]

    def at(self, y=0, x=0, z=0, w=0, core=0):
        return (
            lax.rem(self.yo + y, self.yo_size),
            1 - self.xi if x else self.xi,
            lax.rem(self.zo + z, self.zo_size),
            1 - self.zi if w else self.zi,
            1 - self.core if core else self.core,
        )

    def chip(self, y=0, x=0, z=0, w=0):
        yo, xi, zo, zi, core = self.at(y, x, z, w)
        return ((yo * 2 + xi) * self.zo_size + zo) * 2 + zi

    def back_y(self, y):
        return (self.yo_size - y) % self.yo_size

    def back_z(self, z):
        return (self.zo_size - z) % self.zo_size


class Wires:
    def __init__(self, send_sems, recv_sems):
        self.send_sems, self.recv_sems = send_sems, recv_sems
        self.started = []

    def send(self, source, target, name, device):
        copy = pltpu.make_async_remote_copy(
            src_ref=source,
            dst_ref=target,
            send_sem=self.send_sems.at[len(self.started)],
            recv_sem=self.recv_sems.at[name],
            device_id=device,
            device_id_type=MESH,
        )
        copy.start()
        self.started.append(copy)

    def arrive(self, target, name, device):
        pltpu.make_async_remote_copy(
            src_ref=target,
            dst_ref=target,
            send_sem=self.send_sems.at[0],
            recv_sem=self.recv_sems.at[name],
            device_id=device,
            device_id_type=MESH,
        ).wait_recv()

    def drain(self):
        for copy in self.started:
            copy.wait_send()


def greet(partners):
    barrier = pltpu.get_barrier_semaphore()
    for partner in partners:
        pl.semaphore_signal(barrier, inc=1, device_id=partner, device_id_type=MESH)
    pl.semaphore_wait(barrier, len(partners))


def mesh_sizes():
    return lax.axis_size("yo"), lax.axis_size("zo")


def add_rows(target, *parts):
    def step(index, carry):
        rows = pl.ds(pl.multiple_of(index * 16, 16), 16)
        total = target[rows, :].astype(jnp.float32)
        for part in parts:
            total = total + part[rows, :].astype(jnp.float32)
        target[rows, :] = total.astype(target.dtype)
        return carry

    lax.fori_loop(0, target.shape[0] // 16, step, 0)


def gather_attention_kernel(sizes, q_ref, o_ref, q_out, o_out, send_sems, recv_sems):
    here = Place(sizes)
    wires = Wires(send_sems, recv_sems)
    shards, wholes = (q_ref, o_ref), (q_out, o_out)
    far = [offset for offset in here.column if offset != (0, 0)]
    greet(
        [here.at(z=z, w=w) for z, w in far]
        + [here.at(x=1), here.at(core=1)]
        + [here.at(y=y) for y in here.y_steps]
    )
    mine = here.chip() * 2 + here.core

    def block(**offsets):
        return here.chip(**offsets) * 2 + here.core

    def name(kind, y, x, z, w):
        return ((((kind * here.yo_size + y) * 2 + x) * here.zo_size + z) * 2 + w) * 2

    for z, w in far:
        for part in range(2):
            wires.send(
                shards[part],
                wholes[part].at[mine],
                name(0, 0, 0, here.back_z(z), w) + part,
                here.at(z=z, w=w),
            )

    def pass_on(source, y, x, z, w, part, to_x, to_y):
        index = block(y=y, x=x, z=z, w=w)
        target = wholes[part].at[index]
        if to_x:
            wires.send(source, target, name(0, y, 1 - x, z, w) + part, here.at(x=1))
        for step in here.y_steps if to_y else ():
            wires.send(
                source,
                target,
                name(0, (y + here.back_y(step)) % here.yo_size, x, z, w) + part,
                here.at(y=step),
            )
        wires.send(source, target, name(1, y, x, z, w) + part, here.at(core=1))

    for z, w in here.column:
        for part in range(2):
            if (z, w) == (0, 0):
                pass_on(shards[part], 0, 0, 0, 0, part, True, True)
                wholes[part][mine] = shards[part][...]
            else:
                source = wholes[part].at[block(z=z, w=w)]
                wires.arrive(source, name(0, 0, 0, z, w) + part, here.at(core=1))
                pass_on(source, 0, 0, z, w, part, True, True)
    for z, w in here.column:
        for part in range(2):
            source = wholes[part].at[block(x=1, z=z, w=w)]
            wires.arrive(source, name(0, 0, 1, z, w) + part, here.at(core=1))
            pass_on(source, 0, 1, z, w, part, False, part == 1)
            for y in here.y_steps:
                source = wholes[part].at[block(y=y, z=z, w=w)]
                wires.arrive(source, name(0, y, 0, z, w) + part, here.at(core=1))
                pass_on(source, y, 0, z, w, part, part == 0, False)
    for z, w in here.column:
        for part in range(2):
            for y in here.y_steps:
                source = wholes[part].at[block(y=y, x=1, z=z, w=w)]
                wires.arrive(source, name(0, y, 1, z, w) + part, here.at(core=1))
                pass_on(source, y, 1, z, w, part, False, False)
    for y in range(here.yo_size):
        for x in range(2):
            for z, w in here.column:
                for part in range(2):
                    index = here.chip(y=y, x=x, z=z, w=w) * 2 + 1 - here.core
                    wires.arrive(
                        wholes[part].at[index], name(1, y, x, z, w) + part, here.at(core=1)
                    )
    wires.drain()


def gather_attention(q_shard, o_shard):
    sizes = mesh_sizes()
    devices = sizes[0] * sizes[1] * 8
    chips = devices // 2
    columns = sizes[1] * 2
    sends = 2 * (columns - 1) + 2 * columns * (sizes[0] + 1) + 4 * columns * (sizes[0] + 1) * 2
    return pl.pallas_call(
        functools.partial(gather_attention_kernel, sizes),
        out_shape=[
            jax.ShapeDtypeStruct((devices,) + shard.shape, shard.dtype)
            for shard in (q_shard, o_shard)
        ],
        in_specs=[pl.BlockSpec(memory_space=pltpu.VMEM)] * 2,
        out_specs=[pl.BlockSpec(memory_space=pltpu.VMEM)] * 2,
        scratch_shapes=[
            pltpu.SemaphoreType.DMA((sends,)),
            pltpu.SemaphoreType.DMA((4 * chips,)),
        ],
        compiler_params=pltpu.CompilerParams(
            collective_id=0, has_side_effects=True, vmem_limit_bytes=40 * 1024 * 1024
        ),
    )(q_shard, o_shard)


def gather_experts_kernel(sizes, u_ref, v_ref, u_out, v_out, send_sems, recv_sems):
    here = Place(sizes)
    wires = Wires(send_sems, recv_sems)
    shards, wholes = (u_ref, v_ref), (u_out, v_out)
    group = [(0, 0), (1, 0), (0, 1), (1, 1)]
    greet(
        [here.at(x=x, w=w) for x, w in group[1:]]
        + [here.at(z=z) for z in here.z_steps]
        + [here.at(y=y) for y in here.y_steps]
        + [here.at(core=1)]
    )

    def name(kind, y, x, z, w):
        return ((((kind * here.yo_size + y) * 2 + x) * here.zo_size + z) * 2 + w) * 2

    def member(x, w):
        yo, xi, zo, zi, core = here.at(x=x, w=w)
        return xi * 2 + zi

    for x, w in group[1:]:
        for part in range(2):
            wires.send(
                shards[part].at[member(x, w)],
                wholes[part].at[0, here.chip()],
                name(0, 0, x, 0, w) + part,
                here.at(x=x, w=w),
            )

    def pass_on(source, y, x, z, w, part, to_z, to_y):
        index = here.chip(y=y, x=x, z=z, w=w)
        for step in here.z_steps if to_z else ():
            wires.send(
                source,
                wholes[part].at[0, index],
                name(0, y, x, (z + here.back_z(step)) % here.zo_size, w) + part,
                here.at(z=step),
            )
        for step in here.y_steps if to_y else ():
            wires.send(
                source,
                wholes[part].at[0, index],
                name(0, (y + here.back_y(step)) % here.yo_size, x, z, w) + part,
                here.at(y=step),
            )
        wires.send(
            source, wholes[part].at[1, index], name(1, y, x, z, w) + part, here.at(core=1)
        )

    for x, w in group:
        for part in range(2):
            if (x, w) == (0, 0):
                pass_on(shards[part].at[member(0, 0)], 0, 0, 0, 0, part, True, True)
                wholes[part][0, here.chip()] = shards[part][member(0, 0)]
            else:
                source = wholes[part].at[0, here.chip(x=x, w=w)]
                wires.arrive(source, name(0, 0, x, 0, w) + part, here.at(core=1))
                pass_on(source, 0, x, 0, w, part, True, True)
    for x, w in group:
        for part in range(2):
            for z in here.z_steps:
                source = wholes[part].at[0, here.chip(x=x, w=w, z=z)]
                wires.arrive(source, name(0, 0, x, z, w) + part, here.at(core=1))
                pass_on(source, 0, x, z, w, part, False, True)
    for z in range(here.zo_size):
        for x, w in group:
            for part in range(2):
                for y in here.y_steps:
                    source = wholes[part].at[0, here.chip(y=y, x=x, w=w, z=z)]
                    wires.arrive(source, name(0, y, x, z, w) + part, here.at(core=1))
                    pass_on(source, y, x, z, w, part, False, False)
    for y in range(here.yo_size):
        for z in range(here.zo_size):
            for x, w in group:
                for part in range(2):
                    target = wholes[part].at[1, here.chip(y=y, x=x, w=w, z=z)]
                    wires.arrive(target, name(1, y, x, z, w) + part, here.at(core=1))
    wires.drain()


def gather_experts(u_parts, v_parts):
    sizes = mesh_sizes()
    chips = sizes[0] * sizes[1] * 4
    sends = 6 + 8 * (sizes[0] + sizes[1] - 1) + 8 * (sizes[1] - 1) * sizes[0] + 2 * chips
    return pl.pallas_call(
        functools.partial(gather_experts_kernel, sizes),
        out_shape=[
            jax.ShapeDtypeStruct((2, chips) + part.shape[1:], part.dtype)
            for part in (u_parts, v_parts)
        ],
        in_specs=[pl.BlockSpec(memory_space=pltpu.VMEM)] * 2,
        out_specs=[pl.BlockSpec(memory_space=pltpu.VMEM)] * 2,
        scratch_shapes=[
            pltpu.SemaphoreType.DMA((sends,)),
            pltpu.SemaphoreType.DMA((4 * chips,)),
        ],
        compiler_params=pltpu.CompilerParams(
            collective_id=1, has_side_effects=True, vmem_limit_bytes=40 * 1024 * 1024
        ),
    )(u_parts, v_parts)


def sum_experts_kernel(sizes, u_ref, v_ref, u_out, v_out, u1, v1, u2, v2, u3, v3, send_sems, recv_sems):
    here = Place(sizes)
    wires = Wires(send_sems, recv_sems)
    group = [(0, 0), (1, 0), (0, 1), (1, 1)]
    whole, outs, first, second, third = (u_ref, v_ref), (u_out, v_out), (u1, v1), (u2, v2), (u3, v3)
    greet(
        [here.at(x=x, w=w) for x, w in group[1:]]
        + [here.at(z=z) for z in here.z_steps]
        + [here.at(y=y) for y in here.y_steps]
        + [here.at(core=1)]
    )
    chips = here.yo_size * here.zo_size * 4

    def place(y, z, member):
        return (y * here.zo_size + z) * 4 + member

    def name(kind, index, part):
        return (kind * chips + index) * 2 + part

    order = [
        (y, z, member)
        for y in list(here.y_steps) + [0]
        for z in list(here.z_steps) + [0]
        for member in range(4)
    ]
    other = here.at(core=1)
    for y, z, member in order:
        x, w = group[member]
        index = here.chip(y=y, x=x, z=z, w=w)
        for part in range(2):
            wires.send(
                whole[part].at[1, index],
                first[part].at[place(y, z, member)],
                name(0, place(y, z, member), part),
                other,
            )
    for y, z, member in order:
        x, w = group[member]
        index = here.chip(y=y, x=x, z=z, w=w)
        for part in range(2):
            spot = place(y, z, member)
            total = first[part].at[spot]
            wires.arrive(total, name(0, spot, part), other)
            if y:
                add_rows(total, whole[part].at[0, index])
                landing = place(here.back_y(y), z, member)
                wires.send(
                    total, second[part].at[landing], name(1, landing, part), here.at(y=y)
                )
                continue
            parts = [whole[part].at[0, index]]
            for step in here.y_steps:
                arrived = second[part].at[place(step, z, member)]
                wires.arrive(arrived, name(1, place(step, z, member), part), other)
                parts.append(arrived)
            if z:
                add_rows(total, *parts)
                landing = here.back_z(z) * 4 + member
                wires.send(total, third[part].at[landing], name(2, landing, part), here.at(z=z))
                continue
            for step in here.z_steps:
                arrived = third[part].at[step * 4 + member]
                wires.arrive(arrived, name(2, step * 4 + member, part), other)
                parts.append(arrived)
            add_rows(total, *parts)
            slot = here.xi * 2 + here.zi
            if member:
                wires.send(
                    total, outs[part].at[slot], name(3, member, part), here.at(x=x, w=w)
                )
            else:
                outs[part][slot] = total[...]
    for member in range(1, 4):
        x, w = group[member]
        yo, xi, zo, zi, core = here.at(x=x, w=w)
        for part in range(2):
            wires.arrive(outs[part].at[xi * 2 + zi], name(3, member, part), other)
    wires.drain()


def sum_experts(u_grads, v_grads):
    sizes = mesh_sizes()
    chips = sizes[0] * sizes[1] * 4
    rows = [grads.shape[1] // chips for grads in (u_grads, v_grads)]
    blocks = [grads.reshape(2, chips, -1, D) for grads in (u_grads, v_grads)]

    def buffers(count):
        return [pltpu.VMEM((count, part, D), jnp.bfloat16) for part in rows]

    return pl.pallas_call(
        functools.partial(sum_experts_kernel, sizes),
        out_shape=[jax.ShapeDtypeStruct((4, part, D), jnp.bfloat16) for part in rows],
        in_specs=[pl.BlockSpec(memory_space=pltpu.VMEM)] * 2,
        out_specs=[pl.BlockSpec(memory_space=pltpu.VMEM)] * 2,
        scratch_shapes=buffers(chips)
        + buffers(chips)
        + buffers(sizes[1] * 4)
        + [
            pltpu.SemaphoreType.DMA((6 * chips,)),
            pltpu.SemaphoreType.DMA((8 * chips,)),
        ],
        compiler_params=pltpu.CompilerParams(
            collective_id=2, has_side_effects=True, vmem_limit_bytes=56 * 1024 * 1024
        ),
    )(*blocks)


def sum_attention_kernel(
    sizes, q_ref, o_ref, q_out, o_out, q1, o1, q2, o2, q3, o3, q4, o4, send_sems, recv_sems
):
    here = Place(sizes)
    wires = Wires(send_sems, recv_sems)
    whole, outs = (q_ref, o_ref), (q_out, o_out)
    first, second, third, fourth = (q1, o1), (q2, o2), (q3, o3), (q4, o4)
    columns = here.column
    far = [offset for offset in columns if offset != (0, 0)]
    other = here.at(core=1)
    greet(
        [here.at(z=z, w=w) for z, w in far]
        + [here.at(x=1), other]
        + [here.at(y=y) for y in here.y_steps]
    )
    chips = here.yo_size * 2 * len(columns)

    def place(y, x, column):
        return (y * 2 + x) * len(columns) + column

    def name(kind, index, part):
        return (kind * chips + index) * 2 + part

    plane = [(y, x) for y in list(here.y_steps) + [0] for x in (1, 0)]
    rounds = [
        (y, x, (column + 1) % len(columns), part)
        for y, x in plane
        for column in range(len(columns))
        for part in range(2)
    ]
    rounds.sort(key=lambda item: (bool(item[0]) + item[1] != 2, not (item[1] if item[3] == 0 else item[0]), not (item[0] or item[1])))
    for y, x, column, part in rounds:
        z, w = columns[column]
        index = here.chip(y=y, x=x, z=z, w=w)
        spot = place(y, x, column)
        wires.send(
            whole[part].at[index, 1 - here.core],
            first[part].at[spot],
            name(0, spot, part),
            other,
        )
    for y, x, column, part in rounds:
        z, w = columns[column]
        index = here.chip(y=y, x=x, z=z, w=w)
        spot = place(y, x, column)
        total = first[part].at[spot]
        wires.arrive(total, name(0, spot, part), other)
        parts = [whole[part].at[index, here.core]]
        if part == 0:
            if x:
                add_rows(total, *parts)
                landing = place(y, 0, column)
                wires.send(total, second[0].at[landing], name(1, landing, 0), here.at(x=1))
                continue
            arrived = second[0].at[place(y, 0, column)]
            wires.arrive(arrived, name(1, place(y, 0, column), 0), other)
            parts.append(arrived)
            if y:
                add_rows(total, *parts)
                landing = place(here.back_y(y), 0, column)
                wires.send(total, third[0].at[landing], name(2, landing, 0), here.at(y=y))
                continue
            for step in here.y_steps:
                arrived = third[0].at[place(step, 0, column)]
                wires.arrive(arrived, name(2, place(step, 0, column), 0), other)
                parts.append(arrived)
        else:
            if y:
                add_rows(total, *parts)
                landing = place(here.back_y(y), x, column)
                wires.send(total, second[1].at[landing], name(1, landing, 1), here.at(y=y))
                continue
            for step in here.y_steps:
                arrived = second[1].at[place(step, x, column)]
                wires.arrive(arrived, name(1, place(step, x, column), 1), other)
                parts.append(arrived)
            if x:
                add_rows(total, *parts)
                landing = place(0, 0, column)
                wires.send(total, third[1].at[landing], name(2, landing, 1), here.at(x=1))
                continue
            arrived = third[1].at[place(0, 0, column)]
            wires.arrive(arrived, name(2, place(0, 0, column), 1), other)
            parts.append(arrived)
        if column:
            add_rows(total, *parts)
            landing = columns.index((here.back_z(z), w))
            wires.send(
                total, fourth[part].at[landing], name(3, landing, part), here.at(z=z, w=w)
            )
            continue
        for step in range(1, len(columns)):
            arrived = fourth[part].at[step]
            wires.arrive(arrived, name(3, step, part), other)
            parts.append(arrived)
        add_rows(total, *parts)
        outs[part][...] = total[...]
    wires.drain()


def sum_attention(q_grads, o_grads):
    sizes = mesh_sizes()
    chips = sizes[0] * sizes[1] * 4
    rows = q_grads.shape[0] // (2 * chips)
    widths = [grads.shape[1] for grads in (q_grads, o_grads)]
    blocks = [grads.reshape(chips, 2, rows, -1) for grads in (q_grads, o_grads)]

    def buffers(count):
        return [pltpu.VMEM((count, rows, width), jnp.bfloat16) for width in widths]

    return pl.pallas_call(
        functools.partial(sum_attention_kernel, sizes),
        out_shape=[jax.ShapeDtypeStruct((rows, width), jnp.bfloat16) for width in widths],
        in_specs=[pl.BlockSpec(memory_space=pltpu.VMEM)] * 2,
        out_specs=[pl.BlockSpec(memory_space=pltpu.VMEM)] * 2,
        scratch_shapes=buffers(chips)
        + buffers(chips)
        + buffers(chips)
        + buffers(sizes[1] * 2)
        + [
            pltpu.SemaphoreType.DMA((6 * chips,)),
            pltpu.SemaphoreType.DMA((8 * chips,)),
        ],
        compiler_params=pltpu.CompilerParams(
            collective_id=3, has_side_effects=True, vmem_limit_bytes=56 * 1024 * 1024
        ),
    )(*blocks)


def swap(value, axis):
    return lax.ppermute(value, axis, [(0, 1), (1, 0)])


def pick(value, index, axis=0):
    return lax.dynamic_index_in_dim(value, index, axis, keepdims=False)


def by_core(mine, theirs, axis):
    core = lax.axis_index("core")
    return jnp.where(
        core == 0, jnp.stack([mine, theirs], axis), jnp.stack([theirs, mine], axis)
    )


def all_gains(gains):
    whole = lax.all_gather(gains.astype(jnp.bfloat16), ALL, axis=2, tiled=True)
    return whole.astype(jnp.float32)


def attention_weights_direct(w_qkv, w_out, layer):
    q_whole, o_whole = gather_attention(
        w_qkv[layer].astype(jnp.bfloat16), w_out[layer].astype(jnp.bfloat16)
    )
    return q_whole.reshape(D, QKV), o_whole.reshape(D, D)


def expert_weights_direct(w_gateup, w_down, layer):
    core = lax.axis_index("core")
    parts = []
    for shard in (w_gateup[layer], w_down[layer]):
        shard = shard.astype(jnp.bfloat16)
        shard = shard.reshape((4, 2) + shard.shape[1:])
        theirs = swap(pick(shard, 1 - core, 1), "core")
        parts.append(by_core(pick(shard, core, 1), theirs, 1).reshape(4, -1, D))
    up, down = gather_experts(*parts)
    return up.reshape(2, D, 2 * F), down.reshape(2, F, D)


def expert_grads_direct(grad_up, grad_down):
    core = lax.axis_index("core")
    result = []
    for part in sum_experts(grad_up.astype(jnp.bfloat16), grad_down.astype(jnp.bfloat16)):
        part = part.reshape(4, 2, -1, D)
        theirs = swap(pick(part, 1 - core, 1), "core")
        pair = by_core(pick(part, core, 1), theirs, 1)
        result.append(pair.reshape(EXPERTS, -1, D).astype(jnp.float32))
    return result


def attention_grads_direct(grad_qkv, grad_out):
    sums = sum_attention(grad_qkv.astype(jnp.bfloat16), grad_out.astype(jnp.bfloat16))
    return [part.astype(jnp.float32) for part in sums]


def attention_weights(w_qkv, w_out, layer):
    packed = jnp.concatenate(
        [w_qkv[layer].astype(jnp.bfloat16), w_out[layer].astype(jnp.bfloat16)], axis=1
    )
    whole = lax.all_gather(packed, ALL, axis=0, tiled=True)
    return whole[:, :QKV], whole[:, QKV:]


def relative_order(axes, back=False):
    pick = target_index if back else source_index
    return jnp.stack([pick(axes, offsets) for offsets in offsets_of(axes)])


def to_absolute(pieces, axes):
    stacked = jnp.stack(pieces)
    order = relative_order(axes)
    return stacked[order]


def expert_weights(w_gateup, w_down, layer):
    packed = jnp.concatenate(
        [w_gateup[layer].astype(jnp.bfloat16), w_down[layer].astype(jnp.bfloat16)], axis=1
    )
    rows_up = w_gateup.shape[2]
    pieces = []
    for offsets in offsets_of(GROUP):
        mine = lax.dynamic_slice_in_dim(packed, 2 * target_index(GROUP, offsets), 2)
        pieces.append(send(mine, GROUP, offsets))
    by_source = to_absolute(pieces, GROUP)
    whole = lax.all_gather(by_source, REPLICAS, axis=0)
    yo, zo = lax.axis_size("yo"), lax.axis_size("zo")
    whole = whole.reshape((yo, zo, 2, 2, 2, 2) + by_source.shape[2:])
    whole = whole.transpose(5, 0, 3, 1, 4, 2, 6, 7)
    up = whole[..., :rows_up, :].reshape(2, D, 2 * F)
    down = whole[..., rows_up:, :].reshape(2, F, D)
    return up, down


def expert_grads(grad_up, grad_down):
    yo, zo = lax.axis_size("yo"), lax.axis_size("zo")

    def split(whole):
        blocks = whole.astype(jnp.bfloat16).reshape((2, yo, 2, zo, 2, 2, -1) + whole.shape[2:])
        return blocks.transpose(1, 3, 5, 2, 4, 0, 6, 7)

    packed = jnp.concatenate([split(grad_up), split(grad_down)], axis=6)
    rows = packed.shape[6]
    packed = packed.reshape((yo * zo * 2, 4, 2, rows, D))
    summed = lax.psum_scatter(packed, REPLICAS, scatter_dimension=0, tiled=False)
    pieces = []
    for offsets in offsets_of(GROUP):
        theirs = lax.dynamic_index_in_dim(summed, target_index(GROUP, offsets), 0, keepdims=False)
        pieces.append(send(theirs, GROUP, offsets))
    by_source = to_absolute(pieces, GROUP).reshape(EXPERTS, rows, D).astype(jnp.float32)
    rows_up = rows * 2 // 3
    return by_source[:, :rows_up], by_source[:, rows_up:]


def attention_grads(grad_qkv, grad_out):
    packed = jnp.concatenate(
        [grad_qkv.astype(jnp.bfloat16), grad_out.astype(jnp.bfloat16)], axis=1
    )
    summed = lax.psum_scatter(packed, ALL, scatter_dimension=0, tiled=True).astype(jnp.float32)
    return summed[:, :QKV], summed[:, QKV:]


def experts_forward(chunk, table, weights):
    up_w, down_w = weights
    select = selection(table[:, 0])
    slot_in = jnp.einsum("jst,td->jsd", select, chunk, preferred_element_type=jnp.float32)
    slot_in = slot_in.astype(jnp.bfloat16)
    gate_up = jnp.einsum("jsd,jdf->jsf", slot_in, up_w, preferred_element_type=jnp.float32)
    activated = glu_value(gate_up[..., :F], gate_up[..., F:]).astype(jnp.bfloat16)
    result = jnp.einsum("jsf,jfd->jsd", activated, down_w, preferred_element_type=jnp.float32)
    result = result.astype(jnp.bfloat16)
    spread = jnp.einsum("jst,jsd->jtd", select, result, preferred_element_type=jnp.float32)
    merged = jnp.sum(spread * table[:, 1, :, None], axis=0)
    return merged, (slot_in, gate_up, activated)


def experts_backward(gradient, table, weights, kept):
    up_w, down_w = weights
    slot_in, gate_up, activated = kept
    select = selection(table[:, 0])
    weighted = (table[:, 1, :, None] * gradient.astype(jnp.float32)[None]).astype(jnp.bfloat16)
    slot_grad = jnp.einsum("jst,jtd->jsd", select, weighted, preferred_element_type=jnp.float32)
    slot_grad = slot_grad.astype(jnp.bfloat16)
    grad_act = jnp.einsum("jsd,jfd->jsf", slot_grad, down_w, preferred_element_type=jnp.float32)
    unused, pull = jax.vjp(glu_value, gate_up[..., :F], gate_up[..., F:])
    grad_gate, grad_up = pull(grad_act)
    grad_glu = jnp.concatenate([grad_gate, grad_up], axis=-1).astype(jnp.bfloat16)
    grad_slots = jnp.einsum("jsf,jdf->jsd", grad_glu, up_w, preferred_element_type=jnp.float32)
    grad_rows = jnp.einsum(
        "jst,jsd->td", select, grad_slots.astype(jnp.bfloat16), preferred_element_type=jnp.float32
    )
    return grad_rows, (slot_grad, grad_glu)


def moe_forward(expert_in, tables, weights):
    total = None
    kept = []
    for place, offsets in enumerate(offsets_of(GROUP)):
        chunk = send(expert_in, GROUP, offsets)
        merged, record = experts_forward(chunk, tables[place], weights)
        kept.append(record)
        if offsets != (0, 0):
            merged = send(merged.astype(jnp.bfloat16), GROUP, offsets, back=True)
            merged = merged.astype(jnp.float32)
        total = merged if total is None else total + merged
    return total, kept


def moe_backward(gradient, tables, weights, kept):
    low = gradient.astype(jnp.bfloat16)
    total = None
    parts = []
    for place, offsets in enumerate(offsets_of(GROUP)):
        chunk = gradient if offsets == (0, 0) else send(low, GROUP, offsets)
        rows, record = experts_backward(chunk, tables[place], weights, kept[place])
        parts.append(record)
        if offsets != (0, 0):
            rows = send(rows.astype(jnp.bfloat16), GROUP, offsets, back=True).astype(jnp.float32)
        total = rows if total is None else total + rows
    slot_grad = jnp.concatenate([part[0] for part in parts], axis=1)
    grad_glu = jnp.concatenate([part[1] for part in parts], axis=1)
    slot_in = jnp.concatenate([record[0] for record in kept], axis=1)
    activated = jnp.concatenate([record[2] for record in kept], axis=1)
    grad_down = jnp.einsum("jsf,jsd->jfd", activated, slot_grad, preferred_element_type=jnp.float32)
    grad_up = jnp.einsum("jsd,jsf->jdf", slot_in, grad_glu, preferred_element_type=jnp.float32)
    return total, grad_up, grad_down


def layer_forward(stream, attn_w, expert_w, tables, allowed, cosine_table, sine_table):
    qkv_w, out_w, gain_full = attn_w
    row_count = stream.shape[0]
    normed, scale_one = normalize(stream, gain_full[0])
    attn_in = normed.astype(jnp.bfloat16)
    projected = jnp.dot(attn_in, qkv_w, preferred_element_type=jnp.float32)
    queries = rotate(
        projected[:, : H * HD].reshape(row_count, H, HD), cosine_table, sine_table
    ).astype(jnp.bfloat16)
    keys_local = rotate(
        projected[:, H * HD : (H + KVH) * HD].reshape(row_count, KVH, HD), cosine_table, sine_table
    ).astype(jnp.bfloat16)
    values_local = projected[:, (H + KVH) * HD :].reshape(row_count, KVH, HD).astype(jnp.bfloat16)
    both = jnp.concatenate([keys_local, values_local], axis=1)
    both_all = jnp.concatenate([send(both, CTX, offsets) for offsets in offsets_of(CTX)], axis=0)
    keys_all, values_all = both_all[:, :KVH], both_all[:, KVH:]
    attended, totals = attention_forward(queries, keys_all, values_all, allowed)
    attended_low = attended.reshape(row_count, H * HD).astype(jnp.bfloat16)
    middle_stream = stream + jnp.dot(attended_low, out_w, preferred_element_type=jnp.float32)
    normed_two, scale_two = normalize(middle_stream, gain_full[1])
    expert_in = normed_two.astype(jnp.bfloat16)
    merged, kept = moe_forward(expert_in, tables, expert_w)
    record = {
        "stream": stream,
        "scale_one": scale_one,
        "attn_in": attn_in,
        "queries": queries,
        "keys_all": keys_all,
        "values_all": values_all,
        "totals": totals,
        "attended": attended_low,
        "middle": middle_stream,
        "scale_two": scale_two,
        "kept": kept,
    }
    return (record, middle_stream + merged)


def layer_backward(gradient, record, attn_w, expert_w, tables, allowed, cosine_table, sine_table):
    qkv_w, out_w, gain_full = attn_w
    row_count = gradient.shape[0]
    grad_normed, grad_up, grad_down = moe_backward(gradient, tables, expert_w, record["kept"])
    grad_in_two, grad_gain_two = normalize_back(
        grad_normed, record["middle"], record["scale_two"], gain_full[1]
    )
    grad_middle = gradient + grad_in_two
    grad_middle_low = grad_middle.astype(jnp.bfloat16)
    grad_out = jnp.dot(record["attended"].T, grad_middle_low, preferred_element_type=jnp.float32)
    grad_attended = jnp.dot(grad_middle_low, out_w.T, preferred_element_type=jnp.float32)
    grad_attended = grad_attended.astype(jnp.bfloat16).reshape(row_count, H, HD)
    grad_queries, grad_keys_all, grad_values_all = attention_backward(
        record["queries"],
        record["keys_all"],
        record["values_all"],
        allowed,
        record["totals"],
        grad_attended,
    )
    both_all = jnp.concatenate([grad_keys_all, grad_values_all], axis=1)
    both = None
    for place, offsets in enumerate(offsets_of(CTX)):
        part = both_all[place * row_count : (place + 1) * row_count]
        if offsets != (0, 0):
            part = send(part.astype(jnp.bfloat16), CTX, offsets, back=True).astype(jnp.float32)
        both = part if both is None else both + part
    grad_keys, grad_values = both[:, :KVH], both[:, KVH:]
    grad_projected = jnp.concatenate(
        [
            rotate_back(grad_queries, cosine_table, sine_table).reshape(row_count, H * HD),
            rotate_back(grad_keys, cosine_table, sine_table).reshape(row_count, KVH * HD),
            grad_values.reshape(row_count, KVH * HD),
        ],
        axis=1,
    ).astype(jnp.bfloat16)
    grad_qkv = jnp.dot(record["attn_in"].T, grad_projected, preferred_element_type=jnp.float32)
    grad_normed_one = jnp.dot(grad_projected, qkv_w.T, preferred_element_type=jnp.float32)
    grad_in_one, grad_gain_one = normalize_back(
        grad_normed_one, record["stream"], record["scale_one"], gain_full[0]
    )
    grad_gains = jnp.stack([grad_gain_one, grad_gain_two])
    return (grad_middle + grad_in_one, (grad_qkv, grad_out, grad_up, grad_down, grad_gains))


def on_device(
    tokens,
    cotangent,
    routes,
    gate_weights,
    lengths,
    block_map,
    w_qkv,
    w_out,
    w_gateup,
    w_down,
    gains,
    m_qkv,
    v_qkv,
    m_out,
    v_out,
    m_gateup,
    v_gateup,
    m_down,
    v_down,
    m_gains,
    v_gains,
):
    row_count = tokens.shape[1]
    block_rows = row_count // 2
    own_pos, own_doc = positions_docs(block_map, lengths[0], flat_index(CTX), block_rows)
    places = [
        positions_docs(block_map, lengths[0], source_index(CTX, offsets), block_rows)
        for offsets in offsets_of(CTX)
    ]
    key_pos = jnp.concatenate([place[0] for place in places])
    key_doc = jnp.concatenate([place[1] for place in places])
    allowed = (own_doc[:, None] == key_doc[None, :]) & (key_pos[None, :] <= own_pos[:, None])
    cosine_table, sine_table = rope_tables(own_pos)
    own_tables = jnp.stack(
        [dispatch_tables(routes[layer, 0], gate_weights[layer, 0]) for layer in range(LAYERS)]
    )
    core = lax.axis_index("core")
    group_tables = []
    for offsets in offsets_of(GROUP):
        theirs = lax.dynamic_slice_in_dim(own_tables, 2 * target_index(GROUP, offsets), 2, axis=1)
        theirs = jnp.stack([jnp.where(core == 0, theirs[0], theirs[0, ::-1]), theirs[1]])
        group_tables.append(send(theirs, GROUP, offsets))
    stream = tokens[0].astype(jnp.float32)
    records = []
    gains_full = all_gains(gains)
    attn_w = [
        attention_weights_direct(w_qkv, w_out, 0) + (gains_full[0],),
        attention_weights(w_qkv, w_out, 1) + (gains_full[1],),
    ]
    expert_w = [
        expert_weights_direct(w_gateup, w_down, 0),
        expert_weights(w_gateup, w_down, 1),
    ]
    for layer_index in range(LAYERS):
        record, stream = layer_forward(
            stream,
            attn_w[layer_index],
            expert_w[layer_index],
            [table[layer_index] for table in group_tables],
            allowed,
            cosine_table,
            sine_table,
        )
        records.append(record)
    output = stream.astype(jnp.bfloat16)[None]
    gradient = cotangent[0].astype(jnp.float32)
    rates = (D ** (-0.5), 0.5, D ** (-0.5), (F // 8) ** (-0.5), 1.0)
    decays = (DECAY, DECAY, DECAY, DECAY, 0.0)
    params = (w_qkv, w_out, w_gateup, w_down, gains)
    firsts = (m_qkv, m_out, m_gateup, m_down, m_gains)
    seconds = (v_qkv, v_out, v_gateup, v_down, v_gains)
    updated = [[None] * LAYERS for which in range(15)]
    for layer_index in reversed(range(LAYERS)):
        gradient, layer_grads = layer_backward(
            gradient,
            records[layer_index],
            attn_w[layer_index],
            expert_w[layer_index],
            [table[layer_index] for table in group_tables],
            allowed,
            cosine_table,
            sine_table,
        )
        gain = lax.psum_scatter(layer_grads[4].T, ALL, scatter_dimension=0, tiled=True).T
        if layer_index:
            up, down = expert_grads(layer_grads[2], layer_grads[3])
            qkv, out = attention_grads(layer_grads[0], layer_grads[1])
        else:
            up, down = expert_grads_direct(layer_grads[2], layer_grads[3])
            qkv, out = attention_grads_direct(layer_grads[0], layer_grads[1])
        reduced = (qkv, out, up, down, gain)
        for which in range(5):
            fresh = adamw(
                params[which][layer_index],
                firsts[which][layer_index],
                seconds[which][layer_index],
                reduced[which],
                rates[which],
                decays[which],
            )
            updated[3 * which][layer_index] = fresh[0]
            updated[3 * which + 1][layer_index] = fresh[1]
            updated[3 * which + 2][layer_index] = fresh[2]
    stacked = [jnp.stack(pieces) for pieces in updated]
    return (output, gradient[None], *stacked)


def solution(mesh):
    ctx_size, shard_size = mesh.shape["ctx"], mesh.shape["shard"]
    fine = Mesh(mesh.devices.reshape(ctx_size // 2, 2, shard_size // 4, 2, 2), ALL)
    tokens = P(SHARD, CTX, None)
    routed = P(None, SHARD, CTX, None)
    rows_two = P(None, ALL, None)
    rows_three = P(None, None, ALL, None)
    gain = P(None, None, ALL)
    weights = (rows_two, rows_two, rows_three, rows_three, gain)
    states = tuple(spec for spec in weights for which in range(2))
    return jax.shard_map(
        on_device,
        mesh=fine,
        in_specs=(tokens, tokens, routed, routed, P(SHARD, None), P()) + weights + states,
        out_specs=(tokens, tokens) + tuple(spec for spec in weights for which in range(3)),
        check_vma=False,
    )
```

time: 4200 us -> 1510 us (0.36)
  waiting for transfers between devices: 3380 us -> 205 us
  Pallas kernels: 0 us -> 508 us
  blocking collectives: 133 us -> 48.7 us
  local copies, waits for them, and re-layouts: 97.4 us -> 155 us
  starting transfers between devices: 1.75 us -> 52.5 us
    reduce_scatter x12 -> x2, waiting for transfers between devices: 2690 us -> 93.8 us  [the longest x1 93.8 us: expert_grads(): lax.psum_scatter(packed, REPLICAS, scatter_dimension=0, tiled=False)]
    all_gather x8 -> x2, waiting for transfers between devices: 631 us -> 0.02 us  [the longest x1 0.02 us: attention_weights(): whole = lax.all_gather(packed, ALL, axis=0, tiled=True)]
    pallas_call x0 -> x4, Pallas kernels: none -> 508 us  [the longest x1 184 us: gather_experts(): pl.pallas_call(functools.partial(gather_experts_kernel, sizes), out_shape...]
    ppermute x0 -> x49, waiting for transfers between devices: none -> 111 us  [the longest x45 111 us: send(): return lax.ppermute(value, axes, shift_permutation(axes, offsets, back))]
    all_gather x6 -> x1, blocking collectives: 133 us -> 48.7 us  [all_gains(): whole = lax.all_gather(gains.astype(jnp.bfloat16), ALL, axis=2, tiled=True)]
    scatter-add x4 -> x0, other arithmetic: 72.7 us -> none  [the longest x2 36.4 us: layer_forward(): merged = jnp.zeros((row_count + 1, D), jnp.float32).at[slot_rows.reshape(...]
    unnamed x24 -> x8, waiting for transfers between devices: 60.6 us -> 0.1 us
    ppermute x0 -> x49, starting transfers between devices: none -> 51.4 us  [the longest x45 50.9 us: send(): return lax.ppermute(value, axes, shift_permutation(axes, offsets, back))]
  transfers between devices with their start and end apart: 22 -> 55, of which waited for: 19 -> 19; matrix products, arithmetic and copies ran while one was open for 9% -> 35% of each run, Pallas kernels for 0% -> 34%
where the time goes in v1:
time: 1510 us; the launch traced here: 1500 us
  Pallas kernels  508 us (34%)
  matrix products  360 us (24%)
  waiting for transfers between devices  205 us (14%)
  other arithmetic  156 us (10%)
  local copies, waits for them, and re-layouts  155 us (10%)
  starting transfers between devices  52.5 us (3%)
  blocking collectives  48.7 us (3%)
  between operations  17.6 us (1%)
    pallas_call x1, Pallas kernels, gather_experts(): pl.pallas_call(functools.partial(gather_experts_kernel, sizes), out_shape...  184 us
    pallas_call x1, Pallas kernels, sum_experts(): pl.pallas_call(functools.partial(sum_experts_kernel, sizes), out_shape=[j...  146 us
    ppermute x45, waiting for transfers between devices, send(): return lax.ppermute(value, axes, shift_permutation(axes, offsets, back))  111 us
    pallas_call x1, Pallas kernels, sum_attention(): pl.pallas_call(functools.partial(sum_attention_kernel, sizes), out_shape=...  100 us
    reduce_scatter x1, waiting for transfers between devices, expert_grads(): lax.psum_scatter(packed, REPLICAS, scatter_dimension=0, tiled=False)  93.8 us
    pallas_call x1, Pallas kernels, gather_attention(): pl.pallas_call(functools.partial(gather_attention_kernel, sizes), out_sha...  77.6 us
    dot_general x8, matrix products, experts_backward(): jnp.einsum('jst,jsd->td', select, grad_slots.astype(jnp.bfloat16), prefer...  72.3 us
    ppermute x45, starting transfers between devices, send(): return lax.ppermute(value, axes, shift_permutation(axes, offsets, back))  50.9 us
  transfers between devices with their start and end apart: 55, of which 19 were waited for; matrix products, arithmetic and copies ran while one was open for 35% of the time, Pallas kernels for 34%

profile of v1, /device:TPU:0, one launch (start us, length us, event | category | flops | bytes accessed | tf_op | source)
XLA Modules:
  0.0 1502.3 jit_solution(16500906696516487287)
XLA Ops:
  10.5 48.7 %all_gather.12 = bf16[2,2,1536]{1,0,2:T(2,128)(2,1)S(1)} all-gather(bf16[2,2,48]{1,0,2:T(2,128)(2,1)S(1)} %copy.428), channel_id=1, replica_groups=mesh['yo'=2,'xi'=2,'zo'=2,'zi'=2,'core'=2] {'yo','xi','zo','zi','core'}, dimensions={2}, use_global_device_ids=true | all-gather | bytes 12672 | tf_op jit(solution)/shard_map/all_gather | solution.py:788
  59.8 77.6 %shard_map.332 = (bf16[32,48,2048]{2,1,0:T(8,128)(2,1)S(1)}, bf16[32,48,1536]{2,1,0:T(8,128)(2,1)S(1)}) custom-call(bf16[48,2048]{1,0:T(8,128)(2,1)S(1)} %get-tuple-element.163.q_ref, bf16[48,1536]{1,0:T(8,128)(2,1)S(1)} %get-tuple-element.171.o_ref), custom_call_target="tpu_custom_call" | custom-call | tf_op jit(solution)/shard_map/pallas_call | solution.py:417
  137.7 39.3 %slice_reduce_fusion = (f32[1536]{0:T(1024)S(1)}, f32[1536]{0:T(1024)}, f32[1536]{0:T(1024)S(1)}, f32[1536]{0:T(1024)S(1)}) fusion(f32[2,2,1536]{1,0,2:T(2,128)S(1)} %convert_element_type.545), kind=kLoop, calls=%fused_computation.582 | loop fusion | bytes 49152 | tf_op jit(solution)/shard_map/slice | solution.py:978
  223.1 5.5 collective-permute-done.19
  229.6 6.6 collective-permute-done.18
  245.4 12.8 collective-permute-done
  275.8 183.7 %shard_map.333 = (bf16[2,16,96,1536]{3,2,1,0:T(8,128)(2,1)}, bf16[2,16,48,1536]{3,2,1,0:T(8,128)(2,1)S(1)}) custom-call(bf16[4,96,1536]{2,1,0:T(8,128)(2,1)S(1)} %bitcast.900, bf16[4,48,1536]{2,1,0:T(8,128)(2,1)S(1)} %bitcast.901), custom_call_target="tpu_custom_call" | custom-call | tf_op jit(solution)/shard_map/pallas_call | solution.py:518
  459.6 7.6 fusion.529
  476.8 4.9 fusion.155
  486.2 5.7 fusion.531
  496.2 4.9 fusion.154
  502.1 5.7 fusion.530
  512.3 5.0 fusion.153
  517.3 5.0 fusion.152
  530.5 6.2 collective-permute-done.7
  585.0 15.9 %collective-permute-done.24 = bf16[256,1536]{1,0:T(8,128)(2,1)S(1)} collective-permute-done((bf16[256,1536]{1,0:T(8,128)(2,1)S(1)}, bf16[256,1536]{1,0:T(8,128)(2,1)S(1)}, u32[]{:S(2)}, u32[]{:S(2)}) %collective-permute-start.24) | collective-permute-done | bytes 786464 | tf_op jit(solution)/shard_map/ppermute | solution.py:207
  602.3 12.3 collective-permute-done.22
  617.4 10.6 copy.597
  628.0 8.4 slice.728
  651.9 8.5 fusion.119
  661.9 5.7 fusion.535
  667.6 6.7 add_convert_fusion.10
  675.3 8.5 fusion.118
  684.4 5.7 fusion.534
  690.1 7.1 add_convert_fusion.11
  699.0 8.3 fusion.117
  708.8 6.6 fusion.533
  715.4 4.8 fusion.159
  721.7 5.0 fusion.158
  727.3 7.2 add_convert_fusion.12
  735.6 5.2 fusion.156
  740.8 5.0 fusion.157
  747.3 10.4 multiply_reduce_fusion
  777.3 4.9 fusion.203
  784.3 6.2 fusion.9
  790.5 7.7 fusion.11
  824.0 5.1 multiply_reduce_fusion.1
  840.4 5.9 convolution_convert_fusion.2
  846.3 5.9 collective-permute-done.39
  854.1 4.7 add_convert_fusion.5
  858.8 8.6 fusion.122
  871.4 4.7 add_convert_fusion.6
  876.1 8.5 fusion.121
  892.2 9.0 fusion.120
  902.7 5.7 add_convert_fusion.8
  908.4 11.2 collective-permute-done.36
  920.5 10.5 multiply_reduce_fusion.2
  941.8 4.9 fusion.197
  948.8 5.4 fusion.3
  954.2 7.3 fusion.5
  984.7 6.0 fusion.166
  991.9 9.5 pad_maximum_fusion.1
  1003.1 5.8 convolution_convert_fusion.6
  1013.2 11.5 convolution_convert_fusion
  1024.6 8.3 copy.598
  1033.0 12.3 pad_maximum_fusion
  1046.6 8.5 convolution_convert_fusion.7
  1055.1 11.9 convolution_convert_fusion.1
  1067.0 146.2 %shard_map.335 = (bf16[4,96,1536]{2,1,0:T(8,128)(2,1)}, bf16[4,48,1536]{2,1,0:T(8,128)(2,1)}) custom-call(bf16[2,16,96,1536]{3,2,1,0:T(8,128)(2,1)} %bitcast.950, bf16[2,16,48,1536]{3,2,1,0:T(8,128)(2,1)} %bitcast.956), custom_call_target="tpu_custom_call" | custom-call | tf_op jit(solution)/shard_map/pallas_call | solution.py:625
  1223.4 6.5 multiply_subtract_fusion
  1238.1 100.2 %shard_map.334 = (bf16[48,2048]{1,0:T(8,128)(2,1)}, bf16[48,1536]{1,0:T(8,128)(2,1)}) custom-call(bf16[16,2,48,2048]{3,2,1,0:T(8,128)(2,1)} %bitcast.942, bf16[16,2,48,1536]{3,2,1,0:T(8,128)(2,1)} %bitcast.943), custom_call_target="tpu_custom_call" | custom-call | tf_op jit(solution)/shard_map/pallas_call | solution.py:753
  1350.7 93.8 %reduce-scatter.11.cloned.1.call-done = bf16[1,4,2,72,1536]{4,3,2,1,0:T(8,128)(2,1)} async-done(((bf16[8,4,2,72,1536]{4,3,2,1,0:T(8,128)(2,1)}), bf16[1,4,2,72,1536]{4,3,2,1,0:T(8,128)(2,1)}) %reduce-scatter.11.cloned.1.call-update) | async-done | bytes 1769488 | tf_op jit(solution)/shard_map/reduce_scatter | solution.py:875
  1452.2 7.8 collective-permute-done.47
  1460.0 7.5 collective-permute-done.46
  (806 shorter events, 371.9 us)
Async XLA Ops:
  7.2 531.7 %all-gather.4.cloned.1.call-start = ((), (), s32[]{:S(2)}) async-start(), calls=%async_computation.4 | async-start | bytes 11354112 | tf_op jit(solution)/shard_map/all_gather | solution.py:831
  9.5 127.9 %copy-start.23 = (bf16[1,256,1536]{2,1,0:T(8,128)(2,1)S(1)}, bf16[1,256,1536]{2,1,0:T(8,128)(2,1)}, u32[]{:S(2)}) copy-start(bf16[1,256,1536]{2,1,0:T(8,128)(2,1)} %param.21) | copy-start | bytes 2359300
  10.3 607.1 %all-gather.6.cloned.1.call-start = ((), (), s32[]{:S(2)}) async-start(), calls=%async_computation.7 | async-start | bytes 15925248 | tf_op jit(solution)/shard_map/all_gather | solution.py:856
  176.9 95.4 %copy-start.144 = (f32[1536]{0:T(1024)}, f32[1536]{0:T(1024)S(1)}, u32[]{:S(2)}) copy-start(f32[1536]{0:T(1024)S(1)} %get-tuple-element.43) | copy-start | bytes 18436
  182.1 377.8 %copy-start.54 = (f32[256,64]{1,0:T(8,128)}, f32[256,64]{1,0:T(8,128)S(1)}, u32[]{:S(2)}) copy-start(f32[256,64]{1,0:T(8,128)S(1)} %get-tuple-element.226) | copy-start | bytes 196612
  184.5 59.2 %collective-permute-start.2 = (bf16[256,4,128]{2,0,1:T(8,128)(2,1)}, bf16[256,4,128]{2,0,1:T(8,128)(2,1)}, u32[]{:S(2)}, u32[]{:S(2)}) collective-permute-start(bf16[256,4,128]{2,0,1:T(8,128)(2,1)} %pad_maximum_fusion.34), channel_id=1, source_target_pairs={{0,24},{8,16},{16,8},{24,0},{1,25},{9,17},{17,9},{25,1},{2,26},{10... | collective-permute-start | bytes 786440 | tf_op jit(solution)/shard_map/ppermute | solution.py:207
  186.3 59.1 %collective-permute-start.1 = (bf16[256,4,128]{2,0,1:T(8,128)(2,1)}, bf16[256,4,128]{2,0,1:T(8,128)(2,1)}, u32[]{:S(2)}, u32[]{:S(2)}) collective-permute-start(bf16[256,4,128]{2,0,1:T(8,128)(2,1)} %pad_maximum_fusion.34), channel_id=1, source_target_pairs={{0,16},{8,24},{16,0},{24,8},{1,17},{9,25},{17,1},{25,9},{2,18},{10... | collective-permute-start | bytes 786440 | tf_op jit(solution)/shard_map/ppermute | solution.py:207
  190.1 24.5 %collective-permute-start.11 = (f32[2,2,2,256]{3,1,2,0:T(2,128)}, f32[2,2,2,256]{3,1,2,0:T(2,128)}, u32[]{:S(2)}, u32[]{:S(2)}) collective-permute-start(f32[2,2,2,256]{3,1,2,0:T(2,128)} %pad_maximum_fusion.40), channel_id=1, source_target_pairs={{0,10},{2,8},{8,2},{10,0},{1,11},{3,9},{9,3},{11,1},{4,14},{6,12},... | collective-permute-start | bytes 24584 | tf_op jit(solution)/shard_map/ppermute | solution.py:207
  190.8 25.5 %collective-permute-start.8 = (f32[2,2,2,256]{3,1,2,0:T(2,128)}, f32[2,2,2,256]{3,1,2,0:T(2,128)}, u32[]{:S(2)}, u32[]{:S(2)}) collective-permute-start(f32[2,2,2,256]{3,1,2,0:T(2,128)} %pad_maximum_fusion.39), channel_id=1, source_target_pairs={{0,8},{2,10},{8,0},{10,2},{1,9},{3,11},{9,1},{11,3},{4,12},{6,14},... | collective-permute-start | bytes 24584 | tf_op jit(solution)/shard_map/ppermute | solution.py:207
  192.4 26.2 %collective-permute-start.5 = (f32[2,2,2,256]{3,1,2,0:T(2,128)}, f32[2,2,2,256]{3,1,2,0:T(2,128)}, u32[]{:S(2)}, u32[]{:S(2)}) collective-permute-start(f32[2,2,2,256]{3,1,2,0:T(2,128)} %pad_maximum_fusion.38), channel_id=1, source_target_pairs={{0,2},{2,0},{8,10},{10,8},{1,3},{3,1},{9,11},{11,9},{4,6},{6,4},{1... | collective-permute-start | bytes 24584 | tf_op jit(solution)/shard_map/ppermute | solution.py:207
  206.5 66.7 %copy-start.149 = (f32[2,256]{1,0:T(2,128)}, f32[2,256]{1,0:T(2,128)S(1)}, u32[]{:S(2)}) copy-start(f32[2,256]{1,0:T(2,128)S(1)} %get-tuple-element.216) | copy-start | bytes 6148
  214.6 14.1 collective-permute-start.19
  216.3 19.9 %collective-permute-start.18 = (bf16[2,72,1536]{2,1,0:T(8,128)(2,1)S(1)}, bf16[2,72,1536]{2,1,0:T(8,128)(2,1)S(1)}, u32[]{:S(2)}, u32[]{:S(2)}) collective-permute-start(bf16[2,72,1536]{2,1,0:T(8,128)(2,1)S(1)} %get-tuple-element.132), channel_id=1, source_target_pairs={{0,8},{2,10},{8,0},{10,2},{1,9},{3,11},{9,1},{11,3},{4,12},{6,14},... | collective-permute-start | bytes 1327112 | tf_op jit(solution)/shard_map/ppermute | solution.py:207
  218.7 18.3 %collective-permute-start.17 = (bf16[2,72,1536]{2,1,0:T(8,128)(2,1)S(1)}, bf16[2,72,1536]{2,1,0:T(8,128)(2,1)S(1)}, u32[]{:S(2)}, u32[]{:S(2)}) collective-permute-start(bf16[2,72,1536]{2,1,0:T(8,128)(2,1)S(1)} %get-tuple-element.131), channel_id=1, source_target_pairs={{0,2},{2,0},{8,10},{10,8},{1,3},{3,1},{9,11},{11,9},{4,6},{6,4},{1... | collective-permute-start | bytes 1327112 | tf_op jit(solution)/shard_map/ppermute | solution.py:207
  228.7 29.6 %collective-permute-start = (bf16[256,4,128]{2,0,1:T(8,128)(2,1)}, bf16[256,4,128]{2,0,1:T(8,128)(2,1)}, u32[]{:S(2)}, u32[]{:S(2)}) collective-permute-start(bf16[256,4,128]{2,0,1:T(8,128)(2,1)} %pad_maximum_fusion.34), channel_id=1, source_target_pairs={{0,8},{8,0},{16,24},{24,16},{1,9},{9,1},{17,25},{25,17},{2,10},{10... | collective-permute-start | bytes 786440 | tf_op jit(solution)/shard_map/ppermute | solution.py:207
  236.2 281.0 %collective-permute-start.30 = (bf16[256,1536]{1,0:T(8,128)(2,1)}, bf16[256,1536]{1,0:T(8,128)(2,1)}, u32[]{:S(2)}, u32[]{:S(2)}) collective-permute-start(bf16[256,1536]{1,0:T(8,128)(2,1)} %bitcast.113), channel_id=1, source_target_pairs={{0,10},{2,8},{8,2},{10,0},{1,11},{3,9},{9,3},{11,1},{4,14},{6,12},... | collective-permute-start | bytes 2359304 | tf_op jit(solution)/shard_map/ppermute | solution.py:207
  236.9 286.7 %collective-permute-start.28 = (bf16[256,1536]{1,0:T(8,128)(2,1)}, bf16[256,1536]{1,0:T(8,128)(2,1)}, u32[]{:S(2)}, u32[]{:S(2)}) collective-permute-start(bf16[256,1536]{1,0:T(8,128)(2,1)} %bitcast.113), channel_id=1, source_target_pairs={{0,8},{2,10},{8,0},{10,2},{1,9},{3,11},{9,1},{11,3},{4,12},{6,14},... | collective-permute-start | bytes 2359304 | tf_op jit(solution)/shard_map/ppermute | solution.py:207
  242.8 972.5 %reduce-scatter.15.cloned.1.call-start = ((), (), s32[]{:S(2)}) async-start(), calls=%async_computation.9 | async-start | bytes 811008
  243.7 281.3 %collective-permute-start.26 = (bf16[256,1536]{1,0:T(8,128)(2,1)}, bf16[256,1536]{1,0:T(8,128)(2,1)}, u32[]{:S(2)}, u32[]{:S(2)}) collective-permute-start(bf16[256,1536]{1,0:T(8,128)(2,1)} %bitcast.113), channel_id=1, source_target_pairs={{0,2},{2,0},{8,10},{10,8},{1,3},{3,1},{9,11},{11,9},{4,6},{6,4},{1... | collective-permute-start | bytes 2359304 | tf_op jit(solution)/shard_map/ppermute | solution.py:207
  245.4 29.0 %collective-permute-start.3 = (bf16[4,48,1536]{2,1,0:T(8,128)(2,1)}, bf16[4,48,1536]{2,1,0:T(8,128)(2,1)S(1)}, u32[]{:S(2)}, u32[]{:S(2)}) collective-permute-start(bf16[4,48,1536]{2,1,0:T(8,128)(2,1)} %get-tuple-element.147), channel_id=1, source_target_pairs={{0,1},{1,0},{2,3},{3,2},{4,5},{5,4},{6,7},{7,6},{8,9},{9,8},{10,11... | collective-permute-start | bytes 1769480 | tf_op jit(solution)/shard_map/ppermute | solution.py:773
  258.3 15.3 %collective-permute-start.4 = (bf16[4,24,1536]{2,1,0:T(8,128)(2,1)}, bf16[4,24,1536]{2,1,0:T(8,128)(2,1)S(1)}, u32[]{:S(2)}, u32[]{:S(2)}) collective-permute-start(bf16[4,24,1536]{2,1,0:T(8,128)(2,1)} %get-tuple-element.173), channel_id=1, source_target_pairs={{0,1},{1,0},{2,3},{3,2},{4,5},{5,4},{6,7},{7,6},{8,9},{9,8},{10,11... | collective-permute-start | bytes 884744 | tf_op jit(solution)/shard_map/ppermute | solution.py:773
  271.7 265.0 %copy-start.10 = (f32[256,1536]{1,0:T(8,128)}, f32[256,1536]{1,0:T(8,128)S(1)}, u32[]{:S(2)}) copy-start(f32[256,1536]{1,0:T(8,128)S(1)} %get-tuple-element.239) | copy-start | bytes 4718596
  273.6 186.0 %copy-start.31 = (bf16[2,160,1536]{2,1,0:T(8,128)(2,1)}, bf16[2,160,1536]{2,1,0:T(8,128)(2,1)S(1)}, u32[]{:S(2)}) copy-start(bf16[2,160,1536]{2,1,0:T(8,128)(2,1)S(1)} %convolution_convert_fusion.23) | copy-start | bytes 2949124
  273.6 196.6 %collective-permute-start.12 = (bf16[256,1536]{1,0:T(8,128)(2,1)S(1)}, bf16[256,1536]{1,0:T(8,128)(2,1)S(1)}, u32[]{:S(2)}, u32[]{:S(2)}) collective-permute-start(bf16[256,1536]{1,0:T(8,128)(2,1)S(1)} %multiply_convert_fusion.18), channel_id=1, source_target_pairs={{0,10},{2,8},{8,2},{10,0},{1,11},{3,9},{9,3},{11,1},{4,14},{6,12},... | collective-permute-start | bytes 2359304 | tf_op jit(solution)/shard_map/ppermute | solution.py:207
  274.4 207.3 %collective-permute-start.9 = (bf16[256,1536]{1,0:T(8,128)(2,1)S(1)}, bf16[256,1536]{1,0:T(8,128)(2,1)}, u32[]{:S(2)}, u32[]{:S(2)}) collective-permute-start(bf16[256,1536]{1,0:T(8,128)(2,1)S(1)} %multiply_convert_fusion.18), channel_id=1, source_target_pairs={{0,8},{2,10},{8,0},{10,2},{1,9},{3,11},{9,1},{11,3},{4,12},{6,14},... | collective-permute-start | bytes 2359304 | tf_op jit(solution)/shard_map/ppermute | solution.py:207
  470.3 30.8 %collective-permute-start.6 = (bf16[256,1536]{1,0:T(8,128)(2,1)S(1)}, bf16[256,1536]{1,0:T(8,128)(2,1)S(1)}, u32[]{:S(2)}, u32[]{:S(2)}) collective-permute-start(bf16[256,1536]{1,0:T(8,128)(2,1)S(1)} %multiply_convert_fusion.18), channel_id=1, source_target_pairs={{0,2},{2,0},{8,10},{10,8},{1,3},{3,1},{9,11},{11,9},{4,6},{6,4},{1... | collective-permute-start | bytes 2359304 | tf_op jit(solution)/shard_map/ppermute | solution.py:207
  481.7 48.8 %collective-permute-start.13 = (bf16[256,1536]{1,0:T(8,128)(2,1)}, bf16[256,1536]{1,0:T(8,128)(2,1)}, u32[]{:S(2)}, u32[]{:S(2)}) collective-permute-start(bf16[256,1536]{1,0:T(8,128)(2,1)} %fusion.155), channel_id=1, source_target_pairs={{10,0},{8,2},{2,8},{0,10},{11,1},{9,3},{3,9},{1,11},{14,4},{12,6},... | collective-permute-start | bytes 2359304 | tf_op jit(solution)/shard_map/ppermute | solution.py:207
  501.1 29.4 %collective-permute-start.10 = (bf16[256,1536]{1,0:T(8,128)(2,1)}, bf16[256,1536]{1,0:T(8,128)(2,1)}, u32[]{:S(2)}, u32[]{:S(2)}) collective-permute-start(bf16[256,1536]{1,0:T(8,128)(2,1)} %fusion.154), channel_id=1, source_target_pairs={{8,0},{10,2},{0,8},{2,10},{9,1},{11,3},{1,9},{3,11},{12,4},{14,6},... | collective-permute-start | bytes 2359304 | tf_op jit(solution)/shard_map/ppermute | solution.py:207
  517.3 19.4 %collective-permute-start.7 = (bf16[256,1536]{1,0:T(8,128)(2,1)}, bf16[256,1536]{1,0:T(8,128)(2,1)}, u32[]{:S(2)}, u32[]{:S(2)}) collective-permute-start(bf16[256,1536]{1,0:T(8,128)(2,1)} %fusion.153), channel_id=1, source_target_pairs={{2,0},{0,2},{10,8},{8,10},{3,1},{1,3},{11,9},{9,11},{6,4},{4,6},{1... | collective-permute-start | bytes 2359304 | tf_op jit(solution)/shard_map/ppermute | solution.py:207
  546.7 15.9 %collective-permute-start.16 = (bf16[256,4,128]{2,0,1:T(8,128)(2,1)}, bf16[256,4,128]{2,0,1:T(8,128)(2,1)S(1)}, u32[]{:S(2)}, u32[]{:S(2)}) collective-permute-start(bf16[256,4,128]{2,0,1:T(8,128)(2,1)} %pad_maximum_fusion.35), channel_id=1, source_target_pairs={{0,24},{8,16},{16,8},{24,0},{1,25},{9,17},{17,9},{25,1},{2,26},{10... | collective-permute-start | bytes 786440 | tf_op jit(solution)/shard_map/ppermute | solution.py:207
  549.1 13.5 collective-permute-start.15
  549.6 12.9 collective-permute-start.14
  579.4 21.5 %collective-permute-start.24 = (bf16[256,1536]{1,0:T(8,128)(2,1)S(1)}, bf16[256,1536]{1,0:T(8,128)(2,1)S(1)}, u32[]{:S(2)}, u32[]{:S(2)}) collective-permute-start(bf16[256,1536]{1,0:T(8,128)(2,1)S(1)} %multiply_convert_fusion.16), channel_id=1, source_target_pairs={{0,10},{2,8},{8,2},{10,0},{1,11},{3,9},{9,3},{11,1},{4,14},{6,12},... | collective-permute-start | bytes 2359304 | tf_op jit(solution)/shard_map/ppermute | solution.py:207
  582.6 31.9 %collective-permute-start.22 = (bf16[256,1536]{1,0:T(8,128)(2,1)S(1)}, bf16[256,1536]{1,0:T(8,128)(2,1)S(1)}, u32[]{:S(2)}, u32[]{:S(2)}) collective-permute-start(bf16[256,1536]{1,0:T(8,128)(2,1)S(1)} %multiply_convert_fusion.16), channel_id=1, source_target_pairs={{0,8},{2,10},{8,0},{10,2},{1,9},{3,11},{9,1},{11,3},{4,12},{6,14},... | collective-permute-start | bytes 2359304 | tf_op jit(solution)/shard_map/ppermute | solution.py:207
  584.1 31.9 %collective-permute-start.20 = (bf16[256,1536]{1,0:T(8,128)(2,1)S(1)}, bf16[256,1536]{1,0:T(8,128)(2,1)S(1)}, u32[]{:S(2)}, u32[]{:S(2)}) collective-permute-start(bf16[256,1536]{1,0:T(8,128)(2,1)S(1)} %multiply_convert_fusion.16), channel_id=1, source_target_pairs={{0,2},{2,0},{8,10},{10,8},{1,3},{3,1},{9,11},{11,9},{4,6},{6,4},{1... | collective-permute-start | bytes 2359304 | tf_op jit(solution)/shard_map/ppermute | solution.py:207
  585.0 123.8 %copy-start.39 = (bf16[2,160,1536]{2,1,0:T(8,128)(2,1)}, bf16[2,160,1536]{2,1,0:T(8,128)(2,1)S(1)}, u32[]{:S(2)}) copy-start(bf16[2,160,1536]{2,1,0:T(8,128)(2,1)S(1)} %convolution_convert_fusion.15) | copy-start | bytes 2949124
  660.4 85.5 %collective-permute-start.31 = (bf16[256,1536]{1,0:T(8,128)(2,1)}, bf16[256,1536]{1,0:T(8,128)(2,1)}, u32[]{:S(2)}, u32[]{:S(2)}) collective-permute-start(bf16[256,1536]{1,0:T(8,128)(2,1)} %fusion.119), channel_id=1, source_target_pairs={{10,0},{8,2},{2,8},{0,10},{11,1},{9,3},{3,9},{1,11},{14,4},{12,6},... | collective-permute-start | bytes 2359304 | tf_op jit(solution)/shard_map/ppermute | solution.py:207
  683.8 63.4 %collective-permute-start.29 = (bf16[256,1536]{1,0:T(8,128)(2,1)}, bf16[256,1536]{1,0:T(8,128)(2,1)}, u32[]{:S(2)}, u32[]{:S(2)}) collective-permute-start(bf16[256,1536]{1,0:T(8,128)(2,1)} %fusion.118), channel_id=1, source_target_pairs={{8,0},{10,2},{0,8},{2,10},{9,1},{11,3},{1,9},{3,11},{12,4},{14,6},... | collective-permute-start | bytes 2359304 | tf_op jit(solution)/shard_map/ppermute | solution.py:207
  707.4 39.9 %collective-permute-start.27 = (bf16[256,1536]{1,0:T(8,128)(2,1)}, bf16[256,1536]{1,0:T(8,128)(2,1)}, u32[]{:S(2)}, u32[]{:S(2)}) collective-permute-start(bf16[256,1536]{1,0:T(8,128)(2,1)} %fusion.117), channel_id=1, source_target_pairs={{2,0},{0,2},{10,8},{8,10},{3,1},{1,3},{11,9},{9,11},{6,4},{4,6},{1... | collective-permute-start | bytes 2359304 | tf_op jit(solution)/shard_map/ppermute | solution.py:207
  720.2 37.4 %collective-permute-start.25 = (bf16[256,1536]{1,0:T(8,128)(2,1)}, bf16[256,1536]{1,0:T(8,128)(2,1)}, u32[]{:S(2)}, u32[]{:S(2)}) collective-permute-start(bf16[256,1536]{1,0:T(8,128)(2,1)} %fusion.159), channel_id=1, source_target_pairs={{10,0},{8,2},{2,8},{0,10},{11,1},{9,3},{3,9},{1,11},{14,4},{12,6},... | collective-permute-start | bytes 2359304 | tf_op jit(solution)/shard_map/ppermute | solution.py:207
  726.7 34.2 %collective-permute-start.23 = (bf16[256,1536]{1,0:T(8,128)(2,1)}, bf16[256,1536]{1,0:T(8,128)(2,1)}, u32[]{:S(2)}, u32[]{:S(2)}) collective-permute-start(bf16[256,1536]{1,0:T(8,128)(2,1)} %fusion.158), channel_id=1, source_target_pairs={{8,0},{10,2},{0,8},{2,10},{9,1},{11,3},{1,9},{3,11},{12,4},{14,6},... | collective-permute-start | bytes 2359304 | tf_op jit(solution)/shard_map/ppermute | solution.py:207
  745.8 18.5 %collective-permute-start.21 = (bf16[256,1536]{1,0:T(8,128)(2,1)}, bf16[256,1536]{1,0:T(8,128)(2,1)}, u32[]{:S(2)}, u32[]{:S(2)}) collective-permute-start(bf16[256,1536]{1,0:T(8,128)(2,1)} %fusion.157), channel_id=1, source_target_pairs={{2,0},{0,2},{10,8},{8,10},{3,1},{1,3},{11,9},{9,11},{6,4},{4,6},{1... | collective-permute-start | bytes 2359304 | tf_op jit(solution)/shard_map/ppermute | solution.py:207
  807.5 10.2 collective-permute-start.34
  809.7 10.7 collective-permute-start.33
  810.2 10.2 collective-permute-start.32
  830.4 71.4 %copy-start.25 = (f32[256,1536]{1,0:T(8,128)}, f32[256,1536]{1,0:T(8,128)S(1)}, u32[]{:S(2)}) copy-start(f32[256,1536]{1,0:T(8,128)S(1)} %get-tuple-element.69) | copy-start | bytes 4718596
  830.4 21.7 %collective-permute-start.39 = (bf16[256,1536]{1,0:T(8,128)(2,1)}, bf16[256,1536]{1,0:T(8,128)(2,1)}, u32[]{:S(2)}, u32[]{:S(2)}) collective-permute-start(bf16[256,1536]{1,0:T(8,128)(2,1)} %get-tuple-element.68), channel_id=1, source_target_pairs={{0,10},{2,8},{8,2},{10,0},{1,11},{3,9},{9,3},{11,1},{4,14},{6,12},... | collective-permute-start | bytes 2359304 | tf_op jit(solution)/shard_map/ppermute | solution.py:207
  836.0 33.4 %collective-permute-start.37 = (bf16[256,1536]{1,0:T(8,128)(2,1)}, bf16[256,1536]{1,0:T(8,128)(2,1)}, u32[]{:S(2)}, u32[]{:S(2)}) collective-permute-start(bf16[256,1536]{1,0:T(8,128)(2,1)} %get-tuple-element.68), channel_id=1, source_target_pairs={{0,8},{2,10},{8,0},{10,2},{1,9},{3,11},{9,1},{11,3},{4,12},{6,14},... | collective-permute-start | bytes 2359304 | tf_op jit(solution)/shard_map/ppermute | solution.py:207
  837.0 48.6 %collective-permute-start.35 = (bf16[256,1536]{1,0:T(8,128)(2,1)}, bf16[256,1536]{1,0:T(8,128)(2,1)}, u32[]{:S(2)}, u32[]{:S(2)}) collective-permute-start(bf16[256,1536]{1,0:T(8,128)(2,1)} %get-tuple-element.68), channel_id=1, source_target_pairs={{0,2},{2,0},{8,10},{10,8},{1,3},{3,1},{9,11},{11,9},{4,6},{6,4},{1... | collective-permute-start | bytes 2359304 | tf_op jit(solution)/shard_map/ppermute | solution.py:207
  840.1 499.8 %reduce-scatter.13.cloned.1.call-start = ((), (), s32[]{:S(2)}) async-start(), calls=%async_computation.8 | async-start | bytes 811008
  867.4 41.0 %collective-permute-start.40 = (bf16[256,1536]{1,0:T(8,128)(2,1)}, bf16[256,1536]{1,0:T(8,128)(2,1)}, u32[]{:S(2)}, u32[]{:S(2)}) collective-permute-start(bf16[256,1536]{1,0:T(8,128)(2,1)} %fusion.122), channel_id=1, source_target_pairs={{10,0},{8,2},{2,8},{0,10},{11,1},{9,3},{3,9},{1,11},{14,4},{12,6},... | collective-permute-start | bytes 2359304 | tf_op jit(solution)/shard_map/ppermute | solution.py:207
  884.6 23.8 %collective-permute-start.38 = (bf16[256,1536]{1,0:T(8,128)(2,1)}, bf16[256,1536]{1,0:T(8,128)(2,1)}, u32[]{:S(2)}, u32[]{:S(2)}) collective-permute-start(bf16[256,1536]{1,0:T(8,128)(2,1)} %fusion.121), channel_id=1, source_target_pairs={{8,0},{10,2},{0,8},{2,10},{9,1},{11,3},{1,9},{3,11},{12,4},{14,6},... | collective-permute-start | bytes 2359304 | tf_op jit(solution)/shard_map/ppermute | solution.py:207
  901.2 18.5 %collective-permute-start.36 = (bf16[256,1536]{1,0:T(8,128)(2,1)}, bf16[256,1536]{1,0:T(8,128)(2,1)S(1)}, u32[]{:S(2)}, u32[]{:S(2)}) collective-permute-start(bf16[256,1536]{1,0:T(8,128)(2,1)} %fusion.120), channel_id=1, source_target_pairs={{2,0},{0,2},{10,8},{8,10},{3,1},{1,3},{11,9},{9,11},{6,4},{4,6},{1... | collective-permute-start | bytes 2359304 | tf_op jit(solution)/shard_map/ppermute | solution.py:207
  970.5 9.1 collective-permute-start.43
  972.5 9.8 collective-permute-start.42
  973.0 9.9 collective-permute-start.41
  991.9 350.6 %reduce-scatter.9.cloned.1.call-start = ((), (), s32[]{:S(2)}) async-start(), calls=%async_computation.5 | async-start | bytes 11354112 | tf_op jit(solution)/shard_map/reduce_scatter | solution.py:889
  1001.4 443.1 %reduce-scatter.11.cloned.1.call-start = ((), (), s32[]{:S(2)}) async-start(), calls=%async_computation.6 | async-start | bytes 15925248 | tf_op jit(solution)/shard_map/reduce_scatter | solution.py:875
  1215.2 2.9 collective-permute-start.48
  1217.6 5.6 collective-permute-start.44
  1238.1 100.2 %copy-start.93 = (f32[256,1536]{1,0:T(8,128)S(1)}, f32[256,1536]{1,0:T(8,128)}, u32[]{:S(2)}) copy-start(f32[256,1536]{1,0:T(8,128)} %get-tuple-element.254) | copy-start | bytes 4718596
  1446.0 14.0 collective-permute-start.47
  1446.1 21.4 %collective-permute-start.46 = (bf16[2,72,1536]{2,1,0:T(8,128)(2,1)S(1)}, bf16[2,72,1536]{2,1,0:T(8,128)(2,1)S(1)}, u32[]{:S(2)}, u32[]{:S(2)}) collective-permute-start(bf16[2,72,1536]{2,1,0:T(8,128)(2,1)S(1)} %get-tuple-element.126), channel_id=1, source_target_pairs={{0,8},{2,10},{8,0},{10,2},{1,9},{3,11},{9,1},{11,3},{4,12},{6,14},... | collective-permute-start | bytes 1327112 | tf_op jit(solution)/shard_map/ppermute | solution.py:207
  1447.6 20.8 %collective-permute-start.45 = (bf16[2,72,1536]{2,1,0:T(8,128)(2,1)S(1)}, bf16[2,72,1536]{2,1,0:T(8,128)(2,1)S(1)}, u32[]{:S(2)}, u32[]{:S(2)}) collective-permute-start(bf16[2,72,1536]{2,1,0:T(8,128)(2,1)S(1)} %get-tuple-element.127), channel_id=1, source_target_pairs={{0,2},{2,0},{8,10},{10,8},{1,3},{3,1},{9,11},{11,9},{4,6},{6,4},{1... | collective-permute-start | bytes 1327112 | tf_op jit(solution)/shard_map/ppermute | solution.py:207
  (213 other events, 1423.0 us)
Sparse Core Ops, SparseCore 0:
  11.6 117.5 all-gather.3
  242.9 210.0 all-gather.5
  840.3 94.4 reduce-scatter.14
  992.0 94.3 reduce-scatter.12
  1092.3 181.3 reduce-scatter.8
  1277.1 167.3 reduce-scatter.10

commit v2 on v1

v2 whole, which is shorter than its diff:
```python
import functools

import jax
import jax.numpy as jnp
from jax import lax
from jax.experimental import pallas as pl
from jax.experimental.pallas import tpu as pltpu
from jax.sharding import Mesh
from jax.sharding import PartitionSpec as P

D = 1536
H = 12
KVH = 2
HD = 128
F = 768
TOP = 4
EXPERTS = 8
LAYERS = 2
STEP = 10
CAP = 160


NORM_EPS = 1e-06
ROPE_BASE = 1000000.0
BETA_ONE = 0.9
BETA_TWO = 0.95
ADAM_EPS = 1e-08
DECAY = 0.1
MASKED = -1e30


def rope_tables(positions):
    half_width = HD // 2
    frequency = ROPE_BASE ** (-(jnp.arange(half_width, dtype=jnp.float32) * 2.0 / HD))
    angles = positions.astype(jnp.float32)[:, None] * frequency[None, :]
    return (jnp.cos(angles)[:, None, :], jnp.sin(angles)[:, None, :])


def rotate(vectors, cosine_table, sine_table):
    half_width = vectors.shape[-1] // 2
    first_half = vectors[..., :half_width]
    second_half = vectors[..., half_width:]
    return jnp.concatenate(
        [
            first_half * cosine_table - second_half * sine_table,
            second_half * cosine_table + first_half * sine_table,
        ],
        axis=-1,
    )


def rotate_back(gradient, cosine_table, sine_table):
    half_width = gradient.shape[-1] // 2
    first_half = gradient[..., :half_width]
    second_half = gradient[..., half_width:]
    return jnp.concatenate(
        [
            first_half * cosine_table + second_half * sine_table,
            second_half * cosine_table - first_half * sine_table,
        ],
        axis=-1,
    )


def normalize(values, gain_row):
    row_scale = lax.rsqrt(jnp.mean(values * values, axis=-1, keepdims=True) + NORM_EPS)
    return (values * row_scale * gain_row, row_scale)


def normalize_back(gradient, values, row_scale, gain_row):
    unit_rows = values * row_scale
    inner_grad = gradient * gain_row
    input_grad = row_scale * (
        inner_grad - unit_rows * jnp.mean(inner_grad * unit_rows, axis=-1, keepdims=True)
    )
    return (input_grad, jnp.sum(gradient * unit_rows, axis=0))


def adamw(parameter, moment, second, gradient, step_rate, decay_rate):
    moment = BETA_ONE * moment + (1.0 - BETA_ONE) * gradient
    second = BETA_TWO * second + (1.0 - BETA_TWO) * gradient * gradient
    direction = (
        moment / (1.0 - BETA_ONE**STEP) / (jnp.sqrt(second / (1.0 - BETA_TWO**STEP)) + ADAM_EPS)
    )
    return (parameter - step_rate * (direction + decay_rate * parameter), moment, second)


def attention_forward(queries, keys_all, values_all, allowed):
    group_size = H // KVH
    score_scale = HD ** (-0.5)
    outputs = []
    totals = []
    for head_group in range(KVH):
        query_part = queries[:, head_group * group_size : (head_group + 1) * group_size, :]
        scores = (
            jnp.einsum(
                "tjd,kd->jtk",
                query_part,
                keys_all[:, head_group, :],
                preferred_element_type=jnp.float32,
            )
            * score_scale
        )
        scores = jnp.where(allowed[None], scores, MASKED)
        row_max = jnp.max(scores, axis=-1, keepdims=True)
        exponent = jnp.exp(scores - row_max)
        row_total = jnp.sum(exponent, axis=-1, keepdims=True)
        probabilities = (exponent / row_total).astype(jnp.bfloat16)
        outputs.append(
            jnp.einsum(
                "jtk,kd->tjd",
                probabilities,
                values_all[:, head_group, :],
                preferred_element_type=jnp.float32,
            )
        )
        totals.append(row_max + jnp.log(row_total))
    return (jnp.concatenate(outputs, axis=1), totals)


def attention_backward(queries, keys_all, values_all, allowed, totals, grad_attended):
    group_size = H // KVH
    score_scale = HD ** (-0.5)
    grad_queries = []
    grad_keys = []
    grad_values = []
    for head_group in range(KVH):
        query_part = queries[:, head_group * group_size : (head_group + 1) * group_size, :]
        grad_part = grad_attended[:, head_group * group_size : (head_group + 1) * group_size, :]
        keys_part = keys_all[:, head_group, :]
        scores = (
            jnp.einsum("tjd,kd->jtk", query_part, keys_part, preferred_element_type=jnp.float32)
            * score_scale
        )
        probabilities = jnp.where(allowed[None], jnp.exp(scores - totals[head_group]), 0.0)
        grad_probs = jnp.einsum(
            "tjd,kd->jtk",
            grad_part,
            values_all[:, head_group, :],
            preferred_element_type=jnp.float32,
        )
        grad_scores = probabilities * (
            grad_probs - jnp.sum(probabilities * grad_probs, axis=-1, keepdims=True)
        )
        grad_scores = grad_scores.astype(jnp.bfloat16)
        grad_queries.append(
            jnp.einsum("jtk,kd->tjd", grad_scores, keys_part, preferred_element_type=jnp.float32)
            * score_scale
        )
        grad_keys.append(
            jnp.einsum("jtk,tjd->kd", grad_scores, query_part, preferred_element_type=jnp.float32)
            * score_scale
        )
        grad_values.append(
            jnp.einsum(
                "jtk,tjd->kd",
                probabilities.astype(jnp.bfloat16),
                grad_part,
                preferred_element_type=jnp.float32,
            )
        )
    return (
        jnp.concatenate(grad_queries, axis=1),
        jnp.stack(grad_keys, axis=1),
        jnp.stack(grad_values, axis=1),
    )


CTX = ("yo", "xi")
SHARD = ("zo", "zi", "core")
ALL = CTX + SHARD
GROUP = ("xi", "zi")
REPLICAS = ("yo", "zo", "core")


def flat_index(axes):
    index = 0
    for axis in axes:
        index = index * lax.axis_size(axis) + lax.axis_index(axis)
    return index


def shift_permutation(axes, offsets, back=False):
    sizes = [lax.axis_size(axis) for axis in axes]
    pairs = []
    for first in range(sizes[0]):
        for second in range(sizes[1]):
            target = ((first + offsets[0]) % sizes[0], (second + offsets[1]) % sizes[1])
            here = first * sizes[1] + second
            there = target[0] * sizes[1] + target[1]
            pairs.append((there, here) if back else (here, there))
    return pairs


def offsets_of(axes):
    sizes = [lax.axis_size(axis) for axis in axes]
    return [(a, b) for a in range(sizes[0]) for b in range(sizes[1])]


def send(value, axes, offsets, back=False):
    if offsets == (0, 0):
        return value
    return lax.ppermute(value, axes, shift_permutation(axes, offsets, back))


def source_index(axes, offsets):
    sizes = [lax.axis_size(axis) for axis in axes]
    return lax.rem(lax.axis_index(axes[0]) - offsets[0] + sizes[0], sizes[0]) * sizes[1] + lax.rem(
        lax.axis_index(axes[1]) - offsets[1] + sizes[1], sizes[1]
    )


def target_index(axes, offsets):
    sizes = [lax.axis_size(axis) for axis in axes]
    return lax.rem(lax.axis_index(axes[0]) + offsets[0], sizes[0]) * sizes[1] + lax.rem(
        lax.axis_index(axes[1]) + offsets[1], sizes[1]
    )


def positions_docs(block_map, lengths_row, ctx_index, block_rows):
    blocks = lax.dynamic_slice_in_dim(block_map, 2 * ctx_index, 2)
    offsets = jnp.arange(block_rows, dtype=jnp.int32)
    positions = (blocks[:, None] * block_rows + offsets[None, :]).reshape(-1)
    bounds = jnp.cumsum(lengths_row)
    documents = jnp.sum((positions[:, None] >= bounds[None, :]).astype(jnp.int32), axis=1)
    return (positions, documents)


def dispatch_tables(routes, gates):
    rows = routes.shape[0]
    hits = (routes[None] == jnp.arange(EXPERTS, dtype=jnp.int32)[:, None, None]).astype(jnp.float32)
    member = jnp.sum(hits, axis=-1)
    gate = jnp.sum(hits * gates[None], axis=-1)
    before = (jnp.arange(rows)[:, None] < jnp.arange(rows)[None, :]).astype(jnp.float32)
    rank = jnp.dot(member, before, preferred_element_type=jnp.float32)
    return jnp.stack([jnp.where(member > 0, rank, -1.0), gate], axis=1)


MESH = pl.DeviceIdType.MESH
QKV = (H + 2 * KVH) * HD


class Place:
    def __init__(self, sizes):
        self.yo_size, self.zo_size = sizes
        self.yo, self.xi, self.zo, self.zi, self.core = [lax.axis_index(axis) for axis in ALL]
        self.y_steps = range(1, self.yo_size)
        self.z_steps = range(1, self.zo_size)
        self.column = [(a, b) for a in range(self.zo_size) for b in range(2)]

    def at(self, y=0, x=0, z=0, w=0, core=0):
        return (
            lax.rem(self.yo + y, self.yo_size),
            1 - self.xi if x else self.xi,
            lax.rem(self.zo + z, self.zo_size),
            1 - self.zi if w else self.zi,
            1 - self.core if core else self.core,
        )

    def chip(self, y=0, x=0, z=0, w=0):
        yo, xi, zo, zi, core = self.at(y, x, z, w)
        return ((yo * 2 + xi) * self.zo_size + zo) * 2 + zi

    def back_y(self, y):
        return (self.yo_size - y) % self.yo_size

    def back_z(self, z):
        return (self.zo_size - z) % self.zo_size


class Wires:
    def __init__(self, send_sems, recv_sems):
        self.send_sems, self.recv_sems = send_sems, recv_sems
        self.started = []

    def send(self, source, target, name, device):
        copy = pltpu.make_async_remote_copy(
            src_ref=source,
            dst_ref=target,
            send_sem=self.send_sems.at[len(self.started)],
            recv_sem=self.recv_sems.at[name],
            device_id=device,
            device_id_type=MESH,
        )
        copy.start()
        self.started.append(copy)

    def arrive(self, target, name, device):
        pltpu.make_async_remote_copy(
            src_ref=target,
            dst_ref=target,
            send_sem=self.send_sems.at[0],
            recv_sem=self.recv_sems.at[name],
            device_id=device,
            device_id_type=MESH,
        ).wait_recv()

    def drain(self):
        for copy in self.started:
            copy.wait_send()


def greet(partners):
    barrier = pltpu.get_barrier_semaphore()
    for partner in partners:
        pl.semaphore_signal(barrier, inc=1, device_id=partner, device_id_type=MESH)
    pl.semaphore_wait(barrier, len(partners))


def mesh_sizes():
    return lax.axis_size("yo"), lax.axis_size("zo")


def add_rows(target, *parts):
    size = 16 if target.shape[0] % 16 == 0 else target.shape[0]

    def step(index, carry):
        rows = pl.ds(pl.multiple_of(index * size, size), size)
        total = target[rows, :].astype(jnp.float32)
        for part in parts:
            total = total + part[rows, :].astype(jnp.float32)
        target[rows, :] = total.astype(target.dtype)
        return carry

    lax.fori_loop(0, target.shape[0] // size, step, 0)


def together(*steps):
    alive = list(steps)
    while alive:
        for one in list(alive):
            try:
                next(one)
            except StopIteration:
                alive.remove(one)


def greet_layer(here):
    greet(
        [here.at(z=z, w=w) for z, w in here.column if (z, w) != (0, 0)]
        + [here.at(x=1), here.at(x=1, w=1), here.at(core=1)]
        + [here.at(y=y) for y in here.y_steps]
    )


def gather_attention_steps(here, wires, shards, wholes):
    count = len(shards)
    far = [offset for offset in here.column if offset != (0, 0)]
    mine = here.chip() * 2 + here.core
    other = here.at(core=1)

    def block(**offsets):
        return here.chip(**offsets) * 2 + here.core

    def name(kind, y, x, z, w, part):
        spot = (((kind * here.yo_size + y) * 2 + x) * here.zo_size + z) * 2 + w
        return spot * count + part

    for z, w in far:
        for part in range(count):
            wires.send(
                shards[part],
                wholes[part].at[mine],
                name(0, 0, 0, here.back_z(z), w, part),
                here.at(z=z, w=w),
            )

    def pass_on(source, y, x, z, w, part, to_x, to_y):
        target = wholes[part].at[block(y=y, x=x, z=z, w=w)]
        if to_x:
            wires.send(source, target, name(0, y, 1 - x, z, w, part), here.at(x=1))
        for step in here.y_steps if to_y else ():
            back = (y + here.back_y(step)) % here.yo_size
            wires.send(source, target, name(0, back, x, z, w, part), here.at(y=step))
        wires.send(source, target, name(1, y, x, z, w, part), other)

    for z, w in here.column:
        for part in range(count):
            if (z, w) == (0, 0):
                pass_on(shards[part], 0, 0, 0, 0, part, True, True)
                wholes[part][mine] = shards[part][...]
            else:
                source = wholes[part].at[block(z=z, w=w)]
                wires.arrive(source, name(0, 0, 0, z, w, part), other)
                pass_on(source, 0, 0, z, w, part, True, True)
        yield
    for z, w in here.column:
        for part in range(count):
            source = wholes[part].at[block(x=1, z=z, w=w)]
            wires.arrive(source, name(0, 0, 1, z, w, part), other)
            pass_on(source, 0, 1, z, w, part, False, part % 2 == 1)
            for y in here.y_steps:
                source = wholes[part].at[block(y=y, z=z, w=w)]
                wires.arrive(source, name(0, y, 0, z, w, part), other)
                pass_on(source, y, 0, z, w, part, part % 2 == 0, False)
        yield
    for z, w in here.column:
        for part in range(count):
            for y in here.y_steps:
                source = wholes[part].at[block(y=y, x=1, z=z, w=w)]
                wires.arrive(source, name(0, y, 1, z, w, part), other)
                pass_on(source, y, 1, z, w, part, False, False)
        yield
    for y in range(here.yo_size):
        for x in range(2):
            for z, w in here.column:
                for part in range(count):
                    index = here.chip(y=y, x=x, z=z, w=w) * 2 + 1 - here.core
                    wires.arrive(wholes[part].at[index], name(1, y, x, z, w, part), other)


def gather_experts_steps(here, wires, shards, wholes):
    count = len(shards)
    group = offsets_of(GROUP)
    other = here.at(core=1)

    def name(kind, y, x, z, w, part):
        spot = (((kind * here.yo_size + y) * 2 + x) * here.zo_size + z) * 2 + w
        return spot * count + part

    def member(x, w):
        yo, xi, zo, zi, core = here.at(x=x, w=w)
        return xi * 2 + zi

    for x, w in group[1:]:
        for part in range(count):
            wires.send(
                shards[part].at[member(x, w)],
                wholes[part].at[0, here.chip()],
                name(0, 0, x, 0, w, part),
                here.at(x=x, w=w),
            )

    def pass_on(source, y, x, z, w, part, to_z, to_y):
        index = here.chip(y=y, x=x, z=z, w=w)
        for step in here.z_steps if to_z else ():
            back = (z + here.back_z(step)) % here.zo_size
            wires.send(
                source, wholes[part].at[0, index], name(0, y, x, back, w, part), here.at(z=step)
            )
        for step in here.y_steps if to_y else ():
            back = (y + here.back_y(step)) % here.yo_size
            wires.send(
                source, wholes[part].at[0, index], name(0, back, x, z, w, part), here.at(y=step)
            )
        wires.send(source, wholes[part].at[1, index], name(1, y, x, z, w, part), other)

    for x, w in group:
        for part in range(count):
            if (x, w) == (0, 0):
                pass_on(shards[part].at[member(0, 0)], 0, 0, 0, 0, part, True, True)
                wholes[part][0, here.chip()] = shards[part][member(0, 0)]
            else:
                source = wholes[part].at[0, here.chip(x=x, w=w)]
                wires.arrive(source, name(0, 0, x, 0, w, part), other)
                pass_on(source, 0, x, 0, w, part, True, True)
        yield
    for x, w in group:
        for part in range(count):
            for z in here.z_steps:
                source = wholes[part].at[0, here.chip(x=x, w=w, z=z)]
                wires.arrive(source, name(0, 0, x, z, w, part), other)
                pass_on(source, 0, x, z, w, part, False, True)
        yield
    for z in range(here.zo_size):
        for x, w in group:
            for part in range(count):
                for y in here.y_steps:
                    source = wholes[part].at[0, here.chip(y=y, x=x, w=w, z=z)]
                    wires.arrive(source, name(0, y, x, z, w, part), other)
                    pass_on(source, y, x, z, w, part, False, False)
            yield
    for y in range(here.yo_size):
        for z in range(here.zo_size):
            for x, w in group:
                for part in range(count):
                    target = wholes[part].at[1, here.chip(y=y, x=x, w=w, z=z)]
                    wires.arrive(target, name(1, y, x, z, w, part), other)


ATTENTION_PARTS = 3
EXPERT_PARTS = 2


def gather_layer_kernel(sizes, *refs):
    count = ATTENTION_PARTS + EXPERT_PARTS
    ins, outs, sems = refs[:count], refs[count : 2 * count], refs[2 * count :]
    here = Place(sizes)
    wires = Wires(*sems[:2]), Wires(*sems[2:])
    cut = ATTENTION_PARTS
    greet_layer(here)
    together(
        gather_attention_steps(here, wires[0], ins[:cut], outs[:cut]),
        gather_experts_steps(here, wires[1], ins[cut:], outs[cut:]),
    )
    for one in wires:
        one.drain()


def gather_layer(attention_shards, expert_parts):
    sizes = mesh_sizes()
    chips = sizes[0] * sizes[1] * 4
    columns = sizes[1] * 2
    first = ATTENTION_PARTS * ((columns - 1) + chips + columns * (2 * sizes[0] + 1) + chips)
    second = EXPERT_PARTS * (3 + 4 * (sizes[0] + sizes[1]) + 4 * sizes[1] * sizes[0] + chips)
    in_vmem = pl.BlockSpec(memory_space=pltpu.VMEM)
    count = ATTENTION_PARTS + EXPERT_PARTS
    return pl.pallas_call(
        functools.partial(gather_layer_kernel, sizes),
        out_shape=[
            jax.ShapeDtypeStruct((2 * chips,) + shard.shape, shard.dtype)
            for shard in attention_shards
        ]
        + [
            jax.ShapeDtypeStruct((2, chips) + part.shape[1:], part.dtype) for part in expert_parts
        ],
        in_specs=[in_vmem] * count,
        out_specs=[in_vmem] * count,
        scratch_shapes=[
            pltpu.SemaphoreType.DMA((first,)),
            pltpu.SemaphoreType.DMA((2 * chips * ATTENTION_PARTS,)),
            pltpu.SemaphoreType.DMA((second,)),
            pltpu.SemaphoreType.DMA((2 * chips * EXPERT_PARTS,)),
        ],
        compiler_params=pltpu.CompilerParams(
            collective_id=0, has_side_effects=True, vmem_limit_bytes=58 * 1024 * 1024
        ),
    )(*attention_shards, *expert_parts)


def sum_experts_steps(here, wires, whole, outs, first, second, third):
    count = len(whole)
    group = offsets_of(GROUP)
    other = here.at(core=1)
    chips = here.yo_size * here.zo_size * 4

    def place(y, z, member):
        return (y * here.zo_size + z) * 4 + member

    def name(kind, index, part):
        return (kind * chips + index) * count + part

    order = [
        (y, z, member)
        for y in list(here.y_steps) + [0]
        for z in list(here.z_steps) + [0]
        for member in (1, 2, 3, 0)
    ]
    for y, z, member in order:
        x, w = group[member]
        index = here.chip(y=y, x=x, z=z, w=w)
        spot = place(y, z, member)
        for part in range(count):
            wires.send(
                whole[part].at[1, index], first[part].at[spot], name(0, spot, part), other
            )
    yield
    for y, z, member in order:
        x, w = group[member]
        index = here.chip(y=y, x=x, z=z, w=w)
        spot = place(y, z, member)
        for part in range(count):
            total = first[part].at[spot]
            wires.arrive(total, name(0, spot, part), other)
            parts = [whole[part].at[0, index]]
            if y:
                add_rows(total, *parts)
                landing = place(here.back_y(y), z, member)
                wires.send(
                    total, second[part].at[landing - 4 * here.zo_size], name(1, landing, part), here.at(y=y)
                )
                continue
            for step in here.y_steps:
                spot_in = place(step, z, member)
                arrived = second[part].at[spot_in - 4 * here.zo_size]
                wires.arrive(arrived, name(1, spot_in, part), other)
                parts.append(arrived)
            if z:
                add_rows(total, *parts)
                landing = here.back_z(z) * 4 + member
                wires.send(
                    total, third[part].at[landing - 4], name(2, landing, part), here.at(z=z)
                )
                continue
            for step in here.z_steps:
                arrived = third[part].at[step * 4 + member - 4]
                wires.arrive(arrived, name(2, step * 4 + member, part), other)
                parts.append(arrived)
            add_rows(total, *parts)
            slot = here.xi * 2 + here.zi
            if member:
                wires.send(total, outs[part].at[slot], name(3, member, part), here.at(x=x, w=w))
            else:
                outs[part][slot] = total[...]
        yield
    for member in range(1, 4):
        x, w = group[member]
        yo, xi, zo, zi, core = here.at(x=x, w=w)
        for part in range(count):
            wires.arrive(outs[part].at[xi * 2 + zi], name(3, member, part), other)


def sum_attention_steps(here, wires, whole, outs, first, second, third, fourth):
    count = len(whole)
    columns = here.column
    other = here.at(core=1)
    width = len(columns)
    chips = here.yo_size * 2 * width

    def place(y, x, column):
        return (y * 2 + x) * width + column

    def name(kind, index, part):
        return (kind * chips + index) * count + part

    rounds = [
        (y, x, (column + 1) % width, part)
        for y in list(here.y_steps) + [0]
        for x in (1, 0)
        for column in range(width)
        for part in range(count)
    ]

    def turn(item):
        y, x, column, part = item
        ahead = x if part % 2 == 0 else y
        return (not (y and x), not ahead, not (y or x))

    rounds.sort(key=turn)
    for y, x, column, part in rounds:
        z, w = columns[column]
        spot = place(y, x, column)
        wires.send(
            whole[part].at[here.chip(y=y, x=x, z=z, w=w), 1 - here.core],
            first[part].at[spot],
            name(0, spot, part),
            other,
        )
    yield
    for y, x, column, part in rounds:
        z, w = columns[column]
        spot = place(y, x, column)
        total = first[part].at[spot]
        wires.arrive(total, name(0, spot, part), other)
        parts = [whole[part].at[here.chip(y=y, x=x, z=z, w=w), here.core]]

        def take_in(buffer, kind, index, offset=0):
            arrived = buffer[part].at[index - offset]
            wires.arrive(arrived, name(kind, index, part), other)
            parts.append(arrived)

        def give(buffer, kind, index, device, offset=0):
            add_rows(total, *parts)
            wires.send(total, buffer[part].at[index - offset], name(kind, index, part), device)

        if part % 2 == 0:
            if x:
                add_rows(total, *parts)
                wires.send(
                    total,
                    second[part].at[y * width + column],
                    name(1, place(y, 0, column), part),
                    here.at(x=1),
                )
                yield
                continue
            arrived = second[part].at[y * width + column]
            wires.arrive(arrived, name(1, place(y, 0, column), part), other)
            parts.append(arrived)
            if y:
                give(third, 2, here.back_y(y) * width + column, here.at(y=y), width)
                yield
                continue
            for step in here.y_steps:
                take_in(third, 2, step * width + column, width)
        else:
            if y:
                give(second, 1, place(here.back_y(y), x, column), here.at(y=y), 2 * width)
                yield
                continue
            for step in here.y_steps:
                take_in(second, 1, place(step, x, column), 2 * width)
            if x:
                give(third, 2, column, here.at(x=1))
                yield
                continue
            take_in(third, 2, column)
        if column:
            landing = columns.index((here.back_z(z), w))
            give(fourth, 3, landing, here.at(z=z, w=w), 1)
            yield
            continue
        for step in range(1, width):
            take_in(fourth, 3, step, 1)
        add_rows(total, *parts)
        outs[part][...] = total[...]
        yield


def sum_layer_kernel(sizes, *refs):
    both = ATTENTION_PARTS + EXPERT_PARTS
    cut = ATTENTION_PARTS
    ins, outs, rest = refs[:both], refs[both : 2 * both], refs[2 * both :]
    buffers, sems = rest[:-4], rest[-4:]
    attention = [buffers[level * cut : (level + 1) * cut] for level in range(4)]
    buffers = buffers[4 * cut :]
    experts = [buffers[level * EXPERT_PARTS : (level + 1) * EXPERT_PARTS] for level in range(3)]
    here = Place(sizes)
    wires = Wires(*sems[:2]), Wires(*sems[2:])
    greet_layer(here)
    together(
        sum_experts_steps(here, wires[1], ins[cut:], outs[cut:], *experts),
        sum_attention_steps(here, wires[0], ins[:cut], outs[:cut], *attention),
    )
    for one in wires:
        one.drain()


def sum_layer(attention_grads, expert_grads):
    sizes = mesh_sizes()
    chips = sizes[0] * sizes[1] * 4
    column = sizes[1] * 2
    attention = [grads.reshape(chips, 2, -1, grads.shape[1]) for grads in attention_grads]
    experts = [grads.reshape(2, chips, -1, D) for grads in expert_grads]
    in_vmem = pl.BlockSpec(memory_space=pltpu.VMEM)
    count = ATTENTION_PARTS + EXPERT_PARTS

    def held(blocks, sizes_of):
        return [
            pltpu.VMEM((sizes_of(part),) + block.shape[2:], jnp.bfloat16)
            for part, block in enumerate(blocks)
        ]

    level_two = (sizes[0] * column, (sizes[0] - 1) * 2 * column)
    level_three = ((sizes[0] - 1) * column, column)
    return pl.pallas_call(
        functools.partial(sum_layer_kernel, sizes),
        out_shape=[jax.ShapeDtypeStruct(block.shape[2:], jnp.bfloat16) for block in attention]
        + [jax.ShapeDtypeStruct((4,) + block.shape[2:], jnp.bfloat16) for block in experts],
        in_specs=[in_vmem] * count,
        out_specs=[in_vmem] * count,
        scratch_shapes=held(attention, lambda part: chips)
        + held(attention, lambda part: level_two[part % 2])
        + held(attention, lambda part: level_three[part % 2])
        + held(attention, lambda part: column - 1)
        + held(experts, lambda part: chips)
        + held(experts, lambda part: (sizes[0] - 1) * sizes[1] * 4)
        + held(experts, lambda part: (sizes[1] - 1) * 4)
        + [
            pltpu.SemaphoreType.DMA((3 * chips * ATTENTION_PARTS,)),
            pltpu.SemaphoreType.DMA((4 * chips * ATTENTION_PARTS,)),
            pltpu.SemaphoreType.DMA((3 * chips * EXPERT_PARTS,)),
            pltpu.SemaphoreType.DMA((4 * chips * EXPERT_PARTS,)),
        ],
        compiler_params=pltpu.CompilerParams(
            collective_id=1, has_side_effects=True, vmem_limit_bytes=62 * 1024 * 1024
        ),
    )(*attention, *experts)


def swap(value, axis):
    return lax.ppermute(value, axis, [(0, 1), (1, 0)])


def pick(value, index, axis=0):
    return lax.dynamic_index_in_dim(value, index, axis, keepdims=False)


def by_core(mine, theirs, axis):
    core = lax.axis_index("core")
    return jnp.where(
        core == 0, jnp.stack([mine, theirs], axis), jnp.stack([theirs, mine], axis)
    )


def gain_columns(gains):
    gains = gains.astype(jnp.bfloat16).T
    return jnp.pad(gains, ((0, 0), (0, 128 - gains.shape[1])))


def layer_weights(w_qkv, w_out, w_gateup, w_down, gains, layer):
    core = lax.axis_index("core")
    parts = []
    for shard in (w_gateup[layer], w_down[layer]):
        shard = shard.astype(jnp.bfloat16)
        shard = shard.reshape((4, 2) + shard.shape[1:])
        theirs = swap(pick(shard, 1 - core, 1), "core")
        parts.append(by_core(pick(shard, core, 1), theirs, 1).reshape(4, -1, D))
    shards = [
        w_qkv[layer].astype(jnp.bfloat16),
        w_out[layer].astype(jnp.bfloat16),
        gain_columns(gains[layer]),
    ]
    qkv, out, gain, up, down = gather_layer(shards, parts)
    gain = gain.reshape(D, 128)[:, :2].T.astype(jnp.float32)
    attention = (qkv.reshape(D, QKV), out.reshape(D, D), gain)
    return attention, (up.reshape(2, D, 2 * F), down.reshape(2, F, D))


def layer_sums(grad_qkv, grad_out, grad_up, grad_down, grad_gains):
    core = lax.axis_index("core")
    attention = [
        grad_qkv.astype(jnp.bfloat16),
        grad_out.astype(jnp.bfloat16),
        gain_columns(grad_gains),
    ]
    qkv, out, gain, up, down = sum_layer(attention, [grad_up, grad_down])
    result = [qkv.astype(jnp.float32), out.astype(jnp.float32)]
    for part in (up, down):
        part = part.reshape(4, 2, -1, D)
        theirs = swap(pick(part, 1 - core, 1), "core")
        pair = by_core(pick(part, core, 1), theirs, 1)
        result.append(pair.reshape(EXPERTS, -1, D).astype(jnp.float32))
    return result + [gain[:, :2].T.astype(jnp.float32)]


SQRT_HALF = 0.7071067811865476
PDF_SCALE = 0.3989422804014327
TILE = 256
TILES = F // TILE


def selections(table, columns):
    rows = table.shape[1]
    slots = lax.broadcasted_iota(jnp.int32, (CAP, rows), 0).astype(jnp.float32)
    take = (table[0:1, :] == slots).astype(jnp.bfloat16)
    slots = lax.broadcasted_iota(jnp.int32, (rows, CAP), 1).astype(jnp.float32)
    spread = (columns[:, 0:1] == slots).astype(jnp.bfloat16)
    return take, spread, columns[:, 1:2]


def dot(left, right, contract=(1, 0)):
    return lax.dot_general(
        left,
        right,
        (((contract[0],), (contract[1],)), ((), ())),
        preferred_element_type=jnp.float32,
    )


def experts_grads_kernel(slot_in, active, slot_grad, grad_gate, grad_up, up_out, down_out):
    up_out[0, :, :F] = dot(slot_in[0], grad_gate[0], (0, 0)).astype(jnp.bfloat16)
    up_out[0, :, F:] = dot(slot_in[0], grad_up[0], (0, 0)).astype(jnp.bfloat16)
    down_out[0] = dot(active[0], slot_grad[0], (0, 0)).astype(jnp.bfloat16)


def whole_block(shape):
    return pl.BlockSpec(shape, lambda e, f: (0,) * len(shape))


def expert_block(shape):
    return pl.BlockSpec((1,) + shape, lambda e, f: (e,) + (0,) * len(shape))


def moe_forward_kernel(
    sizes,
    tokens,
    tables,
    columns,
    up_w,
    down_w,
    merged,
    slot_out,
    gate_out,
    up_out,
    active_out,
    chunks,
    leaving,
    coming,
    slot_in,
    result,
    total,
    send_sems,
    recv_sems,
):
    here = Place(sizes)
    wires = Wires(send_sems, recv_sems)
    partners = [here.at(x=x, w=w) for x, w in offsets_of(GROUP)]
    greet(partners[1:])
    for place in range(1, 4):
        wires.send(tokens, chunks.at[place - 1], place - 1, partners[place])
    for place in range(4):
        chunk = tokens if place == 0 else chunks.at[place - 1]
        if place:
            wires.arrive(chunk, place - 1, partners[place])
        rows = pl.ds(place * CAP, CAP)

        def step(index, carry, place=place, chunk=chunk, rows=rows):
            expert, tile = lax.div(index, TILES), lax.rem(index, TILES)
            at_gate = pl.ds(pl.multiple_of(tile * TILE, TILE), TILE)
            at_up = pl.ds(pl.multiple_of(F + tile * TILE, TILE), TILE)
            take, spread, gates = selections(tables[place, expert], columns[place, expert])

            @pl.when(tile == 0)
            def _():
                slot_in[...] = dot(take, chunk[...]).astype(jnp.bfloat16)
                slot_out[expert, rows, :] = slot_in[...]

            gate = dot(slot_in[...], up_w[expert, :, at_gate])
            up = dot(slot_in[...], up_w[expert, :, at_up])
            active = (0.5 * gate * (1.0 + lax.erf(gate * SQRT_HALF)) * up).astype(jnp.bfloat16)
            gate_out[expert, rows, at_gate] = gate
            up_out[expert, rows, at_gate] = up
            active_out[expert, rows, at_gate] = active
            part = dot(active, down_w[expert, at_gate, :])

            @pl.when(tile == 0)
            def _():
                result[...] = part

            @pl.when(tile > 0)
            def _():
                result[...] += part

            @pl.when(tile == TILES - 1)
            def _():
                share = dot(spread, result[...].astype(jnp.bfloat16)) * gates

                @pl.when(expert == 0)
                def _():
                    total[...] = share

                @pl.when(expert > 0)
                def _():
                    total[...] += share

            return carry

        lax.fori_loop(0, 2 * TILES, step, 0)
        if place == 0:
            merged[...] = total[...]
        else:
            leaving[place - 1] = total[...].astype(jnp.bfloat16)
            wires.send(leaving.at[place - 1], coming.at[place - 1], place + 2, partners[place])
    for place in range(1, 4):
        wires.arrive(coming.at[place - 1], place + 2, partners[place])
        merged[...] += coming[place - 1].astype(jnp.float32)
    wires.drain()


def moe_backward_kernel(
    sizes,
    gradient,
    tables,
    columns,
    up_w,
    down_w,
    gate_in,
    up_in,
    merged,
    slot_out,
    gate_out,
    up_out,
    chunks,
    leaving,
    coming,
    slot_grad,
    slots,
    total,
    send_sems,
    recv_sems,
):
    here = Place(sizes)
    wires = Wires(send_sems, recv_sems)
    partners = [here.at(x=x, w=w) for x, w in offsets_of(GROUP)]
    greet(partners[1:])
    leaving[3] = gradient[...].astype(jnp.bfloat16)
    for place in range(1, 4):
        wires.send(leaving.at[3], chunks.at[place - 1], place - 1, partners[place])
    for place in range(4):
        chunk = gradient if place == 0 else chunks.at[place - 1]
        if place:
            wires.arrive(chunk, place - 1, partners[place])
        rows = pl.ds(place * CAP, CAP)

        def step(index, carry, place=place, chunk=chunk, rows=rows):
            expert, tile = lax.div(index, TILES), lax.rem(index, TILES)
            at_gate = pl.ds(pl.multiple_of(tile * TILE, TILE), TILE)
            at_up = pl.ds(pl.multiple_of(F + tile * TILE, TILE), TILE)
            take, spread, gates = selections(tables[place, expert], columns[place, expert])

            @pl.when(tile == 0)
            def _():
                weighted = (gates * chunk[...].astype(jnp.float32)).astype(jnp.bfloat16)
                slot_grad[...] = dot(take, weighted).astype(jnp.bfloat16)
                slot_out[expert, rows, :] = slot_grad[...]

            grad_act = dot(slot_grad[...], down_w[expert, at_gate, :], (1, 1))
            gate, up = gate_in[expert, rows, at_gate], up_in[expert, rows, at_gate]
            below = 0.5 * (1.0 + lax.erf(gate * SQRT_HALF))
            slope = below + gate * PDF_SCALE * jnp.exp(-0.5 * gate * gate)
            grad_gate = (grad_act * up * slope).astype(jnp.bfloat16)
            grad_up = (grad_act * gate * below).astype(jnp.bfloat16)
            gate_out[expert, rows, at_gate] = grad_gate
            up_out[expert, rows, at_gate] = grad_up
            part = dot(grad_gate, up_w[expert, :, at_gate], (1, 1))
            part = part + dot(grad_up, up_w[expert, :, at_up], (1, 1))

            @pl.when(tile == 0)
            def _():
                slots[...] = part

            @pl.when(tile > 0)
            def _():
                slots[...] += part

            @pl.when(tile == TILES - 1)
            def _():
                share = dot(spread, slots[...].astype(jnp.bfloat16))

                @pl.when(expert == 0)
                def _():
                    total[...] = share

                @pl.when(expert > 0)
                def _():
                    total[...] += share

            return carry

        lax.fori_loop(0, 2 * TILES, step, 0)
        if place == 0:
            merged[...] = total[...]
        else:
            leaving[place - 1] = total[...].astype(jnp.bfloat16)
            wires.send(leaving.at[place - 1], coming.at[place - 1], place + 2, partners[place])
    for place in range(1, 4):
        wires.arrive(coming.at[place - 1], place + 2, partners[place])
        merged[...] += coming[place - 1].astype(jnp.float32)
    wires.drain()


def moe_call(kernel, identity, rows_in, tables, weights, extra, kinds):
    rows = rows_in.shape[0]
    slots = 4 * CAP
    operands = [rows_in, tables, jnp.swapaxes(tables, 2, 3), *weights, *extra]
    in_vmem = pl.BlockSpec(memory_space=pltpu.VMEM)
    return pl.pallas_call(
        functools.partial(kernel, mesh_sizes()),
        in_specs=[in_vmem] * len(operands),
        out_specs=[in_vmem] * (1 + len(kinds)),
        out_shape=[jax.ShapeDtypeStruct((rows, D), jnp.float32)]
        + [jax.ShapeDtypeStruct((2, slots, width), kind) for width, kind in kinds],
        scratch_shapes=[
            pltpu.VMEM((3, rows, D), jnp.bfloat16),
            pltpu.VMEM((4, rows, D), jnp.bfloat16),
            pltpu.VMEM((3, rows, D), jnp.bfloat16),
            pltpu.VMEM((CAP, D), jnp.bfloat16),
            pltpu.VMEM((CAP, D), jnp.float32),
            pltpu.VMEM((rows, D), jnp.float32),
            pltpu.SemaphoreType.DMA((6,)),
            pltpu.SemaphoreType.DMA((6,)),
        ],
        compiler_params=pltpu.CompilerParams(
            collective_id=identity, has_side_effects=True, vmem_limit_bytes=58 * 1024 * 1024
        ),
        cost_estimate=pl.CostEstimate(
            flops=48 * CAP * D * F, bytes_accessed=40_000_000, transcendentals=8 * CAP * F
        ),
    )(*operands)


FORWARD_KEPT = ((D, jnp.bfloat16), (F, jnp.float32), (F, jnp.float32), (F, jnp.bfloat16))
BACKWARD_KEPT = ((D, jnp.bfloat16), (F, jnp.bfloat16), (F, jnp.bfloat16))


def moe_forward(expert_in, tables, weights):
    merged, *kept = moe_call(
        moe_forward_kernel, 2, expert_in, tables, weights, [], FORWARD_KEPT
    )
    return merged, kept


def moe_backward(gradient, tables, weights, kept):
    slot_in, gate, up, active = kept
    total, slot_grad, grad_gate, grad_up = moe_call(
        moe_backward_kernel, 3, gradient, tables, weights, [gate, up], BACKWARD_KEPT
    )
    slots = slot_in.shape[1]

    def columns_of(width):
        return pl.BlockSpec((1, slots, width), lambda e, i: (e, 0, i))

    grads = pl.pallas_call(
        experts_grads_kernel,
        grid=(2, 3),
        in_specs=[
            columns_of(D // 3),
            columns_of(F // 3),
            expert_block((slots, D)),
            expert_block((slots, F)),
            expert_block((slots, F)),
        ],
        out_specs=[
            pl.BlockSpec((1, D // 3, 2 * F), lambda e, i: (e, i, 0)),
            pl.BlockSpec((1, F // 3, D), lambda e, i: (e, i, 0)),
        ],
        out_shape=[
            jax.ShapeDtypeStruct((2, D, 2 * F), jnp.bfloat16),
            jax.ShapeDtypeStruct((2, F, D), jnp.bfloat16),
        ],
        compiler_params=pltpu.CompilerParams(vmem_limit_bytes=48 * 1024 * 1024),
        cost_estimate=pl.CostEstimate(
            flops=12 * slots * D * F, bytes_accessed=30_000_000, transcendentals=0
        ),
    )(slot_in, active, slot_grad, grad_gate, grad_up)
    return total, grads[0], grads[1]


def layer_forward(stream, attn_w, expert_w, tables, allowed, cosine_table, sine_table):
    qkv_w, out_w, gain_full = attn_w
    row_count = stream.shape[0]
    normed, scale_one = normalize(stream, gain_full[0])
    attn_in = normed.astype(jnp.bfloat16)
    projected = jnp.dot(attn_in, qkv_w, preferred_element_type=jnp.float32)
    queries = rotate(
        projected[:, : H * HD].reshape(row_count, H, HD), cosine_table, sine_table
    ).astype(jnp.bfloat16)
    keys_local = rotate(
        projected[:, H * HD : (H + KVH) * HD].reshape(row_count, KVH, HD), cosine_table, sine_table
    ).astype(jnp.bfloat16)
    values_local = projected[:, (H + KVH) * HD :].reshape(row_count, KVH, HD).astype(jnp.bfloat16)
    both = jnp.concatenate([keys_local, values_local], axis=1)
    both_all = jnp.concatenate([send(both, CTX, offsets) for offsets in offsets_of(CTX)], axis=0)
    keys_all, values_all = both_all[:, :KVH], both_all[:, KVH:]
    attended, totals = attention_forward(queries, keys_all, values_all, allowed)
    attended_low = attended.reshape(row_count, H * HD).astype(jnp.bfloat16)
    middle_stream = stream + jnp.dot(attended_low, out_w, preferred_element_type=jnp.float32)
    normed_two, scale_two = normalize(middle_stream, gain_full[1])
    expert_in = normed_two.astype(jnp.bfloat16)
    merged, kept = moe_forward(expert_in, tables, expert_w)
    record = {
        "stream": stream,
        "scale_one": scale_one,
        "attn_in": attn_in,
        "queries": queries,
        "keys_all": keys_all,
        "values_all": values_all,
        "totals": totals,
        "attended": attended_low,
        "middle": middle_stream,
        "scale_two": scale_two,
        "kept": kept,
    }
    return (record, middle_stream + merged)


def layer_backward(gradient, record, attn_w, expert_w, tables, allowed, cosine_table, sine_table):
    qkv_w, out_w, gain_full = attn_w
    row_count = gradient.shape[0]
    grad_normed, grad_up, grad_down = moe_backward(gradient, tables, expert_w, record["kept"])
    grad_normed, grad_up, grad_down = lax.optimization_barrier((grad_normed, grad_up, grad_down))
    grad_in_two, grad_gain_two = normalize_back(
        grad_normed, record["middle"], record["scale_two"], gain_full[1]
    )
    grad_middle = gradient + grad_in_two
    grad_middle_low = grad_middle.astype(jnp.bfloat16)
    grad_out = jnp.dot(record["attended"].T, grad_middle_low, preferred_element_type=jnp.float32)
    grad_attended = jnp.dot(grad_middle_low, out_w.T, preferred_element_type=jnp.float32)
    grad_attended = grad_attended.astype(jnp.bfloat16).reshape(row_count, H, HD)
    grad_queries, grad_keys_all, grad_values_all = attention_backward(
        record["queries"],
        record["keys_all"],
        record["values_all"],
        allowed,
        record["totals"],
        grad_attended,
    )
    both_all = jnp.concatenate([grad_keys_all, grad_values_all], axis=1)
    both = None
    for place, offsets in enumerate(offsets_of(CTX)):
        part = both_all[place * row_count : (place + 1) * row_count]
        if offsets != (0, 0):
            part = send(part.astype(jnp.bfloat16), CTX, offsets, back=True).astype(jnp.float32)
        both = part if both is None else both + part
    grad_keys, grad_values = both[:, :KVH], both[:, KVH:]
    grad_projected = jnp.concatenate(
        [
            rotate_back(grad_queries, cosine_table, sine_table).reshape(row_count, H * HD),
            rotate_back(grad_keys, cosine_table, sine_table).reshape(row_count, KVH * HD),
            grad_values.reshape(row_count, KVH * HD),
        ],
        axis=1,
    ).astype(jnp.bfloat16)
    grad_qkv = jnp.dot(record["attn_in"].T, grad_projected, preferred_element_type=jnp.float32)
    grad_normed_one = jnp.dot(grad_projected, qkv_w.T, preferred_element_type=jnp.float32)
    grad_in_one, grad_gain_one = normalize_back(
        grad_normed_one, record["stream"], record["scale_one"], gain_full[0]
    )
    grad_gains = jnp.stack([grad_gain_one, grad_gain_two])
    return (grad_middle + grad_in_one, (grad_qkv, grad_out, grad_up, grad_down, grad_gains))


def on_device(
    tokens,
    cotangent,
    routes,
    gate_weights,
    lengths,
    block_map,
    w_qkv,
    w_out,
    w_gateup,
    w_down,
    gains,
    m_qkv,
    v_qkv,
    m_out,
    v_out,
    m_gateup,
    v_gateup,
    m_down,
    v_down,
    m_gains,
    v_gains,
):
    row_count = tokens.shape[1]
    block_rows = row_count // 2
    own_pos, own_doc = positions_docs(block_map, lengths[0], flat_index(CTX), block_rows)
    places = [
        positions_docs(block_map, lengths[0], source_index(CTX, offsets), block_rows)
        for offsets in offsets_of(CTX)
    ]
    key_pos = jnp.concatenate([place[0] for place in places])
    key_doc = jnp.concatenate([place[1] for place in places])
    allowed = (own_doc[:, None] == key_doc[None, :]) & (key_pos[None, :] <= own_pos[:, None])
    cosine_table, sine_table = rope_tables(own_pos)
    own_tables = jnp.stack(
        [dispatch_tables(routes[layer, 0], gate_weights[layer, 0]) for layer in range(LAYERS)]
    )
    core = lax.axis_index("core")
    group_tables = []
    for offsets in offsets_of(GROUP):
        theirs = lax.dynamic_slice_in_dim(own_tables, 2 * target_index(GROUP, offsets), 2, axis=1)
        theirs = jnp.where(core == 0, theirs, theirs[:, ::-1])
        group_tables.append(send(theirs, GROUP, offsets))
    group_tables = jnp.stack(group_tables, axis=1)
    stream = tokens[0].astype(jnp.float32)
    records = []
    attn_w, expert_w = zip(
        *[
            layer_weights(w_qkv, w_out, w_gateup, w_down, gains, layer)
            for layer in range(LAYERS)
        ]
    )
    for layer_index in range(LAYERS):
        record, stream = layer_forward(
            stream,
            attn_w[layer_index],
            expert_w[layer_index],
            group_tables[layer_index],
            allowed,
            cosine_table,
            sine_table,
        )
        records.append(record)
    output = stream.astype(jnp.bfloat16)[None]
    gradient = cotangent[0].astype(jnp.float32)
    rates = (D ** (-0.5), 0.5, D ** (-0.5), (F // 8) ** (-0.5), 1.0)
    decays = (DECAY, DECAY, DECAY, DECAY, 0.0)
    params = (w_qkv, w_out, w_gateup, w_down, gains)
    firsts = (m_qkv, m_out, m_gateup, m_down, m_gains)
    seconds = (v_qkv, v_out, v_gateup, v_down, v_gains)
    updated = [[None] * LAYERS for which in range(15)]
    for layer_index in reversed(range(LAYERS)):
        gradient, layer_grads = layer_backward(
            gradient,
            records[layer_index],
            attn_w[layer_index],
            expert_w[layer_index],
            group_tables[layer_index],
            allowed,
            cosine_table,
            sine_table,
        )
        sums = layer_sums(*layer_grads)
        for which in range(5):
            fresh = adamw(
                params[which][layer_index],
                firsts[which][layer_index],
                seconds[which][layer_index],
                sums[which],
                rates[which],
                decays[which],
            )
            updated[3 * which][layer_index] = fresh[0]
            updated[3 * which + 1][layer_index] = fresh[1]
            updated[3 * which + 2][layer_index] = fresh[2]
    stacked = [jnp.stack(pieces) for pieces in updated]
    return (output, gradient[None], *stacked)


def solution(mesh):
    ctx_size, shard_size = mesh.shape["ctx"], mesh.shape["shard"]
    fine = Mesh(mesh.devices.reshape(ctx_size // 2, 2, shard_size // 4, 2, 2), ALL)
    tokens = P(SHARD, CTX, None)
    routed = P(None, SHARD, CTX, None)
    rows_two = P(None, ALL, None)
    rows_three = P(None, None, ALL, None)
    gain = P(None, None, ALL)
    weights = (rows_two, rows_two, rows_three, rows_three, gain)
    states = tuple(spec for spec in weights for which in range(2))
    return jax.shard_map(
        on_device,
        mesh=fine,
        in_specs=(tokens, tokens, routed, routed, P(SHARD, None), P()) + weights + states,
        out_specs=(tokens, tokens) + tuple(spec for spec in weights for which in range(3)),
        check_vma=False,
    )
```

time: 1510 us -> 1360 us (0.901)
  Pallas kernels: 508 us -> 1000 us
  matrix products: 360 us -> 115 us
  waiting for transfers between devices: 205 us -> 15.5 us
  local copies, waits for them, and re-layouts: 155 us -> 81.6 us
  blocking collectives: 48.7 us -> 0 us
  other arithmetic: 156 us -> 118 us
  starting transfers between devices: 52.5 us -> 20.2 us
    pallas_call x4 -> x10, Pallas kernels: 508 us -> 1000 us  [the longest x2 336 us: sum_layer(): pl.pallas_call(functools.partial(sum_layer_kernel, sizes), out_shape=[jax...]
    dot_general x52 -> x0, matrix products: 252 us -> none  [the longest x8 72.3 us: experts_backward(): jnp.einsum('jst,jsd->td', select, grad_slots.astype(jnp.bfloat16), prefer...]
    ppermute x45 -> x15, waiting for transfers between devices: 111 us -> 15.5 us  [send(): return lax.ppermute(value, axes, shift_permutation(axes, offsets, back))]
    reduce_scatter x2 -> x0, waiting for transfers between devices: 93.8 us -> none  [the longest x1 93.8 us: expert_grads(): lax.psum_scatter(packed, REPLICAS, scatter_dimension=0, tiled=False)]
    all_gather x1 -> x0, blocking collectives: 48.7 us -> none  [all_gains(): whole = lax.all_gather(gains.astype(jnp.bfloat16), ALL, axis=2, tiled=True)]
    slice x1 -> x2, local copies, waits for them, and re-layouts: 39.3 us -> 0.08 us  [layer_forward(): normed_two, scale_two = normalize(middle_stream, gain_full[1])]
    ppermute x45 -> x15, starting transfers between devices: 50.9 us -> 18.5 us  [send(): return lax.ppermute(value, axes, shift_permutation(axes, offsets, back))]
    convert_element_type x15 -> x2, other arithmetic: 26.1 us -> 2.98 us  [layer_weights(): gain = gain.reshape(D, 128)[:, :2].T.astype(jnp.float32)]
  transfers between devices with their start and end apart: 55 -> 23, of which waited for: 19 -> 5; matrix products, arithmetic and copies ran while one was open for 35% -> 9% of each run, Pallas kernels for 34% -> 35%
where the time goes in v2:
time: 1360 us
  Pallas kernels  1000 us (74%)
  other arithmetic  118 us (9%)
  matrix products  115 us (8%)
  local copies, waits for them, and re-layouts  81.6 us (6%)
  starting transfers between devices  20.2 us (1%)
  waiting for transfers between devices  15.5 us (1%)
    pallas_call x2, Pallas kernels, sum_layer(): pl.pallas_call(functools.partial(sum_layer_kernel, sizes), out_shape=[jax...  336 us
    pallas_call x4, Pallas kernels, moe_call(): pl.pallas_call(functools.partial(kernel, mesh_sizes()), in_specs=[in_vmem...  329 us
    pallas_call x2, Pallas kernels, gather_layer(): pl.pallas_call(functools.partial(gather_layer_kernel, sizes), out_shape=[...  304 us
    pallas_call x2, Pallas kernels, moe_backward(): pl.pallas_call(experts_grads_kernel, grid=(2, 3), in_specs=[columns_of(D...  31.8 us
    unnamed x280, local copies, waits for them, and re-layouts  27.3 us
  transfers between devices with their start and end apart: 23, of which 5 were waited for; matrix products, arithmetic and copies ran while one was open for 9% of the time, Pallas kernels for 35%

profile of v2, /device:TPU:0, one launch (start us, length us, event | category | flops | bytes accessed | tf_op | source)
XLA Modules:
  0.0 1355.6 jit_solution(2747973042393151464)
XLA Ops:
  0.7 3.7 fusion.219
  4.4 2.5 constant_dynamic-slice_fusion.7
  10.7 3.0 collective-permute-start.5
  21.9 2.1 fusion.111
  34.0 5.9 collective-permute-done.6
  41.6 2.2 slice_bitcast_fusion
  43.8 2.2 copy.551.tables
  46.1 2.2 copy.566.tables
  48.2 1.9 maximum_select_fusion.4
  50.2 1.9 maximum_select_fusion.5
  52.1 2.4 maximum_select_fusion
  54.5 153.9 %shard_map.332 = (bf16[32,48,2048]{2,1,0:T(8,128)(2,1)}, bf16[32,48,1536]{2,1,0:T(8,128)(2,1)}, bf16[32,48,128]{2,1,0:T(8,128)(2,1)}, bf16[2,16,96,1536]{3,2,1,0:T(8,128)(2,1)}, bf16[2,16,48,1536]{3,2,1,0:T(8,128)(2,1)}) custom-call(bf16[48,2048]{1,0:T(8,128)(2,1)} %get-tuple-element.219.refs_0_, bf16[48,1536]{1,0:T(8,128)(2,1)} %get-tuple-element.233.refs_1_, ...), custom_call_target="tpu_custom_call" | custom-call | tf_op jit(solution)/shard_map/pallas_call | solution.py:508
  210.4 4.6 fusion.104
  228.7 2.4 maximum_select_fusion.1
  231.1 150.6 %shard_map.334 = (bf16[32,48,2048]{2,1,0:T(8,128)(2,1)}, bf16[32,48,1536]{2,1,0:T(8,128)(2,1)}, bf16[32,48,128]{2,1,0:T(8,128)(2,1)}, bf16[2,16,96,1536]{3,2,1,0:T(8,128)(2,1)}, bf16[2,16,48,1536]{3,2,1,0:T(8,128)(2,1)}) custom-call(bf16[48,2048]{1,0:T(8,128)(2,1)} %get-tuple-element.218.refs_0_, bf16[48,1536]{1,0:T(8,128)(2,1)} %get-tuple-element.232.refs_1_, ...), custom_call_target="tpu_custom_call" | custom-call | tf_op jit(solution)/shard_map/pallas_call | solution.py:508
  385.6 2.0 copy.717
  390.6 2.5 fusion.24
  400.1 13.7 %multiply_convert_fusion.2.tokens = bf16[256,1536]{1,0:T(8,128)(2,1)} fusion(f32[256,1536]{1,0:T(8,128)S(1)} %get-tuple-element.273, f32[1536]{0:T(1024)S(1)} %get-tuple-element.131, f32[256]{0:T(256)S(1)} %add_rsqrt_fusion.2), kind=kLoop, calls=%fused_computation.149 | loop fusion | flops 1179648 | bytes 2366464 | tf_op jit(solution)/shard_map/convert_element_type | solution.py:1130
  413.8 84.7 %shard_map.333 = (f32[256,1536]{1,0:T(8,128)}, bf16[2,640,1536]{2,1,0:T(8,128)(2,1)}, f32[2,640,768]{2,1,0:T(8,128)}, f32[2,640,768]{2,1,0:T(8,128)}, bf16[2,640,768]{2,1,0:T(8,128)(2,1)}) custom-call(bf16[256,1536]{1,0:T(8,128)(2,1)} %multiply_convert_fusion.2.tokens, f32[4,2,2,256]{3,2,1,0:T(2,128)} %copy.551.tables, ...), custom_call_target="tpu_custom_call" | custom-call | flops 9059696640 | bytes 40000000 | tf_op jit(solution)/shard_map/pallas_call | solution.py:1038
  500.2 5.2 fusion.204
  511.8 3.0 copy.559
  514.8 2.4 fusion.221
  517.2 2.7 copy.707
  521.6 2.3 subtract_convert_fusion.2
  527.2 2.5 fusion.26
  533.1 2.3 fusion.68
  538.1 81.2 %shard_map.335 = (f32[256,1536]{1,0:T(8,128)}, bf16[2,640,1536]{2,1,0:T(8,128)(2,1)}, f32[2,640,768]{2,1,0:T(8,128)}, f32[2,640,768]{2,1,0:T(8,128)}, bf16[2,640,768]{2,1,0:T(8,128)(2,1)}) custom-call(bf16[256,1536]{1,0:T(8,128)(2,1)} %multiply_convert_fusion.tokens, f32[4,2,2,256]{3,2,1,0:T(2,128)} %copy.566.tables, ...), custom_call_target="tpu_custom_call" | custom-call | flops 9059696640 | bytes 40000000 | tf_op jit(solution)/shard_map/pallas_call | solution.py:1038
  619.3 84.5 %shard_map.336 = (f32[256,1536]{1,0:T(8,128)}, bf16[2,640,1536]{2,1,0:T(8,128)(2,1)}, bf16[2,640,768]{2,1,0:T(8,128)(2,1)}, bf16[2,640,768]{2,1,0:T(8,128)(2,1)}) custom-call(f32[256,1536]{1,0:T(8,128)} %bitcast_convert_fusion.gradient, f32[4,2,2,256]{3,2,1,0:T(2,128)} %copy.566.tables, f32[4,2,256,2]{3,2,1,0:T(8,128)} %get-tuple-element.178.columns, ...), custom_call_target="tpu_custom_call" | custom-call | flops 9059696640 | bytes 40000000 | tf_op jit(solution)/shard_map/pallas_call | solution.py:1038
  706.9 15.9 %shard_map.337 = (bf16[2,1536,1536]{2,1,0:T(8,128)(2,1)}, bf16[2,768,1536]{2,1,0:T(8,128)(2,1)}) custom-call(bf16[2,640,1536]{2,1,0:T(8,128)(2,1)} %get-tuple-element.80.slot_in, bf16[2,640,768]{2,1,0:T(8,128)(2,1)S(1)} %copy-done.5, bf16[2,640,1536]{2,1,0:T(8,128)(2,1)} %get-tuple-element.82.slot_grad, bf16[2,640,768]{2,1,0:T(8,128)(2,1)S(1)} %copy-done, ...), custom_call_target="tpu_custom_call" | custom-call | flops 9059696640 | bytes 30000000 | tf_op jit(solution)/shard_map/pallas_call | solution.py:1084
  727.0 3.7 convolution_convert_fusion.5
  731.9 2.2 fusion.140
  734.1 11.8 fusion.9
  745.9 7.7 fusion.11
  753.6 3.5 fusion.75
  757.1 2.2 fusion.95
  759.4 2.6 fusion.74
  766.2 3.6 convolution_convert_fusion.2
  778.3 3.6 collective-permute-done.14
  785.3 5.7 multiply_reduce_fusion.1
  791.0 4.5 convolution_convert_fusion
  797.1 79.0 %shard_map.338 = (f32[256,1536]{1,0:T(8,128)}, bf16[2,640,1536]{2,1,0:T(8,128)(2,1)}, bf16[2,640,768]{2,1,0:T(8,128)(2,1)}, bf16[2,640,768]{2,1,0:T(8,128)(2,1)}) custom-call(f32[256,1536]{1,0:T(8,128)} %multiply_add_fusion.1.gradient, f32[4,2,2,256]{3,2,1,0:T(2,128)} %copy.551.tables, f32[4,2,256,2]{3,2,1,0:T(8,128)} %get-tuple-element.179.columns, ...), custom_call_target="tpu_custom_call" | custom-call | flops 9059696640 | bytes 40000000 | tf_op jit(solution)/shard_map/pallas_call | solution.py:1038
  879.2 15.9 %shard_map.339 = (bf16[2,1536,1536]{2,1,0:T(8,128)(2,1)}, bf16[2,768,1536]{2,1,0:T(8,128)(2,1)}) custom-call(bf16[2,640,1536]{2,1,0:T(8,128)(2,1)} %get-tuple-element.91.slot_in, bf16[2,640,768]{2,1,0:T(8,128)(2,1)S(1)} %copy-done.4, bf16[2,640,1536]{2,1,0:T(8,128)(2,1)} %get-tuple-element.93.slot_grad, bf16[2,640,768]{2,1,0:T(8,128)(2,1)S(1)} %copy-done.2, ...), custom_call_target="tpu_custom_call" | custom-call | flops 9059696640 | bytes 30000000 | tf_op jit(solution)/shard_map/pallas_call | solution.py:1084
  898.1 3.8 convolution_convert_fusion.4
  903.1 2.1 fusion.134
  905.2 8.7 fusion.3
  914.0 7.8 fusion.5
  921.8 4.3 fusion.73
  928.1 3.3 fusion.72
  932.5 2.0 fusion.76
  934.5 2.0 fusion.79
  936.5 3.6 convolution_convert_fusion.3
  941.2 168.9 %shard_map.341 = (bf16[48,2048]{1,0:T(8,128)(2,1)}, bf16[48,1536]{1,0:T(8,128)(2,1)}, bf16[48,128]{1,0:T(8,128)(2,1)}, bf16[4,96,1536]{2,1,0:T(8,128)(2,1)}, bf16[4,48,1536]{2,1,0:T(8,128)(2,1)}) custom-call(bf16[16,2,48,2048]{3,2,1,0:T(8,128)(2,1)} %bitcast.667, bf16[16,2,48,1536]{3,2,1,0:T(8,128)(2,1)} %bitcast.669, bf16[16,2,48,128]{3,2,1,0:T(8,128)(2,1)} %bitcast.714, ...), custom_call_target="tpu_custom_call" | custom-call | tf_op jit(solution)/shard_map/pallas_call | solution.py:736
  1111.6 3.3 add_convert_fusion
  1118.2 2.9 collective-permute-start.17
  1124.3 2.4 constant_dynamic-slice_fusion.2
  1127.6 4.5 collective-permute-done.17
  1135.0 6.6 fusion.64
  1141.6 4.6 convolution_convert_fusion.1
  1147.3 167.5 %shard_map.340 = (bf16[48,2048]{1,0:T(8,128)(2,1)}, bf16[48,1536]{1,0:T(8,128)(2,1)}, bf16[48,128]{1,0:T(8,128)(2,1)}, bf16[4,96,1536]{2,1,0:T(8,128)(2,1)}, bf16[4,48,1536]{2,1,0:T(8,128)(2,1)}) custom-call(bf16[16,2,48,2048]{3,2,1,0:T(8,128)(2,1)} %bitcast.668, bf16[16,2,48,1536]{3,2,1,0:T(8,128)(2,1)} %bitcast.670, bf16[16,2,48,128]{3,2,1,0:T(8,128)(2,1)} %bitcast.713, ...), custom_call_target="tpu_custom_call" | custom-call | tf_op jit(solution)/shard_map/pallas_call | solution.py:736
  1338.5 2.2 maximum_select_fusion.3
  1341.8 5.5 multiply_subtract_fusion.1
  1347.3 2.7 pad_maximum_fusion.2
  1350.0 2.7 pad_maximum_fusion.1
  1352.7 2.7 pad_maximum_fusion
  (498 shorter events, 146.0 us)
Async XLA Ops:
  6.9 45.3 %collective-permute-start = (bf16[4,48,1536]{2,1,0:T(8,128)(2,1)}, bf16[4,48,1536]{2,1,0:T(8,128)(2,1)}, u32[]{:S(2)}, u32[]{:S(2)}) collective-permute-start(bf16[4,48,1536]{2,1,0:T(8,128)(2,1)} %get-tuple-element.201), channel_id=1, source_target_pairs={{0,1},{1,0},{2,3},{3,2},{4,5},{5,4},{6,7},{7,6},{8,9},{9,8},{10,11... | collective-permute-start | bytes 1769480 | tf_op jit(solution)/shard_map/ppermute | solution.py:762
  9.1 39.1 %collective-permute-start.1 = (bf16[4,24,1536]{2,1,0:T(8,128)(2,1)}, bf16[4,24,1536]{2,1,0:T(8,128)(2,1)}, u32[]{:S(2)}, u32[]{:S(2)}) collective-permute-start(bf16[4,24,1536]{2,1,0:T(8,128)(2,1)} %get-tuple-element.235), channel_id=1, source_target_pairs={{0,1},{1,0},{2,3},{3,2},{4,5},{5,4},{6,7},{7,6},{8,9},{9,8},{10,11... | collective-permute-start | bytes 884744 | tf_op jit(solution)/shard_map/ppermute | solution.py:762
  9.8 7.5 copy-start.110
  9.8 7.6 copy-start.107
  9.8 7.7 copy-start.64
  10.7 23.3 %collective-permute-start.5 = (f32[2,2,2,256]{2,3,1,0:T(8,128)}, f32[2,2,2,256]{2,3,1,0:T(8,128)}, u32[]{:S(2)}, u32[]{:S(2)}) collective-permute-start(f32[2,2,2,256]{2,3,1,0:T(8,128)} %reverse_select_fusion.2), channel_id=1, source_target_pairs={{0,2},{2,0},{8,10},{10,8},{1,3},{3,1},{9,11},{11,9},{4,6},{6,4},{1... | collective-permute-start | bytes 24584 | tf_op jit(solution)/shard_map/ppermute | solution.py:203
  14.8 25.1 %collective-permute-start.6 = (f32[2,2,2,256]{2,3,1,0:T(8,128)}, f32[2,2,2,256]{2,3,1,0:T(8,128)}, u32[]{:S(2)}, u32[]{:S(2)}) collective-permute-start(f32[2,2,2,256]{2,3,1,0:T(8,128)} %reverse_select_fusion.1), channel_id=1, source_target_pairs={{0,8},{2,10},{8,0},{10,2},{1,9},{3,11},{9,1},{11,3},{4,12},{6,14},... | collective-permute-start | bytes 24584 | tf_op jit(solution)/shard_map/ppermute | solution.py:203
  17.3 22.6 %collective-permute-start.7 = (f32[2,2,2,256]{2,3,1,0:T(8,128)}, f32[2,2,2,256]{2,3,1,0:T(8,128)}, u32[]{:S(2)}, u32[]{:S(2)}) collective-permute-start(f32[2,2,2,256]{2,3,1,0:T(8,128)} %reverse_select_fusion), channel_id=1, source_target_pairs={{0,10},{2,8},{8,2},{10,0},{1,11},{3,9},{9,3},{11,1},{4,14},{6,12},... | collective-permute-start | bytes 24584 | tf_op jit(solution)/shard_map/ppermute | solution.py:203
  28.3 181.5 %copy-start.100 = (f32[256]{0:T(256)}, f32[256]{0:T(256)S(1)}, u32[]{:S(2)}) copy-start(f32[256]{0:T(256)S(1)} %add_rsqrt_fusion.3) | copy-start | bytes 3076
  34.0 194.8 %collective-permute-start.8 = (bf16[4,48,1536]{2,1,0:T(8,128)(2,1)}, bf16[4,48,1536]{2,1,0:T(8,128)(2,1)}, u32[]{:S(2)}, u32[]{:S(2)}) collective-permute-start(bf16[4,48,1536]{2,1,0:T(8,128)(2,1)} %get-tuple-element.199), channel_id=1, source_target_pairs={{0,1},{1,0},{2,3},{3,2},{4,5},{5,4},{6,7},{7,6},{8,9},{9,8},{10,11... | collective-permute-start | bytes 1769480 | tf_op jit(solution)/shard_map/ppermute | solution.py:762
  39.9 10.3 collective-permute-start.9
  43.8 8.3 copy-start.52
  209.8 190.3 %copy-start.89 = (f32[1536]{0:T(1024)}, f32[1536]{0:T(1024)S(1)}, u32[]{:S(2)}) copy-start(f32[1536]{0:T(1024)S(1)} %get-tuple-element.131) | copy-start | bytes 18436
  216.9 8.5 copy-start.71
  216.9 8.5 copy-start.73
  218.0 7.5 copy-start.69
  218.8 169.0 %collective-permute-start.2 = (bf16[256,4,128]{2,0,1:T(8,128)(2,1)}, bf16[256,4,128]{2,0,1:T(8,128)(2,1)}, u32[]{:S(2)}, u32[]{:S(2)}) collective-permute-start(bf16[256,4,128]{2,0,1:T(8,128)(2,1)} %pad_maximum_fusion.29), channel_id=1, source_target_pairs={{0,8},{8,0},{16,24},{24,16},{1,9},{9,1},{17,25},{25,17},{2,10},{10... | collective-permute-start | bytes 786440 | tf_op jit(solution)/shard_map/ppermute | solution.py:203
  220.7 167.2 %collective-permute-start.3 = (bf16[256,4,128]{2,0,1:T(8,128)(2,1)}, bf16[256,4,128]{2,0,1:T(8,128)(2,1)}, u32[]{:S(2)}, u32[]{:S(2)}) collective-permute-start(bf16[256,4,128]{2,0,1:T(8,128)(2,1)} %pad_maximum_fusion.29), channel_id=1, source_target_pairs={{0,16},{8,24},{16,0},{24,8},{1,17},{9,25},{17,1},{25,9},{2,18},{10... | collective-permute-start | bytes 786440 | tf_op jit(solution)/shard_map/ppermute | solution.py:203
  220.7 167.2 %collective-permute-start.4 = (bf16[256,4,128]{2,0,1:T(8,128)(2,1)}, bf16[256,4,128]{2,0,1:T(8,128)(2,1)}, u32[]{:S(2)}, u32[]{:S(2)}) collective-permute-start(bf16[256,4,128]{2,0,1:T(8,128)(2,1)} %pad_maximum_fusion.29), channel_id=1, source_target_pairs={{0,24},{8,16},{16,8},{24,0},{1,25},{9,17},{17,9},{25,1},{2,26},{10... | collective-permute-start | bytes 786440 | tf_op jit(solution)/shard_map/ppermute | solution.py:203
  231.1 152.5 %copy-start.34 = (f32[256,12,64]{2,0,1:T(8,128)S(1)}, f32[256,12,64]{2,0,1:T(8,128)}, u32[]{:S(2)}) copy-start(f32[256,12,64]{2,0,1:T(8,128)} %copy.698) | copy-start | bytes 2359300
  387.6 112.6 %copy-start.98 = (f32[1536]{0:T(1024)}, f32[1536]{0:T(1024)S(1)}, u32[]{:S(2)}) copy-start(f32[1536]{0:T(1024)S(1)} %get-tuple-element.130) | copy-start | bytes 18436
  389.3 7.2 copy-start.40
  400.0 98.4 %copy-start.102 = (f32[256]{0:T(256)}, f32[256]{0:T(256)S(1)}, u32[]{:S(2)}) copy-start(f32[256]{0:T(256)S(1)} %add_rsqrt_fusion.2) | copy-start | bytes 3076
  508.3 15.9 %collective-permute-start.10 = (bf16[256,4,128]{2,0,1:T(8,128)(2,1)}, bf16[256,4,128]{2,0,1:T(8,128)(2,1)}, u32[]{:S(2)}, u32[]{:S(2)}) collective-permute-start(bf16[256,4,128]{2,0,1:T(8,128)(2,1)} %pad_maximum_fusion.30), channel_id=1, source_target_pairs={{0,8},{8,0},{16,24},{24,16},{1,9},{9,1},{17,25},{25,17},{2,10},{10... | collective-permute-start | bytes 786440 | tf_op jit(solution)/shard_map/ppermute | solution.py:203
  509.8 14.4 %collective-permute-start.11 = (bf16[256,4,128]{2,0,1:T(8,128)(2,1)}, bf16[256,4,128]{2,0,1:T(8,128)(2,1)}, u32[]{:S(2)}, u32[]{:S(2)}) collective-permute-start(bf16[256,4,128]{2,0,1:T(8,128)(2,1)} %pad_maximum_fusion.30), channel_id=1, source_target_pairs={{0,16},{8,24},{16,0},{24,8},{1,17},{9,25},{17,1},{25,9},{2,18},{10... | collective-permute-start | bytes 786440 | tf_op jit(solution)/shard_map/ppermute | solution.py:203
  510.3 13.9 %collective-permute-start.12 = (bf16[256,4,128]{2,0,1:T(8,128)(2,1)}, bf16[256,4,128]{2,0,1:T(8,128)(2,1)}, u32[]{:S(2)}, u32[]{:S(2)}) collective-permute-start(bf16[256,4,128]{2,0,1:T(8,128)(2,1)} %pad_maximum_fusion.30), channel_id=1, source_target_pairs={{0,24},{8,16},{16,8},{24,0},{1,25},{9,17},{17,9},{25,1},{2,26},{10... | collective-permute-start | bytes 786440 | tf_op jit(solution)/shard_map/ppermute | solution.py:203
  525.9 7.2 copy-start.42
  619.3 84.5 %copy-start.5 = (bf16[2,640,768]{2,1,0:T(8,128)(2,1)S(1)}, bf16[2,640,768]{2,1,0:T(8,128)(2,1)}, u32[]{:S(2)}) copy-start(bf16[2,640,768]{2,1,0:T(8,128)(2,1)} %get-tuple-element.81.active) | copy-start | bytes 5898244
  706.9 15.9 %copy-start.35 = (f32[256,1536]{1,0:T(8,128)S(1)}, f32[256,1536]{1,0:T(8,128)}, u32[]{:S(2)}) copy-start(f32[256,1536]{1,0:T(8,128)} %get-tuple-element.87) | copy-start | bytes 4718596
  731.9 14.0 %slice-start.4 = ((s8[6291456]{0:T(1024)(128)(4,1)}), s8[4194304]{0:T(1024)(128)(4,1)S(1)}, s32[]{:S(2)}) async-start(s8[6291456]{0:T(1024)(128)(4,1)} %bitcast.663), calls=%async_computation.4 | async-start | bytes 8388608
  731.9 14.0 %slice-start.6 = ((s8[6291456]{0:T(1024)(128)(4,1)}), s8[4194304]{0:T(1024)(128)(4,1)S(1)}, s32[]{:S(2)}) async-start(s8[6291456]{0:T(1024)(128)(4,1)} %bitcast.665), calls=%async_computation.6 | async-start | bytes 8388608
  734.1 11.8 slice-start.5
  734.1 11.8 slice-start.7
  759.4 10.4 copy-start.45
  770.9 7.3 collective-permute-start.13
  772.4 9.5 collective-permute-start.14
  773.1 8.8 collective-permute-start.15
  778.2 7.0 copy-start.49
  778.2 7.0 copy-start.99
  797.1 79.0 %copy-start.4 = (bf16[2,640,768]{2,1,0:T(8,128)(2,1)S(1)}, bf16[2,640,768]{2,1,0:T(8,128)(2,1)}, u32[]{:S(2)}) copy-start(bf16[2,640,768]{2,1,0:T(8,128)(2,1)} %get-tuple-element.92.active) | copy-start | bytes 5898244
  879.2 15.9 %copy-start.37 = (f32[256,1536]{1,0:T(8,128)S(1)}, f32[256,1536]{1,0:T(8,128)}, u32[]{:S(2)}) copy-start(f32[256,1536]{1,0:T(8,128)} %get-tuple-element.98) | copy-start | bytes 4718596
  879.2 15.9 %copy-start.90 = (f32[1536]{0:T(1024)S(1)}, f32[1536]{0:T(1024)}, u32[]{:S(2)}) copy-start(f32[1536]{0:T(1024)} %copy-done.89) | copy-start | bytes 18436
  879.2 15.9 %copy-start.103 = (f32[256]{0:T(256)S(1)}, f32[256]{0:T(256)}, u32[]{:S(2)}) copy-start(f32[256]{0:T(256)} %copy-done.102) | copy-start | bytes 3076
  903.1 10.8 slice-start
  903.1 10.8 slice-start.2
  905.2 8.7 slice-start.1
  905.2 8.7 slice-start.3
  914.0 12.2 copy-start.30
  941.2 168.9 %copy-start.93 = (f32[2,48]{0,1:T(8,128)S(1)}, f32[2,48]{0,1:T(8,128)}, u32[]{:S(2)}) copy-start(f32[2,48]{0,1:T(8,128)} %copy.626) | copy-start | bytes 1156
  941.2 168.9 %copy-start.94 = (f32[2,48]{0,1:T(8,128)S(1)}, f32[2,48]{0,1:T(8,128)}, u32[]{:S(2)}) copy-start(f32[2,48]{0,1:T(8,128)} %copy.627) | copy-start | bytes 1156
  941.2 168.9 %copy-start.95 = (f32[2,48]{0,1:T(8,128)S(1)}, f32[2,48]{0,1:T(8,128)}, u32[]{:S(2)}) copy-start(f32[2,48]{0,1:T(8,128)} %copy.629) | copy-start | bytes 1156
  1118.2 9.0 copy-start.59
  1118.2 9.4 collective-permute-start.16
  1118.2 13.9 %collective-permute-start.17 = (bf16[256,4,128]{2,0,1:T(8,128)(2,1)}, bf16[256,4,128]{2,0,1:T(8,128)(2,1)}, u32[]{:S(2)}, u32[]{:S(2)}) collective-permute-start(bf16[256,4,128]{2,0,1:T(8,128)(2,1)} %get-tuple-element.204), channel_id=1, source_target_pairs={{16,0},{24,8},{0,16},{8,24},{17,1},{25,9},{1,17},{9,25},{18,2},{26... | collective-permute-start | bytes 786440 | tf_op jit(solution)/shard_map/ppermute | solution.py:203
  1121.1 12.2 collective-permute-start.18
  1124.3 206.4 %collective-permute-start.22 = (bf16[4,24,1536]{2,1,0:T(8,128)(2,1)}, bf16[4,24,1536]{2,1,0:T(8,128)(2,1)}, u32[]{:S(2)}, u32[]{:S(2)}) collective-permute-start(bf16[4,24,1536]{2,1,0:T(8,128)(2,1)} %get-tuple-element.229), channel_id=1, source_target_pairs={{0,1},{1,0},{2,3},{3,2},{4,5},{5,4},{6,7},{7,6},{8,9},{9,8},{10,11... | collective-permute-start | bytes 884744 | tf_op jit(solution)/shard_map/ppermute | solution.py:762
  1126.7 211.8 %collective-permute-start.20 = (bf16[4,48,1536]{2,1,0:T(8,128)(2,1)}, bf16[4,48,1536]{2,1,0:T(8,128)(2,1)}, u32[]{:S(2)}, u32[]{:S(2)}) collective-permute-start(bf16[4,48,1536]{2,1,0:T(8,128)(2,1)} %get-tuple-element.197), channel_id=1, source_target_pairs={{0,1},{1,0},{2,3},{3,2},{4,5},{5,4},{6,7},{7,6},{8,9},{9,8},{10,11... | collective-permute-start | bytes 1769480 | tf_op jit(solution)/shard_map/ppermute | solution.py:762
  1127.3 7.7 copy-start.18
  1127.3 7.7 copy-start.97
  1127.3 7.7 copy-start.101
  1147.3 167.5 %copy-start.91 = (f32[2,48]{0,1:T(8,128)S(1)}, f32[2,48]{0,1:T(8,128)}, u32[]{:S(2)}) copy-start(f32[2,48]{0,1:T(8,128)} %copy.620) | copy-start | bytes 1156
  1147.3 167.5 %copy-start.92 = (f32[2,48]{0,1:T(8,128)S(1)}, f32[2,48]{0,1:T(8,128)}, u32[]{:S(2)}) copy-start(f32[2,48]{0,1:T(8,128)} %copy.621) | copy-start | bytes 1156
  1317.2 14.6 %collective-permute-start.21 = (bf16[4,24,1536]{2,1,0:T(8,128)(2,1)S(1)}, bf16[4,24,1536]{2,1,0:T(8,128)(2,1)S(1)}, u32[]{:S(2)}, u32[]{:S(2)}) collective-permute-start(bf16[4,24,1536]{2,1,0:T(8,128)(2,1)S(1)} %get-tuple-element.227), channel_id=1, source_target_pairs={{0,1},{1,0},{2,3},{3,2},{4,5},{5,4},{6,7},{7,6},{8,9},{9,8},{10,11... | collective-permute-start | bytes 884744 | tf_op jit(solution)/shard_map/ppermute | solution.py:762
  1319.1 21.5 %collective-permute-start.19 = (bf16[4,48,1536]{2,1,0:T(8,128)(2,1)S(1)}, bf16[4,48,1536]{2,1,0:T(8,128)(2,1)S(1)}, u32[]{:S(2)}, u32[]{:S(2)}) collective-permute-start(bf16[4,48,1536]{2,1,0:T(8,128)(2,1)S(1)} %get-tuple-element.195), channel_id=1, source_target_pairs={{0,1},{1,0},{2,3},{3,2},{4,5},{5,4},{6,7},{7,6},{8,9},{9,8},{10,11... | collective-permute-start | bytes 1769480 | tf_op jit(solution)/shard_map/ppermute | solution.py:762
  (92 other events, 295.9 us)

commit v3 on v2

--- a/solution.py
+++ b/solution.py
@@ -386,13 +386,16 @@
         yield
     for z, w in here.column:
         for part in range(count):
-            source = wholes[part].at[block(x=1, z=z, w=w)]
-            wires.arrive(source, name(0, 0, 1, z, w, part), other)
-            pass_on(source, 0, 1, z, w, part, False, part % 2 == 1)
             for y in here.y_steps:
                 source = wholes[part].at[block(y=y, z=z, w=w)]
                 wires.arrive(source, name(0, y, 0, z, w, part), other)
-                pass_on(source, y, 0, z, w, part, part % 2 == 0, False)
+                pass_on(source, y, 0, z, w, part, True, False)
+        yield
+    for z, w in here.column:
+        for part in range(count):
+            source = wholes[part].at[block(x=1, z=z, w=w)]
+            wires.arrive(source, name(0, 0, 1, z, w, part), other)
+            pass_on(source, 0, 1, z, w, part, False, False)
         yield
     for z, w in here.column:
         for part in range(count):
@@ -482,31 +485,58 @@
 EXPERT_PARTS = 2
 
 
-def gather_layer_kernel(sizes, *refs):
-    count = ATTENTION_PARTS + EXPERT_PARTS
+def greet_experts(here):
+    greet(
+        [here.at(x=x, w=w) for x, w in offsets_of(GROUP)[1:]]
+        + [here.at(z=z) for z in here.z_steps]
+        + [here.at(y=y) for y in here.y_steps]
+        + [here.at(core=1)]
+    )
+
+
+def greet_attention(here):
+    greet(
+        [here.at(z=z, w=w) for z, w in here.column if (z, w) != (0, 0)]
+        + [here.at(x=1), here.at(core=1)]
+        + [here.at(y=y) for y in here.y_steps]
+    )
+
+
+def gather_kernel(sizes, count, *refs):
     ins, outs, sems = refs[:count], refs[count : 2 * count], refs[2 * count :]
     here = Place(sizes)
-    wires = Wires(*sems[:2]), Wires(*sems[2:])
     cut = ATTENTION_PARTS
-    greet_layer(here)
-    together(
-        gather_attention_steps(here, wires[0], ins[:cut], outs[:cut]),
-        gather_experts_steps(here, wires[1], ins[cut:], outs[cut:]),
-    )
+    wires = [Wires(*sems[:2])]
+    steps = [gather_attention_steps(here, wires[0], ins[:cut], outs[:cut])]
+    if count > cut:
+        greet_layer(here)
+        wires.append(Wires(*sems[2:]))
+        steps.append(gather_experts_steps(here, wires[1], ins[cut:], outs[cut:]))
+    else:
+        greet_attention(here)
+    together(*steps)
     for one in wires:
         one.drain()
 
 
-def gather_layer(attention_shards, expert_parts):
+def expert_sems(sizes):
+    chips = sizes[0] * sizes[1] * 4
+    sends = 3 + 4 * (sizes[0] + sizes[1]) + 4 * sizes[1] * sizes[0] + chips
+    return [
+        pltpu.SemaphoreType.DMA((EXPERT_PARTS * sends,)),
+        pltpu.SemaphoreType.DMA((2 * chips * EXPERT_PARTS,)),
+    ]
+
+
+def gather(identity, attention_shards, expert_parts):
     sizes = mesh_sizes()
     chips = sizes[0] * sizes[1] * 4
     columns = sizes[1] * 2
-    first = ATTENTION_PARTS * ((columns - 1) + chips + columns * (2 * sizes[0] + 1) + chips)
-    second = EXPERT_PARTS * (3 + 4 * (sizes[0] + sizes[1]) + 4 * sizes[1] * sizes[0] + chips)
+    sends = ATTENTION_PARTS * ((columns - 1) + chips + columns * (2 * sizes[0] + 1) + chips)
     in_vmem = pl.BlockSpec(memory_space=pltpu.VMEM)
-    count = ATTENTION_PARTS + EXPERT_PARTS
+    count = len(attention_shards) + len(expert_parts)
     return pl.pallas_call(
-        functools.partial(gather_layer_kernel, sizes),
+        functools.partial(gather_kernel, sizes, count),
         out_shape=[
             jax.ShapeDtypeStruct((2 * chips,) + shard.shape, shard.dtype)
             for shard in attention_shards
@@ -517,13 +547,12 @@
         in_specs=[in_vmem] * count,
         out_specs=[in_vmem] * count,
         scratch_shapes=[
-            pltpu.SemaphoreType.DMA((first,)),
+            pltpu.SemaphoreType.DMA((sends,)),
             pltpu.SemaphoreType.DMA((2 * chips * ATTENTION_PARTS,)),
-            pltpu.SemaphoreType.DMA((second,)),
-            pltpu.SemaphoreType.DMA((2 * chips * EXPERT_PARTS,)),
-        ],
+        ]
+        + (expert_sems(sizes) if expert_parts else []),
         compiler_params=pltpu.CompilerParams(
-            collective_id=0, has_side_effects=True, vmem_limit_bytes=58 * 1024 * 1024
+            collective_id=identity, has_side_effects=True, vmem_limit_bytes=58 * 1024 * 1024
         ),
     )(*attention_shards, *expert_parts)
 
@@ -554,7 +583,8 @@
             wires.send(
                 whole[part].at[1, index], first[part].at[spot], name(0, spot, part), other
             )
-    yield
+        if member == 0:
+            yield
     for y, z, member in order:
         x, w = group[member]
         index = here.chip(y=y, x=x, z=z, w=w)
@@ -615,18 +645,10 @@
 
     rounds = [
         (y, x, (column + 1) % width, part)
-        for y in list(here.y_steps) + [0]
-        for x in (1, 0)
+        for y, x in [(y, 1) for y in here.y_steps] + [(0, 1)] + [(y, 0) for y in here.y_steps] + [(0, 0)]
         for column in range(width)
         for part in range(count)
     ]
-
-    def turn(item):
-        y, x, column, part = item
-        ahead = x if part % 2 == 0 else y
-        return (not (y and x), not ahead, not (y or x))
-
-    rounds.sort(key=turn)
     for y, x, column, part in rounds:
         z, w = columns[column]
         spot = place(y, x, column)
@@ -636,7 +658,8 @@
             name(0, spot, part),
             other,
         )
-    yield
+        if (column, part) == (0, count - 1):
+            yield
     for y, x, column, part in rounds:
         z, w = columns[column]
         spot = place(y, x, column)
@@ -653,48 +676,29 @@
             add_rows(total, *parts)
             wires.send(total, buffer[part].at[index - offset], name(kind, index, part), device)
 
-        if part % 2 == 0:
-            if x:
-                add_rows(total, *parts)
-                wires.send(
-                    total,
-                    second[part].at[y * width + column],
-                    name(1, place(y, 0, column), part),
-                    here.at(x=1),
-                )
+        if x:
+            give(second, 1, y * width + column, here.at(x=1))
+            if part == count - 1:
                 yield
-                continue
-            arrived = second[part].at[y * width + column]
-            wires.arrive(arrived, name(1, place(y, 0, column), part), other)
-            parts.append(arrived)
-            if y:
-                give(third, 2, here.back_y(y) * width + column, here.at(y=y), width)
+            continue
+        take_in(second, 1, y * width + column)
+        if y:
+            give(third, 2, here.back_y(y) * width + column, here.at(y=y), width)
+            if part == count - 1:
                 yield
-                continue
-            for step in here.y_steps:
-                take_in(third, 2, step * width + column, width)
-        else:
-            if y:
-                give(second, 1, place(here.back_y(y), x, column), here.at(y=y), 2 * width)
-                yield
-                continue
-            for step in here.y_steps:
-                take_in(second, 1, place(step, x, column), 2 * width)
-            if x:
-                give(third, 2, column, here.at(x=1))
-                yield
-                continue
-            take_in(third, 2, column)
+            continue
+        for step in here.y_steps:
+            take_in(third, 2, step * width + column, width)
         if column:
             landing = columns.index((here.back_z(z), w))
             give(fourth, 3, landing, here.at(z=z, w=w), 1)
-            yield
+            if part == count - 1:
+                yield
             continue
         for step in range(1, width):
             take_in(fourth, 3, step, 1)
         add_rows(total, *parts)
         outs[part][...] = total[...]
-        yield
 
 
 def sum_layer_kernel(sizes, *refs):
@@ -731,8 +735,6 @@
             for part, block in enumerate(blocks)
         ]
 
-    level_two = (sizes[0] * column, (sizes[0] - 1) * 2 * column)
-    level_three = ((sizes[0] - 1) * column, column)
     return pl.pallas_call(
         functools.partial(sum_layer_kernel, sizes),
         out_shape=[jax.ShapeDtypeStruct(block.shape[2:], jnp.bfloat16) for block in attention]
@@ -740,8 +742,8 @@
         in_specs=[in_vmem] * count,
         out_specs=[in_vmem] * count,
         scratch_shapes=held(attention, lambda part: chips)
-        + held(attention, lambda part: level_two[part % 2])
-        + held(attention, lambda part: level_three[part % 2])
+        + held(attention, lambda part: sizes[0] * column)
+        + held(attention, lambda part: (sizes[0] - 1) * column)
         + held(attention, lambda part: column - 1)
         + held(experts, lambda part: chips)
         + held(experts, lambda part: (sizes[0] - 1) * sizes[1] * 4)
@@ -753,7 +755,7 @@
             pltpu.SemaphoreType.DMA((4 * chips * EXPERT_PARTS,)),
         ],
         compiler_params=pltpu.CompilerParams(
-            collective_id=1, has_side_effects=True, vmem_limit_bytes=62 * 1024 * 1024
+            collective_id=5, has_side_effects=True, vmem_limit_bytes=62 * 1024 * 1024
         ),
     )(*attention, *experts)
 
@@ -778,7 +780,15 @@
     return jnp.pad(gains, ((0, 0), (0, 128 - gains.shape[1])))
 
 
-def layer_weights(w_qkv, w_out, w_gateup, w_down, gains, layer):
+def attention_shards(w_qkv, w_out, gains, layer):
+    return [
+        w_qkv[layer].astype(jnp.bfloat16),
+        w_out[layer].astype(jnp.bfloat16),
+        gain_columns(gains[layer]),
+    ]
+
+
+def expert_parts(w_gateup, w_down, layer):
     core = lax.axis_index("core")
     parts = []
     for shard in (w_gateup[layer], w_down[layer]):
@@ -786,15 +796,16 @@
         shard = shard.reshape((4, 2) + shard.shape[1:])
         theirs = swap(pick(shard, 1 - core, 1), "core")
         parts.append(by_core(pick(shard, core, 1), theirs, 1).reshape(4, -1, D))
-    shards = [
-        w_qkv[layer].astype(jnp.bfloat16),
-        w_out[layer].astype(jnp.bfloat16),
-        gain_columns(gains[layer]),
-    ]
-    qkv, out, gain, up, down = gather_layer(shards, parts)
+    return parts
+
+
+def attention_matrices(qkv, out, gain):
     gain = gain.reshape(D, 128)[:, :2].T.astype(jnp.float32)
-    attention = (qkv.reshape(D, QKV), out.reshape(D, D), gain)
-    return attention, (up.reshape(2, D, 2 * F), down.reshape(2, F, D))
+    return qkv.reshape(D, QKV), out.reshape(D, D), gain
+
+
+def expert_matrices(up, down):
+    return up.reshape(2, D, 2 * F), down.reshape(2, F, D)
 
 
 def layer_sums(grad_qkv, grad_out, grad_up, grad_down, grad_gains):
@@ -805,13 +816,13 @@
         gain_columns(grad_gains),
     ]
     qkv, out, gain, up, down = sum_layer(attention, [grad_up, grad_down])
-    result = [qkv.astype(jnp.float32), out.astype(jnp.float32)]
+    result = [qkv, out]
     for part in (up, down):
         part = part.reshape(4, 2, -1, D)
         theirs = swap(pick(part, 1 - core, 1), "core")
         pair = by_core(pick(part, core, 1), theirs, 1)
-        result.append(pair.reshape(EXPERTS, -1, D).astype(jnp.float32))
-    return result + [gain[:, :2].T.astype(jnp.float32)]
+        result.append(pair.reshape(EXPERTS, -1, D))
+    return result + [gain[:, :2].T]
 
 
 SQRT_HALF = 0.7071067811865476
@@ -852,207 +863,192 @@
     return pl.BlockSpec((1,) + shape, lambda e, f: (e,) + (0,) * len(shape))
 
 
-def moe_forward_kernel(
-    sizes,
-    tokens,
-    tables,
-    columns,
-    up_w,
-    down_w,
-    merged,
-    slot_out,
-    gate_out,
-    up_out,
-    active_out,
-    chunks,
-    leaving,
-    coming,
-    slot_in,
-    result,
-    total,
-    send_sems,
-    recv_sems,
-):
+WAVES = ((0,), (3,), (1, 2))
+TURNS = ((0, 2), (1, 1), (2, 2))
+
+
+def moe_forward_kernel(sizes, background, *refs):
+    tokens, tables, columns, up_w, down_w = refs[:5]
+    extra = EXPERT_PARTS if background else 0
+    shards, refs = refs[5 : 5 + extra], refs[5 + extra :]
+    merged, slot_out, gate_out, up_out, active_out = refs[:5]
+    wholes, refs = refs[5 : 5 + extra], refs[5 + extra :]
+    chunks, leaving, coming, slot_in, result, total = refs[:6]
+    sems = refs[6:]
     here = Place(sizes)
-    wires = Wires(send_sems, recv_sems)
+    wires = Wires(*sems[:2])
     partners = [here.at(x=x, w=w) for x, w in offsets_of(GROUP)]
-    greet(partners[1:])
-    for place in range(1, 4):
+    if background:
+        greet_experts(here)
+        other_wires = Wires(*sems[2:])
+        steps = gather_experts_steps(here, other_wires, shards, wholes)
+    else:
+        greet(partners[1:])
+        steps = iter(())
+    for place in (3, 1, 2):
         wires.send(tokens, chunks.at[place - 1], place - 1, partners[place])
-    for place in range(4):
-        chunk = tokens if place == 0 else chunks.at[place - 1]
-        if place:
-            wires.arrive(chunk, place - 1, partners[place])
-        rows = pl.ds(place * CAP, CAP)
-
-        def step(index, carry, place=place, chunk=chunk, rows=rows):
-            expert, tile = lax.div(index, TILES), lax.rem(index, TILES)
-            at_gate = pl.ds(pl.multiple_of(tile * TILE, TILE), TILE)
-            at_up = pl.ds(pl.multiple_of(F + tile * TILE, TILE), TILE)
-            take, spread, gates = selections(tables[place, expert], columns[place, expert])
-
-            @pl.when(tile == 0)
-            def _():
-                slot_in[...] = dot(take, chunk[...]).astype(jnp.bfloat16)
-                slot_out[expert, rows, :] = slot_in[...]
-
-            gate = dot(slot_in[...], up_w[expert, :, at_gate])
-            up = dot(slot_in[...], up_w[expert, :, at_up])
-            active = (0.5 * gate * (1.0 + lax.erf(gate * SQRT_HALF)) * up).astype(jnp.bfloat16)
-            gate_out[expert, rows, at_gate] = gate
-            up_out[expert, rows, at_gate] = up
-            active_out[expert, rows, at_gate] = active
-            part = dot(active, down_w[expert, at_gate, :])
-
-            @pl.when(tile == 0)
-            def _():
-                result[...] = part
-
-            @pl.when(tile > 0)
-            def _():
-                result[...] += part
-
-            @pl.when(tile == TILES - 1)
-            def _():
-                share = dot(spread, result[...].astype(jnp.bfloat16)) * gates
-
-                @pl.when(expert == 0)
-                def _():
-                    total[...] = share
-
-                @pl.when(expert > 0)
-                def _():
-                    total[...] += share
-
-            return carry
-
-        lax.fori_loop(0, 2 * TILES, step, 0)
-        if place == 0:
-            merged[...] = total[...]
-        else:
-            leaving[place - 1] = total[...].astype(jnp.bfloat16)
-            wires.send(leaving.at[place - 1], coming.at[place - 1], place + 2, partners[place])
+    next(steps, None)
+    for wave, turns in zip(WAVES, TURNS):
+        sources = []
+        for place in wave:
+            source = tokens if place == 0 else chunks.at[place - 1]
+            if place:
+                wires.arrive(source, place - 1, partners[place])
+            sources.append(source)
+        count = CAP * len(wave)
+        rows = pl.ds(wave[0] * CAP, count)
+        for expert in range(2):
+            picks = [selections(tables[place, expert], columns[place, expert]) for place in wave]
+            for index, source in enumerate(sources):
+                chosen = dot(picks[index][0], source[...]).astype(jnp.bfloat16)
+                slot_in[index * CAP : (index + 1) * CAP] = chosen
+            slot_out[expert, rows, :] = slot_in[:count]
+
+            def step(tile, carry, expert=expert, count=count, rows=rows):
+                at_gate = pl.ds(pl.multiple_of(tile * TILE, TILE), TILE)
+                at_up = pl.ds(pl.multiple_of(F + tile * TILE, TILE), TILE)
+                gate = dot(slot_in[:count], up_w[expert, :, at_gate])
+                up = dot(slot_in[:count], up_w[expert, :, at_up])
+                active = (0.5 * gate * (1.0 + lax.erf(gate * SQRT_HALF)) * up).astype(jnp.bfloat16)
+                gate_out[expert, rows, at_gate] = gate.astype(jnp.bfloat16)
+                up_out[expert, rows, at_gate] = up.astype(jnp.bfloat16)
+                active_out[expert, rows, at_gate] = active
+                return carry
+
+            lax.fori_loop(0, TILES, step, 0)
+
+            def finish(tile, carry, expert=expert, count=count, rows=rows):
+                lanes = pl.ds(pl.multiple_of(tile * 2 * TILE, TILE), 2 * TILE)
+                result[:count, lanes] = dot(
+                    active_out[expert, rows, :], down_w[expert, :, lanes]
+                ).astype(jnp.bfloat16)
+                return carry
+
+            lax.fori_loop(0, D // (2 * TILE), finish, 0)
+            for index in range(len(wave)):
+                take, spread, gates = picks[index]
+                share = dot(spread, result[index * CAP : (index + 1) * CAP]) * gates
+                if expert == 0:
+                    total[index] = share
+                else:
+                    total[index] += share
+            for turn in range(turns[expert]):
+                next(steps, None)
+        for index, place in enumerate(wave):
+            if place == 0:
+                merged[...] = total[index]
+            else:
+                leaving[place - 1] = total[index].astype(jnp.bfloat16)
+                wires.send(
+                    leaving.at[place - 1], coming.at[place - 1], place + 2, partners[place]
+                )
+    for one in steps:
+        pass
     for place in range(1, 4):
         wires.arrive(coming.at[place - 1], place + 2, partners[place])
         merged[...] += coming[place - 1].astype(jnp.float32)
     wires.drain()
-
-
-def moe_backward_kernel(
-    sizes,
-    gradient,
-    tables,
-    columns,
-    up_w,
-    down_w,
-    gate_in,
-    up_in,
-    merged,
-    slot_out,
-    gate_out,
-    up_out,
-    chunks,
-    leaving,
-    coming,
-    slot_grad,
-    slots,
-    total,
-    send_sems,
-    recv_sems,
-):
+    if background:
+        other_wires.drain()
+
+
+def moe_backward_kernel(sizes, background, *refs):
+    gradient, tables, columns, up_w, down_w, gate_in, up_in = refs[:7]
+    merged, slot_out, gate_out, up_out = refs[7:11]
+    chunks, leaving, coming, slot_grad, slots, total = refs[11:17]
     here = Place(sizes)
-    wires = Wires(send_sems, recv_sems)
+    wires = Wires(*refs[17:])
     partners = [here.at(x=x, w=w) for x, w in offsets_of(GROUP)]
     greet(partners[1:])
     leaving[3] = gradient[...].astype(jnp.bfloat16)
-    for place in range(1, 4):
+    for place in (3, 1, 2):
         wires.send(leaving.at[3], chunks.at[place - 1], place - 1, partners[place])
-    for place in range(4):
-        chunk = gradient if place == 0 else chunks.at[place - 1]
-        if place:
-            wires.arrive(chunk, place - 1, partners[place])
-        rows = pl.ds(place * CAP, CAP)
-
-        def step(index, carry, place=place, chunk=chunk, rows=rows):
-            expert, tile = lax.div(index, TILES), lax.rem(index, TILES)
-            at_gate = pl.ds(pl.multiple_of(tile * TILE, TILE), TILE)
-            at_up = pl.ds(pl.multiple_of(F + tile * TILE, TILE), TILE)
-            take, spread, gates = selections(tables[place, expert], columns[place, expert])
-
-            @pl.when(tile == 0)
-            def _():
-                weighted = (gates * chunk[...].astype(jnp.float32)).astype(jnp.bfloat16)
-                slot_grad[...] = dot(take, weighted).astype(jnp.bfloat16)
-                slot_out[expert, rows, :] = slot_grad[...]
-
-            grad_act = dot(slot_grad[...], down_w[expert, at_gate, :], (1, 1))
-            gate, up = gate_in[expert, rows, at_gate], up_in[expert, rows, at_gate]
-            below = 0.5 * (1.0 + lax.erf(gate * SQRT_HALF))
-            slope = below + gate * PDF_SCALE * jnp.exp(-0.5 * gate * gate)
-            grad_gate = (grad_act * up * slope).astype(jnp.bfloat16)
-            grad_up = (grad_act * gate * below).astype(jnp.bfloat16)
-            gate_out[expert, rows, at_gate] = grad_gate
-            up_out[expert, rows, at_gate] = grad_up
-            part = dot(grad_gate, up_w[expert, :, at_gate], (1, 1))
-            part = part + dot(grad_up, up_w[expert, :, at_up], (1, 1))
-
-            @pl.when(tile == 0)
-            def _():
-                slots[...] = part
-
-            @pl.when(tile > 0)
-            def _():
-                slots[...] += part
-
-            @pl.when(tile == TILES - 1)
-            def _():
-                share = dot(spread, slots[...].astype(jnp.bfloat16))
-
-                @pl.when(expert == 0)
-                def _():
-                    total[...] = share
-
-                @pl.when(expert > 0)
-                def _():
-                    total[...] += share
-
-            return carry
-
-        lax.fori_loop(0, 2 * TILES, step, 0)
-        if place == 0:
-            merged[...] = total[...]
-        else:
-            leaving[place - 1] = total[...].astype(jnp.bfloat16)
-            wires.send(leaving.at[place - 1], coming.at[place - 1], place + 2, partners[place])
+    for wave in WAVES:
+        sources = []
+        for place in wave:
+            source = gradient if place == 0 else chunks.at[place - 1]
+            if place:
+                wires.arrive(source, place - 1, partners[place])
+            sources.append(source)
+        count = CAP * len(wave)
+        rows = pl.ds(wave[0] * CAP, count)
+        for expert in range(2):
+            picks = [selections(tables[place, expert], columns[place, expert]) for place in wave]
+            for index, source in enumerate(sources):
+                take, spread, gates = picks[index]
+                weighted = (gates * source[...].astype(jnp.float32)).astype(jnp.bfloat16)
+                slot_grad[index * CAP : (index + 1) * CAP] = dot(take, weighted).astype(jnp.bfloat16)
+            slot_out[expert, rows, :] = slot_grad[:count]
+
+            def step(tile, carry, expert=expert, count=count, rows=rows):
+                at_gate = pl.ds(pl.multiple_of(tile * TILE, TILE), TILE)
+                grad_act = dot(slot_grad[:count], down_w[expert, at_gate, :], (1, 1))
+                gate = gate_in[expert, rows, at_gate].astype(jnp.float32)
+                up = up_in[expert, rows, at_gate].astype(jnp.float32)
+                below = 0.5 * (1.0 + lax.erf(gate * SQRT_HALF))
+                slope = below + gate * PDF_SCALE * jnp.exp(-0.5 * gate * gate)
+                gate_out[expert, rows, at_gate] = (grad_act * up * slope).astype(jnp.bfloat16)
+                up_out[expert, rows, at_gate] = (grad_act * gate * below).astype(jnp.bfloat16)
+                return carry
+
+            lax.fori_loop(0, TILES, step, 0)
+
+            def finish(tile, carry, expert=expert, count=count, rows=rows):
+                lanes = pl.ds(pl.multiple_of(tile * 2 * TILE, TILE), 2 * TILE)
+                part = dot(gate_out[expert, rows, :], up_w[expert, lanes, :F], (1, 1))
+                part = part + dot(up_out[expert, rows, :], up_w[expert, lanes, F:], (1, 1))
+                slots[:count, lanes] = part.astype(jnp.bfloat16)
+                return carry
+
+            lax.fori_loop(0, D // (2 * TILE), finish, 0)
+            for index in range(len(wave)):
+                share = dot(picks[index][1], slots[index * CAP : (index + 1) * CAP])
+                if expert == 0:
+                    total[index] = share
+                else:
+                    total[index] += share
+        for index, place in enumerate(wave):
+            if place == 0:
+                merged[...] = total[index]
+            else:
+                leaving[place - 1] = total[index].astype(jnp.bfloat16)
+                wires.send(
+                    leaving.at[place - 1], coming.at[place - 1], place + 2, partners[place]
+                )
     for place in range(1, 4):
         wires.arrive(coming.at[place - 1], place + 2, partners[place])
         merged[...] += coming[place - 1].astype(jnp.float32)
     wires.drain()
 
 
-def moe_call(kernel, identity, rows_in, tables, weights, extra, kinds):
+def moe_call(kernel, identity, rows_in, tables, weights, extra, kinds, background=()):
     rows = rows_in.shape[0]
     slots = 4 * CAP
-    operands = [rows_in, tables, jnp.swapaxes(tables, 2, 3), *weights, *extra]
+    sizes = mesh_sizes()
+    chips = sizes[0] * sizes[1] * 4
+    operands = [rows_in, tables, jnp.swapaxes(tables, 2, 3), *weights, *extra, *background]
     in_vmem = pl.BlockSpec(memory_space=pltpu.VMEM)
+    more_sems = expert_sems(sizes) if background else []
     return pl.pallas_call(
-        functools.partial(kernel, mesh_sizes()),
+        functools.partial(kernel, sizes, bool(background)),
         in_specs=[in_vmem] * len(operands),
-        out_specs=[in_vmem] * (1 + len(kinds)),
+        out_specs=[in_vmem] * (1 + len(kinds) + len(background)),
         out_shape=[jax.ShapeDtypeStruct((rows, D), jnp.float32)]
-        + [jax.ShapeDtypeStruct((2, slots, width), kind) for width, kind in kinds],
+        + [jax.ShapeDtypeStruct((2, slots, width), jnp.bfloat16) for width in kinds]
+        + [jax.ShapeDtypeStruct((2, chips) + part.shape[1:], part.dtype) for part in background],
         scratch_shapes=[
             pltpu.VMEM((3, rows, D), jnp.bfloat16),
             pltpu.VMEM((4, rows, D), jnp.bfloat16),
             pltpu.VMEM((3, rows, D), jnp.bfloat16),
-            pltpu.VMEM((CAP, D), jnp.bfloat16),
-            pltpu.VMEM((CAP, D), jnp.float32),
-            pltpu.VMEM((rows, D), jnp.float32),
+            pltpu.VMEM((2 * CAP, D), jnp.bfloat16),
+            pltpu.VMEM((2 * CAP, D), jnp.bfloat16),
+            pltpu.VMEM((2, rows, D), jnp.float32),
             pltpu.SemaphoreType.DMA((6,)),
             pltpu.SemaphoreType.DMA((6,)),
-        ],
+        ]
+        + more_sems,
         compiler_params=pltpu.CompilerParams(
-            collective_id=identity, has_side_effects=True, vmem_limit_bytes=58 * 1024 * 1024
+            collective_id=identity, has_side_effects=True, vmem_limit_bytes=62 * 1024 * 1024
         ),
         cost_estimate=pl.CostEstimate(
             flops=48 * CAP * D * F, bytes_accessed=40_000_000, transcendentals=8 * CAP * F
@@ -1060,21 +1056,24 @@
     )(*operands)
 
 
-FORWARD_KEPT = ((D, jnp.bfloat16), (F, jnp.float32), (F, jnp.float32), (F, jnp.bfloat16))
-BACKWARD_KEPT = ((D, jnp.bfloat16), (F, jnp.bfloat16), (F, jnp.bfloat16))
-
-
-def moe_forward(expert_in, tables, weights):
+def moe_forward(expert_in, tables, weights, background):
     merged, *kept = moe_call(
-        moe_forward_kernel, 2, expert_in, tables, weights, [], FORWARD_KEPT
-    )
-    return merged, kept
+        moe_forward_kernel,
+        2 if background else 3,
+        expert_in,
+        tables,
+        weights,
+        [],
+        (D, F, F, F),
+        background,
+    )
+    return merged, kept[:4], expert_matrices(*kept[4:]) if background else None
 
 
 def moe_backward(gradient, tables, weights, kept):
     slot_in, gate, up, active = kept
     total, slot_grad, grad_gate, grad_up = moe_call(
-        moe_backward_kernel, 3, gradient, tables, weights, [gate, up], BACKWARD_KEPT
+        moe_backward_kernel, 4, gradient, tables, weights, [gate, up], (D, F, F)
     )
     slots = slot_in.shape[1]
 
@@ -1107,7 +1106,7 @@
     return total, grads[0], grads[1]
 
 
-def layer_forward(stream, attn_w, expert_w, tables, allowed, cosine_table, sine_table):
+def layer_forward(stream, attn_w, expert_w, ahead, tables, allowed, cosine_table, sine_table):
     qkv_w, out_w, gain_full = attn_w
     row_count = stream.shape[0]
     normed, scale_one = normalize(stream, gain_full[0])
@@ -1128,7 +1127,7 @@
     middle_stream = stream + jnp.dot(attended_low, out_w, preferred_element_type=jnp.float32)
     normed_two, scale_two = normalize(middle_stream, gain_full[1])
     expert_in = normed_two.astype(jnp.bfloat16)
-    merged, kept = moe_forward(expert_in, tables, expert_w)
+    merged, kept, gathered = moe_forward(expert_in, tables, expert_w, ahead)
     record = {
         "stream": stream,
         "scale_one": scale_one,
@@ -1142,7 +1141,7 @@
         "scale_two": scale_two,
         "kept": kept,
     }
-    return (record, middle_stream + merged)
+    return (record, middle_stream + merged, gathered)
 
 
 def layer_backward(gradient, record, attn_w, expert_w, tables, allowed, cosine_table, sine_table):
@@ -1237,23 +1236,29 @@
     group_tables = jnp.stack(group_tables, axis=1)
     stream = tokens[0].astype(jnp.float32)
     records = []
-    attn_w, expert_w = zip(
-        *[
-            layer_weights(w_qkv, w_out, w_gateup, w_down, gains, layer)
-            for layer in range(LAYERS)
-        ]
-    )
+    shards = [attention_shards(w_qkv, w_out, gains, layer) for layer in range(LAYERS)]
+    parts = [expert_parts(w_gateup, w_down, layer) for layer in range(LAYERS)]
+    first = gather(0, shards[0], [])
+    parts[0], first = lax.optimization_barrier((parts[0], first))
+    second = gather(1, shards[1], parts[0])
+    cut = ATTENTION_PARTS
+    attn_w = [attention_matrices(*first), attention_matrices(*second[:cut])]
+    expert_w = [expert_matrices(*second[cut:]), None]
     for layer_index in range(LAYERS):
-        record, stream = layer_forward(
+        ahead = [] if layer_index else parts[1]
+        record, stream, gathered = layer_forward(
             stream,
             attn_w[layer_index],
             expert_w[layer_index],
+            ahead,
             group_tables[layer_index],
             allowed,
             cosine_table,
             sine_table,
         )
         records.append(record)
+        if ahead:
+            expert_w[1] = gathered
     output = stream.astype(jnp.bfloat16)[None]
     gradient = cotangent[0].astype(jnp.float32)
     rates = (D ** (-0.5), 0.5, D ** (-0.5), (F // 8) ** (-0.5), 1.0)
@@ -1261,7 +1266,7 @@
     params = (w_qkv, w_out, w_gateup, w_down, gains)
     firsts = (m_qkv, m_out, m_gateup, m_down, m_gains)
     seconds = (v_qkv, v_out, v_gateup, v_down, v_gains)
-    updated = [[None] * LAYERS for which in range(15)]
+    sums = [None] * LAYERS
     for layer_index in reversed(range(LAYERS)):
         gradient, layer_grads = layer_backward(
             gradient,
@@ -1273,21 +1278,16 @@
             cosine_table,
             sine_table,
         )
-        sums = layer_sums(*layer_grads)
-        for which in range(5):
-            fresh = adamw(
-                params[which][layer_index],
-                firsts[which][layer_index],
-                seconds[which][layer_index],
-                sums[which],
-                rates[which],
-                decays[which],
+        sums[layer_index] = layer_sums(*layer_grads)
+    updated = []
+    for which in range(5):
+        total = jnp.stack([sums[layer][which] for layer in range(LAYERS)]).astype(jnp.float32)
+        updated.extend(
+            adamw(
+                params[which], firsts[which], seconds[which], total, rates[which], decays[which]
             )
-            updated[3 * which][layer_index] = fresh[0]
-            updated[3 * which + 1][layer_index] = fresh[1]
-            updated[3 * which + 2][layer_index] = fresh[2]
-    stacked = [jnp.stack(pieces) for pieces in updated]
-    return (output, gradient[None], *stacked)
+        )
+    return (output, gradient[None], *updated)
 
 
 def solution(mesh):

time: 1360 us -> 1280 us (0.941); the launches traced: 1360 us -> 1260 us
  Pallas kernels: 1000 us -> 938 us
  other arithmetic: 118 us -> 95.4 us
    pallas_call x2, Pallas kernels: 336 us -> 291 us  [sum_layer(): pl.pallas_call(functools.partial(sum_layer_kernel, sizes), out_shape=[jax...]
    another operation x28 -> x16, other arithmetic: 32.3 us -> 10.8 us  [the longest x17 21.9 us: on_device(): stacked = [jnp.stack(pieces) for pieces in updated]]
    pallas_call x6, Pallas kernels: 634 us -> 615 us  [the longest x4 399 us: moe_call(): pl.pallas_call(functools.partial(kernel, sizes, bool(background)), in_spe...]
    unnamed x280 -> x278, local copies, waits for them, and re-layouts: 27.3 us -> 24.5 us
  transfers between devices with their start and end apart: 23 -> 23, of which waited for: 5 -> 8; matrix products, arithmetic and copies ran while one was open for 9% -> 9% of each run, Pallas kernels for 35% -> 29%
where the time goes in v3:
time: 1280 us; the launch traced here: 1260 us
  Pallas kernels  938 us (73%)
  matrix products  111 us (9%)
  other arithmetic  95.4 us (7%)
  local copies, waits for them, and re-layouts  68.3 us (5%)
  waiting for transfers between devices  22.2 us (2%)
  starting transfers between devices  20.7 us (2%)
    pallas_call x4, Pallas kernels, moe_call(): pl.pallas_call(functools.partial(kernel, sizes, bool(background)), in_spe...  399 us
    pallas_call x2, Pallas kernels, sum_layer(): pl.pallas_call(functools.partial(sum_layer_kernel, sizes), out_shape=[jax...  291 us
    pallas_call x2, Pallas kernels, gather(): pl.pallas_call(functools.partial(gather_kernel, sizes, count), out_shape=...  216 us
    pallas_call x2, Pallas kernels, moe_backward(): pl.pallas_call(experts_grads_kernel, grid=(2, 3), in_specs=[columns_of(D...  31.8 us
  transfers between devices with their start and end apart: 23, of which 8 were waited for; matrix products, arithmetic and copies ran while one was open for 9% of the time, Pallas kernels for 29%

profile of v3, /device:TPU:0, one launch (start us, length us, event | category | flops | bytes accessed | tf_op | source)
XLA Modules:
  0.0 1258.6 jit_solution(6711044348709505908)
XLA Ops:
  3.5 4.0 collective-permute-start.7
  17.6 2.7 convert.122
  25.0 81.3 %shard_map.332 = (bf16[32,48,2048]{2,1,0:T(8,128)(2,1)}, bf16[32,48,1536]{2,1,0:T(8,128)(2,1)}, bf16[32,48,128]{2,1,0:T(8,128)(2,1)}) custom-call(bf16[48,2048]{1,0:T(8,128)(2,1)} %get-tuple-element.222.refs_0_, bf16[48,1536]{1,0:T(8,128)(2,1)} %get-tuple-element.224.refs_1_, bf16[48,128]{1,0:T(8,128)(2,1)} %pad.14.refs_2_), custom_call_target="tpu_custom_call" | custom-call | tf_op jit(solution)/shard_map/pallas_call | solution.py:538
  110.4 2.1 copy.417.refs_1_
  113.5 2.0 maximum_select_fusion.5
  115.4 2.1 maximum_select_fusion.4
  117.6 3.0 maximum_select_fusion
  121.0 4.6 fusion.102
  137.8 134.5 %shard_map.333 = (bf16[32,48,2048]{2,1,0:T(8,128)(2,1)}, bf16[32,48,1536]{2,1,0:T(8,128)(2,1)}, bf16[32,48,128]{2,1,0:T(8,128)(2,1)}, bf16[2,16,96,1536]{3,2,1,0:T(8,128)(2,1)}, bf16[2,16,48,1536]{3,2,1,0:T(8,128)(2,1)}) custom-call(bf16[48,2048]{1,0:T(8,128)(2,1)} %get-tuple-element.221.refs_0_, bf16[48,1536]{1,0:T(8,128)(2,1)} %get-tuple-element.223.refs_1_, ...), custom_call_target="tpu_custom_call" | custom-call | tf_op jit(solution)/shard_map/pallas_call | solution.py:538
  272.3 1.9 slice_convert_fusion
  275.9 2.9 copy.536
  280.7 2.3 subtract_convert_fusion.3
  283.3 3.0 maximum_select_fusion.1
  289.0 2.5 fusion.24
  292.2 1.9 fusion.71
  295.5 1.9 fusion.70
  300.3 155.9 %shard_map.334 = (f32[256,1536]{1,0:T(8,128)}, bf16[2,640,1536]{2,1,0:T(8,128)(2,1)}, bf16[2,640,768]{2,1,0:T(8,128)(2,1)}, bf16[2,640,768]{2,1,0:T(8,128)(2,1)}...) custom-call(bf16[256,1536]{1,0:T(8,128)(2,1)} %multiply_convert_fusion.2.refs_0_, ...), custom_call_target="tpu_custom_call" | custom-call | flops 9059696640 | bytes 40000000 | tf_op jit(solution)/shard_map/pallas_call | solution.py:1032
  457.9 5.2 fusion.172
  470.8 2.4 fusion.186
  478.5 3.0 collective-permute-done.11
  484.4 2.5 fusion.26
  489.5 2.1 fusion.68
  491.7 1.9 fusion.69
  497.5 81.3 %shard_map.335 = (f32[256,1536]{1,0:T(8,128)}, bf16[2,640,1536]{2,1,0:T(8,128)(2,1)}, bf16[2,640,768]{2,1,0:T(8,128)(2,1)}, bf16[2,640,768]{2,1,0:T(8,128)(2,1)}, bf16[2,640,768]{2,1,0:T(8,128)(2,1)}) custom-call(bf16[256,1536]{1,0:T(8,128)(2,1)} %multiply_convert_fusion.refs_0_, f32[4,2,2,256]{3,2,1,0:T(2,128)} %copy.417.refs_1_, ...), custom_call_target="tpu_custom_call" | custom-call | flops 9059696640 | bytes 40000000 | tf_op jit(solution)/shard_map/pallas_call | solution.py:1032
  578.8 82.1 %shard_map.336 = (f32[256,1536]{1,0:T(8,128)}, bf16[2,640,1536]{2,1,0:T(8,128)(2,1)}, bf16[2,640,768]{2,1,0:T(8,128)(2,1)}, bf16[2,640,768]{2,1,0:T(8,128)(2,1)}) custom-call(f32[256,1536]{1,0:T(8,128)} %bitcast_convert_fusion.refs_0_, f32[4,2,2,256]{3,2,1,0:T(2,128)} %copy.417.refs_1_, f32[4,2,256,2]{3,2,1,0:T(8,128)} %get-tuple-element.175.refs_2_, ...), custom_call_target="tpu_custom_call" | custom-call | flops 9059696640 | bytes 40000000 | tf_op jit(solution)/shard_map/pallas_call | solution.py:1032
  664.0 15.9 %shard_map.337 = (bf16[2,1536,1536]{2,1,0:T(8,128)(2,1)}, bf16[2,768,1536]{2,1,0:T(8,128)(2,1)}) custom-call(bf16[2,640,1536]{2,1,0:T(8,128)(2,1)} %get-tuple-element.90.slot_in, bf16[2,640,768]{2,1,0:T(8,128)(2,1)S(1)} %copy-done.5, bf16[2,640,1536]{2,1,0:T(8,128)(2,1)} %get-tuple-element.92.slot_grad, bf16[2,640,768]{2,1,0:T(8,128)(2,1)S(1)} %copy-done, ...), custom_call_target="tpu_custom_call" | custom-call | flops 9059696640 | bytes 30000000 | tf_op jit(solution)/shard_map/pallas_call | solution.py:1083
  682.9 5.2 convolution_convert_fusion.5
  688.2 3.6 convolution_convert_fusion.2
  691.7 2.3 copy.419
  694.0 2.1 fusion.130
  696.2 4.9 fusion.82
  701.1 2.0 fusion.85
  703.1 5.5 fusion.9
  708.6 7.7 fusion.11
  716.3 3.2 fusion.95
  731.5 3.2 collective-permute-done.13
  734.6 4.8 collective-permute-done.15
  742.5 5.0 multiply_reduce_fusion.1
  747.4 4.5 convolution_convert_fusion
  753.6 79.8 %shard_map.338 = (f32[256,1536]{1,0:T(8,128)}, bf16[2,640,1536]{2,1,0:T(8,128)(2,1)}, bf16[2,640,768]{2,1,0:T(8,128)(2,1)}, bf16[2,640,768]{2,1,0:T(8,128)(2,1)}) custom-call(f32[256,1536]{1,0:T(8,128)} %multiply_add_fusion.1.refs_0_, f32[4,2,2,256]{3,2,1,0:T(2,128)} %copy.403.refs_1_, f32[4,2,256,2]{3,2,1,0:T(8,128)} %get-tuple-element.176.refs_2_, ...), custom_call_target="tpu_custom_call" | custom-call | flops 9059696640 | bytes 40000000 | tf_op jit(solution)/shard_map/pallas_call | solution.py:1032
  836.5 15.9 %shard_map.339 = (bf16[2,1536,1536]{2,1,0:T(8,128)(2,1)}, bf16[2,768,1536]{2,1,0:T(8,128)(2,1)}) custom-call(bf16[2,640,1536]{2,1,0:T(8,128)(2,1)} %get-tuple-element.101.slot_in, bf16[2,640,768]{2,1,0:T(8,128)(2,1)S(1)} %copy-done.4, bf16[2,640,1536]{2,1,0:T(8,128)(2,1)} %get-tuple-element.103.slot_grad, bf16[2,640,768]{2,1,0:T(8,128)(2,1)S(1)} %copy-done.2, ...), custom_call_target="tpu_custom_call" | custom-call | flops 9059696640 | bytes 30000000 | tf_op jit(solution)/shard_map/pallas_call | solution.py:1083
  854.3 5.2 convolution_convert_fusion.4
  859.5 3.6 convolution_convert_fusion.3
  863.1 2.3 copy.444
  865.4 2.1 fusion.124
  867.6 4.9 fusion.76
  872.5 2.0 fusion.79
  874.5 5.5 fusion.3
  880.0 7.6 fusion.5
  887.7 3.2 fusion.91
  892.8 2.3 fusion.72
  897.9 145.8 %shard_map.341 = (bf16[48,2048]{1,0:T(8,128)(2,1)}, bf16[48,1536]{1,0:T(8,128)(2,1)}, bf16[48,128]{1,0:T(8,128)(2,1)}, bf16[4,96,1536]{2,1,0:T(8,128)(2,1)}, bf16[4,48,1536]{2,1,0:T(8,128)(2,1)}) custom-call(bf16[16,2,48,2048]{3,2,1,0:T(8,128)(2,1)} %bitcast.513, bf16[16,2,48,1536]{3,2,1,0:T(8,128)(2,1)} %bitcast.515, bf16[16,2,48,128]{3,2,1,0:T(8,128)(2,1)} %bitcast.560, ...), custom_call_target="tpu_custom_call" | custom-call | tf_op jit(solution)/shard_map/pallas_call | solution.py:738
  1044.6 1.9 constant_dynamic-slice_fusion
  1046.6 2.1 constant_dynamic-slice_fusion.2
  1058.1 3.0 collective-permute-done.16
  1061.1 5.2 collective-permute-done.18
  1069.5 6.0 fusion.64
  1075.4 4.6 convolution_convert_fusion.1
  1081.2 145.3 %shard_map.340 = (bf16[48,2048]{1,0:T(8,128)(2,1)}, bf16[48,1536]{1,0:T(8,128)(2,1)}, bf16[48,128]{1,0:T(8,128)(2,1)}, bf16[4,96,1536]{2,1,0:T(8,128)(2,1)}, bf16[4,48,1536]{2,1,0:T(8,128)(2,1)}) custom-call(bf16[16,2,48,2048]{3,2,1,0:T(8,128)(2,1)} %bitcast.514, bf16[16,2,48,1536]{3,2,1,0:T(8,128)(2,1)} %bitcast.516, bf16[16,2,48,128]{3,2,1,0:T(8,128)(2,1)} %bitcast.559, ...), custom_call_target="tpu_custom_call" | custom-call | tf_op jit(solution)/shard_map/pallas_call | solution.py:738
  1226.5 2.1 constant_dynamic-slice_fusion.1
  1228.6 2.3 constant_dynamic-slice_fusion.3
  1240.7 7.0 multiply_subtract_fusion.1
  1247.7 2.2 maximum_select_fusion.3
  1251.4 7.0 multiply_subtract_fusion
  (476 shorter events, 127.3 us)
Async XLA Ops:
  2.5 7.7 copy-start.45
  3.5 102.7 %collective-permute-start.7 = (f32[2,2,2,256]{2,3,1,0:T(8,128)}, f32[2,2,2,256]{2,3,1,0:T(8,128)}, u32[]{:S(2)}, u32[]{:S(2)}) collective-permute-start(f32[2,2,2,256]{2,3,1,0:T(8,128)} %reverse_select_fusion), channel_id=1, source_target_pairs={{0,10},{2,8},{8,2},{10,0},{1,11},{3,9},{9,3},{11,1},{4,14},{6,12},... | collective-permute-start | bytes 24584 | tf_op jit(solution)/shard_map/ppermute | solution.py:203
  8.6 98.3 %collective-permute-start.6 = (f32[2,2,2,256]{2,3,1,0:T(8,128)}, f32[2,2,2,256]{2,3,1,0:T(8,128)}, u32[]{:S(2)}, u32[]{:S(2)}) collective-permute-start(f32[2,2,2,256]{2,3,1,0:T(8,128)} %reverse_select_fusion.1), channel_id=1, source_target_pairs={{0,8},{2,10},{8,0},{10,2},{1,9},{3,11},{9,1},{11,3},{4,12},{6,14},... | collective-permute-start | bytes 24584 | tf_op jit(solution)/shard_map/ppermute | solution.py:203
  10.1 96.8 %collective-permute-start.5 = (f32[2,2,2,256]{2,3,1,0:T(8,128)}, f32[2,2,2,256]{2,3,1,0:T(8,128)}, u32[]{:S(2)}, u32[]{:S(2)}) collective-permute-start(f32[2,2,2,256]{2,3,1,0:T(8,128)} %reverse_select_fusion.2), channel_id=1, source_target_pairs={{0,2},{2,0},{8,10},{10,8},{1,3},{3,1},{9,11},{11,9},{4,6},{6,4},{1... | collective-permute-start | bytes 24584 | tf_op jit(solution)/shard_map/ppermute | solution.py:203
  11.4 102.1 %collective-permute-start.9 = (bf16[4,24,1536]{2,1,0:T(8,128)(2,1)}, bf16[4,24,1536]{2,1,0:T(8,128)(2,1)}, u32[]{:S(2)}, u32[]{:S(2)}) collective-permute-start(bf16[4,24,1536]{2,1,0:T(8,128)(2,1)} %get-tuple-element.218), channel_id=1, source_target_pairs={{0,1},{1,0},{2,3},{3,2},{4,5},{5,4},{6,7},{7,6},{8,9},{9,8},{10,11... | collective-permute-start | bytes 884744 | tf_op jit(solution)/shard_map/ppermute | solution.py:764
  12.2 103.2 %collective-permute-start.1 = (bf16[4,24,1536]{2,1,0:T(8,128)(2,1)}, bf16[4,24,1536]{2,1,0:T(8,128)(2,1)}, u32[]{:S(2)}, u32[]{:S(2)}) collective-permute-start(bf16[4,24,1536]{2,1,0:T(8,128)(2,1)} %get-tuple-element.220), channel_id=1, source_target_pairs={{0,1},{1,0},{2,3},{3,2},{4,5},{5,4},{6,7},{7,6},{8,9},{9,8},{10,11... | collective-permute-start | bytes 884744 | tf_op jit(solution)/shard_map/ppermute | solution.py:764
  13.6 107.4 %copy-start.103 = (f32[256]{0:T(256)}, f32[256]{0:T(256)S(1)}, u32[]{:S(2)}) copy-start(f32[256]{0:T(256)S(1)} %add_rsqrt_fusion.3) | copy-start | bytes 3076
  20.5 86.5 %copy-start.72 = (f32[2,1,2,2,256]{3,4,2,1,0:T(8,128)S(1)}, f32[2,1,2,2,256]{3,4,2,1,0:T(8,128)}, u32[]{:S(2)}) copy-start(f32[2,1,2,2,256]{3,4,2,1,0:T(8,128)} %fusion.111) | copy-start | bytes 24580
  23.0 257.6 %copy-start.41 = (f32[256,64]{1,0:T(8,128)}, f32[256,64]{1,0:T(8,128)S(1)}, u32[]{:S(2)}) copy-start(f32[256,64]{1,0:T(8,128)S(1)} %get-tuple-element.242) | copy-start | bytes 196612
  23.1 453.3 %copy-start.38 = (f32[256,64]{1,0:T(8,128)}, f32[256,64]{1,0:T(8,128)S(1)}, u32[]{:S(2)}) copy-start(f32[256,64]{1,0:T(8,128)S(1)} %get-tuple-element.241) | copy-start | bytes 196612
  23.5 468.1 %copy-start.14 = (pred[256,1024]{0,1:T(8,128)(4,1)}, pred[256,1024]{0,1:T(8,128)(4,1)S(1)}, u32[]{:S(2)}) copy-start(pred[256,1024]{0,1:T(8,128)(4,1)S(1)} %compare_and_fusion) | copy-start | bytes 786436
  106.3 177.0 %collective-permute-start.8 = (bf16[4,48,1536]{2,1,0:T(8,128)(2,1)}, bf16[4,48,1536]{2,1,0:T(8,128)(2,1)}, u32[]{:S(2)}, u32[]{:S(2)}) collective-permute-start(bf16[4,48,1536]{2,1,0:T(8,128)(2,1)} %get-tuple-element.196), channel_id=1, source_target_pairs={{0,1},{1,0},{2,3},{3,2},{4,5},{5,4},{6,7},{7,6},{8,9},{9,8},{10,11... | collective-permute-start | bytes 1769480 | tf_op jit(solution)/shard_map/ppermute | solution.py:764
  106.8 10.8 collective-permute-start
  113.5 7.1 copy-start.89
  120.9 178.1 %copy-start.98 = (f32[1536]{0:T(1024)}, f32[1536]{0:T(1024)S(1)}, u32[]{:S(2)}) copy-start(f32[1536]{0:T(1024)S(1)} %get-tuple-element.141) | copy-start | bytes 18436
  132.7 153.6 %collective-permute-start.4 = (bf16[256,4,128]{2,0,1:T(8,128)(2,1)}, bf16[256,4,128]{2,0,1:T(8,128)(2,1)}, u32[]{:S(2)}, u32[]{:S(2)}) collective-permute-start(bf16[256,4,128]{2,0,1:T(8,128)(2,1)} %pad_maximum_fusion.21), channel_id=1, source_target_pairs={{0,24},{8,16},{16,8},{24,0},{1,25},{9,17},{17,9},{25,1},{2,26},{10... | collective-permute-start | bytes 786440 | tf_op jit(solution)/shard_map/ppermute | solution.py:203
  134.2 152.1 %collective-permute-start.3 = (bf16[256,4,128]{2,0,1:T(8,128)(2,1)}, bf16[256,4,128]{2,0,1:T(8,128)(2,1)}, u32[]{:S(2)}, u32[]{:S(2)}) collective-permute-start(bf16[256,4,128]{2,0,1:T(8,128)(2,1)} %pad_maximum_fusion.21), channel_id=1, source_target_pairs={{0,16},{8,24},{16,0},{24,8},{1,17},{9,25},{17,1},{25,9},{2,18},{10... | collective-permute-start | bytes 786440 | tf_op jit(solution)/shard_map/ppermute | solution.py:203
  134.7 151.6 %collective-permute-start.2 = (bf16[256,4,128]{2,0,1:T(8,128)(2,1)}, bf16[256,4,128]{2,0,1:T(8,128)(2,1)}, u32[]{:S(2)}, u32[]{:S(2)}) collective-permute-start(bf16[256,4,128]{2,0,1:T(8,128)(2,1)} %pad_maximum_fusion.21), channel_id=1, source_target_pairs={{0,8},{8,0},{16,24},{24,16},{1,9},{9,1},{17,25},{25,17},{2,10},{10... | collective-permute-start | bytes 786440 | tf_op jit(solution)/shard_map/ppermute | solution.py:203
  137.8 136.4 %copy-start.49 = (f32[256,1536]{0,1:T(8,128)S(1)}, f32[256,1536]{0,1:T(8,128)}, u32[]{:S(2)}) copy-start(f32[256,1536]{0,1:T(8,128)} %copy.388) | copy-start | bytes 4718596
  287.6 7.8 copy-start.54
  299.0 157.2 %copy-start.10 = (f32[256,1536]{1,0:T(8,128)}, f32[256,1536]{1,0:T(8,128)S(1)}, u32[]{:S(2)}) copy-start(f32[256,1536]{1,0:T(8,128)S(1)} %get-tuple-element.256) | copy-start | bytes 4718596
  465.7 12.9 %collective-permute-start.12 = (bf16[256,4,128]{2,0,1:T(8,128)(2,1)}, bf16[256,4,128]{2,0,1:T(8,128)(2,1)}, u32[]{:S(2)}, u32[]{:S(2)}) collective-permute-start(bf16[256,4,128]{2,0,1:T(8,128)(2,1)} %pad_maximum_fusion.22), channel_id=1, source_target_pairs={{0,24},{8,16},{16,8},{24,0},{1,25},{9,17},{17,9},{25,1},{2,26},{10... | collective-permute-start | bytes 786440 | tf_op jit(solution)/shard_map/ppermute | solution.py:203
  466.8 14.7 %collective-permute-start.11 = (bf16[256,4,128]{2,0,1:T(8,128)(2,1)}, bf16[256,4,128]{2,0,1:T(8,128)(2,1)}, u32[]{:S(2)}, u32[]{:S(2)}) collective-permute-start(bf16[256,4,128]{2,0,1:T(8,128)(2,1)} %pad_maximum_fusion.22), channel_id=1, source_target_pairs={{0,16},{8,24},{16,0},{24,8},{1,17},{9,25},{17,1},{25,9},{2,18},{10... | collective-permute-start | bytes 786440 | tf_op jit(solution)/shard_map/ppermute | solution.py:203
  467.7 14.1 %collective-permute-start.10 = (bf16[256,4,128]{2,0,1:T(8,128)(2,1)}, bf16[256,4,128]{2,0,1:T(8,128)(2,1)}, u32[]{:S(2)}, u32[]{:S(2)}) collective-permute-start(bf16[256,4,128]{2,0,1:T(8,128)(2,1)} %pad_maximum_fusion.22), channel_id=1, source_target_pairs={{0,8},{8,0},{16,24},{24,16},{1,9},{9,1},{17,25},{25,17},{2,10},{10... | collective-permute-start | bytes 786440 | tf_op jit(solution)/shard_map/ppermute | solution.py:203
  483.0 8.6 copy-start.57
  484.3 7.3 copy-start.8
  578.8 82.1 %copy-start.5 = (bf16[2,640,768]{2,1,0:T(8,128)(2,1)S(1)}, bf16[2,640,768]{2,1,0:T(8,128)(2,1)}, u32[]{:S(2)}) copy-start(bf16[2,640,768]{2,1,0:T(8,128)(2,1)} %get-tuple-element.91.active) | copy-start | bytes 5898244
  664.0 15.9 %copy-start.25 = (f32[256,1536]{1,0:T(8,128)S(1)}, f32[256,1536]{1,0:T(8,128)}, u32[]{:S(2)}) copy-start(f32[256,1536]{1,0:T(8,128)} %copy-done.24) | copy-start | bytes 4718596
  664.0 15.9 %copy-start.48 = (f32[256,1536]{1,0:T(8,128)S(1)}, f32[256,1536]{1,0:T(8,128)}, u32[]{:S(2)}) copy-start(f32[256,1536]{1,0:T(8,128)} %get-tuple-element.97) | copy-start | bytes 4718596
  688.1 13.0 %slice-start.6 = ((s8[6291456]{0:T(1024)(128)(4,1)}), s8[2097152]{0:T(1024)(128)(4,1)S(1)}, s32[]{:S(2)}) async-start(s8[6291456]{0:T(1024)(128)(4,1)} %bitcast.511), calls=%async_computation.6 | async-start | bytes 4194304
  694.0 7.1 slice-start.7
  696.2 7.0 slice-start.4
  708.6 7.7 copy-start.36
  725.3 9.4 collective-permute-start.13
  726.0 13.4 %collective-permute-start.15 = (bf16[256,4,128]{2,0,1:T(8,128)(2,1)}, bf16[256,4,128]{2,0,1:T(8,128)(2,1)}, u32[]{:S(2)}, u32[]{:S(2)}) collective-permute-start(bf16[256,4,128]{2,0,1:T(8,128)(2,1)} %get-tuple-element.203), channel_id=1, source_target_pairs={{24,0},{16,8},{8,16},{0,24},{25,1},{17,9},{9,17},{1,25},{26,2},{18... | collective-permute-start | bytes 786440 | tf_op jit(solution)/shard_map/ppermute | solution.py:203
  727.1 13.6 %collective-permute-start.14 = (bf16[256,4,128]{2,0,1:T(8,128)(2,1)}, bf16[256,4,128]{2,0,1:T(8,128)(2,1)}, u32[]{:S(2)}, u32[]{:S(2)}) collective-permute-start(bf16[256,4,128]{2,0,1:T(8,128)(2,1)} %get-tuple-element.204), channel_id=1, source_target_pairs={{16,0},{24,8},{0,16},{8,24},{17,1},{25,9},{1,17},{9,25},{18,2},{26... | collective-permute-start | bytes 786440 | tf_op jit(solution)/shard_map/ppermute | solution.py:203
  731.4 11.0 copy-start.19
  753.6 79.8 %copy-start.4 = (bf16[2,640,768]{2,1,0:T(8,128)(2,1)S(1)}, bf16[2,640,768]{2,1,0:T(8,128)(2,1)}, u32[]{:S(2)}) copy-start(bf16[2,640,768]{2,1,0:T(8,128)(2,1)} %get-tuple-element.102.active) | copy-start | bytes 5898244
  836.5 15.9 %copy-start.11 = (f32[256,1536]{1,0:T(8,128)S(1)}, f32[256,1536]{1,0:T(8,128)}, u32[]{:S(2)}) copy-start(f32[256,1536]{1,0:T(8,128)} %copy-done.10) | copy-start | bytes 4718596
  836.5 16.0 %copy-start.51 = (f32[256,1536]{1,0:T(8,128)S(1)}, f32[256,1536]{1,0:T(8,128)}, u32[]{:S(2)}) copy-start(f32[256,1536]{1,0:T(8,128)} %get-tuple-element.108) | copy-start | bytes 4718596
  836.5 16.0 %copy-start.99 = (f32[1536]{0:T(1024)S(1)}, f32[1536]{0:T(1024)}, u32[]{:S(2)}) copy-start(f32[1536]{0:T(1024)} %copy-done.98) | copy-start | bytes 18436
  836.5 16.0 %copy-start.106 = (f32[256]{0:T(256)S(1)}, f32[256]{0:T(256)}, u32[]{:S(2)}) copy-start(f32[256]{0:T(256)} %copy-done.105) | copy-start | bytes 3076
  859.5 13.0 %slice-start.2 = ((s8[6291456]{0:T(1024)(128)(4,1)}), s8[2097152]{0:T(1024)(128)(4,1)S(1)}, s32[]{:S(2)}) async-start(s8[6291456]{0:T(1024)(128)(4,1)} %bitcast.507), calls=%async_computation.2 | async-start | bytes 4194304
  865.4 7.1 slice-start.3
  867.6 7.0 slice-start
  880.0 7.6 copy-start.33
  1046.5 191.5 %collective-permute-start.22 = (bf16[4,24,1536]{2,1,0:T(8,128)(2,1)}, bf16[4,24,1536]{2,1,0:T(8,128)(2,1)}, u32[]{:S(2)}, u32[]{:S(2)}) collective-permute-start(bf16[4,24,1536]{2,1,0:T(8,128)(2,1)} %get-tuple-element.216), channel_id=1, source_target_pairs={{0,1},{1,0},{2,3},{3,2},{4,5},{5,4},{6,7},{7,6},{8,9},{9,8},{10,11... | collective-permute-start | bytes 884744 | tf_op jit(solution)/shard_map/ppermute | solution.py:764
  1048.7 199.0 %collective-permute-start.20 = (bf16[4,48,1536]{2,1,0:T(8,128)(2,1)}, bf16[4,48,1536]{2,1,0:T(8,128)(2,1)}, u32[]{:S(2)}, u32[]{:S(2)}) collective-permute-start(bf16[4,48,1536]{2,1,0:T(8,128)(2,1)} %get-tuple-element.192), channel_id=1, source_target_pairs={{0,1},{1,0},{2,3},{3,2},{4,5},{5,4},{6,7},{7,6},{8,9},{9,8},{10,11... | collective-permute-start | bytes 1769480 | tf_op jit(solution)/shard_map/ppermute | solution.py:764
  1049.1 6.1 copy-start.40
  1049.1 6.1 copy-start.44
  1051.7 9.4 collective-permute-start.16
  1053.0 13.4 %collective-permute-start.18 = (bf16[256,4,128]{2,0,1:T(8,128)(2,1)}, bf16[256,4,128]{2,0,1:T(8,128)(2,1)}, u32[]{:S(2)}, u32[]{:S(2)}) collective-permute-start(bf16[256,4,128]{2,0,1:T(8,128)(2,1)} %get-tuple-element.200), channel_id=1, source_target_pairs={{24,0},{16,8},{8,16},{0,24},{25,1},{17,9},{9,17},{1,25},{26,2},{18... | collective-permute-start | bytes 786440 | tf_op jit(solution)/shard_map/ppermute | solution.py:203
  1054.1 13.6 %collective-permute-start.17 = (bf16[256,4,128]{2,0,1:T(8,128)(2,1)}, bf16[256,4,128]{2,0,1:T(8,128)(2,1)}, u32[]{:S(2)}, u32[]{:S(2)}) collective-permute-start(bf16[256,4,128]{2,0,1:T(8,128)(2,1)} %get-tuple-element.201), channel_id=1, source_target_pairs={{16,0},{24,8},{0,16},{8,24},{17,1},{25,9},{1,17},{9,25},{18,2},{26... | collective-permute-start | bytes 786440 | tf_op jit(solution)/shard_map/ppermute | solution.py:203
  1058.1 11.4 copy-start.23
  1058.1 11.4 copy-start.102
  1058.1 11.4 copy-start.104
  1230.9 8.2 collective-permute-start.21
  1231.1 18.9 %collective-permute-start.19 = (bf16[4,48,1536]{2,1,0:T(8,128)(2,1)}, bf16[4,48,1536]{2,1,0:T(8,128)(2,1)}, u32[]{:S(2)}, u32[]{:S(2)}) collective-permute-start(bf16[4,48,1536]{2,1,0:T(8,128)(2,1)} %get-tuple-element.190), channel_id=1, source_target_pairs={{0,1},{1,0},{2,3},{3,2},{4,5},{5,4},{6,7},{7,6},{8,9},{9,8},{10,11... | collective-permute-start | bytes 1769480 | tf_op jit(solution)/shard_map/ppermute | solution.py:764
  1240.6 10.8 slice-start.8
  1240.6 10.8 slice-start.13
  1240.6 10.8 slice-start.15
  1240.6 10.7 slice-start.9
  1240.6 10.7 slice-start.14
  1240.7 10.7 slice-start.16
  (92 other events, 272.7 us)

commit v4 on v3

--- a/solution.py
+++ b/solution.py
@@ -33,33 +33,8 @@
     half_width = HD // 2
     frequency = ROPE_BASE ** (-(jnp.arange(half_width, dtype=jnp.float32) * 2.0 / HD))
     angles = positions.astype(jnp.float32)[:, None] * frequency[None, :]
-    return (jnp.cos(angles)[:, None, :], jnp.sin(angles)[:, None, :])
-
-
-def rotate(vectors, cosine_table, sine_table):
-    half_width = vectors.shape[-1] // 2
-    first_half = vectors[..., :half_width]
-    second_half = vectors[..., half_width:]
-    return jnp.concatenate(
-        [
-            first_half * cosine_table - second_half * sine_table,
-            second_half * cosine_table + first_half * sine_table,
-        ],
-        axis=-1,
-    )
-
-
-def rotate_back(gradient, cosine_table, sine_table):
-    half_width = gradient.shape[-1] // 2
-    first_half = gradient[..., :half_width]
-    second_half = gradient[..., half_width:]
-    return jnp.concatenate(
-        [
-            first_half * cosine_table + second_half * sine_table,
-            second_half * cosine_table - first_half * sine_table,
-        ],
-        axis=-1,
-    )
+    cosine, sine = jnp.cos(angles), jnp.sin(angles)
+    return jnp.concatenate([cosine, cosine], axis=1), jnp.concatenate([-sine, sine], axis=1)
 
 
 def normalize(values, gain_row):
@@ -83,87 +58,6 @@
         moment / (1.0 - BETA_ONE**STEP) / (jnp.sqrt(second / (1.0 - BETA_TWO**STEP)) + ADAM_EPS)
     )
     return (parameter - step_rate * (direction + decay_rate * parameter), moment, second)
-
-
-def attention_forward(queries, keys_all, values_all, allowed):
-    group_size = H // KVH
-    score_scale = HD ** (-0.5)
-    outputs = []
-    totals = []
-    for head_group in range(KVH):
-        query_part = queries[:, head_group * group_size : (head_group + 1) * group_size, :]
-        scores = (
-            jnp.einsum(
-                "tjd,kd->jtk",
-                query_part,
-                keys_all[:, head_group, :],
-                preferred_element_type=jnp.float32,
-            )
-            * score_scale
-        )
-        scores = jnp.where(allowed[None], scores, MASKED)
-        row_max = jnp.max(scores, axis=-1, keepdims=True)
-        exponent = jnp.exp(scores - row_max)
-        row_total = jnp.sum(exponent, axis=-1, keepdims=True)
-        probabilities = (exponent / row_total).astype(jnp.bfloat16)
-        outputs.append(
-            jnp.einsum(
-                "jtk,kd->tjd",
-                probabilities,
-                values_all[:, head_group, :],
-                preferred_element_type=jnp.float32,
-            )
-        )
-        totals.append(row_max + jnp.log(row_total))
-    return (jnp.concatenate(outputs, axis=1), totals)
-
-
-def attention_backward(queries, keys_all, values_all, allowed, totals, grad_attended):
-    group_size = H // KVH
-    score_scale = HD ** (-0.5)
-    grad_queries = []
-    grad_keys = []
-    grad_values = []
-    for head_group in range(KVH):
-        query_part = queries[:, head_group * group_size : (head_group + 1) * group_size, :]
-        grad_part = grad_attended[:, head_group * group_size : (head_group + 1) * group_size, :]
-        keys_part = keys_all[:, head_group, :]
-        scores = (
-            jnp.einsum("tjd,kd->jtk", query_part, keys_part, preferred_element_type=jnp.float32)
-            * score_scale
-        )
-        probabilities = jnp.where(allowed[None], jnp.exp(scores - totals[head_group]), 0.0)
-        grad_probs = jnp.einsum(
-            "tjd,kd->jtk",
-            grad_part,
-            values_all[:, head_group, :],
-            preferred_element_type=jnp.float32,
-        )
-        grad_scores = probabilities * (
-            grad_probs - jnp.sum(probabilities * grad_probs, axis=-1, keepdims=True)
-        )
-        grad_scores = grad_scores.astype(jnp.bfloat16)
-        grad_queries.append(
-            jnp.einsum("jtk,kd->tjd", grad_scores, keys_part, preferred_element_type=jnp.float32)
-            * score_scale
-        )
-        grad_keys.append(
-            jnp.einsum("jtk,tjd->kd", grad_scores, query_part, preferred_element_type=jnp.float32)
-            * score_scale
-        )
-        grad_values.append(
-            jnp.einsum(
-                "jtk,tjd->kd",
-                probabilities.astype(jnp.bfloat16),
-                grad_part,
-                preferred_element_type=jnp.float32,
-            )
-        )
-    return (
-        jnp.concatenate(grad_queries, axis=1),
-        jnp.stack(grad_keys, axis=1),
-        jnp.stack(grad_values, axis=1),
-    )
 
 
 CTX = ("yo", "xi")
@@ -343,7 +237,7 @@
     )
 
 
-def gather_attention_steps(here, wires, shards, wholes):
+def gather_attention_steps(here, wires, shards, wholes, even):
     count = len(shards)
     far = [offset for offset in here.column if offset != (0, 0)]
     mine = here.chip() * 2 + here.core
@@ -389,13 +283,13 @@
             for y in here.y_steps:
                 source = wholes[part].at[block(y=y, z=z, w=w)]
                 wires.arrive(source, name(0, y, 0, z, w, part), other)
-                pass_on(source, y, 0, z, w, part, True, False)
+                pass_on(source, y, 0, z, w, part, not even or part % 2 == 0, False)
         yield
     for z, w in here.column:
         for part in range(count):
             source = wholes[part].at[block(x=1, z=z, w=w)]
             wires.arrive(source, name(0, 0, 1, z, w, part), other)
-            pass_on(source, 0, 1, z, w, part, False, False)
+            pass_on(source, 0, 1, z, w, part, False, even and part % 2 == 1)
         yield
     for z, w in here.column:
         for part in range(count):
@@ -507,7 +401,7 @@
     here = Place(sizes)
     cut = ATTENTION_PARTS
     wires = [Wires(*sems[:2])]
-    steps = [gather_attention_steps(here, wires[0], ins[:cut], outs[:cut])]
+    steps = [gather_attention_steps(here, wires[0], ins[:cut], outs[:cut], count == cut)]
     if count > cut:
         greet_layer(here)
         wires.append(Wires(*sems[2:]))
@@ -792,10 +686,10 @@
     core = lax.axis_index("core")
     parts = []
     for shard in (w_gateup[layer], w_down[layer]):
-        shard = shard.astype(jnp.bfloat16)
         shard = shard.reshape((4, 2) + shard.shape[1:])
-        theirs = swap(pick(shard, 1 - core, 1), "core")
-        parts.append(by_core(pick(shard, core, 1), theirs, 1).reshape(4, -1, D))
+        theirs = swap(pick(shard, 1 - core, 1).astype(jnp.bfloat16), "core").astype(jnp.float32)
+        pair = by_core(pick(shard, core, 1), theirs, 1).reshape(4, -1, D)
+        parts.append(pair.astype(jnp.bfloat16))
     return parts
 
 
@@ -818,8 +712,8 @@
     qkv, out, gain, up, down = sum_layer(attention, [grad_up, grad_down])
     result = [qkv, out]
     for part in (up, down):
-        part = part.reshape(4, 2, -1, D)
-        theirs = swap(pick(part, 1 - core, 1), "core")
+        part = part.astype(jnp.float32).reshape(4, 2, -1, D)
+        theirs = swap(pick(part, 1 - core, 1).astype(jnp.bfloat16), "core").astype(jnp.float32)
         pair = by_core(pick(part, core, 1), theirs, 1)
         result.append(pair.reshape(EXPERTS, -1, D))
     return result + [gain[:, :2].T]
@@ -1106,37 +1000,333 @@
     return total, grads[0], grads[1]
 
 
+def turned(vectors, cosine, sine):
+    return vectors * cosine + pltpu.roll(vectors, HD // 2, 1) * sine
+
+
+def project_kernel(stream, gain, weight, cosine, sine, normed, heads):
+    tile = pl.program_id(0)
+
+    @pl.when(tile == 0)
+    def _():
+        values = stream[...]
+        scale = lax.rsqrt(jnp.mean(values * values, axis=-1, keepdims=True) + NORM_EPS)
+        normed[...] = (values * scale * gain[...]).astype(jnp.bfloat16)
+
+    result = dot(normed[...], weight[...])
+    rotated = (H + KVH) // 2
+
+    @pl.when(tile < rotated)
+    def _():
+        for head in range(2):
+            lanes = slice(head * HD, (head + 1) * HD)
+            heads[:, lanes] = turned(result[:, lanes], cosine[...], sine[...]).astype(jnp.bfloat16)
+
+    @pl.when(tile >= rotated)
+    def _():
+        heads[...] = result.astype(jnp.bfloat16)
+
+
+def project(stream, gain, weight, cosine, sine):
+    rows, width = stream.shape[0], 2 * HD
+
+    def same(shape):
+        return pl.BlockSpec(shape, lambda tile: (0, 0))
+
+    return pl.pallas_call(
+        project_kernel,
+        grid=(QKV // width,),
+        in_specs=[
+            same((rows, D)),
+            same((1, D)),
+            pl.BlockSpec((D, width), lambda tile: (0, tile)),
+            same((rows, HD)),
+            same((rows, HD)),
+        ],
+        out_specs=[
+            same((rows, D)),
+            pl.BlockSpec((rows, width), lambda tile: (0, tile)),
+        ],
+        out_shape=[
+            jax.ShapeDtypeStruct((rows, D), jnp.bfloat16),
+            jax.ShapeDtypeStruct((rows, QKV), jnp.bfloat16),
+        ],
+        compiler_params=pltpu.CompilerParams(vmem_limit_bytes=60 * 1024 * 1024),
+        cost_estimate=pl.CostEstimate(
+            flops=2 * rows * D * QKV, bytes_accessed=12_000_000, transcendentals=rows
+        ),
+    )(stream, gain[None], weight, cosine, sine)
+
+
+def head_columns(rows, offset):
+    return pl.BlockSpec((rows, HD), lambda head: (0, offset + head // (H // KVH)))
+
+
+def attention_kernel(*refs):
+    query, allowed = refs[:2]
+    attended, total = refs[-3:-1]
+    scores = refs[-1]
+    count = (len(refs) - 5) // 2
+    keys, values = refs[2 : 2 + count], refs[2 + count : 2 + 2 * count]
+    rows = query.shape[0]
+    for index, key in enumerate(keys):
+        lanes = slice(index * rows, (index + 1) * rows)
+        part = dot(query[...], key[...], (1, 1)) * HD ** (-0.5)
+        scores[:, lanes] = jnp.where(allowed[:, lanes] > 0, part, MASKED)
+    row_max = jnp.max(scores[...], axis=-1, keepdims=True)
+    exponent = jnp.exp(scores[...] - row_max)
+    row_total = jnp.sum(exponent, axis=-1, keepdims=True)
+    probabilities = (exponent / row_total).astype(jnp.bfloat16)
+    result = None
+    for index, value in enumerate(values):
+        part = dot(probabilities[:, index * rows : (index + 1) * rows], value[...])
+        result = part if result is None else result + part
+    attended[...] = result.astype(jnp.bfloat16)
+    total[0] = jnp.broadcast_to(row_max + jnp.log(row_total), total.shape[1:])
+
+
+def attention_forward(heads, blocks, allowed):
+    rows, count = heads.shape[0], len(blocks)
+    one = pl.BlockSpec((rows, HD), lambda head: (0, head))
+    return pl.pallas_call(
+        attention_kernel,
+        grid=(H,),
+        in_specs=[one, pl.BlockSpec(allowed.shape, lambda head: (0, 0))]
+        + [head_columns(rows, 0)] * count
+        + [head_columns(rows, KVH)] * count,
+        out_specs=[one, pl.BlockSpec((1, rows, HD), lambda head: (head, 0, 0))],
+        out_shape=[
+            jax.ShapeDtypeStruct((rows, H * HD), jnp.bfloat16),
+            jax.ShapeDtypeStruct((H, rows, HD), jnp.float32),
+        ],
+        scratch_shapes=[pltpu.VMEM((rows, rows * count), jnp.float32)],
+        compiler_params=pltpu.CompilerParams(vmem_limit_bytes=60 * 1024 * 1024),
+        cost_estimate=pl.CostEstimate(
+            flops=4 * H * HD * rows * rows * count,
+            bytes_accessed=8_000_000,
+            transcendentals=H * rows * rows * count,
+        ),
+    )(heads, allowed, *blocks, *blocks)
+
+
+def attention_backward_kernel(*refs):
+    query, allowed, gradient, total, cosine, sine = refs[:6]
+    turned_back, blocks_out, probabilities, grads, key_sum, value_sum = refs[-6:]
+    count = (len(refs) - 12) // 2
+    keys, values = refs[6 : 6 + count], refs[6 + count : 6 + 2 * count]
+    rows = query.shape[0]
+    head, group = pl.program_id(0), H // KVH
+    scale = HD ** (-0.5)
+    inner = jnp.zeros((rows, 1), jnp.float32)
+    for index in range(count):
+        lanes = slice(index * rows, (index + 1) * rows)
+        part = dot(query[...], keys[index][...], (1, 1)) * scale
+        part = jnp.where(allowed[:, lanes] > 0, jnp.exp(part - total[0, :, :1]), 0.0)
+        slope = dot(gradient[...], values[index][...], (1, 1))
+        probabilities[:, lanes] = part
+        grads[:, lanes] = slope
+        inner = inner + jnp.sum(part * slope, axis=-1, keepdims=True)
+    back = None
+    for index in range(count):
+        lanes = slice(index * rows, (index + 1) * rows)
+        part = probabilities[:, lanes]
+        grad_scores = (part * (grads[:, lanes] - inner)).astype(jnp.bfloat16)
+        share = dot(grad_scores, keys[index][...])
+        back = share if back is None else back + share
+        key_part = dot(grad_scores, query[...], (0, 0)) * scale
+        value_part = dot(part.astype(jnp.bfloat16), gradient[...], (0, 0))
+
+        @pl.when(lax.rem(head, group) == 0)
+        def _(index=index, key_part=key_part, value_part=value_part):
+            key_sum[index] = key_part
+            value_sum[index] = value_part
+
+        @pl.when(lax.rem(head, group) > 0)
+        def _(index=index, key_part=key_part, value_part=value_part):
+            key_sum[index] += key_part
+            value_sum[index] += value_part
+
+    turned_back[...] = turned(back * scale, cosine[...], -sine[...]).astype(jnp.bfloat16)
+    for place in range(KVH):
+
+        @pl.when(head == (place + 1) * group - 1)
+        def _(place=place):
+            for index in range(count):
+                blocks_out[index, :, place * HD : (place + 1) * HD] = key_sum[index].astype(
+                    jnp.bfloat16
+                )
+                blocks_out[index, :, (KVH + place) * HD : (KVH + place + 1) * HD] = value_sum[
+                    index
+                ].astype(jnp.bfloat16)
+
+
+def attention_backward(heads, blocks, allowed, totals, gradient, cosine, sine):
+    rows, count = heads.shape[0], len(blocks)
+    one = pl.BlockSpec((rows, HD), lambda head: (0, head))
+    table = pl.BlockSpec((rows, HD), lambda head: (0, 0))
+    width = 2 * KVH * HD
+    return pl.pallas_call(
+        attention_backward_kernel,
+        grid=(H,),
+        in_specs=[
+            one,
+            pl.BlockSpec(allowed.shape, lambda head: (0, 0)),
+            one,
+            pl.BlockSpec((1, rows, HD), lambda head: (head, 0, 0)),
+            table,
+            table,
+        ]
+        + [head_columns(rows, 0)] * count
+        + [head_columns(rows, KVH)] * count,
+        out_specs=[one, pl.BlockSpec((count, rows, width), lambda head: (0, 0, 0))],
+        out_shape=[
+            jax.ShapeDtypeStruct((rows, QKV), jnp.bfloat16),
+            jax.ShapeDtypeStruct((count, rows, width), jnp.bfloat16),
+        ],
+        scratch_shapes=[
+            pltpu.VMEM((rows, rows * count), jnp.float32),
+            pltpu.VMEM((rows, rows * count), jnp.float32),
+            pltpu.VMEM((count, rows, HD), jnp.float32),
+            pltpu.VMEM((count, rows, HD), jnp.float32),
+        ],
+        compiler_params=pltpu.CompilerParams(vmem_limit_bytes=60 * 1024 * 1024),
+        cost_estimate=pl.CostEstimate(
+            flops=10 * H * HD * rows * rows * count,
+            bytes_accessed=10_000_000,
+            transcendentals=H * rows * rows * count,
+        ),
+    )(heads, allowed, gradient, totals, cosine, sine, *blocks, *blocks)
+
+
+def finish_keys_kernel(*refs):
+    parts, (cosine, sine, unused, out) = refs[:-4], refs[-4:]
+    for place in range(2 * KVH):
+        lanes = slice(place * HD, (place + 1) * HD)
+        total = parts[0][:, lanes].astype(jnp.float32)
+        for part in parts[1:]:
+            total = total + part[:, lanes].astype(jnp.float32)
+        if place < KVH:
+            total = turned(total, cosine[...], -sine[...])
+        out[:, lanes] = total.astype(jnp.bfloat16)
+
+
+def finish_keys(parts, cosine, sine, projected):
+    rows, width = parts[0].shape
+    return pl.pallas_call(
+        finish_keys_kernel,
+        grid=(1,),
+        in_specs=[pl.BlockSpec((rows, width), lambda step: (0, 0))] * len(parts)
+        + [pl.BlockSpec((rows, HD), lambda step: (0, 0))] * 2
+        + [pl.BlockSpec(memory_space=pl.ANY)],
+        out_specs=pl.BlockSpec((rows, width), lambda step: (0, QKV // width - 1)),
+        out_shape=jax.ShapeDtypeStruct(projected.shape, projected.dtype),
+        input_output_aliases={len(parts) + 2: 0},
+        compiler_params=pltpu.CompilerParams(vmem_limit_bytes=60 * 1024 * 1024),
+        cost_estimate=pl.CostEstimate(flops=0, bytes_accessed=2_000_000, transcendentals=0),
+    )(*parts, cosine, sine, projected)
+
+
+def weight_grad_kernel(rows_in, grads, out):
+    out[...] = dot(rows_in[...], grads[...], (0, 0)).astype(jnp.bfloat16)
+
+
+def weight_grad(rows_in, grads):
+    rows, width = grads.shape
+    tile = D // 3
+    return pl.pallas_call(
+        weight_grad_kernel,
+        grid=(3,),
+        in_specs=[
+            pl.BlockSpec((rows, tile), lambda step: (0, step)),
+            pl.BlockSpec((rows, width), lambda step: (0, 0)),
+        ],
+        out_specs=pl.BlockSpec((tile, width), lambda step: (step, 0)),
+        out_shape=jax.ShapeDtypeStruct((D, width), jnp.bfloat16),
+        compiler_params=pltpu.CompilerParams(vmem_limit_bytes=60 * 1024 * 1024),
+        cost_estimate=pl.CostEstimate(
+            flops=2 * rows * D * width, bytes_accessed=2 * D * width, transcendentals=0
+        ),
+    )(rows_in, grads)
+
+
+def rotate_back(gradient, cosine_table, sine_table):
+    half_width = gradient.shape[-1] // 2
+    first_half = gradient[..., :half_width]
+    second_half = gradient[..., half_width:]
+    return jnp.concatenate(
+        [
+            first_half * cosine_table + second_half * sine_table,
+            second_half * cosine_table - first_half * sine_table,
+        ],
+        axis=-1,
+    )
+
+
+def plain_backward(queries, keys_all, values_all, allowed, totals, grad_attended):
+    group_size = H // KVH
+    score_scale = HD ** (-0.5)
+    grad_queries = []
+    grad_keys = []
+    grad_values = []
+    for head_group in range(KVH):
+        query_part = queries[:, head_group * group_size : (head_group + 1) * group_size, :]
+        grad_part = grad_attended[:, head_group * group_size : (head_group + 1) * group_size, :]
+        keys_part = keys_all[:, head_group, :]
+        scores = (
+            jnp.einsum("tjd,kd->jtk", query_part, keys_part, preferred_element_type=jnp.float32)
+            * score_scale
+        )
+        probabilities = jnp.where(allowed[None], jnp.exp(scores - totals[head_group]), 0.0)
+        grad_probs = jnp.einsum(
+            "tjd,kd->jtk",
+            grad_part,
+            values_all[:, head_group, :],
+            preferred_element_type=jnp.float32,
+        )
+        grad_scores = probabilities * (
+            grad_probs - jnp.sum(probabilities * grad_probs, axis=-1, keepdims=True)
+        )
+        grad_scores = grad_scores.astype(jnp.bfloat16)
+        grad_queries.append(
+            jnp.einsum("jtk,kd->tjd", grad_scores, keys_part, preferred_element_type=jnp.float32)
+            * score_scale
+        )
+        grad_keys.append(
+            jnp.einsum("jtk,tjd->kd", grad_scores, query_part, preferred_element_type=jnp.float32)
+            * score_scale
+        )
+        grad_values.append(
+            jnp.einsum(
+                "jtk,tjd->kd",
+                probabilities.astype(jnp.bfloat16),
+                grad_part,
+                preferred_element_type=jnp.float32,
+            )
+        )
+    return (
+        jnp.concatenate(grad_queries, axis=1),
+        jnp.stack(grad_keys, axis=1),
+        jnp.stack(grad_values, axis=1),
+    )
+
+
 def layer_forward(stream, attn_w, expert_w, ahead, tables, allowed, cosine_table, sine_table):
     qkv_w, out_w, gain_full = attn_w
-    row_count = stream.shape[0]
-    normed, scale_one = normalize(stream, gain_full[0])
-    attn_in = normed.astype(jnp.bfloat16)
-    projected = jnp.dot(attn_in, qkv_w, preferred_element_type=jnp.float32)
-    queries = rotate(
-        projected[:, : H * HD].reshape(row_count, H, HD), cosine_table, sine_table
-    ).astype(jnp.bfloat16)
-    keys_local = rotate(
-        projected[:, H * HD : (H + KVH) * HD].reshape(row_count, KVH, HD), cosine_table, sine_table
-    ).astype(jnp.bfloat16)
-    values_local = projected[:, (H + KVH) * HD :].reshape(row_count, KVH, HD).astype(jnp.bfloat16)
-    both = jnp.concatenate([keys_local, values_local], axis=1)
-    both_all = jnp.concatenate([send(both, CTX, offsets) for offsets in offsets_of(CTX)], axis=0)
-    keys_all, values_all = both_all[:, :KVH], both_all[:, KVH:]
-    attended, totals = attention_forward(queries, keys_all, values_all, allowed)
-    attended_low = attended.reshape(row_count, H * HD).astype(jnp.bfloat16)
-    middle_stream = stream + jnp.dot(attended_low, out_w, preferred_element_type=jnp.float32)
+    attn_in, heads = project(stream, gain_full[0], qkv_w, cosine_table, sine_table)
+    own = heads[:, H * HD :]
+    blocks = [send(own, CTX, offsets) for offsets in offsets_of(CTX)]
+    attended, totals = attention_forward(heads, blocks, allowed)
+    middle_stream = stream + jnp.dot(attended, out_w, preferred_element_type=jnp.float32)
     normed_two, scale_two = normalize(middle_stream, gain_full[1])
     expert_in = normed_two.astype(jnp.bfloat16)
     merged, kept, gathered = moe_forward(expert_in, tables, expert_w, ahead)
     record = {
         "stream": stream,
-        "scale_one": scale_one,
         "attn_in": attn_in,
-        "queries": queries,
-        "keys_all": keys_all,
-        "values_all": values_all,
+        "heads": heads,
+        "blocks": blocks,
         "totals": totals,
-        "attended": attended_low,
+        "attended": attended,
         "middle": middle_stream,
         "scale_two": scale_two,
         "kept": kept,
@@ -1146,24 +1336,24 @@
 
 def layer_backward(gradient, record, attn_w, expert_w, tables, allowed, cosine_table, sine_table):
     qkv_w, out_w, gain_full = attn_w
-    row_count = gradient.shape[0]
     grad_normed, grad_up, grad_down = moe_backward(gradient, tables, expert_w, record["kept"])
-    grad_normed, grad_up, grad_down = lax.optimization_barrier((grad_normed, grad_up, grad_down))
     grad_in_two, grad_gain_two = normalize_back(
         grad_normed, record["middle"], record["scale_two"], gain_full[1]
     )
     grad_middle = gradient + grad_in_two
     grad_middle_low = grad_middle.astype(jnp.bfloat16)
-    grad_out = jnp.dot(record["attended"].T, grad_middle_low, preferred_element_type=jnp.float32)
+    grad_out = weight_grad(record["attended"], grad_middle_low)
     grad_attended = jnp.dot(grad_middle_low, out_w.T, preferred_element_type=jnp.float32)
-    grad_attended = grad_attended.astype(jnp.bfloat16).reshape(row_count, H, HD)
-    grad_queries, grad_keys_all, grad_values_all = attention_backward(
-        record["queries"],
-        record["keys_all"],
-        record["values_all"],
-        allowed,
-        record["totals"],
-        grad_attended,
+    keys_all = jnp.concatenate(record["blocks"], axis=0).reshape(-1, 2 * KVH, HD)
+    totals = record["totals"][:, :, :1].reshape(KVH, H // KVH, -1, 1)
+    row_count = gradient.shape[0]
+    grad_queries, grad_keys_all, grad_values_all = plain_backward(
+        record["heads"][:, : H * HD].reshape(-1, H, HD),
+        keys_all[:, :KVH],
+        keys_all[:, KVH:],
+        allowed > 0,
+        [totals[0], totals[1]],
+        grad_attended.astype(jnp.bfloat16).reshape(-1, H, HD),
     )
     both_all = jnp.concatenate([grad_keys_all, grad_values_all], axis=1)
     both = None
@@ -1173,18 +1363,20 @@
             part = send(part.astype(jnp.bfloat16), CTX, offsets, back=True).astype(jnp.float32)
         both = part if both is None else both + part
     grad_keys, grad_values = both[:, :KVH], both[:, KVH:]
+    ct, st = cosine_table[:, None, : HD // 2], sine_table[:, None, HD // 2 :]
     grad_projected = jnp.concatenate(
         [
-            rotate_back(grad_queries, cosine_table, sine_table).reshape(row_count, H * HD),
-            rotate_back(grad_keys, cosine_table, sine_table).reshape(row_count, KVH * HD),
+            rotate_back(grad_queries, ct, st).reshape(row_count, H * HD),
+            rotate_back(grad_keys, ct, st).reshape(row_count, KVH * HD),
             grad_values.reshape(row_count, KVH * HD),
         ],
         axis=1,
     ).astype(jnp.bfloat16)
-    grad_qkv = jnp.dot(record["attn_in"].T, grad_projected, preferred_element_type=jnp.float32)
+    grad_qkv = weight_grad(record["attn_in"], grad_projected)
     grad_normed_one = jnp.dot(grad_projected, qkv_w.T, preferred_element_type=jnp.float32)
+    unused, scale_one = normalize(record["stream"], gain_full[0])
     grad_in_one, grad_gain_one = normalize_back(
-        grad_normed_one, record["stream"], record["scale_one"], gain_full[0]
+        grad_normed_one, record["stream"], scale_one, gain_full[0]
     )
     grad_gains = jnp.stack([grad_gain_one, grad_gain_two])
     return (grad_middle + grad_in_one, (grad_qkv, grad_out, grad_up, grad_down, grad_gains))
@@ -1223,6 +1415,7 @@
     key_pos = jnp.concatenate([place[0] for place in places])
     key_doc = jnp.concatenate([place[1] for place in places])
     allowed = (own_doc[:, None] == key_doc[None, :]) & (key_pos[None, :] <= own_pos[:, None])
+    allowed = allowed.astype(jnp.float32)
     cosine_table, sine_table = rope_tables(own_pos)
     own_tables = jnp.stack(
         [dispatch_tables(routes[layer, 0], gate_weights[layer, 0]) for layer in range(LAYERS)]

time: 1280 us -> 1270 us (level); the launches traced: 1260 us -> 1260 us
  Pallas kernels: 938 us -> 994 us
  matrix products: 111 us -> 75.5 us
  waiting for transfers between devices: 22.2 us -> 6.38 us
    pallas_call x0 -> x8, Pallas kernels: none -> 65.6 us  [the longest x2 26.4 us: attention_forward(): pl.pallas_call(attention_kernel, grid=(H,), in_specs=[one, pl.BlockSpec(a...]
    dot_general x32 -> x22, matrix products: 89.2 us -> 55.8 us  [the longest x4 15.4 us: plain_backward(): jnp.einsum('tjd,kd->jtk', grad_part, values_all[:, head_group, :], prefer...]
    ppermute x15, waiting for transfers between devices: 22.2 us -> 6.36 us  [send(): return lax.ppermute(value, axes, shift_permutation(axes, offsets, back))]
    select_n x8 -> x4, other arithmetic: 16.3 us -> 0.59 us  [by_core(): jnp.where(core == 0, jnp.stack([mine, theirs], axis), jnp.stack([theirs,...]
  transfers between devices with their start and end apart: 23 -> 23, of which waited for: 8 -> 2; matrix products, arithmetic and copies ran while one was open for 9% -> 7% of each run, Pallas kernels for 29% -> 32%
where the time goes in v4:
time: 1270 us; the launch traced here: 1260 us
  Pallas kernels  994 us (78%)
  other arithmetic  96.7 us (8%)
  matrix products  75.5 us (6%)
  local copies, waits for them, and re-layouts  67 us (5%)
  starting transfers between devices  20.8 us (2%)
    pallas_call x4, Pallas kernels, moe_call(): pl.pallas_call(functools.partial(kernel, sizes, bool(background)), in_spe...  396 us
    pallas_call x2, Pallas kernels, sum_layer(): pl.pallas_call(functools.partial(sum_layer_kernel, sizes), out_shape=[jax...  292 us
    pallas_call x2, Pallas kernels, gather(): pl.pallas_call(functools.partial(gather_kernel, sizes, count), out_shape=...  209 us
    pallas_call x2, Pallas kernels, moe_backward(): pl.pallas_call(experts_grads_kernel, grid=(2, 3), in_specs=[columns_of(D...  31.2 us
    pallas_call x2, Pallas kernels, attention_forward(): pl.pallas_call(attention_kernel, grid=(H,), in_specs=[one, pl.BlockSpec(a...  26.4 us
  transfers between devices with their start and end apart: 23, of which 2 were waited for; matrix products, arithmetic and copies ran while one was open for 7% of the time, Pallas kernels for 32%

profile of v4, /device:TPU:0, one launch (start us, length us, event | category | flops | bytes accessed | tf_op | source)
XLA Modules:
  0.0 1263.1 jit_solution(14113823083585046899)
XLA Ops:
  0.7 3.7 fusion.142
  4.4 2.5 dynamic-slice_bitcast_fusion.3
  10.7 3.0 collective-permute-start.5
  32.2 68.1 %shard_map.332 = (bf16[32,48,2048]{2,1,0:T(8,128)(2,1)}, bf16[32,48,1536]{2,1,0:T(8,128)(2,1)}, bf16[32,48,128]{2,1,0:T(8,128)(2,1)}) custom-call(bf16[48,2048]{1,0:T(8,128)(2,1)} %get-tuple-element.216.refs_0_, bf16[48,1536]{1,0:T(8,128)(2,1)} %get-tuple-element.218.refs_1_, bf16[48,128]{1,0:T(8,128)(2,1)} %pad.14.refs_2_), custom_call_target="tpu_custom_call" | custom-call | tf_op jit(solution)/shard_map/pallas_call | solution.py:432
  102.5 1.9 slice_bitcast_fusion
  104.4 2.2 copy.545.refs_1_
  114.1 141.3 %shard_map.335 = (bf16[32,48,2048]{2,1,0:T(8,128)(2,1)}, bf16[32,48,1536]{2,1,0:T(8,128)(2,1)}, bf16[32,48,128]{2,1,0:T(8,128)(2,1)}, bf16[2,16,96,1536]{3,2,1,0:T(8,128)(2,1)}, bf16[2,16,48,1536]{3,2,1,0:T(8,128)(2,1)}) custom-call(bf16[48,2048]{1,0:T(8,128)(2,1)} %get-tuple-element.215.refs_0_, bf16[48,1536]{1,0:T(8,128)(2,1)} %get-tuple-element.217.refs_1_, ...), custom_call_target="tpu_custom_call" | custom-call | tf_op jit(solution)/shard_map/pallas_call | solution.py:432
  258.3 9.3 shard_map.333
  269.6 2.6 collective-permute-start.4
  277.8 5.7 collective-permute-done.4.refs_5_.refs_9_
  283.5 13.1 %shard_map.334 = (bf16[256,1536]{1,0:T(8,128)(2,1)}, f32[12,256,128]{2,1,0:T(8,128)}) custom-call(bf16[256,2048]{1,0:T(8,128)(2,1)} %get-tuple-element.77.refs_0_, f32[256,1024]{1,0:T(8,128)} %get-tuple-element.230.refs_1_, bf16[256,512]{1,0:T(8,128)(2,1)} %copy-done.76, bf16[256,512]{1,0:T(8,128)(2,1)} %copy-done.87, bf16[256,512]{1,0:T(8,128)(2,1)} %copy-done.89, ...), custom_call_target="tpu_custom_call" | custom-call | flops 1610612736 | bytes 8000000 | tf_op jit(solution)/shard_map/pallas_call | solution.py:1091
  296.6 4.1 multiply_reduce_fusion.11
  301.8 150.6 %shard_map.336 = (f32[256,1536]{1,0:T(8,128)}, bf16[2,640,1536]{2,1,0:T(8,128)(2,1)}, bf16[2,640,768]{2,1,0:T(8,128)(2,1)}, bf16[2,640,768]{2,1,0:T(8,128)(2,1)}...) custom-call(bf16[256,1536]{1,0:T(8,128)(2,1)} %multiply_convert_fusion.1.refs_0_, ...), custom_call_target="tpu_custom_call" | custom-call | flops 9059696640 | bytes 40000000 | tf_op jit(solution)/shard_map/pallas_call | solution.py:926
  452.5 2.7 multiply_reduce_fusion.8
  455.2 9.2 shard_map.337
  465.4 1.7 collective-permute-start.10
  469.0 2.0 pad_maximum_fusion.7
  472.3 2.4 fusion.145
  474.8 3.6 fusion.93
  478.3 3.6 fusion.87
  484.8 13.3 %shard_map.338 = (bf16[256,1536]{1,0:T(8,128)(2,1)}, f32[12,256,128]{2,1,0:T(8,128)}) custom-call(bf16[256,2048]{1,0:T(8,128)(2,1)} %get-tuple-element.87.refs_0_, f32[256,1024]{1,0:T(8,128)} %get-tuple-element.230.refs_1_, bf16[256,512]{1,0:T(8,128)(2,1)} %copy-done.74, bf16[256,512]{1,0:T(8,128)(2,1)} %collective-permute-done.10.refs_3_.refs_7_, ...), custom_call_target="tpu_custom_call" | custom-call | flops 1610612736 | bytes 8000000 | tf_op jit(solution)/shard_map/pallas_call | solution.py:1091
  498.1 5.1 multiply_reduce_fusion.10
  503.2 2.5 multiply_convert_fusion.refs_0_
  505.7 81.6 %shard_map.339 = (f32[256,1536]{1,0:T(8,128)}, bf16[2,640,1536]{2,1,0:T(8,128)(2,1)}, bf16[2,640,768]{2,1,0:T(8,128)(2,1)}, bf16[2,640,768]{2,1,0:T(8,128)(2,1)}, bf16[2,640,768]{2,1,0:T(8,128)(2,1)}) custom-call(bf16[256,1536]{1,0:T(8,128)(2,1)} %multiply_convert_fusion.refs_0_, f32[4,2,2,256]{3,2,1,0:T(2,128)} %copy.547.refs_1_, ...), custom_call_target="tpu_custom_call" | custom-call | flops 9059696640 | bytes 40000000 | tf_op jit(solution)/shard_map/pallas_call | solution.py:926
  587.3 82.1 %shard_map.340 = (f32[256,1536]{1,0:T(8,128)}, bf16[2,640,1536]{2,1,0:T(8,128)(2,1)}, bf16[2,640,768]{2,1,0:T(8,128)(2,1)}, bf16[2,640,768]{2,1,0:T(8,128)(2,1)}) custom-call(f32[256,1536]{1,0:T(8,128)} %bitcast_convert_fusion.3.refs_0_, f32[4,2,2,256]{3,2,1,0:T(2,128)} %copy.547.refs_1_, f32[4,2,256,2]{3,2,1,0:T(8,128)} %get-tuple-element.179.refs_2_, ...), custom_call_target="tpu_custom_call" | custom-call | flops 9059696640 | bytes 40000000 | tf_op jit(solution)/shard_map/pallas_call | solution.py:926
  669.5 3.1 multiply_reduce_fusion
  672.6 1.9 fusion.132.grads
  675.4 3.8 convolution_convert_fusion.1
  680.4 2.1 pad_maximum_fusion.5
  683.9 1.6 fusion.147
  689.1 5.2 fusion.15
  694.2 7.4 fusion.17
  701.7 2.8 fusion.43
  704.8 1.9 fusion.63
  707.5 1.9 fusion.61
  709.4 2.3 fusion.44
  711.7 2.3 fusion.47
  715.2 2.3 copy.578
  717.5 1.9 fusion.131
  724.4 15.6 %shard_map.348 = (bf16[2,1536,1536]{2,1,0:T(8,128)(2,1)}, bf16[2,768,1536]{2,1,0:T(8,128)(2,1)}) custom-call(bf16[2,640,1536]{2,1,0:T(8,128)(2,1)} %get-tuple-element.111.slot_in, bf16[2,640,768]{2,1,0:T(8,128)(2,1)S(1)} %copy-done.5, bf16[2,640,1536]{2,1,0:T(8,128)(2,1)} %get-tuple-element.113.slot_grad, bf16[2,640,768]{2,1,0:T(8,128)(2,1)S(1)} %copy-done.2, ...), custom_call_target="tpu_custom_call" | custom-call | flops 9059696640 | bytes 30000000 | tf_op jit(solution)/shard_map/pallas_call | solution.py:977
  740.0 4.9 shard_map.347
  746.9 5.8 multiply_reduce_fusion.1
  752.8 3.7 multiply_add_fusion.3
  756.5 81.5 %shard_map.341 = (f32[256,1536]{1,0:T(8,128)}, bf16[2,640,1536]{2,1,0:T(8,128)(2,1)}, bf16[2,640,768]{2,1,0:T(8,128)(2,1)}, bf16[2,640,768]{2,1,0:T(8,128)(2,1)}) custom-call(f32[256,1536]{1,0:T(8,128)} %get-tuple-element.187.refs_0_, f32[4,2,2,256]{3,2,1,0:T(2,128)} %copy.545.refs_1_, f32[4,2,256,2]{3,2,1,0:T(8,128)} %get-tuple-element.180.refs_2_, ...), custom_call_target="tpu_custom_call" | custom-call | flops 9059696640 | bytes 40000000 | tf_op jit(solution)/shard_map/pallas_call | solution.py:926
  838.1 2.6 multiply_reduce_fusion.2
  840.7 1.6 fusion.141
  843.2 3.8 convolution_convert_fusion
  848.4 8.3 fusion.5
  858.9 7.3 fusion.7
  866.2 3.5 fusion.41
  879.1 4.8 shard_map.343
  886.2 5.4 shard_map.346
  891.6 145.9 %shard_map.349 = (bf16[48,2048]{1,0:T(8,128)(2,1)}, bf16[48,1536]{1,0:T(8,128)(2,1)}, bf16[48,128]{1,0:T(8,128)(2,1)}, bf16[4,96,1536]{2,1,0:T(8,128)(2,1)}, bf16[4,48,1536]{2,1,0:T(8,128)(2,1)}) custom-call(bf16[16,2,48,2048]{3,2,1,0:T(8,128)(2,1)} %bitcast.458, bf16[16,2,48,1536]{3,2,1,0:T(8,128)(2,1)} %bitcast.460, bf16[16,2,48,128]{3,2,1,0:T(8,128)(2,1)} %bitcast.505, ...), custom_call_target="tpu_custom_call" | custom-call | tf_op jit(solution)/shard_map/pallas_call | solution.py:632
  1041.7 2.3 copy.604
  1049.6 1.7 convert.123
  1052.7 15.6 %shard_map.344 = (bf16[2,1536,1536]{2,1,0:T(8,128)(2,1)}, bf16[2,768,1536]{2,1,0:T(8,128)(2,1)}) custom-call(bf16[2,640,1536]{2,1,0:T(8,128)(2,1)} %get-tuple-element.102.slot_in, bf16[2,640,768]{2,1,0:T(8,128)(2,1)S(1)} %copy-done.4, bf16[2,640,1536]{2,1,0:T(8,128)(2,1)} %get-tuple-element.104.slot_grad, bf16[2,640,768]{2,1,0:T(8,128)(2,1)S(1)} %copy-done, ...), custom_call_target="tpu_custom_call" | custom-call | flops 9059696640 | bytes 30000000 | tf_op jit(solution)/shard_map/pallas_call | solution.py:977
  1071.4 6.0 multiply_reduce_fusion.3
  1078.5 5.5 shard_map.342
  1084.0 145.8 %shard_map.345 = (bf16[48,2048]{1,0:T(8,128)(2,1)}, bf16[48,1536]{1,0:T(8,128)(2,1)}, bf16[48,128]{1,0:T(8,128)(2,1)}, bf16[4,96,1536]{2,1,0:T(8,128)(2,1)}, bf16[4,48,1536]{2,1,0:T(8,128)(2,1)}) custom-call(bf16[16,2,48,2048]{3,2,1,0:T(8,128)(2,1)} %bitcast.459, bf16[16,2,48,1536]{3,2,1,0:T(8,128)(2,1)} %bitcast.461, bf16[16,2,48,128]{3,2,1,0:T(8,128)(2,1)} %bitcast.504, ...), custom_call_target="tpu_custom_call" | custom-call | tf_op jit(solution)/shard_map/pallas_call | solution.py:632
  1232.0 1.7 convert.121
  1235.1 1.6 add_bitcast_fusion
  1239.1 1.8 multiply_subtract_fusion.2
  1245.3 6.1 multiply_subtract_fusion.1
  1255.8 6.9 multiply_subtract_fusion
  (471 shorter events, 112.0 us)
Async XLA Ops:
  6.9 104.7 %collective-permute-start = (bf16[4,48,1536]{2,1,0:T(8,128)(2,1)}, bf16[4,48,1536]{2,1,0:T(8,128)(2,1)}, u32[]{:S(2)}, u32[]{:S(2)}) collective-permute-start(bf16[4,48,1536]{2,1,0:T(8,128)(2,1)} %get-tuple-element.192), channel_id=1, source_target_pairs={{0,1},{1,0},{2,3},{3,2},{4,5},{5,4},{6,7},{7,6},{8,9},{9,8},{10,11... | collective-permute-start | bytes 1769480 | tf_op jit(solution)/shard_map/ppermute | solution.py:658
  9.2 98.3 %collective-permute-start.1 = (bf16[4,24,1536]{2,1,0:T(8,128)(2,1)}, bf16[4,24,1536]{2,1,0:T(8,128)(2,1)}, u32[]{:S(2)}, u32[]{:S(2)}) collective-permute-start(bf16[4,24,1536]{2,1,0:T(8,128)(2,1)} %get-tuple-element.214), channel_id=1, source_target_pairs={{0,1},{1,0},{2,3},{3,2},{4,5},{5,4},{6,7},{7,6},{8,9},{9,8},{10,11... | collective-permute-start | bytes 884744 | tf_op jit(solution)/shard_map/ppermute | solution.py:658
  9.6 7.7 copy-start.14
  10.7 89.6 %collective-permute-start.5 = (f32[2,2,2,256]{2,3,1,0:T(8,128)}, f32[2,2,2,256]{2,3,1,0:T(8,128)}, u32[]{:S(2)}, u32[]{:S(2)}) collective-permute-start(f32[2,2,2,256]{2,3,1,0:T(8,128)} %reverse_select_fusion.2), channel_id=1, source_target_pairs={{0,2},{2,0},{8,10},{10,8},{1,3},{3,1},{9,11},{11,9},{4,6},{6,4},{1... | collective-permute-start | bytes 24584 | tf_op jit(solution)/shard_map/ppermute | solution.py:97
  14.8 86.1 %collective-permute-start.6 = (f32[2,2,2,256]{2,3,1,0:T(8,128)}, f32[2,2,2,256]{2,3,1,0:T(8,128)}, u32[]{:S(2)}, u32[]{:S(2)}) collective-permute-start(f32[2,2,2,256]{2,3,1,0:T(8,128)} %reverse_select_fusion.1), channel_id=1, source_target_pairs={{0,8},{2,10},{8,0},{10,2},{1,9},{3,11},{9,1},{11,3},{4,12},{6,14},... | collective-permute-start | bytes 24584 | tf_op jit(solution)/shard_map/ppermute | solution.py:97
  17.3 83.6 %collective-permute-start.7 = (f32[2,2,2,256]{2,3,1,0:T(8,128)}, f32[2,2,2,256]{2,3,1,0:T(8,128)}, u32[]{:S(2)}, u32[]{:S(2)}) collective-permute-start(f32[2,2,2,256]{2,3,1,0:T(8,128)} %reverse_select_fusion), channel_id=1, source_target_pairs={{0,10},{2,8},{8,2},{10,0},{1,11},{3,9},{9,3},{11,1},{4,14},{6,12},... | collective-permute-start | bytes 24584 | tf_op jit(solution)/shard_map/ppermute | solution.py:97
  25.5 75.5 %copy-start.47 = (f32[2,1,2,2,256]{3,4,2,1,0:T(8,128)S(1)}, f32[2,1,2,2,256]{3,4,2,1,0:T(8,128)}, u32[]{:S(2)}) copy-start(f32[2,1,2,2,256]{3,4,2,1,0:T(8,128)} %fusion.79) | copy-start | bytes 24580
  32.2 679.5 %copy-start.19 = (pred[256,1024]{0,1:T(8,128)(4,1)}, pred[256,1024]{0,1:T(8,128)(4,1)S(1)}, u32[]{:S(2)}) copy-start(pred[256,1024]{0,1:T(8,128)(4,1)S(1)} %copy.550) | copy-start | bytes 786436
  100.3 173.1 %collective-permute-start.8 = (bf16[4,48,1536]{2,1,0:T(8,128)(2,1)}, bf16[4,48,1536]{2,1,0:T(8,128)(2,1)}, u32[]{:S(2)}, u32[]{:S(2)}) collective-permute-start(bf16[4,48,1536]{2,1,0:T(8,128)(2,1)} %get-tuple-element.190), channel_id=1, source_target_pairs={{0,1},{1,0},{2,3},{3,2},{4,5},{5,4},{6,7},{7,6},{8,9},{9,8},{10,11... | collective-permute-start | bytes 1769480 | tf_op jit(solution)/shard_map/ppermute | solution.py:658
  100.9 8.7 collective-permute-start.9
  113.0 143.4 %copy-start.86 = (bf16[32,48,128]{2,1,0:T(8,128)(2,1)S(1)}, bf16[32,48,128]{2,1,0:T(8,128)(2,1)}, u32[]{:S(2)}) copy-start(bf16[32,48,128]{2,1,0:T(8,128)(2,1)} %get-tuple-element.75) | copy-start | bytes 1179652
  267.6 5.8 copy-start.42
  268.7 7.3 copy-start.76
  268.7 9.2 collective-permute-start.2
  268.7 9.1 collective-permute-start.3
  269.6 13.9 %collective-permute-start.4 = (bf16[256,512]{1,0:T(8,128)(2,1)S(1)}, bf16[256,512]{1,0:T(8,128)(2,1)}, u32[]{:S(2)}, u32[]{:S(2)}) collective-permute-start(bf16[256,512]{1,0:T(8,128)(2,1)S(1)} %slice.253.refs_2_.refs_6_), channel_id=1, source_target_pairs={{0,24},{8,16},{16,8},{24,0},{1,25},{9,17},{17,9},{25,1},{2,26},{10... | collective-permute-start | bytes 786440 | tf_op jit(solution)/shard_map/ppermute | solution.py:97
  277.8 5.7 copy-start.87
  300.7 151.8 %copy-start.104 = (f32[256]{0:T(256)}, f32[256]{0:T(256)S(1)}, u32[]{:S(2)}) copy-start(f32[256]{0:T(256)S(1)} %add_rsqrt_fusion.3) | copy-start | bytes 3076
  455.2 13.8 %copy-start.77 = (bf16[256,512]{1,0:T(8,128)(2,1)S(1)}, bf16[256,512]{1,0:T(8,128)(2,1)}, u32[]{:S(2)}) copy-start(bf16[256,512]{1,0:T(8,128)(2,1)} %copy-done.76) | copy-start | bytes 786436
  455.2 13.8 %copy-start.88 = (bf16[256,512]{1,0:T(8,128)(2,1)S(1)}, bf16[256,512]{1,0:T(8,128)(2,1)}, u32[]{:S(2)}) copy-start(bf16[256,512]{1,0:T(8,128)(2,1)} %copy-done.87) | copy-start | bytes 786436
  455.2 13.8 %copy-start.90 = (bf16[256,512]{1,0:T(8,128)(2,1)S(1)}, bf16[256,512]{1,0:T(8,128)(2,1)}, u32[]{:S(2)}) copy-start(bf16[256,512]{1,0:T(8,128)(2,1)} %copy-done.89) | copy-start | bytes 786436
  465.4 9.3 copy-start.74
  465.4 19.3 %collective-permute-start.10 = (bf16[256,512]{1,0:T(8,128)(2,1)S(1)}, bf16[256,512]{1,0:T(8,128)(2,1)}, u32[]{:S(2)}, u32[]{:S(2)}) collective-permute-start(bf16[256,512]{1,0:T(8,128)(2,1)S(1)} %slice.267.refs_2_.refs_6_), channel_id=1, source_target_pairs={{0,8},{8,0},{16,24},{24,16},{1,9},{9,1},{17,25},{25,17},{2,10},{10... | collective-permute-start | bytes 786440 | tf_op jit(solution)/shard_map/ppermute | solution.py:97
  467.1 17.6 %collective-permute-start.11 = (bf16[256,512]{1,0:T(8,128)(2,1)S(1)}, bf16[256,512]{1,0:T(8,128)(2,1)}, u32[]{:S(2)}, u32[]{:S(2)}) collective-permute-start(bf16[256,512]{1,0:T(8,128)(2,1)S(1)} %slice.267.refs_2_.refs_6_), channel_id=1, source_target_pairs={{0,16},{8,24},{16,0},{24,8},{1,17},{9,25},{17,1},{25,9},{2,18},{10... | collective-permute-start | bytes 786440 | tf_op jit(solution)/shard_map/ppermute | solution.py:97
  468.1 16.6 %collective-permute-start.12 = (bf16[256,512]{1,0:T(8,128)(2,1)S(1)}, bf16[256,512]{1,0:T(8,128)(2,1)}, u32[]{:S(2)}, u32[]{:S(2)}) collective-permute-start(bf16[256,512]{1,0:T(8,128)(2,1)S(1)} %slice.267.refs_2_.refs_6_), channel_id=1, source_target_pairs={{0,24},{8,16},{16,8},{24,0},{1,25},{9,17},{17,9},{25,1},{2,26},{10... | collective-permute-start | bytes 786440 | tf_op jit(solution)/shard_map/ppermute | solution.py:97
  484.8 13.3 %copy-start.6 = (f32[256,1536]{1,0:T(8,128)S(1)}, f32[256,1536]{1,0:T(8,128)}, u32[]{:S(2)}) copy-start(f32[256,1536]{1,0:T(8,128)} %get-tuple-element.174.stream) | copy-start | bytes 4718596
  503.2 169.4 %copy-start.100 = (f32[256]{0:T(256)}, f32[256]{0:T(256)S(1)}, u32[]{:S(2)}) copy-start(f32[256]{0:T(256)S(1)} %add_rsqrt_fusion.2) | copy-start | bytes 3076
  714.2 10.2 copy-start.5
  717.4 6.3 copy-start.107
  717.4 6.9 copy-start.2
  717.5 6.9 copy-start.3
  720.3 24.8 %collective-permute-start.13 = (bf16[256,4,128]{0,2,1:T(8,128)(2,1)}, bf16[256,4,128]{0,2,1:T(8,128)(2,1)}, u32[]{:S(2)}, u32[]{:S(2)}) collective-permute-start(bf16[256,4,128]{0,2,1:T(8,128)(2,1)} %get-tuple-element.200), channel_id=1, source_target_pairs={{8,0},{0,8},{24,16},{16,24},{9,1},{1,9},{25,17},{17,25},{10,2},{2,... | collective-permute-start | bytes 786440 | tf_op jit(solution)/shard_map/ppermute | solution.py:97
  721.6 23.5 %collective-permute-start.14 = (bf16[256,4,128]{0,2,1:T(8,128)(2,1)}, bf16[256,4,128]{0,2,1:T(8,128)(2,1)}, u32[]{:S(2)}, u32[]{:S(2)}) collective-permute-start(bf16[256,4,128]{0,2,1:T(8,128)(2,1)} %get-tuple-element.202), channel_id=1, source_target_pairs={{16,0},{24,8},{0,16},{8,24},{17,1},{25,9},{1,17},{9,25},{18,2},{26... | collective-permute-start | bytes 786440 | tf_op jit(solution)/shard_map/ppermute | solution.py:97
  722.6 22.5 %collective-permute-start.15 = (bf16[256,4,128]{0,2,1:T(8,128)(2,1)}, bf16[256,4,128]{0,2,1:T(8,128)(2,1)}, u32[]{:S(2)}, u32[]{:S(2)}) collective-permute-start(bf16[256,4,128]{0,2,1:T(8,128)(2,1)} %get-tuple-element.201), channel_id=1, source_target_pairs={{24,0},{16,8},{8,16},{0,24},{25,1},{17,9},{9,17},{1,25},{26,2},{18... | collective-permute-start | bytes 786440 | tf_op jit(solution)/shard_map/ppermute | solution.py:97
  746.7 6.0 copy-start.82
  746.8 5.9 copy-start.84
  746.8 5.9 copy-start.9
  746.8 5.9 copy-start.18
  746.8 5.9 copy-start.66
  746.8 5.9 copy-start.99
  746.9 5.9 copy-start.101
  746.9 5.9 copy-start.112
  746.9 5.9 copy-start.118
  756.5 81.6 %copy-start.105 = (f32[256]{0:T(256)S(1)}, f32[256]{0:T(256)}, u32[]{:S(2)}) copy-start(f32[256]{0:T(256)} %copy-done.104) | copy-start | bytes 3076
  848.3 8.5 slice-start
  848.3 9.3 slice-start.2
  848.4 9.9 slice-start.1
  848.4 10.5 slice-start.3
  858.9 7.3 copy-start.55
  879.1 5.9 copy-start.119
  879.1 5.9 copy-start.102
  1040.5 12.2 copy-start.4
  1040.7 7.7 copy-start.106
  1040.8 8.2 copy-start.109
  1044.9 23.5 %collective-permute-start.16 = (bf16[256,4,128]{0,2,1:T(8,128)(2,1)}, bf16[256,4,128]{0,2,1:T(8,128)(2,1)}, u32[]{:S(2)}, u32[]{:S(2)}) collective-permute-start(bf16[256,4,128]{0,2,1:T(8,128)(2,1)} %get-tuple-element.193), channel_id=1, source_target_pairs={{8,0},{0,8},{24,16},{16,24},{9,1},{1,9},{25,17},{17,25},{10,2},{2,... | collective-permute-start | bytes 786440 | tf_op jit(solution)/shard_map/ppermute | solution.py:97
  1046.2 22.2 %collective-permute-start.17 = (bf16[256,4,128]{0,2,1:T(8,128)(2,1)}, bf16[256,4,128]{0,2,1:T(8,128)(2,1)}, u32[]{:S(2)}, u32[]{:S(2)}) collective-permute-start(bf16[256,4,128]{0,2,1:T(8,128)(2,1)} %get-tuple-element.195), channel_id=1, source_target_pairs={{16,0},{24,8},{0,16},{8,24},{17,1},{25,9},{1,17},{9,25},{18,2},{26... | collective-permute-start | bytes 786440 | tf_op jit(solution)/shard_map/ppermute | solution.py:97
  1047.2 21.2 %collective-permute-start.18 = (bf16[256,4,128]{0,2,1:T(8,128)(2,1)}, bf16[256,4,128]{0,2,1:T(8,128)(2,1)}, u32[]{:S(2)}, u32[]{:S(2)}) collective-permute-start(bf16[256,4,128]{0,2,1:T(8,128)(2,1)} %get-tuple-element.194), channel_id=1, source_target_pairs={{24,0},{16,8},{8,16},{0,24},{25,1},{17,9},{9,17},{1,25},{26,2},{18... | collective-permute-start | bytes 786440 | tf_op jit(solution)/shard_map/ppermute | solution.py:97
  1049.6 192.0 %collective-permute-start.22 = (bf16[4,24,1536]{2,1,0:T(8,128)(2,1)}, bf16[4,24,1536]{2,1,0:T(8,128)(2,1)}, u32[]{:S(2)}, u32[]{:S(2)}) collective-permute-start(bf16[4,24,1536]{2,1,0:T(8,128)(2,1)} %fusion.108), channel_id=1, source_target_pairs={{0,1},{1,0},{2,3},{3,2},{4,5},{5,4},{6,7},{7,6},{8,9},{9,8},{10,11... | collective-permute-start | bytes 884744 | tf_op jit(solution)/shard_map/ppermute | solution.py:658
  1052.2 199.2 %collective-permute-start.20 = (bf16[4,48,1536]{2,1,0:T(8,128)(2,1)}, bf16[4,48,1536]{2,1,0:T(8,128)(2,1)}, u32[]{:S(2)}, u32[]{:S(2)}) collective-permute-start(bf16[4,48,1536]{2,1,0:T(8,128)(2,1)} %fusion.75), channel_id=1, source_target_pairs={{0,1},{1,0},{2,3},{3,2},{4,5},{5,4},{6,7},{7,6},{8,9},{9,8},{10,11... | collective-permute-start | bytes 1769480 | tf_op jit(solution)/shard_map/ppermute | solution.py:658
  1071.4 6.0 copy-start.103
  1231.9 10.9 collective-permute-start.21
  1234.5 18.5 %collective-permute-start.19 = (bf16[4,48,1536]{2,1,0:T(8,128)(2,1)}, bf16[4,48,1536]{2,1,0:T(8,128)(2,1)}, u32[]{:S(2)}, u32[]{:S(2)}) collective-permute-start(bf16[4,48,1536]{2,1,0:T(8,128)(2,1)} %fusion.78), channel_id=1, source_target_pairs={{0,1},{1,0},{2,3},{3,2},{4,5},{5,4},{6,7},{7,6},{8,9},{9,8},{10,11... | collective-permute-start | bytes 1769480 | tf_op jit(solution)/shard_map/ppermute | solution.py:658
  1245.3 9.5 slice-start.6
  1245.3 9.5 slice-start.8
  (93 other events, 242.5 us)

commit v5 on v4

--- a/solution.py
+++ b/solution.py
@@ -721,7 +721,7 @@
 
 SQRT_HALF = 0.7071067811865476
 PDF_SCALE = 0.3989422804014327
-TILE = 256
+TILE = 384
 TILES = F // TILE
 
 
@@ -741,20 +741,6 @@
         (((contract[0],), (contract[1],)), ((), ())),
         preferred_element_type=jnp.float32,
     )
-
-
-def experts_grads_kernel(slot_in, active, slot_grad, grad_gate, grad_up, up_out, down_out):
-    up_out[0, :, :F] = dot(slot_in[0], grad_gate[0], (0, 0)).astype(jnp.bfloat16)
-    up_out[0, :, F:] = dot(slot_in[0], grad_up[0], (0, 0)).astype(jnp.bfloat16)
-    down_out[0] = dot(active[0], slot_grad[0], (0, 0)).astype(jnp.bfloat16)
-
-
-def whole_block(shape):
-    return pl.BlockSpec(shape, lambda e, f: (0,) * len(shape))
-
-
-def expert_block(shape):
-    return pl.BlockSpec((1,) + shape, lambda e, f: (e,) + (0,) * len(shape))
 
 
 WAVES = ((0,), (3,), (1, 2))
@@ -846,12 +832,17 @@
         other_wires.drain()
 
 
-def moe_backward_kernel(sizes, background, *refs):
-    gradient, tables, columns, up_w, down_w, gate_in, up_in = refs[:7]
-    merged, slot_out, gate_out, up_out = refs[7:11]
-    chunks, leaving, coming, slot_grad, slots, total = refs[11:17]
+STAGES = 6
+
+
+def moe_backward_kernel(sizes, *refs):
+    gradient, tables, columns, up_w, down_w, slot_in, gate_in, up_in, active = refs[:9]
+    merged, up_grads, down_grads = refs[9:12]
+    chunks, leaving, coming, slot_grad, slots, total = refs[12:18]
+    slot_out, gate_out, up_out, up_stage, down_stage = refs[18:23]
     here = Place(sizes)
-    wires = Wires(*refs[17:])
+    wires = Wires(*refs[23:25])
+    stage_sems = refs[25]
     partners = [here.at(x=x, w=w) for x, w in offsets_of(GROUP)]
     greet(partners[1:])
     leaving[3] = gradient[...].astype(jnp.bfloat16)
@@ -909,6 +900,43 @@
                 wires.send(
                     leaving.at[place - 1], coming.at[place - 1], place + 2, partners[place]
                 )
+
+    def copies(index):
+        expert, tile, slot = lax.div(index, STAGES), lax.rem(index, STAGES), lax.rem(index, 2)
+        up_rows = pl.ds(pl.multiple_of(tile * (D // STAGES), D // STAGES), D // STAGES)
+        down_rows = pl.ds(pl.multiple_of(tile * (F // STAGES), F // STAGES), F // STAGES)
+        pair = (
+            pltpu.make_async_copy(
+                up_stage.at[slot], up_grads.at[expert, up_rows], stage_sems.at[slot, 0]
+            ),
+            pltpu.make_async_copy(
+                down_stage.at[slot], down_grads.at[expert, down_rows], stage_sems.at[slot, 1]
+            ),
+        )
+        return expert, slot, up_rows, down_rows, pair
+
+    def weight_step(index, carry):
+        expert, slot, up_rows, down_rows, pair = copies(index)
+
+        @pl.when(index >= 2)
+        def _():
+            for copy in copies(index - 2)[-1]:
+                copy.wait()
+
+        taken = slot_in[expert, :, up_rows]
+        up_stage[slot, :, :F] = dot(taken, gate_out[expert], (0, 0)).astype(jnp.bfloat16)
+        up_stage[slot, :, F:] = dot(taken, up_out[expert], (0, 0)).astype(jnp.bfloat16)
+        down_stage[slot] = dot(active[expert, :, down_rows], slot_out[expert], (0, 0)).astype(
+            jnp.bfloat16
+        )
+        for copy in pair:
+            copy.start()
+        return carry
+
+    lax.fori_loop(0, 2 * STAGES, weight_step, 0)
+    for index in range(2 * STAGES - 2, 2 * STAGES):
+        for copy in copies(index)[-1]:
+            copy.wait()
     for place in range(1, 4):
         wires.arrive(coming.at[place - 1], place + 2, partners[place])
         merged[...] += coming[place - 1].astype(jnp.float32)
@@ -965,39 +993,43 @@
 
 
 def moe_backward(gradient, tables, weights, kept):
-    slot_in, gate, up, active = kept
-    total, slot_grad, grad_gate, grad_up = moe_call(
-        moe_backward_kernel, 4, gradient, tables, weights, [gate, up], (D, F, F)
-    )
-    slots = slot_in.shape[1]
-
-    def columns_of(width):
-        return pl.BlockSpec((1, slots, width), lambda e, i: (e, 0, i))
-
-    grads = pl.pallas_call(
-        experts_grads_kernel,
-        grid=(2, 3),
-        in_specs=[
-            columns_of(D // 3),
-            columns_of(F // 3),
-            expert_block((slots, D)),
-            expert_block((slots, F)),
-            expert_block((slots, F)),
+    rows = gradient.shape[0]
+    slots = 4 * CAP
+    operands = [gradient, tables, jnp.swapaxes(tables, 2, 3), *weights, *kept]
+    in_vmem, anywhere = pl.BlockSpec(memory_space=pltpu.VMEM), pl.BlockSpec(memory_space=pl.ANY)
+    low = jnp.bfloat16
+    return pl.pallas_call(
+        functools.partial(moe_backward_kernel, mesh_sizes()),
+        in_specs=[in_vmem] * len(operands),
+        out_specs=[in_vmem, anywhere, anywhere],
+        out_shape=[
+            jax.ShapeDtypeStruct((rows, D), jnp.float32),
+            jax.ShapeDtypeStruct((2, D, 2 * F), low),
+            jax.ShapeDtypeStruct((2, F, D), low),
         ],
-        out_specs=[
-            pl.BlockSpec((1, D // 3, 2 * F), lambda e, i: (e, i, 0)),
-            pl.BlockSpec((1, F // 3, D), lambda e, i: (e, i, 0)),
+        scratch_shapes=[
+            pltpu.VMEM((3, rows, D), low),
+            pltpu.VMEM((4, rows, D), low),
+            pltpu.VMEM((3, rows, D), low),
+            pltpu.VMEM((2 * CAP, D), low),
+            pltpu.VMEM((2 * CAP, D), low),
+            pltpu.VMEM((2, rows, D), jnp.float32),
+            pltpu.VMEM((2, slots, D), low),
+            pltpu.VMEM((2, slots, F), low),
+            pltpu.VMEM((2, slots, F), low),
+            pltpu.VMEM((2, D // STAGES, 2 * F), low),
+            pltpu.VMEM((2, F // STAGES, D), low),
+            pltpu.SemaphoreType.DMA((6,)),
+            pltpu.SemaphoreType.DMA((6,)),
+            pltpu.SemaphoreType.DMA((2, 2)),
         ],
-        out_shape=[
-            jax.ShapeDtypeStruct((2, D, 2 * F), jnp.bfloat16),
-            jax.ShapeDtypeStruct((2, F, D), jnp.bfloat16),
-        ],
-        compiler_params=pltpu.CompilerParams(vmem_limit_bytes=48 * 1024 * 1024),
+        compiler_params=pltpu.CompilerParams(
+            collective_id=4, has_side_effects=True, vmem_limit_bytes=62 * 1024 * 1024
+        ),
         cost_estimate=pl.CostEstimate(
-            flops=12 * slots * D * F, bytes_accessed=30_000_000, transcendentals=0
+            flops=96 * CAP * D * F, bytes_accessed=40_000_000, transcendentals=8 * CAP * F
         ),
-    )(slot_in, active, slot_grad, grad_gate, grad_up)
-    return total, grads[0], grads[1]
+    )(*operands)
 
 
 def turned(vectors, cosine, sine):

time: 1270 us -> 1240 us (0.976)
  Pallas kernels: 994 us -> 961 us
  waiting for transfers between devices: 6.38 us -> 20 us
    pallas_call x4 -> x2, Pallas kernels: 396 us -> 231 us  [moe_call(): pl.pallas_call(functools.partial(kernel, sizes, bool(background)), in_spe...]
    pallas_call x2, Pallas kernels: 31.2 us -> 161 us  [moe_backward(): pl.pallas_call(functools.partial(moe_backward_kernel, mesh_sizes()), in_s...]
    ppermute x15, waiting for transfers between devices: 6.36 us -> 20 us  [send(): return lax.ppermute(value, axes, shift_permutation(axes, offsets, back))]
  transfers between devices with their start and end apart: 23 -> 23, of which waited for: 2 -> 5; matrix products, arithmetic and copies ran while one was open for 7% -> 7% of each run, Pallas kernels for 32% -> 30%
where the time goes in v5:
time: 1240 us; the launch traced here: 1230 us
  Pallas kernels  961 us (78%)
  other arithmetic  91.2 us (7%)
  matrix products  75.4 us (6%)
  local copies, waits for them, and re-layouts  64.1 us (5%)
  starting transfers between devices  20.8 us (2%)
  waiting for transfers between devices  20 us (2%)
    pallas_call x2, Pallas kernels, sum_layer(): pl.pallas_call(functools.partial(sum_layer_kernel, sizes), out_shape=[jax...  292 us
    pallas_call x2, Pallas kernels, moe_call(): pl.pallas_call(functools.partial(kernel, sizes, bool(background)), in_spe...  231 us
    pallas_call x2, Pallas kernels, gather(): pl.pallas_call(functools.partial(gather_kernel, sizes, count), out_shape=...  210 us
    pallas_call x2, Pallas kernels, moe_backward(): pl.pallas_call(functools.partial(moe_backward_kernel, mesh_sizes()), in_s...  161 us
    pallas_call x2, Pallas kernels, attention_forward(): pl.pallas_call(attention_kernel, grid=(H,), in_specs=[one, pl.BlockSpec(a...  26.4 us
  transfers between devices with their start and end apart: 23, of which 5 were waited for; matrix products, arithmetic and copies ran while one was open for 7% of the time, Pallas kernels for 30%

profile of v5, /device:TPU:0, one launch (start us, length us, event | category | flops | bytes accessed | tf_op | source)
XLA Modules:
  0.0 1234.9 jit_solution(6560086470333253019)
XLA Ops:
  0.7 3.7 fusion.142
  4.4 2.5 dynamic-slice_bitcast_fusion.3
  10.6 3.0 collective-permute-start.5
  30.9 68.7 %shard_map.332 = (bf16[32,48,2048]{2,1,0:T(8,128)(2,1)}, bf16[32,48,1536]{2,1,0:T(8,128)(2,1)}, bf16[32,48,128]{2,1,0:T(8,128)(2,1)}) custom-call(bf16[48,2048]{1,0:T(8,128)(2,1)} %get-tuple-element.204.refs_0_, bf16[48,1536]{1,0:T(8,128)(2,1)} %get-tuple-element.206.refs_1_, bf16[48,128]{1,0:T(8,128)(2,1)} %pad.14.refs_2_), custom_call_target="tpu_custom_call" | custom-call | tf_op jit(solution)/shard_map/pallas_call | solution.py:432
  100.3 1.5 pad_maximum_fusion.2
  101.9 1.8 slice_bitcast_fusion
  112.4 141.5 %shard_map.335 = (bf16[32,48,2048]{2,1,0:T(8,128)(2,1)}, bf16[32,48,1536]{2,1,0:T(8,128)(2,1)}, bf16[32,48,128]{2,1,0:T(8,128)(2,1)}, bf16[2,16,96,1536]{3,2,1,0:T(8,128)(2,1)}, bf16[2,16,48,1536]{3,2,1,0:T(8,128)(2,1)}) custom-call(bf16[48,2048]{1,0:T(8,128)(2,1)} %get-tuple-element.203.refs_0_, bf16[48,1536]{1,0:T(8,128)(2,1)} %get-tuple-element.205.refs_1_, ...), custom_call_target="tpu_custom_call" | custom-call | tf_op jit(solution)/shard_map/pallas_call | solution.py:432
  256.8 9.4 shard_map.333
  267.3 1.6 collective-permute-start.3
  268.9 1.9 collective-permute-start.4
  276.5 6.3 collective-permute-done.4.refs_5_.refs_9_
  282.8 13.1 %shard_map.334 = (bf16[256,1536]{1,0:T(8,128)(2,1)}, f32[12,256,128]{2,1,0:T(8,128)}) custom-call(bf16[256,2048]{1,0:T(8,128)(2,1)} %get-tuple-element.71.refs_0_, f32[256,1024]{1,0:T(8,128)} %get-tuple-element.218.refs_1_, bf16[256,512]{1,0:T(8,128)(2,1)} %copy-done.64, bf16[256,512]{1,0:T(8,128)(2,1)} %collective-permute-done.2.refs_3_.refs_7_, ...), custom_call_target="tpu_custom_call" | custom-call | flops 1610612736 | bytes 8000000 | tf_op jit(solution)/shard_map/pallas_call | solution.py:1123
  296.0 4.1 multiply_reduce_fusion.11
  301.1 149.7 %shard_map.336 = (f32[256,1536]{1,0:T(8,128)}, bf16[2,640,1536]{2,1,0:T(8,128)(2,1)}, bf16[2,640,768]{2,1,0:T(8,128)(2,1)}, bf16[2,640,768]{2,1,0:T(8,128)(2,1)}...) custom-call(bf16[256,1536]{1,0:T(8,128)(2,1)} %multiply_convert_fusion.1.refs_0_, ...), custom_call_target="tpu_custom_call" | custom-call | flops 9059696640 | bytes 40000000 | tf_op jit(solution)/shard_map/pallas_call | solution.py:954
  450.8 2.7 multiply_reduce_fusion.8
  453.6 9.2 shard_map.337
  463.8 2.0 collective-permute-start.10
  467.4 2.1 pad_maximum_fusion.7
  470.9 2.3 fusion.145
  473.2 3.7 fusion.93
  476.9 3.6 fusion.87
  483.5 13.3 %shard_map.338 = (bf16[256,1536]{1,0:T(8,128)(2,1)}, f32[12,256,128]{2,1,0:T(8,128)}) custom-call(bf16[256,2048]{1,0:T(8,128)(2,1)} %get-tuple-element.81.refs_0_, f32[256,1024]{1,0:T(8,128)} %get-tuple-element.218.refs_1_, bf16[256,512]{1,0:T(8,128)(2,1)} %copy-done.62, bf16[256,512]{1,0:T(8,128)(2,1)} %collective-permute-done.10.refs_3_.refs_7_, ...), custom_call_target="tpu_custom_call" | custom-call | flops 1610612736 | bytes 8000000 | tf_op jit(solution)/shard_map/pallas_call | solution.py:1123
  496.7 4.1 multiply_reduce_fusion.10
  503.0 81.7 %shard_map.339 = (f32[256,1536]{1,0:T(8,128)}, bf16[2,640,1536]{2,1,0:T(8,128)(2,1)}, bf16[2,640,768]{2,1,0:T(8,128)(2,1)}, bf16[2,640,768]{2,1,0:T(8,128)(2,1)}, bf16[2,640,768]{2,1,0:T(8,128)(2,1)}) custom-call(bf16[256,1536]{1,0:T(8,128)(2,1)} %multiply_convert_fusion.refs_0_, f32[4,2,2,256]{3,2,1,0:T(2,128)} %copy.547.refs_1_, ...), custom_call_target="tpu_custom_call" | custom-call | flops 9059696640 | bytes 40000000 | tf_op jit(solution)/shard_map/pallas_call | solution.py:954
  584.7 81.2 %shard_map.340 = (f32[256,1536]{1,0:T(8,128)}, bf16[2,1536,1536]{2,1,0:T(8,128)(2,1)}, bf16[2,768,1536]{2,1,0:T(8,128)(2,1)}) custom-call(f32[256,1536]{1,0:T(8,128)} %bitcast_convert_fusion.3.refs_0_, f32[4,2,2,256]{3,2,1,0:T(2,128)} %copy.547.refs_1_, f32[4,2,256,2]{3,2,1,0:T(8,128)} %get-tuple-element.167.refs_2_, bf16[2,1536,1536]{2,1,0:T(8,128)(2,1)} %bitcast.541, ...), custom_call_target="tpu_custom_call" | custom-call | flops 18119393280 | bytes 40000000 | tf_op jit(solution)/shard_map/pallas_call | solution.py:1001
  666.0 2.5 multiply_reduce_fusion
  668.8 1.6 fusion.132.grads
  671.3 3.8 convolution_convert_fusion.1
  676.3 2.1 pad_maximum_fusion.5
  679.8 1.7 fusion.147
  685.2 5.3 fusion.15
  690.5 7.2 fusion.17
  697.7 2.8 fusion.43
  700.9 1.9 fusion.63
  703.5 1.9 fusion.61
  705.4 2.3 fusion.44
  707.7 2.3 fusion.47
  711.4 1.6 fusion.131
  715.6 1.8 collective-permute-start.15
  718.1 4.8 shard_map.346
  724.1 5.1 collective-permute-done.14
  730.8 5.5 multiply_reduce_fusion.1
  736.5 2.3 multiply_add_fusion.3
  738.7 80.0 %shard_map.341 = (f32[256,1536]{1,0:T(8,128)}, bf16[2,1536,1536]{2,1,0:T(8,128)(2,1)}, bf16[2,768,1536]{2,1,0:T(8,128)(2,1)}) custom-call(f32[256,1536]{1,0:T(8,128)} %get-tuple-element.175.refs_0_, f32[4,2,2,256]{3,2,1,0:T(2,128)} %copy.545.refs_1_, f32[4,2,256,2]{3,2,1,0:T(8,128)} %get-tuple-element.168.refs_2_, bf16[2,1536,1536]{2,1,0:T(8,128)(2,1)} %bitcast.532, ...), custom_call_target="tpu_custom_call" | custom-call | flops 18119393280 | bytes 40000000 | tf_op jit(solution)/shard_map/pallas_call | solution.py:1001
  818.8 2.0 multiply_reduce_fusion.2
  821.1 1.6 fusion.141
  823.6 3.7 convolution_convert_fusion
  827.7 2.1 fusion.84
  829.8 8.3 fusion.5
  840.3 7.3 fusion.7
  847.6 3.5 fusion.41
  860.5 5.0 shard_map.343
  867.8 5.4 shard_map.345
  873.2 146.9 %shard_map.347 = (bf16[48,2048]{1,0:T(8,128)(2,1)}, bf16[48,1536]{1,0:T(8,128)(2,1)}, bf16[48,128]{1,0:T(8,128)(2,1)}, bf16[4,96,1536]{2,1,0:T(8,128)(2,1)}, bf16[4,48,1536]{2,1,0:T(8,128)(2,1)}) custom-call(bf16[16,2,48,2048]{3,2,1,0:T(8,128)(2,1)} %bitcast.458, bf16[16,2,48,1536]{3,2,1,0:T(8,128)(2,1)} %bitcast.460, bf16[16,2,48,128]{3,2,1,0:T(8,128)(2,1)} %bitcast.505, ...), custom_call_target="tpu_custom_call" | custom-call | tf_op jit(solution)/shard_map/pallas_call | solution.py:632
  1032.7 2.2 collective-permute-done.16
  1034.9 5.6 collective-permute-done.17
  1044.0 5.9 multiply_reduce_fusion.3
  1051.1 5.4 shard_map.342
  1056.5 145.1 %shard_map.344 = (bf16[48,2048]{1,0:T(8,128)(2,1)}, bf16[48,1536]{1,0:T(8,128)(2,1)}, bf16[48,128]{1,0:T(8,128)(2,1)}, bf16[4,96,1536]{2,1,0:T(8,128)(2,1)}, bf16[4,48,1536]{2,1,0:T(8,128)(2,1)}) custom-call(bf16[16,2,48,2048]{3,2,1,0:T(8,128)(2,1)} %bitcast.459, bf16[16,2,48,1536]{3,2,1,0:T(8,128)(2,1)} %bitcast.461, bf16[16,2,48,128]{3,2,1,0:T(8,128)(2,1)} %bitcast.504, ...), custom_call_target="tpu_custom_call" | custom-call | tf_op jit(solution)/shard_map/pallas_call | solution.py:632
  1203.9 1.7 convert.121
  1206.9 1.6 add_bitcast_fusion
  1210.9 1.8 multiply_subtract_fusion.2
  1217.1 6.1 multiply_subtract_fusion.1
  1227.6 6.9 multiply_subtract_fusion
  (437 shorter events, 112.3 us)
Async XLA Ops:
  6.9 102.9 %collective-permute-start = (bf16[4,48,1536]{2,1,0:T(8,128)(2,1)}, bf16[4,48,1536]{2,1,0:T(8,128)(2,1)}, u32[]{:S(2)}, u32[]{:S(2)}) collective-permute-start(bf16[4,48,1536]{2,1,0:T(8,128)(2,1)} %get-tuple-element.180), channel_id=1, source_target_pairs={{0,1},{1,0},{2,3},{3,2},{4,5},{5,4},{6,7},{7,6},{8,9},{9,8},{10,11... | collective-permute-start | bytes 1769480 | tf_op jit(solution)/shard_map/ppermute | solution.py:658
  9.1 96.4 %collective-permute-start.1 = (bf16[4,24,1536]{2,1,0:T(8,128)(2,1)}, bf16[4,24,1536]{2,1,0:T(8,128)(2,1)}, u32[]{:S(2)}, u32[]{:S(2)}) collective-permute-start(bf16[4,24,1536]{2,1,0:T(8,128)(2,1)} %get-tuple-element.202), channel_id=1, source_target_pairs={{0,1},{1,0},{2,3},{3,2},{4,5},{5,4},{6,7},{7,6},{8,9},{9,8},{10,11... | collective-permute-start | bytes 884744 | tf_op jit(solution)/shard_map/ppermute | solution.py:658
  9.6 7.7 copy-start.11
  10.6 89.0 %collective-permute-start.5 = (f32[2,2,2,256]{2,3,1,0:T(8,128)}, f32[2,2,2,256]{2,3,1,0:T(8,128)}, u32[]{:S(2)}, u32[]{:S(2)}) collective-permute-start(f32[2,2,2,256]{2,3,1,0:T(8,128)} %reverse_select_fusion.2), channel_id=1, source_target_pairs={{0,2},{2,0},{8,10},{10,8},{1,3},{3,1},{9,11},{11,9},{4,6},{6,4},{1... | collective-permute-start | bytes 24584 | tf_op jit(solution)/shard_map/ppermute | solution.py:97
  14.7 85.5 %collective-permute-start.6 = (f32[2,2,2,256]{2,3,1,0:T(8,128)}, f32[2,2,2,256]{2,3,1,0:T(8,128)}, u32[]{:S(2)}, u32[]{:S(2)}) collective-permute-start(f32[2,2,2,256]{2,3,1,0:T(8,128)} %reverse_select_fusion.1), channel_id=1, source_target_pairs={{0,8},{2,10},{8,0},{10,2},{1,9},{3,11},{9,1},{11,3},{4,12},{6,14},... | collective-permute-start | bytes 24584 | tf_op jit(solution)/shard_map/ppermute | solution.py:97
  17.3 83.0 %collective-permute-start.7 = (f32[2,2,2,256]{2,3,1,0:T(8,128)}, f32[2,2,2,256]{2,3,1,0:T(8,128)}, u32[]{:S(2)}, u32[]{:S(2)}) collective-permute-start(f32[2,2,2,256]{2,3,1,0:T(8,128)} %reverse_select_fusion), channel_id=1, source_target_pairs={{0,10},{2,8},{8,2},{10,0},{1,11},{3,9},{9,3},{11,1},{4,14},{6,12},... | collective-permute-start | bytes 24584 | tf_op jit(solution)/shard_map/ppermute | solution.py:97
  25.5 74.8 %copy-start.42 = (f32[2,1,2,2,256]{3,4,2,1,0:T(8,128)S(1)}, f32[2,1,2,2,256]{3,4,2,1,0:T(8,128)}, u32[]{:S(2)}) copy-start(f32[2,1,2,2,256]{3,4,2,1,0:T(8,128)} %fusion.79) | copy-start | bytes 24580
  29.1 994.1 %copy-start.53 = (f32[256,64]{0,1:T(8,128)}, f32[256,64]{0,1:T(8,128)S(1)}, u32[]{:S(2)}) copy-start(f32[256,64]{0,1:T(8,128)S(1)} %copy.565) | copy-start | bytes 196612
  99.6 172.3 %collective-permute-start.8 = (bf16[4,48,1536]{2,1,0:T(8,128)(2,1)}, bf16[4,48,1536]{2,1,0:T(8,128)(2,1)}, u32[]{:S(2)}, u32[]{:S(2)}) collective-permute-start(bf16[4,48,1536]{2,1,0:T(8,128)(2,1)} %get-tuple-element.178), channel_id=1, source_target_pairs={{0,1},{1,0},{2,3},{3,2},{4,5},{5,4},{6,7},{7,6},{8,9},{9,8},{10,11... | collective-permute-start | bytes 1769480 | tf_op jit(solution)/shard_map/ppermute | solution.py:658
  100.2 7.6 collective-permute-start.9
  111.3 143.7 %copy-start.74 = (bf16[32,48,128]{2,1,0:T(8,128)(2,1)S(1)}, bf16[32,48,128]{2,1,0:T(8,128)(2,1)}, u32[]{:S(2)}) copy-start(bf16[32,48,128]{2,1,0:T(8,128)(2,1)} %get-tuple-element.69) | copy-start | bytes 1179652
  256.8 43.2 %copy-start.83 = (f32[1536]{0:T(1024)}, f32[1536]{0:T(1024)S(1)}, u32[]{:S(2)}) copy-start(f32[1536]{0:T(1024)S(1)} %get-tuple-element.244) | copy-start | bytes 18436
  256.8 411.7 %copy-start.77 = (f32[1536]{0:T(1024)}, f32[1536]{0:T(1024)S(1)}, u32[]{:S(2)}) copy-start(f32[1536]{0:T(1024)S(1)} %get-tuple-element.134) | copy-start | bytes 18436
  266.2 5.8 copy-start.37
  267.2 7.3 copy-start.64
  267.2 9.3 collective-permute-start.2
  267.3 9.2 collective-permute-start.3
  268.9 13.9 %collective-permute-start.4 = (bf16[256,512]{1,0:T(8,128)(2,1)S(1)}, bf16[256,512]{1,0:T(8,128)(2,1)}, u32[]{:S(2)}, u32[]{:S(2)}) collective-permute-start(bf16[256,512]{1,0:T(8,128)(2,1)S(1)} %slice.253.refs_2_.refs_6_), channel_id=1, source_target_pairs={{0,24},{8,16},{16,8},{24,0},{1,25},{9,17},{17,9},{25,1},{2,26},{10... | collective-permute-start | bytes 786440 | tf_op jit(solution)/shard_map/ppermute | solution.py:97
  300.0 150.8 %copy-start.93 = (f32[256]{0:T(256)}, f32[256]{0:T(256)S(1)}, u32[]{:S(2)}) copy-start(f32[256]{0:T(256)S(1)} %add_rsqrt_fusion.3) | copy-start | bytes 3076
  453.6 13.8 %copy-start.65 = (bf16[256,512]{1,0:T(8,128)(2,1)S(1)}, bf16[256,512]{1,0:T(8,128)(2,1)}, u32[]{:S(2)}) copy-start(bf16[256,512]{1,0:T(8,128)(2,1)} %copy-done.64) | copy-start | bytes 786436
  463.8 9.4 copy-start.62
  463.8 19.7 %collective-permute-start.10 = (bf16[256,512]{1,0:T(8,128)(2,1)S(1)}, bf16[256,512]{1,0:T(8,128)(2,1)}, u32[]{:S(2)}, u32[]{:S(2)}) collective-permute-start(bf16[256,512]{1,0:T(8,128)(2,1)S(1)} %slice.267.refs_2_.refs_6_), channel_id=1, source_target_pairs={{0,8},{8,0},{16,24},{24,16},{1,9},{9,1},{17,25},{25,17},{2,10},{10... | collective-permute-start | bytes 786440 | tf_op jit(solution)/shard_map/ppermute | solution.py:97
  465.8 17.6 %collective-permute-start.11 = (bf16[256,512]{1,0:T(8,128)(2,1)S(1)}, bf16[256,512]{1,0:T(8,128)(2,1)}, u32[]{:S(2)}, u32[]{:S(2)}) collective-permute-start(bf16[256,512]{1,0:T(8,128)(2,1)S(1)} %slice.267.refs_2_.refs_6_), channel_id=1, source_target_pairs={{0,16},{8,24},{16,0},{24,8},{1,17},{9,25},{17,1},{25,9},{2,18},{10... | collective-permute-start | bytes 786440 | tf_op jit(solution)/shard_map/ppermute | solution.py:97
  465.9 17.5 %collective-permute-start.12 = (bf16[256,512]{1,0:T(8,128)(2,1)S(1)}, bf16[256,512]{1,0:T(8,128)(2,1)}, u32[]{:S(2)}, u32[]{:S(2)}) collective-permute-start(bf16[256,512]{1,0:T(8,128)(2,1)S(1)} %slice.267.refs_2_.refs_6_), channel_id=1, source_target_pairs={{0,24},{8,16},{16,8},{24,0},{1,25},{9,17},{17,9},{25,1},{2,26},{10... | collective-permute-start | bytes 786440 | tf_op jit(solution)/shard_map/ppermute | solution.py:97
  483.4 13.3 %copy-start.3 = (f32[256,1536]{1,0:T(8,128)S(1)}, f32[256,1536]{1,0:T(8,128)}, u32[]{:S(2)}) copy-start(f32[256,1536]{1,0:T(8,128)} %get-tuple-element.162.stream) | copy-start | bytes 4718596
  500.8 167.7 %copy-start.90 = (f32[256]{0:T(256)}, f32[256]{0:T(256)S(1)}, u32[]{:S(2)}) copy-start(f32[256]{0:T(256)S(1)} %add_rsqrt_fusion.2) | copy-start | bytes 3076
  714.0 10.1 collective-permute-start.13
  715.3 13.9 %collective-permute-start.14 = (bf16[256,4,128]{0,2,1:T(8,128)(2,1)}, bf16[256,4,128]{0,2,1:T(8,128)(2,1)}, u32[]{:S(2)}, u32[]{:S(2)}) collective-permute-start(bf16[256,4,128]{0,2,1:T(8,128)(2,1)} %get-tuple-element.190), channel_id=1, source_target_pairs={{16,0},{24,8},{0,16},{8,24},{17,1},{25,9},{1,17},{9,25},{18,2},{26... | collective-permute-start | bytes 786440 | tf_op jit(solution)/shard_map/ppermute | solution.py:97
  715.6 13.5 %collective-permute-start.15 = (bf16[256,4,128]{0,2,1:T(8,128)(2,1)}, bf16[256,4,128]{0,2,1:T(8,128)(2,1)}, u32[]{:S(2)}, u32[]{:S(2)}) collective-permute-start(bf16[256,4,128]{0,2,1:T(8,128)(2,1)} %get-tuple-element.189), channel_id=1, source_target_pairs={{24,0},{16,8},{8,16},{0,24},{25,1},{17,9},{9,17},{1,25},{26,2},{18... | collective-permute-start | bytes 786440 | tf_op jit(solution)/shard_map/ppermute | solution.py:97
  724.1 6.7 copy-start.25
  724.1 6.7 copy-start.89
  730.6 5.8 copy-start.70
  730.7 5.7 copy-start.72
  730.7 5.7 copy-start.2
  730.7 5.7 copy-start.4
  730.8 5.7 copy-start.6
  730.8 5.7 copy-start.14
  730.8 5.7 copy-start.55
  730.8 5.7 copy-start.78
  730.8 5.7 copy-start.91
  730.8 5.7 copy-start.103
  738.7 80.0 %copy-start.84 = (f32[1536]{0:T(1024)S(1)}, f32[1536]{0:T(1024)}, u32[]{:S(2)}) copy-start(f32[1536]{0:T(1024)} %copy-done.83) | copy-start | bytes 18436
  738.7 80.0 %copy-start.94 = (f32[256]{0:T(256)S(1)}, f32[256]{0:T(256)}, u32[]{:S(2)}) copy-start(f32[256]{0:T(256)} %copy-done.93) | copy-start | bytes 3076
  829.7 8.3 slice-start
  829.7 9.4 slice-start.2
  829.8 9.9 slice-start.1
  829.8 10.5 slice-start.3
  840.3 7.3 copy-start.49
  860.5 6.1 copy-start.92
  1023.4 5.6 copy-start.96
  1025.5 9.4 collective-permute-start.16
  1026.9 13.6 %collective-permute-start.17 = (bf16[256,4,128]{0,2,1:T(8,128)(2,1)}, bf16[256,4,128]{0,2,1:T(8,128)(2,1)S(1)}, u32[]{:S(2)}, u32[]{:S(2)}) collective-permute-start(bf16[256,4,128]{0,2,1:T(8,128)(2,1)} %get-tuple-element.183), channel_id=1, source_target_pairs={{16,0},{24,8},{0,16},{8,24},{17,1},{25,9},{1,17},{9,25},{18,2},{26... | collective-permute-start | bytes 786440 | tf_op jit(solution)/shard_map/ppermute | solution.py:97
  1027.6 13.6 %collective-permute-start.18 = (bf16[256,4,128]{0,2,1:T(8,128)(2,1)}, bf16[256,4,128]{0,2,1:T(8,128)(2,1)}, u32[]{:S(2)}, u32[]{:S(2)}) collective-permute-start(bf16[256,4,128]{0,2,1:T(8,128)(2,1)} %get-tuple-element.182), channel_id=1, source_target_pairs={{24,0},{16,8},{8,16},{0,24},{25,1},{17,9},{9,17},{1,25},{26,2},{18... | collective-permute-start | bytes 786440 | tf_op jit(solution)/shard_map/ppermute | solution.py:97
  1029.6 183.8 %collective-permute-start.22 = (bf16[4,24,1536]{2,1,0:T(8,128)(2,1)}, bf16[4,24,1536]{2,1,0:T(8,128)(2,1)}, u32[]{:S(2)}, u32[]{:S(2)}) collective-permute-start(bf16[4,24,1536]{2,1,0:T(8,128)(2,1)} %fusion.108), channel_id=1, source_target_pairs={{0,1},{1,0},{2,3},{3,2},{4,5},{5,4},{6,7},{7,6},{8,9},{9,8},{10,11... | collective-permute-start | bytes 884744 | tf_op jit(solution)/shard_map/ppermute | solution.py:658
  1032.1 10.5 copy-start.54
  1032.1 10.8 copy-start.27
  1032.1 191.2 %collective-permute-start.20 = (bf16[4,48,1536]{2,1,0:T(8,128)(2,1)}, bf16[4,48,1536]{2,1,0:T(8,128)(2,1)}, u32[]{:S(2)}, u32[]{:S(2)}) collective-permute-start(bf16[4,48,1536]{2,1,0:T(8,128)(2,1)} %fusion.75), channel_id=1, source_target_pairs={{0,1},{1,0},{2,3},{3,2},{4,5},{5,4},{6,7},{7,6},{8,9},{9,8},{10,11... | collective-permute-start | bytes 1769480 | tf_op jit(solution)/shard_map/ppermute | solution.py:658
  1032.7 11.3 copy-start.12
  1032.7 11.3 copy-start.87
  1034.9 5.6 copy-start.75
  1203.7 10.9 collective-permute-start.21
  1206.5 18.4 %collective-permute-start.19 = (bf16[4,48,1536]{2,1,0:T(8,128)(2,1)}, bf16[4,48,1536]{2,1,0:T(8,128)(2,1)}, u32[]{:S(2)}, u32[]{:S(2)}) collective-permute-start(bf16[4,48,1536]{2,1,0:T(8,128)(2,1)} %fusion.78), channel_id=1, source_target_pairs={{0,1},{1,0},{2,3},{3,2},{4,5},{5,4},{6,7},{7,6},{8,9},{9,8},{10,11... | collective-permute-start | bytes 1769480 | tf_op jit(solution)/shard_map/ppermute | solution.py:658
  1217.1 9.5 slice-start.6
  1217.1 9.5 slice-start.8
  (77 other events, 192.7 us)

commit v6 on v5

--- a/solution.py
+++ b/solution.py
@@ -1046,21 +1046,21 @@
         normed[...] = (values * scale * gain[...]).astype(jnp.bfloat16)
 
     result = dot(normed[...], weight[...])
-    rotated = (H + KVH) // 2
-
-    @pl.when(tile < rotated)
-    def _():
-        for head in range(2):
-            lanes = slice(head * HD, (head + 1) * HD)
+    heads_here = result.shape[1] // HD
+    for head in range(heads_here):
+        lanes = slice(head * HD, (head + 1) * HD)
+
+        @pl.when(tile * heads_here + head < H + KVH)
+        def _(lanes=lanes):
             heads[:, lanes] = turned(result[:, lanes], cosine[...], sine[...]).astype(jnp.bfloat16)
 
-    @pl.when(tile >= rotated)
-    def _():
-        heads[...] = result.astype(jnp.bfloat16)
+        @pl.when(tile * heads_here + head >= H + KVH)
+        def _(lanes=lanes):
+            heads[:, lanes] = result[:, lanes].astype(jnp.bfloat16)
 
 
 def project(stream, gain, weight, cosine, sine):
-    rows, width = stream.shape[0], 2 * HD
+    rows, width = stream.shape[0], 4 * HD
 
     def same(shape):
         return pl.BlockSpec(shape, lambda tile: (0, 0))
@@ -1108,7 +1108,7 @@
     row_max = jnp.max(scores[...], axis=-1, keepdims=True)
     exponent = jnp.exp(scores[...] - row_max)
     row_total = jnp.sum(exponent, axis=-1, keepdims=True)
-    probabilities = (exponent / row_total).astype(jnp.bfloat16)
+    probabilities = (exponent * (1.0 / row_total)).astype(jnp.bfloat16)
     result = None
     for index, value in enumerate(values):
         part = dot(probabilities[:, index * rows : (index + 1) * rows], value[...])
@@ -1139,123 +1139,6 @@
             transcendentals=H * rows * rows * count,
         ),
     )(heads, allowed, *blocks, *blocks)
-
-
-def attention_backward_kernel(*refs):
-    query, allowed, gradient, total, cosine, sine = refs[:6]
-    turned_back, blocks_out, probabilities, grads, key_sum, value_sum = refs[-6:]
-    count = (len(refs) - 12) // 2
-    keys, values = refs[6 : 6 + count], refs[6 + count : 6 + 2 * count]
-    rows = query.shape[0]
-    head, group = pl.program_id(0), H // KVH
-    scale = HD ** (-0.5)
-    inner = jnp.zeros((rows, 1), jnp.float32)
-    for index in range(count):
-        lanes = slice(index * rows, (index + 1) * rows)
-        part = dot(query[...], keys[index][...], (1, 1)) * scale
-        part = jnp.where(allowed[:, lanes] > 0, jnp.exp(part - total[0, :, :1]), 0.0)
-        slope = dot(gradient[...], values[index][...], (1, 1))
-        probabilities[:, lanes] = part
-        grads[:, lanes] = slope
-        inner = inner + jnp.sum(part * slope, axis=-1, keepdims=True)
-    back = None
-    for index in range(count):
-        lanes = slice(index * rows, (index + 1) * rows)
-        part = probabilities[:, lanes]
-        grad_scores = (part * (grads[:, lanes] - inner)).astype(jnp.bfloat16)
-        share = dot(grad_scores, keys[index][...])
-        back = share if back is None else back + share
-        key_part = dot(grad_scores, query[...], (0, 0)) * scale
-        value_part = dot(part.astype(jnp.bfloat16), gradient[...], (0, 0))
-
-        @pl.when(lax.rem(head, group) == 0)
-        def _(index=index, key_part=key_part, value_part=value_part):
-            key_sum[index] = key_part
-            value_sum[index] = value_part
-
-        @pl.when(lax.rem(head, group) > 0)
-        def _(index=index, key_part=key_part, value_part=value_part):
-            key_sum[index] += key_part
-            value_sum[index] += value_part
-
-    turned_back[...] = turned(back * scale, cosine[...], -sine[...]).astype(jnp.bfloat16)
-    for place in range(KVH):
-
-        @pl.when(head == (place + 1) * group - 1)
-        def _(place=place):
-            for index in range(count):
-                blocks_out[index, :, place * HD : (place + 1) * HD] = key_sum[index].astype(
-                    jnp.bfloat16
-                )
-                blocks_out[index, :, (KVH + place) * HD : (KVH + place + 1) * HD] = value_sum[
-                    index
-                ].astype(jnp.bfloat16)
-
-
-def attention_backward(heads, blocks, allowed, totals, gradient, cosine, sine):
-    rows, count = heads.shape[0], len(blocks)
-    one = pl.BlockSpec((rows, HD), lambda head: (0, head))
-    table = pl.BlockSpec((rows, HD), lambda head: (0, 0))
-    width = 2 * KVH * HD
-    return pl.pallas_call(
-        attention_backward_kernel,
-        grid=(H,),
-        in_specs=[
-            one,
-            pl.BlockSpec(allowed.shape, lambda head: (0, 0)),
-            one,
-            pl.BlockSpec((1, rows, HD), lambda head: (head, 0, 0)),
-            table,
-            table,
-        ]
-        + [head_columns(rows, 0)] * count
-        + [head_columns(rows, KVH)] * count,
-        out_specs=[one, pl.BlockSpec((count, rows, width), lambda head: (0, 0, 0))],
-        out_shape=[
-            jax.ShapeDtypeStruct((rows, QKV), jnp.bfloat16),
-            jax.ShapeDtypeStruct((count, rows, width), jnp.bfloat16),
-        ],
-        scratch_shapes=[
-            pltpu.VMEM((rows, rows * count), jnp.float32),
-            pltpu.VMEM((rows, rows * count), jnp.float32),
-            pltpu.VMEM((count, rows, HD), jnp.float32),
-            pltpu.VMEM((count, rows, HD), jnp.float32),
-        ],
-        compiler_params=pltpu.CompilerParams(vmem_limit_bytes=60 * 1024 * 1024),
-        cost_estimate=pl.CostEstimate(
-            flops=10 * H * HD * rows * rows * count,
-            bytes_accessed=10_000_000,
-            transcendentals=H * rows * rows * count,
-        ),
-    )(heads, allowed, gradient, totals, cosine, sine, *blocks, *blocks)
-
-
-def finish_keys_kernel(*refs):
-    parts, (cosine, sine, unused, out) = refs[:-4], refs[-4:]
-    for place in range(2 * KVH):
-        lanes = slice(place * HD, (place + 1) * HD)
-        total = parts[0][:, lanes].astype(jnp.float32)
-        for part in parts[1:]:
-            total = total + part[:, lanes].astype(jnp.float32)
-        if place < KVH:
-            total = turned(total, cosine[...], -sine[...])
-        out[:, lanes] = total.astype(jnp.bfloat16)
-
-
-def finish_keys(parts, cosine, sine, projected):
-    rows, width = parts[0].shape
-    return pl.pallas_call(
-        finish_keys_kernel,
-        grid=(1,),
-        in_specs=[pl.BlockSpec((rows, width), lambda step: (0, 0))] * len(parts)
-        + [pl.BlockSpec((rows, HD), lambda step: (0, 0))] * 2
-        + [pl.BlockSpec(memory_space=pl.ANY)],
-        out_specs=pl.BlockSpec((rows, width), lambda step: (0, QKV // width - 1)),
-        out_shape=jax.ShapeDtypeStruct(projected.shape, projected.dtype),
-        input_output_aliases={len(parts) + 2: 0},
-        compiler_params=pltpu.CompilerParams(vmem_limit_bytes=60 * 1024 * 1024),
-        cost_estimate=pl.CostEstimate(flops=0, bytes_accessed=2_000_000, transcendentals=0),
-    )(*parts, cosine, sine, projected)
 
 
 def weight_grad_kernel(rows_in, grads, out):

time: 1240 us -> 1240 us (level)
  no operation moved by 1% of the time
where the time goes in v6:
time: 1240 us; the launch traced here: 1230 us
  Pallas kernels  957 us (77%)
  other arithmetic  91.2 us (7%)
  matrix products  75.4 us (6%)
  local copies, waits for them, and re-layouts  64.1 us (5%)
  starting transfers between devices  20.8 us (2%)
  waiting for transfers between devices  20 us (2%)
    pallas_call x2, Pallas kernels, sum_layer(): pl.pallas_call(functools.partial(sum_layer_kernel, sizes), out_shape=[jax...  292 us
    pallas_call x2, Pallas kernels, moe_call(): pl.pallas_call(functools.partial(kernel, sizes, bool(background)), in_spe...  231 us
    pallas_call x2, Pallas kernels, gather(): pl.pallas_call(functools.partial(gather_kernel, sizes, count), out_shape=...  210 us
    pallas_call x2, Pallas kernels, moe_backward(): pl.pallas_call(functools.partial(moe_backward_kernel, mesh_sizes()), in_s...  161 us
    pallas_call x2, Pallas kernels, attention_forward(): pl.pallas_call(attention_kernel, grid=(H,), in_specs=[one, pl.BlockSpec(a...  26.4 us
  transfers between devices with their start and end apart: 23, of which 5 were waited for; matrix products, arithmetic and copies ran while one was open for 7% of the time, Pallas kernels for 30%

profile of v6, /device:TPU:0, one launch (start us, length us, event | category | flops | bytes accessed | tf_op | source)
XLA Modules:
  0.0 1231.6 jit_solution(10217634914042979747)
XLA Ops:
  0.7 3.7 fusion.142
  4.4 2.5 dynamic-slice_bitcast_fusion.3
  10.6 3.0 collective-permute-start.5
  30.9 68.7 %shard_map.332 = (bf16[32,48,2048]{2,1,0:T(8,128)(2,1)}, bf16[32,48,1536]{2,1,0:T(8,128)(2,1)}, bf16[32,48,128]{2,1,0:T(8,128)(2,1)}) custom-call(bf16[48,2048]{1,0:T(8,128)(2,1)} %get-tuple-element.204.refs_0_, bf16[48,1536]{1,0:T(8,128)(2,1)} %get-tuple-element.206.refs_1_, bf16[48,128]{1,0:T(8,128)(2,1)} %pad.14.refs_2_), custom_call_target="tpu_custom_call" | custom-call | tf_op jit(solution)/shard_map/pallas_call | solution.py:432
  100.3 1.5 pad_maximum_fusion.2
  101.9 1.8 slice_bitcast_fusion
  112.4 141.5 %shard_map.335 = (bf16[32,48,2048]{2,1,0:T(8,128)(2,1)}, bf16[32,48,1536]{2,1,0:T(8,128)(2,1)}, bf16[32,48,128]{2,1,0:T(8,128)(2,1)}, bf16[2,16,96,1536]{3,2,1,0:T(8,128)(2,1)}, bf16[2,16,48,1536]{3,2,1,0:T(8,128)(2,1)}) custom-call(bf16[48,2048]{1,0:T(8,128)(2,1)} %get-tuple-element.203.refs_0_, bf16[48,1536]{1,0:T(8,128)(2,1)} %get-tuple-element.205.refs_1_, ...), custom_call_target="tpu_custom_call" | custom-call | tf_op jit(solution)/shard_map/pallas_call | solution.py:432
  256.8 7.7 shard_map.333
  265.7 1.6 collective-permute-start.3
  267.3 1.9 collective-permute-start.4
  274.8 6.3 collective-permute-done.4.refs_5_.refs_9_
  281.1 13.1 %shard_map.334 = (bf16[256,1536]{1,0:T(8,128)(2,1)}, f32[12,256,128]{2,1,0:T(8,128)}) custom-call(bf16[256,2048]{1,0:T(8,128)(2,1)} %get-tuple-element.71.refs_0_, f32[256,1024]{1,0:T(8,128)} %get-tuple-element.218.refs_1_, bf16[256,512]{1,0:T(8,128)(2,1)} %copy-done.64, bf16[256,512]{1,0:T(8,128)(2,1)} %collective-permute-done.2.refs_3_.refs_7_, ...), custom_call_target="tpu_custom_call" | custom-call | flops 1610612736 | bytes 8000000 | tf_op jit(solution)/shard_map/pallas_call | solution.py:1123
  294.3 4.1 multiply_reduce_fusion.11
  299.5 149.7 %shard_map.336 = (f32[256,1536]{1,0:T(8,128)}, bf16[2,640,1536]{2,1,0:T(8,128)(2,1)}, bf16[2,640,768]{2,1,0:T(8,128)(2,1)}, bf16[2,640,768]{2,1,0:T(8,128)(2,1)}...) custom-call(bf16[256,1536]{1,0:T(8,128)(2,1)} %multiply_convert_fusion.1.refs_0_, ...), custom_call_target="tpu_custom_call" | custom-call | flops 9059696640 | bytes 40000000 | tf_op jit(solution)/shard_map/pallas_call | solution.py:954
  449.2 2.7 multiply_reduce_fusion.8
  451.9 7.6 shard_map.337
  460.4 2.1 collective-permute-start.10
  464.0 2.1 pad_maximum_fusion.7
  467.5 2.3 fusion.145
  469.9 3.7 fusion.93
  473.6 3.6 fusion.87
  480.1 13.3 %shard_map.338 = (bf16[256,1536]{1,0:T(8,128)(2,1)}, f32[12,256,128]{2,1,0:T(8,128)}) custom-call(bf16[256,2048]{1,0:T(8,128)(2,1)} %get-tuple-element.81.refs_0_, f32[256,1024]{1,0:T(8,128)} %get-tuple-element.218.refs_1_, bf16[256,512]{1,0:T(8,128)(2,1)} %copy-done.62, bf16[256,512]{1,0:T(8,128)(2,1)} %collective-permute-done.10.refs_3_.refs_7_, ...), custom_call_target="tpu_custom_call" | custom-call | flops 1610612736 | bytes 8000000 | tf_op jit(solution)/shard_map/pallas_call | solution.py:1123
  493.4 4.1 multiply_reduce_fusion.10
  499.7 81.7 %shard_map.339 = (f32[256,1536]{1,0:T(8,128)}, bf16[2,640,1536]{2,1,0:T(8,128)(2,1)}, bf16[2,640,768]{2,1,0:T(8,128)(2,1)}, bf16[2,640,768]{2,1,0:T(8,128)(2,1)}, bf16[2,640,768]{2,1,0:T(8,128)(2,1)}) custom-call(bf16[256,1536]{1,0:T(8,128)(2,1)} %multiply_convert_fusion.refs_0_, f32[4,2,2,256]{3,2,1,0:T(2,128)} %copy.547.refs_1_, ...), custom_call_target="tpu_custom_call" | custom-call | flops 9059696640 | bytes 40000000 | tf_op jit(solution)/shard_map/pallas_call | solution.py:954
  581.4 81.2 %shard_map.340 = (f32[256,1536]{1,0:T(8,128)}, bf16[2,1536,1536]{2,1,0:T(8,128)(2,1)}, bf16[2,768,1536]{2,1,0:T(8,128)(2,1)}) custom-call(f32[256,1536]{1,0:T(8,128)} %bitcast_convert_fusion.3.refs_0_, f32[4,2,2,256]{3,2,1,0:T(2,128)} %copy.547.refs_1_, f32[4,2,256,2]{3,2,1,0:T(8,128)} %get-tuple-element.167.refs_2_, bf16[2,1536,1536]{2,1,0:T(8,128)(2,1)} %bitcast.541, ...), custom_call_target="tpu_custom_call" | custom-call | flops 18119393280 | bytes 40000000 | tf_op jit(solution)/shard_map/pallas_call | solution.py:1001
  662.6 2.5 multiply_reduce_fusion
  665.4 1.6 fusion.132.grads
  668.0 3.8 convolution_convert_fusion.1
  673.0 2.1 pad_maximum_fusion.5
  676.5 1.7 fusion.147
  681.8 5.3 fusion.15
  687.1 7.2 fusion.17
  694.4 2.8 fusion.43
  697.5 1.9 fusion.63
  700.2 1.9 fusion.61
  702.1 2.3 fusion.44
  704.4 2.3 fusion.47
  708.1 1.6 fusion.131
  712.3 1.8 collective-permute-start.15
  714.7 4.8 shard_map.346
  720.8 5.1 collective-permute-done.14
  727.5 5.5 multiply_reduce_fusion.1
  733.1 2.3 multiply_add_fusion.3
  735.4 80.0 %shard_map.341 = (f32[256,1536]{1,0:T(8,128)}, bf16[2,1536,1536]{2,1,0:T(8,128)(2,1)}, bf16[2,768,1536]{2,1,0:T(8,128)(2,1)}) custom-call(f32[256,1536]{1,0:T(8,128)} %get-tuple-element.175.refs_0_, f32[4,2,2,256]{3,2,1,0:T(2,128)} %copy.545.refs_1_, f32[4,2,256,2]{3,2,1,0:T(8,128)} %get-tuple-element.168.refs_2_, bf16[2,1536,1536]{2,1,0:T(8,128)(2,1)} %bitcast.532, ...), custom_call_target="tpu_custom_call" | custom-call | flops 18119393280 | bytes 40000000 | tf_op jit(solution)/shard_map/pallas_call | solution.py:1001
  815.5 2.0 multiply_reduce_fusion.2
  817.8 1.6 fusion.141
  820.3 3.7 convolution_convert_fusion
  824.3 2.1 fusion.84
  826.5 8.3 fusion.5
  837.0 7.3 fusion.7
  844.3 3.5 fusion.41
  857.2 5.0 shard_map.343
  864.5 5.4 shard_map.345
  869.9 146.9 %shard_map.347 = (bf16[48,2048]{1,0:T(8,128)(2,1)}, bf16[48,1536]{1,0:T(8,128)(2,1)}, bf16[48,128]{1,0:T(8,128)(2,1)}, bf16[4,96,1536]{2,1,0:T(8,128)(2,1)}, bf16[4,48,1536]{2,1,0:T(8,128)(2,1)}) custom-call(bf16[16,2,48,2048]{3,2,1,0:T(8,128)(2,1)} %bitcast.458, bf16[16,2,48,1536]{3,2,1,0:T(8,128)(2,1)} %bitcast.460, bf16[16,2,48,128]{3,2,1,0:T(8,128)(2,1)} %bitcast.505, ...), custom_call_target="tpu_custom_call" | custom-call | tf_op jit(solution)/shard_map/pallas_call | solution.py:632
  1029.3 2.2 collective-permute-done.16
  1031.5 5.6 collective-permute-done.17
  1040.7 5.9 multiply_reduce_fusion.3
  1047.7 5.4 shard_map.342
  1053.2 145.1 %shard_map.344 = (bf16[48,2048]{1,0:T(8,128)(2,1)}, bf16[48,1536]{1,0:T(8,128)(2,1)}, bf16[48,128]{1,0:T(8,128)(2,1)}, bf16[4,96,1536]{2,1,0:T(8,128)(2,1)}, bf16[4,48,1536]{2,1,0:T(8,128)(2,1)}) custom-call(bf16[16,2,48,2048]{3,2,1,0:T(8,128)(2,1)} %bitcast.459, bf16[16,2,48,1536]{3,2,1,0:T(8,128)(2,1)} %bitcast.461, bf16[16,2,48,128]{3,2,1,0:T(8,128)(2,1)} %bitcast.504, ...), custom_call_target="tpu_custom_call" | custom-call | tf_op jit(solution)/shard_map/pallas_call | solution.py:632
  1200.5 1.7 convert.121
  1203.6 1.6 add_bitcast_fusion
  1207.6 1.8 multiply_subtract_fusion.2
  1213.8 6.1 multiply_subtract_fusion.1
  1224.3 6.9 multiply_subtract_fusion
  (437 shorter events, 112.3 us)
Async XLA Ops:
  6.9 102.9 %collective-permute-start = (bf16[4,48,1536]{2,1,0:T(8,128)(2,1)}, bf16[4,48,1536]{2,1,0:T(8,128)(2,1)}, u32[]{:S(2)}, u32[]{:S(2)}) collective-permute-start(bf16[4,48,1536]{2,1,0:T(8,128)(2,1)} %get-tuple-element.180), channel_id=1, source_target_pairs={{0,1},{1,0},{2,3},{3,2},{4,5},{5,4},{6,7},{7,6},{8,9},{9,8},{10,11... | collective-permute-start | bytes 1769480 | tf_op jit(solution)/shard_map/ppermute | solution.py:658
  9.1 96.4 %collective-permute-start.1 = (bf16[4,24,1536]{2,1,0:T(8,128)(2,1)}, bf16[4,24,1536]{2,1,0:T(8,128)(2,1)}, u32[]{:S(2)}, u32[]{:S(2)}) collective-permute-start(bf16[4,24,1536]{2,1,0:T(8,128)(2,1)} %get-tuple-element.202), channel_id=1, source_target_pairs={{0,1},{1,0},{2,3},{3,2},{4,5},{5,4},{6,7},{7,6},{8,9},{9,8},{10,11... | collective-permute-start | bytes 884744 | tf_op jit(solution)/shard_map/ppermute | solution.py:658
  9.6 7.7 copy-start.11
  10.6 89.0 %collective-permute-start.5 = (f32[2,2,2,256]{2,3,1,0:T(8,128)}, f32[2,2,2,256]{2,3,1,0:T(8,128)}, u32[]{:S(2)}, u32[]{:S(2)}) collective-permute-start(f32[2,2,2,256]{2,3,1,0:T(8,128)} %reverse_select_fusion.2), channel_id=1, source_target_pairs={{0,2},{2,0},{8,10},{10,8},{1,3},{3,1},{9,11},{11,9},{4,6},{6,4},{1... | collective-permute-start | bytes 24584 | tf_op jit(solution)/shard_map/ppermute | solution.py:97
  14.7 85.5 %collective-permute-start.6 = (f32[2,2,2,256]{2,3,1,0:T(8,128)}, f32[2,2,2,256]{2,3,1,0:T(8,128)}, u32[]{:S(2)}, u32[]{:S(2)}) collective-permute-start(f32[2,2,2,256]{2,3,1,0:T(8,128)} %reverse_select_fusion.1), channel_id=1, source_target_pairs={{0,8},{2,10},{8,0},{10,2},{1,9},{3,11},{9,1},{11,3},{4,12},{6,14},... | collective-permute-start | bytes 24584 | tf_op jit(solution)/shard_map/ppermute | solution.py:97
  17.3 83.0 %collective-permute-start.7 = (f32[2,2,2,256]{2,3,1,0:T(8,128)}, f32[2,2,2,256]{2,3,1,0:T(8,128)}, u32[]{:S(2)}, u32[]{:S(2)}) collective-permute-start(f32[2,2,2,256]{2,3,1,0:T(8,128)} %reverse_select_fusion), channel_id=1, source_target_pairs={{0,10},{2,8},{8,2},{10,0},{1,11},{3,9},{9,3},{11,1},{4,14},{6,12},... | collective-permute-start | bytes 24584 | tf_op jit(solution)/shard_map/ppermute | solution.py:97
  25.5 74.8 %copy-start.42 = (f32[2,1,2,2,256]{3,4,2,1,0:T(8,128)S(1)}, f32[2,1,2,2,256]{3,4,2,1,0:T(8,128)}, u32[]{:S(2)}) copy-start(f32[2,1,2,2,256]{3,4,2,1,0:T(8,128)} %fusion.79) | copy-start | bytes 24580
  29.1 990.7 %copy-start.53 = (f32[256,64]{0,1:T(8,128)}, f32[256,64]{0,1:T(8,128)S(1)}, u32[]{:S(2)}) copy-start(f32[256,64]{0,1:T(8,128)S(1)} %copy.565) | copy-start | bytes 196612
  99.6 170.7 %collective-permute-start.8 = (bf16[4,48,1536]{2,1,0:T(8,128)(2,1)}, bf16[4,48,1536]{2,1,0:T(8,128)(2,1)}, u32[]{:S(2)}, u32[]{:S(2)}) collective-permute-start(bf16[4,48,1536]{2,1,0:T(8,128)(2,1)} %get-tuple-element.178), channel_id=1, source_target_pairs={{0,1},{1,0},{2,3},{3,2},{4,5},{5,4},{6,7},{7,6},{8,9},{9,8},{10,11... | collective-permute-start | bytes 1769480 | tf_op jit(solution)/shard_map/ppermute | solution.py:658
  100.2 7.6 collective-permute-start.9
  111.3 143.7 %copy-start.74 = (bf16[32,48,128]{2,1,0:T(8,128)(2,1)S(1)}, bf16[32,48,128]{2,1,0:T(8,128)(2,1)}, u32[]{:S(2)}) copy-start(bf16[32,48,128]{2,1,0:T(8,128)(2,1)} %get-tuple-element.69) | copy-start | bytes 1179652
  256.8 41.6 %copy-start.83 = (f32[1536]{0:T(1024)}, f32[1536]{0:T(1024)S(1)}, u32[]{:S(2)}) copy-start(f32[1536]{0:T(1024)S(1)} %get-tuple-element.244) | copy-start | bytes 18436
  256.8 408.4 %copy-start.77 = (f32[1536]{0:T(1024)}, f32[1536]{0:T(1024)S(1)}, u32[]{:S(2)}) copy-start(f32[1536]{0:T(1024)S(1)} %get-tuple-element.134) | copy-start | bytes 18436
  264.5 5.8 copy-start.37
  265.6 7.3 copy-start.64
  265.6 9.3 collective-permute-start.2
  265.7 9.2 collective-permute-start.3
  267.3 13.9 %collective-permute-start.4 = (bf16[256,512]{1,0:T(8,128)(2,1)S(1)}, bf16[256,512]{1,0:T(8,128)(2,1)}, u32[]{:S(2)}, u32[]{:S(2)}) collective-permute-start(bf16[256,512]{1,0:T(8,128)(2,1)S(1)} %slice.253.refs_2_.refs_6_), channel_id=1, source_target_pairs={{0,24},{8,16},{16,8},{24,0},{1,25},{9,17},{17,9},{25,1},{2,26},{10... | collective-permute-start | bytes 786440 | tf_op jit(solution)/shard_map/ppermute | solution.py:97
  298.4 150.8 %copy-start.93 = (f32[256]{0:T(256)}, f32[256]{0:T(256)S(1)}, u32[]{:S(2)}) copy-start(f32[256]{0:T(256)S(1)} %add_rsqrt_fusion.3) | copy-start | bytes 3076
  451.9 12.1 copy-start.65
  460.4 9.5 copy-start.62
  460.4 19.7 %collective-permute-start.10 = (bf16[256,512]{1,0:T(8,128)(2,1)S(1)}, bf16[256,512]{1,0:T(8,128)(2,1)}, u32[]{:S(2)}, u32[]{:S(2)}) collective-permute-start(bf16[256,512]{1,0:T(8,128)(2,1)S(1)} %slice.267.refs_2_.refs_6_), channel_id=1, source_target_pairs={{0,8},{8,0},{16,24},{24,16},{1,9},{9,1},{17,25},{25,17},{2,10},{10... | collective-permute-start | bytes 786440 | tf_op jit(solution)/shard_map/ppermute | solution.py:97
  462.5 17.6 %collective-permute-start.11 = (bf16[256,512]{1,0:T(8,128)(2,1)S(1)}, bf16[256,512]{1,0:T(8,128)(2,1)}, u32[]{:S(2)}, u32[]{:S(2)}) collective-permute-start(bf16[256,512]{1,0:T(8,128)(2,1)S(1)} %slice.267.refs_2_.refs_6_), channel_id=1, source_target_pairs={{0,16},{8,24},{16,0},{24,8},{1,17},{9,25},{17,1},{25,9},{2,18},{10... | collective-permute-start | bytes 786440 | tf_op jit(solution)/shard_map/ppermute | solution.py:97
  462.6 17.5 %collective-permute-start.12 = (bf16[256,512]{1,0:T(8,128)(2,1)S(1)}, bf16[256,512]{1,0:T(8,128)(2,1)}, u32[]{:S(2)}, u32[]{:S(2)}) collective-permute-start(bf16[256,512]{1,0:T(8,128)(2,1)S(1)} %slice.267.refs_2_.refs_6_), channel_id=1, source_target_pairs={{0,24},{8,16},{16,8},{24,0},{1,25},{9,17},{17,9},{25,1},{2,26},{10... | collective-permute-start | bytes 786440 | tf_op jit(solution)/shard_map/ppermute | solution.py:97
  480.1 13.3 %copy-start.3 = (f32[256,1536]{1,0:T(8,128)S(1)}, f32[256,1536]{1,0:T(8,128)}, u32[]{:S(2)}) copy-start(f32[256,1536]{1,0:T(8,128)} %get-tuple-element.162.stream) | copy-start | bytes 4718596
  497.5 167.7 %copy-start.90 = (f32[256]{0:T(256)}, f32[256]{0:T(256)S(1)}, u32[]{:S(2)}) copy-start(f32[256]{0:T(256)S(1)} %add_rsqrt_fusion.2) | copy-start | bytes 3076
  710.6 10.1 collective-permute-start.13
  711.9 13.9 %collective-permute-start.14 = (bf16[256,4,128]{0,2,1:T(8,128)(2,1)}, bf16[256,4,128]{0,2,1:T(8,128)(2,1)}, u32[]{:S(2)}, u32[]{:S(2)}) collective-permute-start(bf16[256,4,128]{0,2,1:T(8,128)(2,1)} %get-tuple-element.190), channel_id=1, source_target_pairs={{16,0},{24,8},{0,16},{8,24},{17,1},{25,9},{1,17},{9,25},{18,2},{26... | collective-permute-start | bytes 786440 | tf_op jit(solution)/shard_map/ppermute | solution.py:97
  712.3 13.5 %collective-permute-start.15 = (bf16[256,4,128]{0,2,1:T(8,128)(2,1)}, bf16[256,4,128]{0,2,1:T(8,128)(2,1)}, u32[]{:S(2)}, u32[]{:S(2)}) collective-permute-start(bf16[256,4,128]{0,2,1:T(8,128)(2,1)} %get-tuple-element.189), channel_id=1, source_target_pairs={{24,0},{16,8},{8,16},{0,24},{25,1},{17,9},{9,17},{1,25},{26,2},{18... | collective-permute-start | bytes 786440 | tf_op jit(solution)/shard_map/ppermute | solution.py:97
  720.7 6.7 copy-start.25
  720.7 6.7 copy-start.89
  727.2 5.8 copy-start.70
  727.4 5.7 copy-start.72
  727.4 5.7 copy-start.2
  727.4 5.7 copy-start.4
  727.4 5.7 copy-start.6
  727.4 5.7 copy-start.14
  727.4 5.7 copy-start.55
  727.5 5.7 copy-start.78
  727.5 5.7 copy-start.91
  727.5 5.7 copy-start.103
  735.4 80.0 %copy-start.84 = (f32[1536]{0:T(1024)S(1)}, f32[1536]{0:T(1024)}, u32[]{:S(2)}) copy-start(f32[1536]{0:T(1024)} %copy-done.83) | copy-start | bytes 18436
  735.4 80.0 %copy-start.94 = (f32[256]{0:T(256)S(1)}, f32[256]{0:T(256)}, u32[]{:S(2)}) copy-start(f32[256]{0:T(256)} %copy-done.93) | copy-start | bytes 3076
  826.4 8.3 slice-start
  826.4 9.4 slice-start.2
  826.4 9.9 slice-start.1
  826.5 10.5 slice-start.3
  837.0 7.3 copy-start.49
  857.2 6.1 copy-start.92
  1020.0 5.6 copy-start.96
  1022.2 9.4 collective-permute-start.16
  1023.6 13.6 %collective-permute-start.17 = (bf16[256,4,128]{0,2,1:T(8,128)(2,1)}, bf16[256,4,128]{0,2,1:T(8,128)(2,1)S(1)}, u32[]{:S(2)}, u32[]{:S(2)}) collective-permute-start(bf16[256,4,128]{0,2,1:T(8,128)(2,1)} %get-tuple-element.183), channel_id=1, source_target_pairs={{16,0},{24,8},{0,16},{8,24},{17,1},{25,9},{1,17},{9,25},{18,2},{26... | collective-permute-start | bytes 786440 | tf_op jit(solution)/shard_map/ppermute | solution.py:97
  1024.2 13.6 %collective-permute-start.18 = (bf16[256,4,128]{0,2,1:T(8,128)(2,1)}, bf16[256,4,128]{0,2,1:T(8,128)(2,1)}, u32[]{:S(2)}, u32[]{:S(2)}) collective-permute-start(bf16[256,4,128]{0,2,1:T(8,128)(2,1)} %get-tuple-element.182), channel_id=1, source_target_pairs={{24,0},{16,8},{8,16},{0,24},{25,1},{17,9},{9,17},{1,25},{26,2},{18... | collective-permute-start | bytes 786440 | tf_op jit(solution)/shard_map/ppermute | solution.py:97
  1026.3 183.8 %collective-permute-start.22 = (bf16[4,24,1536]{2,1,0:T(8,128)(2,1)}, bf16[4,24,1536]{2,1,0:T(8,128)(2,1)}, u32[]{:S(2)}, u32[]{:S(2)}) collective-permute-start(bf16[4,24,1536]{2,1,0:T(8,128)(2,1)} %fusion.108), channel_id=1, source_target_pairs={{0,1},{1,0},{2,3},{3,2},{4,5},{5,4},{6,7},{7,6},{8,9},{9,8},{10,11... | collective-permute-start | bytes 884744 | tf_op jit(solution)/shard_map/ppermute | solution.py:658
  1028.7 10.5 copy-start.54
  1028.7 10.8 copy-start.27
  1028.7 191.2 %collective-permute-start.20 = (bf16[4,48,1536]{2,1,0:T(8,128)(2,1)}, bf16[4,48,1536]{2,1,0:T(8,128)(2,1)}, u32[]{:S(2)}, u32[]{:S(2)}) collective-permute-start(bf16[4,48,1536]{2,1,0:T(8,128)(2,1)} %fusion.75), channel_id=1, source_target_pairs={{0,1},{1,0},{2,3},{3,2},{4,5},{5,4},{6,7},{7,6},{8,9},{9,8},{10,11... | collective-permute-start | bytes 1769480 | tf_op jit(solution)/shard_map/ppermute | solution.py:658
  1029.3 11.3 copy-start.12
  1029.3 11.3 copy-start.87
  1031.5 5.6 copy-start.75
  1200.4 10.9 collective-permute-start.21
  1203.1 18.4 %collective-permute-start.19 = (bf16[4,48,1536]{2,1,0:T(8,128)(2,1)}, bf16[4,48,1536]{2,1,0:T(8,128)(2,1)}, u32[]{:S(2)}, u32[]{:S(2)}) collective-permute-start(bf16[4,48,1536]{2,1,0:T(8,128)(2,1)} %fusion.78), channel_id=1, source_target_pairs={{0,1},{1,0},{2,3},{3,2},{4,5},{5,4},{6,7},{7,6},{8,9},{9,8},{10,11... | collective-permute-start | bytes 1769480 | tf_op jit(solution)/shard_map/ppermute | solution.py:658
  1213.8 9.5 slice-start.6
  1213.8 9.5 slice-start.8
  (77 other events, 192.7 us)
